TPU v7x, 32 devices: a whole 2x2x4 slice. The times are simulated.
32 devices in a mesh: gx: 8 (over y, x, core), gy: 4 (over z).
Axes of the slice: x: 2, y: 2, z: 4, core: 2. Of those that a mesh axis runs over, the one named last changes fastest.
Arguments:
- sample_model_status: float32 [3, 80, 64, 1024], P(None, None, 'gy', 'gx'), may hold values from -6 to 6
- friction_rate: float32 [64, 1024], P('gy', 'gx'), may hold values from 0.02 to 0.3
- obs_value: float32 [24], replicated, may hold values from -6 to 6
- obs_error: float32 [24], replicated, may hold values from 0.25 to 2
- taper: float32 [7], replicated, may hold values from 0.2 to 1
- order: int32 [24], replicated, may hold values from 0 to 23, each once
- owner: int32 [24], replicated, may hold values from 0 to 31
- observation_cell: int32 [24], replicated, may hold values from 0 to 6143
- reach: int32 [24], replicated, may hold values from 0 to 6
Outputs:
- analysis: float32 [3, 80, 64, 1024], P(None, None, 'gy', 'gx')
Inputs may be any that keep to these rules, and one draw needn't show every extreme that they name: `order`: each observation index appears once. `owner`: device o stands at index o // 4 along gx and o % 4 along gy.
All inputs are finite; a program needn't handle non-finite values.
Results may differ from a plain program's by a relative error of at most 0.0001.
Values sent between devices are 32-bit elements; how exact they have to be, the bound alone decides.
No kernel may reach another device: no remote copies, remote signals or barrier semaphores. Data moves between devices by JAX's collectives and lax.ppermute only.
A program may use at most 64 MiB of HBM per device.

v0:
```python
import jax
import jax.numpy as jnp
from jax import lax
from jax.sharding import PartitionSpec as P

STEPS = 4
BATCHES = 3


courant = 0.4
coriolis = 0.1
epsilon = 1e-06
highest = lax.Precision.HIGHEST


def extended(block, sides, width):
    for axis, dim in sides:
        count = lax.axis_size(axis)
        forward = [(i, i + 1) for i in range(count - 1)]
        backward = [(target, source) for source, target in forward]
        low = lax.ppermute(
            lax.slice_in_dim(block, block.shape[dim] - width, None, axis=dim), axis, forward
        )
        high = lax.ppermute(lax.slice_in_dim(block, 0, width, axis=dim), axis, backward)
        block = jnp.concatenate([low, block, high], axis=dim)
    return block


def along_cols(field):
    padded = jnp.pad(field, ((0, 0), (0, 0), (1, 1)))
    return 0.5 * (padded[:, :, 2:] - padded[:, :, :-2])


def along_rows(field):
    padded = jnp.pad(field, ((0, 0), (1, 1), (0, 0)))
    return 0.5 * (padded[:, 2:, :] - padded[:, :-2, :])


def taper_weight(tile_x, tile_y, owner, reach, taper, rows_tiles):
    owner_x = owner // rows_tiles
    owner_y = owner % rows_tiles
    distance = jnp.maximum(jnp.abs(tile_x - owner_x), jnp.abs(tile_y - owner_y))
    vertical_levels = jnp.arange(taper.shape[0], dtype=jnp.int32)
    capped = jnp.minimum(distance, taper.shape[0] - 1)
    picked = jnp.sum(
        jnp.where(capped[..., None] == vertical_levels, taper, jnp.zeros_like(taper)), axis=-1
    )
    return jnp.where(distance <= reach, picked, jnp.zeros_like(picked))


def observe_step(priors, which, obs_value, obs_error):
    member_count = priors.shape[1]
    prior = priors[which]
    prior_mean = jnp.mean(prior)
    anomaly = prior - prior_mean
    variance = jnp.sum(anomaly * anomaly) / (member_count - 1) + epsilon
    error_var = obs_error[which]
    observed = obs_value[which]
    post_mean = (prior_mean * error_var + observed * variance) / (variance + error_var)
    shrink = jnp.sqrt(error_var / (variance + error_var))
    increment = post_mean - prior_mean + (shrink - 1.0) * anomaly
    scaled = 1.0 / ((member_count - 1) * variance)
    return (anomaly, increment, scaled)


def body(
    sample_model_status,
    friction_rate,
    obs_value,
    obs_error,
    taper,
    order,
    owner,
    observation_cell,
    reach,
):
    member_count = sample_model_status.shape[1]
    rows_local = sample_model_status.shape[2]
    cols_local = sample_model_status.shape[3]
    margin = 2 * STEPS
    padded = extended(sample_model_status, (("gy", 2), ("gx", 3)), margin)
    drag_pad = extended(friction_rate, (("gy", 0), ("gx", 1)), margin)
    row_ids = (
        lax.axis_index("gy") * rows_local
        - margin
        + jnp.arange(rows_local + 2 * margin, dtype=jnp.int32)
    )
    col_ids = (
        lax.axis_index("gx") * cols_local
        - margin
        + jnp.arange(cols_local + 2 * margin, dtype=jnp.int32)
    )
    row_ok = (row_ids >= 0) & (row_ids < rows_local * lax.axis_size("gy"))
    col_ok = (col_ids >= 0) & (col_ids < cols_local * lax.axis_size("gx"))
    inside_tile = (row_ok[:, None] & col_ok[None, :]).astype(jnp.float32)
    surface_height, flow_x, northward_current = (padded[0], padded[1], padded[2])
    for time_step in range(STEPS):
        surface_height = (
            surface_height - courant * (along_cols(flow_x) + along_rows(northward_current))
        ) * inside_tile
        new_x = (
            (1.0 - drag_pad) * flow_x
            - courant * along_cols(surface_height)
            + coriolis * northward_current
        ) * inside_tile
        new_y = (
            (1.0 - drag_pad) * northward_current
            - courant * along_rows(surface_height)
            - coriolis * flow_x
        ) * inside_tile
        flow_x, northward_current = (new_x, new_y)
    whole = jnp.stack([surface_height, flow_x, northward_current])
    sample_model_status = whole[:, :, margin : margin + rows_local, margin : margin + cols_local]
    myself_x = lax.axis_index("gx")
    mine_patch_north_index = lax.axis_index("gy")
    size_y = lax.axis_size("gy")
    myself = myself_x * size_y + mine_patch_north_index
    field_id = observation_cell // (rows_local * cols_local)
    place = observation_cell % (rows_local * cols_local)
    owned = (owner == myself)[:, None]
    owner_x = owner // size_y
    owner_y = owner % size_y
    obs_weights = taper_weight(
        owner_x[:, None], owner_y[:, None], owner[None, :], reach[None, :], taper, size_y
    )
    own_weights = taper_weight(myself_x, mine_patch_north_index, owner, reach, taper, size_y)
    identity = jnp.eye(member_count, dtype=jnp.float32)

    def advance(position, carry):
        priors, transform = carry
        which = order[position]
        anomaly, increment, scaled = observe_step(priors, which, obs_value, obs_error)
        along = jnp.dot(priors, anomaly, precision=highest)
        priors = priors + (obs_weights[:, which] * scaled * along)[:, None] * increment[None, :]
        mapped = jnp.dot(transform, anomaly, precision=highest)
        transform = transform + (own_weights[which] * scaled * mapped)[:, None] * increment[None, :]
        return (priors, transform)

    total_obs = order.shape[0]
    batch_size = total_obs // BATCHES
    priors = jnp.zeros((total_obs, member_count), jnp.float32)
    for batch_no in range(BATCHES):
        chosen = order[batch_no * batch_size : (batch_no + 1) * batch_size]
        flat = sample_model_status.reshape(3, member_count, rows_local * cols_local)
        picked = flat[field_id, :, place]
        collected = lax.psum(jnp.where(owned, picked, jnp.zeros_like(picked))[chosen], ("gx", "gy"))
        priors = priors.at[chosen].set(collected)
        priors, transform = lax.fori_loop(
            batch_no * batch_size, (batch_no + 1) * batch_size, advance, (priors, identity)
        )
        sample_model_status = jnp.einsum(
            "fmrc,mn->fnrc", sample_model_status, transform, precision=highest
        )
    return sample_model_status


def solution(mesh):
    in_specs = (P(None, None, "gy", "gx"), P("gy", "gx"), P(), P(), P(), P(), P(), P(), P())
    out_specs = P(None, None, "gy", "gx")
    return jax.shard_map(body, mesh=mesh, in_specs=in_specs, out_specs=out_specs, check_vma=False)
```

profile of v0, /device:TPU:0, one launch (start us, length us, event | category | flops | bytes accessed | tf_op | source)
XLA Modules:
  0.0 508.0 jit_solution(8739719796810620448)
XLA Ops:
  2.8 5.9 %collective-permute-start = (f32[3,80,8,128]{3,1,2,0:T(8,128)}, f32[3,80,8,128]{3,1,2,0:T(8,128)}, u32[]{:S(2)}, u32[]{:S(2)}) collective-permute-start(f32[3,80,8,128]{3,1,2,0:T(8,128)} %copy.83), channel_id=1, source_target_pairs={{0,1},{1,2},{2,3},{4,5},{5,6},{6,7},{8,9},{9,10},{10,11},{12,13},{... | collective-permute-start | bytes 2949128 | tf_op jit(solution)/shard_map/ppermute | solution.py:21
  10.2 4.5 collective-permute-start.4
  17.9 11.2 %collective-permute-done.4 = f32[8,128]{1,0:T(8,128)S(1)} collective-permute-done((f32[8,128]{1,0:T(8,128)S(1)}, f32[8,128]{1,0:T(8,128)S(1)}, u32[]{:S(2)}, u32[]{:S(2)}) %collective-permute-start.4) | collective-permute-done | bytes 4128 | tf_op jit(solution)/shard_map/ppermute | solution.py:21
  29.1 5.0 collective-permute-done.5
  37.4 4.4 fusion.73
  41.8 2.7 copy.53
  45.8 2.7 copy.54
  49.9 4.7 collective-permute-start.6
  56.2 2.7 collective-permute-done.7
  59.0 2.6 copy.55
  64.1 6.5 %pad_maximum_fusion = f32[3,80,32,144]{3,1,2,0:T(8,128)S(1)} fusion(f32[3,80,32,8]{3,1,2,0:T(8,128)} %copy.56, f32[3,80,32,128]{3,1,2,0:T(8,128)} %copy-done, f32[3,80,32,8]{3,1,2,0:T(8,128)} %copy.55), kind=kLoop, calls=%fused_computation.51 | loop fusion | flops 2211840 | bytes 8847360 | tf_op jit(solution)/shard_map/concatenate | solution.py:25
  72.5 2.6 add_multiply_fusion.2
  76.7 2.6 add_multiply_fusion.1
  80.9 2.6 add_multiply_fusion
  85.1 2.8 multiply_bitcast_fusion
  93.2 42.3 %psum.21 = f32[8,80]{1,0:T(8,128)S(1)} all-reduce(f32[8,80]{1,0:T(8,128)S(1)} %gather_fusion.1), channel_id=1, replica_groups=mesh['gx'=8,'gy'=4] {'gx','gy'}, use_global_device_ids=true, to_apply=%region_0.1 | all-reduce | flops 640 | bytes 5120 | tf_op jit(solution)/shard_map/psum | solution.py:146
  136.3 92.9 %while.55 = (s32[]{:T(128)}, f32[24,80]{1,0:T(8,128)S(1)}, f32[80,80]{1,0:T(8,128)S(1)}, s32[24]{0:T(128)S(1)}, f32[24,24]{0,1:T(8,128)S(1)}, /*index=5*/f32[24]...) while((s32[]{:T(128)}, f32[24,80]{1,0:T(8,128)S(1)}, ...), condition=%wide.region_7.8_spmd, body=%wide.region_4.7_spmd.sunk | while | flops 117105 | bytes 104103 | solution.py:148
  229.2 3.1 convolution_bitcast_fusion.8
  232.3 3.3 copy.75
  237.9 39.7 %psum.22 = f32[8,80]{1,0:T(8,128)S(1)} all-reduce(f32[8,80]{1,0:T(8,128)S(1)} %gather_fusion.3), channel_id=1, replica_groups=mesh['gx'=8,'gy'=4] {'gx','gy'}, use_global_device_ids=true, to_apply=%region_8.9 | all-reduce | flops 640 | bytes 5120 | tf_op jit(solution)/shard_map/psum | solution.py:146
  278.2 91.3 %while.56 = (s32[]{:T(128)}, f32[24,80]{1,0:T(8,128)S(1)}, f32[80,80]{1,0:T(8,128)S(1)}, s32[24]{0:T(128)S(1)}, f32[24,24]{0,1:T(8,128)S(1)}, /*index=5*/f32[24]...) while((s32[]{:T(128)}, f32[24,80]{1,0:T(8,128)S(1)}, ...), condition=%wide.region_13.14_spmd, body=%wide.region_10.13_spmd.sunk | while | flops 117109 | bytes 104165 | solution.py:148
  369.5 3.3 convolution_bitcast_fusion.7
  377.4 40.4 %psum.23 = f32[8,80]{1,0:T(8,128)S(1)} all-reduce(f32[8,80]{1,0:T(8,128)S(1)} %gather_fusion.5), channel_id=1, replica_groups=mesh['gx'=8,'gy'=4] {'gx','gy'}, use_global_device_ids=true, to_apply=%region_14.15 | all-reduce | flops 640 | bytes 5120 | tf_op jit(solution)/shard_map/psum | solution.py:146
  418.4 85.8 %while.57 = (s32[]{:T(128)}, f32[24,80]{1,0:T(8,128)S(1)}, f32[80,80]{1,0:T(8,128)S(1)}, s32[24]{0:T(128)S(1)}, f32[24,24]{0,1:T(8,128)S(1)}, /*index=5*/f32[24]...) while((s32[]{:T(128)}, f32[24,80]{1,0:T(8,128)S(1)}, ...), condition=%wide.region_19.20_spmd, body=%wide.region_16.19_spmd.sunk | while | flops 117109 | bytes 104165 | solution.py:148
  (366 shorter events, 145.8 us)
Async XLA Ops:
  1.7 14.5 %copy-start.10 = (s32[24]{0:T(128)S(1)}, s32[24]{0:T(128)}, u32[]{:S(2)}) copy-start(s32[24]{0:T(128)} %param.20) | copy-start | bytes 292
  1.7 14.6 %copy-start.15 = (s32[24]{0:T(128)S(1)}, s32[24]{0:T(128)}, u32[]{:S(2)}) copy-start(s32[24]{0:T(128)} %param.21) | copy-start | bytes 292
  1.7 14.7 %copy-start.14 = (f32[7]{0:T(128)S(1)}, f32[7]{0:T(128)}, u32[]{:S(2)}) copy-start(f32[7]{0:T(128)} %param.19) | copy-start | bytes 88
  1.7 14.9 %copy-start.12 = (s32[24]{0:T(128)S(1)}, s32[24]{0:T(128)}, u32[]{:S(2)}) copy-start(s32[24]{0:T(128)} %param.23) | copy-start | bytes 292
  1.7 33.7 %copy-start.5 = (f32[3,80,16,128]{3,2,1,0:T(8,128)S(1)}, f32[3,80,16,128]{3,2,1,0:T(8,128)}, u32[]{:S(2)}) copy-start(f32[3,80,16,128]{3,2,1,0:T(8,128)} %param.15) | copy-start | bytes 5898244
  2.8 31.3 %collective-permute-start = (f32[3,80,8,128]{3,1,2,0:T(8,128)}, f32[3,80,8,128]{3,1,2,0:T(8,128)}, u32[]{:S(2)}, u32[]{:S(2)}) collective-permute-start(f32[3,80,8,128]{3,1,2,0:T(8,128)} %copy.83), channel_id=1, source_target_pairs={{0,1},{1,2},{2,3},{4,5},{5,6},{6,7},{8,9},{9,10},{10,11},{12,13},{... | collective-permute-start | bytes 2949128 | tf_op jit(solution)/shard_map/ppermute | solution.py:21
  8.9 27.2 %collective-permute-start.1 = (f32[3,80,8,128]{3,1,2,0:T(8,128)S(1)}, f32[3,80,8,128]{3,1,2,0:T(8,128)}, u32[]{:S(2)}, u32[]{:S(2)}) collective-permute-start(f32[3,80,8,128]{3,1,2,0:T(8,128)S(1)} %copy.84), channel_id=1, source_target_pairs={{1,0},{2,1},{3,2},{5,4},{6,5},{7,6},{9,8},{10,9},{11,10},{13,12},{... | collective-permute-start | bytes 2949128 | tf_op jit(solution)/shard_map/ppermute | solution.py:24
  10.2 18.9 %collective-permute-start.4 = (f32[8,128]{1,0:T(8,128)S(1)}, f32[8,128]{1,0:T(8,128)S(1)}, u32[]{:S(2)}, u32[]{:S(2)}) collective-permute-start(f32[8,128]{1,0:T(8,128)S(1)} %get-tuple-element.823), channel_id=1, source_target_pairs={{0,1},{1,2},{2,3},{4,5},{5,6},{6,7},{8,9},{9,10},{10,11},{12,13},{... | collective-permute-start | bytes 12296 | tf_op jit(solution)/shard_map/ppermute | solution.py:21
  14.8 19.4 %collective-permute-start.5 = (f32[8,128]{1,0:T(8,128)S(1)}, f32[8,128]{1,0:T(8,128)S(1)}, u32[]{:S(2)}, u32[]{:S(2)}) collective-permute-start(f32[8,128]{1,0:T(8,128)S(1)} %get-tuple-element.822), channel_id=1, source_target_pairs={{1,0},{2,1},{3,2},{5,4},{6,5},{7,6},{9,8},{10,9},{11,10},{13,12},{... | collective-permute-start | bytes 12296 | tf_op jit(solution)/shard_map/ppermute | solution.py:24
  16.1 40.0 %copy-start.1 = (f32[80,80]{1,0:T(8,128)}, f32[80,80]{1,0:T(8,128)S(1)}, u32[]{:S(2)}) copy-start(f32[80,80]{1,0:T(8,128)S(1)} %fusion.62) | copy-start | bytes 76804
  16.3 19.8 %copy-start.7 = (s32[8]{0:T(128)}, s32[8]{0:T(128)S(1)}, u32[]{:S(2)}) copy-start(s32[8]{0:T(128)S(1)} %get-tuple-element.825) | copy-start | bytes 100
  16.3 19.8 %copy-start.13 = (s32[8]{0:T(128)}, s32[8]{0:T(128)S(1)}, u32[]{:S(2)}) copy-start(s32[8]{0:T(128)S(1)} %get-tuple-element.826) | copy-start | bytes 100
  44.5 14.5 %collective-permute-start.2 = (f32[3,80,32,8]{1,3,2,0:T(8,128)S(1)}, f32[3,80,32,8]{1,3,2,0:T(8,128)S(1)}, u32[]{:S(2)}, u32[]{:S(2)}) collective-permute-start(f32[3,80,32,8]{1,3,2,0:T(8,128)S(1)} %copy.53), channel_id=1, source_target_pairs={{0,4},{4,8},{8,12},{12,16},{16,20},{20,24},{24,28},{1,5},{5,9},{9,... | collective-permute-start | bytes 737288 | tf_op jit(solution)/shard_map/ppermute | solution.py:21
  48.5 13.1 %collective-permute-start.3 = (f32[3,80,32,8]{1,3,2,0:T(8,128)S(1)}, f32[3,80,32,8]{1,3,2,0:T(8,128)S(1)}, u32[]{:S(2)}, u32[]{:S(2)}) collective-permute-start(f32[3,80,32,8]{1,3,2,0:T(8,128)S(1)} %copy.54), channel_id=1, source_target_pairs={{4,0},{8,4},{12,8},{16,12},{20,16},{24,20},{28,24},{5,1},{9,5},{13... | collective-permute-start | bytes 737288 | tf_op jit(solution)/shard_map/ppermute | solution.py:24
  49.9 6.3 %collective-permute-start.6 = (f32[32,8]{1,0:T(8,128)S(1)}, f32[32,8]{1,0:T(8,128)S(1)}, u32[]{:S(2)}, u32[]{:S(2)}) collective-permute-start(f32[32,8]{1,0:T(8,128)S(1)} %get-tuple-element.820), channel_id=1, source_target_pairs={{0,4},{4,8},{8,12},{12,16},{16,20},{20,24},{24,28},{1,5},{5,9},{9,... | collective-permute-start | bytes 3080 | tf_op jit(solution)/shard_map/ppermute | solution.py:21
  54.6 4.3 collective-permute-start.7
  88.5 47.7 %copy-start.3 = (f32[80,80]{1,0:T(8,128)S(1)}, f32[80,80]{1,0:T(8,128)}, u32[]{:S(2)}) copy-start(f32[80,80]{1,0:T(8,128)} %copy-done.1) | copy-start | bytes 76804
  88.6 47.7 %copy-start.11 = (s32[24]{0:T(128)S(1)}, s32[24]{0:T(128)}, u32[]{:S(2)}) copy-start(s32[24]{0:T(128)} %param.20) | copy-start | bytes 292
  88.6 47.7 %copy-start.16 = (f32[24]{0:T(128)S(1)}, f32[24]{0:T(128)}, u32[]{:S(2)}) copy-start(f32[24]{0:T(128)} %compare_select_fusion.5) | copy-start | bytes 292
  88.6 47.7 %copy-start.18 = (f32[24]{0:T(128)S(1)}, f32[24]{0:T(128)}, u32[]{:S(2)}) copy-start(f32[24]{0:T(128)} %param.18) | copy-start | bytes 292
  88.6 47.7 %copy-start.19 = (f32[24]{0:T(128)S(1)}, f32[24]{0:T(128)}, u32[]{:S(2)}) copy-start(f32[24]{0:T(128)} %param.17) | copy-start | bytes 292
  232.3 45.3 %copy-start.8 = (s32[8]{0:T(128)S(1)}, s32[8]{0:T(128)}, u32[]{:S(2)}) copy-start(s32[8]{0:T(128)} %copy-done.7) | copy-start | bytes 100
  232.3 45.9 %copy-start.4 = (f32[80,80]{1,0:T(8,128)S(1)}, f32[80,80]{1,0:T(8,128)}, u32[]{:S(2)}) copy-start(f32[80,80]{1,0:T(8,128)} %copy-done.1) | copy-start | bytes 76804
  372.9 45.5 %copy-start.2 = (f32[80,80]{1,0:T(8,128)S(1)}, f32[80,80]{1,0:T(8,128)}, u32[]{:S(2)}) copy-start(f32[80,80]{1,0:T(8,128)} %copy-done.1) | copy-start | bytes 76804
  (4 other events, 31.5 us)
where the time goes:
time: 511 us; the launch traced here: 508 us
  loops' own time  166 us (32%)
  blocking collectives  122 us (24%)
  local copies, waits for them, and re-layouts  102 us (20%)
  other arithmetic  61.3 us (12%)
  starting transfers between devices  21.8 us (4%)
  waiting for transfers between devices  19 us (4%)
  matrix products  15 us (3%)
    another operation x3, loops' own time, body(): lax.fori_loop(batch_no * batch_size, (batch_no + 1) * batch_size, advance...  166 us
    psum x3, blocking collectives, body(): lax.psum(jnp.where(owned, picked, jnp.zeros_like(picked))[chosen], ('gx',...  122 us
    ppermute x4, starting transfers between devices, extended(): lax.ppermute(lax.slice_in_dim(block, block.shape[dim] - width, None, axis...  16.5 us
    dynamic_slice x24, local copies, waits for them, and re-layouts, observe_step(): observed = obs_value[which]  16.1 us
    reduce_sum x24, other arithmetic, observe_step(): variance = jnp.sum(anomaly * anomaly) / (member_count - 1) + epsilon  15.8 us
    reduce_sum x24, other arithmetic, observe_step(): prior_mean = jnp.mean(prior)  15.7 us
    dynamic_slice x24, local copies, waits for them, and re-layouts, advance(): which = order[position]  15.6 us
    dynamic_slice x24, local copies, waits for them, and re-layouts, advance(): own_weights[which] * scaled * mapped  15.3 us
  transfers between devices with their start and end apart: 8, of which 3 were waited for; matrix products, arithmetic and copies ran while one was open for 2% of the time, Pallas kernels for 0%

commit v1 on v0

v1 whole, which is shorter than its diff:
```python
import functools

import jax
import jax.numpy as jnp
from jax import lax
from jax.experimental import pallas as pl
from jax.experimental.pallas import tpu as pltpu
from jax.sharding import PartitionSpec as P

STEPS = 4
MARGIN = 2 * STEPS
EPS = 1e-06
NT = (((1,), (1,)), ((), ()))
HIGHEST = lax.Precision.HIGHEST
F32 = jnp.float32
BF16 = jnp.bfloat16
VMEM_LIMIT = 48 * 1024 * 1024

VSPEC = pl.BlockSpec(memory_space=pltpu.VMEM)
SSPEC = pl.BlockSpec(memory_space=pltpu.SMEM)


def lanes_of(shape):
    return lax.broadcasted_iota(jnp.int32, shape, len(shape) - 1)


def sublanes_of(shape):
    return lax.broadcasted_iota(jnp.int32, shape, len(shape) - 2)


def roll_lanes(x, shift):
    size = x.shape[-1]
    shift = shift % size
    return x if shift == 0 else pltpu.roll(x, shift, x.ndim - 1)


def pack_kernel(members, rows, x_ref, drag_ref, left_ref, right_ref):
    cols = x_ref.shape[1]
    lane = lanes_of((8, cols))
    count = 3 * members

    def group(g, carry):
        left = jnp.zeros((8, cols), F32)
        right = jnp.zeros((8, cols), F32)
        for r in range(rows):
            row = x_ref[pl.ds(g * 8 * rows + r, 8, stride=rows), :]
            here = (lane >= MARGIN * r) & (lane < MARGIN * (r + 1))
            left = jnp.where(here, roll_lanes(row, MARGIN * r), left)
            right = jnp.where(here, roll_lanes(row, MARGIN * (r + 1)), right)
        left_ref[pl.ds(pl.multiple_of(g * 8, 8), 8), :] = left
        right_ref[pl.ds(pl.multiple_of(g * 8, 8), 8), :] = right
        return carry

    lax.fori_loop(0, count // 8, group, 0)
    left = jnp.zeros((8, cols), F32)
    right = jnp.zeros((8, cols), F32)
    for r in range(rows):
        row = jnp.broadcast_to(drag_ref[r : r + 1, :], (8, cols))
        here = (lane >= MARGIN * r) & (lane < MARGIN * (r + 1))
        left = jnp.where(here, roll_lanes(row, MARGIN * r), left)
        right = jnp.where(here, roll_lanes(row, MARGIN * (r + 1)), right)
    left_ref[count : count + 8, :] = left
    right_ref[count : count + 8, :] = right


def pack(x, drag, members):
    rows, cols = drag.shape
    out = jax.ShapeDtypeStruct((3 * members + 8, cols), F32)
    return pl.pallas_call(
        functools.partial(pack_kernel, members, rows),
        out_shape=(out, out),
        in_specs=[VSPEC, VSPEC],
        out_specs=(VSPEC, VSPEC),
        compiler_params=pltpu.CompilerParams(vmem_limit_bytes=VMEM_LIMIT),
    )(x, drag)


def wide_row(lane, main, left, left_at, right, right_at):
    cols = main.shape[1]
    halo = jnp.where(lane >= cols - MARGIN, roll_lanes(left, cols - MARGIN - left_at), 0.0)
    halo = jnp.where(lane < MARGIN, roll_lanes(right, -right_at), halo)
    return jnp.concatenate([main, halo], axis=1)


def forecast_kernel(
    members, rows,
    place_ref, order_ref, owner_ref, cell_ref,
    x_ref, above_ref, below_ref, left_ref, right_ref, cabove_ref, cbelow_ref,
    drag_ref, dabove_ref, dbelow_ref,
    out_ref, prior_ref,
    state, keep, slope,
):
    cols = x_ref.shape[1]
    wide = 2 * cols
    total = rows + 2 * MARGIN
    lane = lanes_of((8, cols))
    half = cols // 2
    count = 3 * members

    wlane = lanes_of((8, wide))
    first_x, last_x = place_ref[1], place_ref[2]
    first_y, last_y = place_ref[3], place_ref[4]
    outside = ((first_x == 1) & (wlane >= wide - MARGIN)) | ((last_x == 1) & (wlane >= cols) & (wlane < cols + MARGIN))
    unused = (wlane >= cols + MARGIN) & (wlane < wide - MARGIN)
    factor = jnp.where(outside | unused, 0.0, -0.2)
    for r in range(total):
        if r < MARGIN:
            main = dabove_ref[r : r + 1, :]
            left, la = cabove_ref[count : count + 8, :], MARGIN * r
            right, ra = left, half + MARGIN * r
            ok = jnp.where(first_y == 1, 0.0, 1.0)
        elif r < MARGIN + rows:
            main = drag_ref[r - MARGIN : r - MARGIN + 1, :]
            left, la = left_ref[count : count + 8, :], MARGIN * (r - MARGIN)
            right, ra = right_ref[count : count + 8, :], MARGIN * (r - MARGIN)
            ok = 1.0
        else:
            main = dbelow_ref[r - MARGIN - rows : r - MARGIN - rows + 1, :]
            left, la = cbelow_ref[count : count + 8, :], MARGIN * (r - MARGIN - rows)
            right, ra = left, half + MARGIN * (r - MARGIN - rows)
            ok = jnp.where(last_y == 1, 0.0, 1.0)
        main = jnp.broadcast_to(main, (8, cols))
        keep[r] = 1.0 - wide_row(lane, main, left, la, right, ra)
        slope[r] = factor * ok

    def group(g, carry):
        for f in range(3):
            at = f * members + g * 8
            at8 = pl.multiple_of(at, 8)
            ledge, redge = left_ref[pl.ds(at8, 8), :], right_ref[pl.ds(at8, 8), :]
            cab, cbe = cabove_ref[pl.ds(at8, 8), :], cbelow_ref[pl.ds(at8, 8), :]
            for r in range(total):
                if r < MARGIN:
                    main = above_ref[pl.ds(at * MARGIN + r, 8, stride=MARGIN), :]
                    value = wide_row(lane, main, cab, MARGIN * r, cab, half + MARGIN * r)
                elif r < MARGIN + rows:
                    q = r - MARGIN
                    main = x_ref[pl.ds(at * rows + q, 8, stride=rows), :]
                    value = wide_row(lane, main, ledge, MARGIN * q, redge, MARGIN * q)
                else:
                    q = r - MARGIN - rows
                    main = below_ref[pl.ds(at * MARGIN + q, 8, stride=MARGIN), :]
                    value = wide_row(lane, main, cbe, MARGIN * q, cbe, half + MARGIN * q)
                state[f, r] = value
        for step in range(STEPS):
            reach = 2 * (STEPS - step) - 1
            for r in range(MARGIN - reach, MARGIN + rows + reach):
                u = state[1, r]
                div = (roll_lanes(u, -1) - roll_lanes(u, 1)) + (state[2, r + 1] - state[2, r - 1])
                state[0, r] = state[0, r] + slope[r] * div
            reach -= 1
            for r in range(MARGIN - reach, MARGIN + rows + reach):
                h = state[0, r]
                u, v = state[1, r], state[2, r]
                k, c = keep[r], slope[r]
                state[1, r] = k * u + c * (roll_lanes(h, -1) - roll_lanes(h, 1)) + 0.1 * v
                state[2, r] = k * v + c * (state[0, r + 1] - state[0, r - 1]) - 0.1 * u
        for f in range(3):
            for r in range(rows):
                out_ref[f * rows + r, pl.ds(pl.multiple_of(g * 8, 8), 8), :] = state[f, MARGIN + r, :, 0:cols]
        return carry

    lax.fori_loop(0, members // 8, group, 0)

    prior_ref[...] = jnp.zeros_like(prior_ref)
    for i in range(order_ref.shape[0]):
        which = order_ref[i]

        @pl.when(owner_ref[which] == place_ref[0])
        def _():
            cell = cell_ref[which]
            column = cell % cols
            one = jnp.where(lane == column, 1.0, 0.0)
            prior_ref[i : i + 1, 0:members] = lax.dot_general(
                one, out_ref[cell // cols], NT, precision=HIGHEST, preferred_element_type=F32
            )[0:1]


def forecast(place, order, owner, cell, x, above, below, left, right, cabove, cbelow, drag, dabove, dbelow, members):
    rows, cols = drag.shape
    total = rows + 2 * MARGIN
    return pl.pallas_call(
        functools.partial(forecast_kernel, members, rows),
        out_shape=(
            jax.ShapeDtypeStruct((3 * rows, members, cols), F32),
            jax.ShapeDtypeStruct((order.shape[0], cols), F32),
        ),
        in_specs=[SSPEC] * 4 + [VSPEC] * 10,
        out_specs=(VSPEC, VSPEC),
        scratch_shapes=[
            pltpu.VMEM((3, total, 8, 2 * cols), F32),
            pltpu.VMEM((total, 8, 2 * cols), F32),
            pltpu.VMEM((total, 8, 2 * cols), F32),
        ],
        compiler_params=pltpu.CompilerParams(vmem_limit_bytes=VMEM_LIMIT),
    )(place, order, owner, cell, x, above, below, left, right, cabove, cbelow, drag, dabove, dbelow)


def localize(distance, reach, taper_ref):
    picked = jnp.zeros(distance.shape, F32)
    levels = taper_ref.shape[0]
    capped = jnp.minimum(distance, levels - 1)
    for d in range(levels):
        picked = jnp.where(capped == d, taper_ref[d], picked)
    return jnp.where(distance <= reach, picked, 0.0)


def assimilate_kernel(
    members, rows,
    place_ref, order_ref, owner_ref, reach_ref, value_ref, error_ref, taper_ref,
    prior_ref, forecast_ref,
    out_ref,
):
    n_obs = order_ref.shape[0]
    cols = prior_ref.shape[1]
    size_y = place_ref[5]
    lane1 = lanes_of((1, cols))
    lane = lanes_of((n_obs, cols))
    sub = sublanes_of((n_obs, cols))

    tile_row = jnp.zeros((1, cols), jnp.int32)
    tile_col = jnp.zeros((n_obs, cols), jnp.int32)
    reach_row = jnp.zeros((1, cols), jnp.int32)
    reach_col = jnp.zeros((n_obs, cols), jnp.int32)
    which = [order_ref[i] for i in range(n_obs)]
    for i, k in enumerate(which):
        tile_row = jnp.where(lane1 == i, owner_ref[k], tile_row)
        tile_col = jnp.where(sub == i, owner_ref[k], tile_col)
        reach_row = jnp.where(lane1 == i, reach_ref[k], reach_row)
        reach_col = jnp.where(sub == i, reach_ref[k], reach_col)
    rx, ry = tile_row // size_y, tile_row % size_y
    cx, cy = tile_col // size_y, tile_col % size_y
    distance = jnp.maximum(jnp.abs(cx - rx), jnp.abs(cy - ry))
    onto = localize(distance, reach_row, taper_ref)
    onto_t = localize(distance, reach_col, taper_ref)
    mine = place_ref[0]
    own = localize(
        jnp.maximum(jnp.abs(mine // size_y - rx), jnp.abs(mine % size_y - ry)), reach_row, taper_ref
    )

    priors = prior_ref[...]
    inside = lane < members
    mean_col = jnp.sum(jnp.where(inside, priors, 0.0), axis=1, keepdims=True) / members
    anomalies = jnp.where(inside, priors - mean_col, 0.0)
    padded = jnp.concatenate([anomalies, jnp.zeros((cols - n_obs, cols), F32)], axis=0)
    unit = jnp.where(lanes_of((members, cols)) == sublanes_of((members, cols)), 1.0, 0.0)
    table = lax.dot_general(
        jnp.concatenate([anomalies, unit], axis=0), padded, NT, precision=HIGHEST, preferred_element_type=F32
    )
    mean = jnp.zeros((1, cols), F32)
    for i in range(n_obs):
        mean = jnp.where(lane1 == i, mean_col[i : i + 1, :], mean)

    scales = jnp.zeros((1, cols), F32)
    increments = []
    for i, k in enumerate(which):
        error = error_ref[k]
        row = table[i : i + 1, :]
        column = table[:, i : i + 1]
        power = row[:, i : i + 1]
        variance = power / (members - 1) + EPS
        inverse = 1.0 / (variance + error)
        scaled = 1.0 / ((members - 1) * variance)
        shift = variance * (value_ref[k] - mean[:, i : i + 1]) * inverse
        shrink = jnp.sqrt(error * inverse) - 1.0
        weight = scaled * own[:, i : i + 1]
        alpha_row = onto_t[i : i + 1, :] * row * scaled
        later = lane1 > i
        h = jnp.where(later, shrink * alpha_row, 0.0)
        q = jnp.where(later, shrink * (row + h * power), 0.0)
        alpha = jnp.concatenate(
            [onto[:, i : i + 1] * column[:n_obs] * scaled, column[n_obs:] * weight], axis=0
        )
        table = table + column * h + alpha * q
        mean = mean + alpha_row * shift
        now = anomalies[i : i + 1, :]
        increments.append(shift + shrink * now)
        anomalies = anomalies + jnp.where(sub > i, shrink * alpha[:n_obs], 0.0) * now
        scales = jnp.where(lane1 == i, weight, scales)
    left = table[n_obs:, :] * scales
    right = jnp.where(inside, jnp.concatenate(increments, axis=0), 0.0)
    right = jnp.concatenate([right, jnp.zeros((cols - n_obs, cols), F32)], axis=0)
    change = jnp.dot(left, right, precision=HIGHEST, preferred_element_type=F32)
    change = jnp.concatenate([change, jnp.zeros((cols - members, cols), F32)], axis=0)
    change = jnp.transpose(change)[:members, :]
    high = change.astype(BF16).astype(F32)
    low = change - high
    zero = jnp.zeros((members, cols), F32)
    high = jnp.concatenate([high, zero], axis=1)
    low = jnp.concatenate([low, zero], axis=1)
    factor = (high + roll_lanes(high, members) + roll_lanes(low, 2 * members)).astype(BF16)

    block = 4
    for at in range(0, 3 * rows, block):
        x = jnp.concatenate([forecast_ref[at + b] for b in range(block)], axis=1)
        xh = x.astype(BF16)
        xl = (x - xh.astype(F32)).astype(BF16)
        stack = jnp.concatenate([xh, xl, xh, jnp.zeros((2 * cols - 3 * members, block * cols), BF16)], axis=0)
        y = x + jnp.dot(factor, stack, preferred_element_type=F32)
        for b in range(block):
            f, r = divmod(at + b, rows)
            out_ref[pl.ds(f * members * rows + r, members, stride=rows), :] = y[:, b * cols : (b + 1) * cols]


def assimilate(place, order, owner, reach, value, error, taper, priors, states, members, rows):
    cols = priors.shape[1]
    return pl.pallas_call(
        functools.partial(assimilate_kernel, members, rows),
        out_shape=jax.ShapeDtypeStruct((3 * members * rows, cols), F32),
        in_specs=[SSPEC] * 7 + [VSPEC] * 2,
        out_specs=VSPEC,
        compiler_params=pltpu.CompilerParams(vmem_limit_bytes=VMEM_LIMIT),
    )(place, order, owner, reach, value, error, taper, priors, states)


def to_neighbours(axis, lower, upper):
    count = lax.axis_size(axis)
    forward = [(i, i + 1) for i in range(count - 1)]
    backward = [(target, source) for source, target in forward]
    return lax.ppermute(upper, axis, forward), lax.ppermute(lower, axis, backward)


def add_over(x, axes):
    for axis in axes:
        count = lax.axis_size(axis)
        if count & (count - 1):
            x = lax.psum(x, axis)
            continue
        span = 1
        while span < count:
            x = x + lax.ppermute(x, axis, [(i, i ^ span) for i in range(count)])
            span *= 2
    return x


def body(status, drag, value, error, taper, order, owner, cell, reach):
    members, rows, cols = status.shape[1:]
    ix, iy = lax.axis_index("gx"), lax.axis_index("gy")
    size_x, size_y = lax.axis_size("gx"), lax.axis_size("gy")
    place = jnp.stack(
        [
            ix * size_y + iy,
            (ix == 0).astype(jnp.int32),
            (ix == size_x - 1).astype(jnp.int32),
            (iy == 0).astype(jnp.int32),
            (iy == size_y - 1).astype(jnp.int32),
            jnp.int32(size_y),
        ]
    ).astype(jnp.int32)
    flat = status.reshape(3 * members * rows, cols)
    upper = status[:, :, rows - MARGIN :, :].reshape(-1, cols)
    lower = status[:, :, :MARGIN, :].reshape(-1, cols)
    above, below = to_neighbours("gy", lower, upper)
    first, last = pack(flat, drag, members)
    left, right = to_neighbours("gx", first, last)
    half = cols // 2
    count = left.shape[0]
    small_lower = jnp.concatenate(
        [jnp.concatenate([left[:, :half], right[:, :half]], axis=1), drag[:MARGIN]], axis=0
    )
    small_upper = jnp.concatenate(
        [jnp.concatenate([left[:, half:], right[:, half:]], axis=1), drag[rows - MARGIN :]], axis=0
    )
    cabove, cbelow = to_neighbours("gy", small_lower, small_upper)
    states, priors = forecast(
        place, order, owner, cell, flat, above, below, left, right, cabove, cbelow,
        drag, cabove[count:], cbelow[count:], members,
    )
    priors = add_over(priors, ("gx", "gy"))
    result = assimilate(place, order, owner, reach, value, error, taper, priors, states, members, rows)
    return result.reshape(status.shape)


def solution(mesh):
    in_specs = (P(None, None, "gy", "gx"), P("gy", "gx"), P(), P(), P(), P(), P(), P(), P())
    out_specs = P(None, None, "gy", "gx")
    return jax.shard_map(body, mesh=mesh, in_specs=in_specs, out_specs=out_specs, check_vma=False)
```

time: 511 us -> 80.8 us (0.16)
  loops' own time: 166 us -> 0 us
  blocking collectives: 122 us -> 0 us
  local copies, waits for them, and re-layouts: 102 us -> 3.63 us
  other arithmetic: 61.3 us -> 1.53 us
  Pallas kernels: 0 us -> 21.8 us
  matrix products: 15 us -> 0 us
  waiting for transfers between devices: 19 us -> 27.7 us
    another operation x3 -> x0, loops' own time: 166 us -> none  [body(): lax.fori_loop(batch_no * batch_size, (batch_no + 1) * batch_size, advance...]
    psum x3 -> x0, blocking collectives: 122 us -> none  [body(): lax.psum(jnp.where(owned, picked, jnp.zeros_like(picked))[chosen], ('gx',...]
    dynamic_slice x96 -> x0, local copies, waits for them, and re-layouts: 62.2 us -> none  [the longest x24 16.1 us: observe_step(): observed = obs_value[which]]
    reduce_sum x50 -> x0, other arithmetic: 31.7 us -> none  [the longest x24 15.8 us: observe_step(): variance = jnp.sum(anomaly * anomaly) / (member_count - 1) + epsilon]
    pallas_call x0 -> x3, Pallas kernels: none -> 21.8 us  [the longest x1 12.3 us: forecast(): pl.pallas_call(functools.partial(forecast_kernel, members, rows), out_sha...]
    dot_general x51 -> x0, matrix products: 15 us -> none  [the longest x3 8.24 us: body(): jnp.einsum('fmrc,mn->fnrc', sample_model_status, transform, precision=hig...]
    mul x31 -> x0, other arithmetic: 14.2 us -> none  [the longest x3 7.85 us: body(): ((1.0 - drag_pad) * flow_x - courant * along_cols(surface_height) + corio...]
    slice x6, local copies, waits for them, and re-layouts: 11.5 us -> 1.26 us  [the longest x1 1.07 us: body(): lower = status[:, :, :MARGIN, :].reshape(-1, cols)]
  transfers between devices with their start and end apart: 8 -> 11, of which waited for: 3 -> 7; matrix products, arithmetic and copies ran while one was open for 2% -> 4% of each run, Pallas kernels for 0% -> 0%
where the time goes in v1:
time: 80.8 us; the launch traced here: 80.5 us
  waiting for transfers between devices  27.7 us (34%)
  starting transfers between devices  25.5 us (32%)
  Pallas kernels  21.8 us (27%)
  local copies, waits for them, and re-layouts  3.63 us (4%)
  other arithmetic  1.53 us (2%)
    ppermute x3, waiting for transfers between devices, to_neighbours(): lax.ppermute(upper, axis, forward)  14.7 us
    pallas_call x1, Pallas kernels, forecast(): pl.pallas_call(functools.partial(forecast_kernel, members, rows), out_sha...  12.3 us
    ppermute x3, starting transfers between devices, to_neighbours(): lax.ppermute(upper, axis, forward)  11.3 us
    ppermute x5, starting transfers between devices, add_over(): x = x + lax.ppermute(x, axis, [(i, i ^ span) for i in range(count)])  10.2 us
    ppermute x5, waiting for transfers between devices, add_over(): x = x + lax.ppermute(x, axis, [(i, i ^ span) for i in range(count)])  8.56 us
    pallas_call x1, Pallas kernels, assimilate(): pl.pallas_call(functools.partial(assimilate_kernel, members, rows), out_s...  6.38 us
    ppermute x3, waiting for transfers between devices, to_neighbours(): lax.ppermute(lower, axis, backward)  4.46 us
    ppermute x3, starting transfers between devices, to_neighbours(): lax.ppermute(lower, axis, backward)  4 us
  transfers between devices with their start and end apart: 11, of which 7 were waited for; matrix products, arithmetic and copies ran while one was open for 4% of the time, Pallas kernels for 0%

profile of v1, /device:TPU:0, one launch (start us, length us, event | category | flops | bytes accessed | tf_op | source)
XLA Modules:
  0.0 80.5 jit_solution(3244855672813630642)
XLA Ops:
  0.0 1.5 %copy-done = f32[3,80,16,128]{3,2,1,0:T(8,128)S(1)} copy-done((f32[3,80,16,128]{3,2,1,0:T(8,128)S(1)}, f32[3,80,16,128]{3,2,1,0:T(8,128)}, u32[]{:S(2)}) %copy-start) | copy-done | bytes 1966104
  2.2 3.2 %shard_map.91 = (f32[248,128]{1,0:T(8,128)S(1)}, f32[248,128]{1,0:T(8,128)S(1)}) custom-call(f32[3840,128]{1,0:T(8,128)S(1)} %bitcast.10, f32[16,128]{1,0:T(8,128)S(1)} %copy-done.1), custom_call_target="tpu_custom_call" | custom-call | tf_op jit(solution)/shard_map/pallas_call | solution.py:69
  5.4 2.4 %collective-permute-start.2 = (f32[248,128]{1,0:T(8,128)S(1)}, f32[248,128]{1,0:T(8,128)S(1)}, u32[]{:S(2)}, u32[]{:S(2)}) collective-permute-start(f32[248,128]{1,0:T(8,128)S(1)} %get-tuple-element.9), channel_id=1, source_target_pairs={{0,4},{4,8},{8,12},{12,16},{16,20},{20,24},{24,28},{1,5},{5,9},{9,... | collective-permute-start | bytes 380936 | tf_op jit(solution)/shard_map/ppermute | solution.py:320
  7.9 1.4 %collective-permute-start.3 = (f32[248,128]{1,0:T(8,128)S(1)}, f32[248,128]{1,0:T(8,128)S(1)}, u32[]{:S(2)}, u32[]{:S(2)}) collective-permute-start(f32[248,128]{1,0:T(8,128)S(1)} %get-tuple-element.10), channel_id=1, source_target_pairs={{4,0},{8,4},{12,8},{16,12},{20,16},{24,20},{28,24},{5,1},{9,5},{13... | collective-permute-start | bytes 380936 | tf_op jit(solution)/shard_map/ppermute | solution.py:320
  9.3 1.1 %fusion = (f32[3,80,8,128]{3,2,1,0:T(8,128)S(1)}, f32[3,80,8,128]{3,2,1,0:T(8,128)}) fusion(f32[3,80,16,128]{3,2,1,0:T(8,128)S(1)} %copy-done), kind=kLoop, calls=%fused_computation.2 | loop fusion | bytes 3932160 | tf_op jit(solution)/shard_map/slice | solution.py:352
  10.4 4.4 %collective-permute-start = (f32[1920,128]{1,0:T(8,128)}, f32[1920,128]{1,0:T(8,128)S(1)}, u32[]{:S(2)}, u32[]{:S(2)}) collective-permute-start(f32[1920,128]{1,0:T(8,128)} %bitcast.6), channel_id=1, source_target_pairs={{0,1},{1,2},{2,3},{4,5},{5,6},{6,7},{8,9},{9,10},{10,11},{12,13},{... | collective-permute-start | bytes 2949128 | tf_op jit(solution)/shard_map/ppermute | solution.py:320
  14.7 1.3 %collective-permute-start.1 = (f32[1920,128]{1,0:T(8,128)S(1)}, f32[1920,128]{1,0:T(8,128)S(1)}, u32[]{:S(2)}, u32[]{:S(2)}) collective-permute-start(f32[1920,128]{1,0:T(8,128)S(1)} %bitcast.11), channel_id=1, source_target_pairs={{1,0},{2,1},{3,2},{5,4},{6,5},{7,6},{9,8},{10,9},{11,10},{13,12},{... | collective-permute-start | bytes 2949128 | tf_op jit(solution)/shard_map/ppermute | solution.py:320
  16.3 0.8 pad_maximum_fusion
  17.0 4.5 %collective-permute-start.4 = (f32[256,128]{1,0:T(8,128)}, f32[256,128]{1,0:T(8,128)S(1)}, u32[]{:S(2)}, u32[]{:S(2)}) collective-permute-start(f32[256,128]{1,0:T(8,128)} %pad_maximum_fusion), channel_id=1, source_target_pairs={{0,1},{1,2},{2,3},{4,5},{5,6},{6,7},{8,9},{9,10},{10,11},{12,13},{... | collective-permute-start | bytes 393224 | tf_op jit(solution)/shard_map/ppermute | solution.py:320
  22.3 1.3 %collective-permute-start.5 = (f32[256,128]{1,0:T(8,128)}, f32[256,128]{1,0:T(8,128)S(1)}, u32[]{:S(2)}, u32[]{:S(2)}) collective-permute-start(f32[256,128]{1,0:T(8,128)} %pad_maximum_fusion.1), channel_id=1, source_target_pairs={{1,0},{2,1},{3,2},{5,4},{6,5},{7,6},{9,8},{10,9},{11,10},{13,12},{... | collective-permute-start | bytes 393224 | tf_op jit(solution)/shard_map/ppermute | solution.py:320
  23.7 14.7 %collective-permute-done.4.cabove_ref = f32[256,128]{1,0:T(8,128)S(1)} collective-permute-done((f32[256,128]{1,0:T(8,128)}, f32[256,128]{1,0:T(8,128)S(1)}, u32[]{:S(2)}, u32[]{:S(2)}) %collective-permute-start.4) | collective-permute-done | bytes 131104 | tf_op jit(solution)/shard_map/ppermute | solution.py:320
  38.4 4.5 %collective-permute-done.5.cbelow_ref = f32[256,128]{1,0:T(8,128)S(1)} collective-permute-done((f32[256,128]{1,0:T(8,128)}, f32[256,128]{1,0:T(8,128)S(1)}, u32[]{:S(2)}, u32[]{:S(2)}) %collective-permute-start.5) | collective-permute-done | bytes 131104 | tf_op jit(solution)/shard_map/ppermute | solution.py:320
  43.0 12.3 %shard_map.92 = (f32[48,80,128]{2,1,0:T(8,128)S(1)}, f32[24,128]{1,0:T(8,128)S(1)}) custom-call(s32[6]{0:T(128)S(1)} %stack.39.place_ref, s32[24]{0:T(128)S(1)} %copy-done.3, s32[24]{0:T(128)S(1)} %copy-done.4, s32[24]{0:T(128)S(1)} %copy-done.5, f32[3840,128]{1,0:T(8,128)} %bitcast.9, f32[1920,128]{1,0:T(8,128)S(1)} %collective-permute-done.above_ref, ...), custom_call_target="tpu_custom_call" | custom-call | tf_op jit(solution)/shard_map/pallas_call | solution.py:182
  55.2 1.0 %collective-permute-start.6 = (f32[24,128]{1,0:T(8,128)S(1)}, f32[24,128]{1,0:T(8,128)S(1)}, u32[]{:S(2)}, u32[]{:S(2)}) collective-permute-start(f32[24,128]{1,0:T(8,128)S(1)} %get-tuple-element.11), channel_id=1, source_target_pairs={{0,4},{4,0},{8,12},{12,8},{16,20},{20,16},{24,28},{28,24},{1,5},{5... | collective-permute-start | bytes 36872 | tf_op jit(solution)/shard_map/ppermute | solution.py:331
  56.2 0.8 %collective-permute-done.6 = f32[24,128]{1,0:T(8,128)S(1)} collective-permute-done((f32[24,128]{1,0:T(8,128)S(1)}, f32[24,128]{1,0:T(8,128)S(1)}, u32[]{:S(2)}, u32[]{:S(2)}) %collective-permute-start.6) | collective-permute-done | bytes 12320 | tf_op jit(solution)/shard_map/ppermute | solution.py:331
  57.1 3.2 %collective-permute-start.7 = (f32[24,128]{1,0:T(8,128)S(1)}, f32[24,128]{1,0:T(8,128)S(1)}, u32[]{:S(2)}, u32[]{:S(2)}) collective-permute-start(f32[24,128]{1,0:T(8,128)S(1)} %add.19), channel_id=1, source_target_pairs={{0,8},{4,12},{8,0},{12,4},{16,24},{20,28},{24,16},{28,20},{1,9},{5... | collective-permute-start | bytes 36872 | tf_op jit(solution)/shard_map/ppermute | solution.py:331
  60.2 1.7 %collective-permute-done.7 = f32[24,128]{1,0:T(8,128)S(1)} collective-permute-done((f32[24,128]{1,0:T(8,128)S(1)}, f32[24,128]{1,0:T(8,128)S(1)}, u32[]{:S(2)}, u32[]{:S(2)}) %collective-permute-start.7) | collective-permute-done | bytes 12320 | tf_op jit(solution)/shard_map/ppermute | solution.py:331
  61.9 2.2 %collective-permute-start.8 = (f32[24,128]{1,0:T(8,128)S(1)}, f32[24,128]{1,0:T(8,128)S(1)}, u32[]{:S(2)}, u32[]{:S(2)}) collective-permute-start(f32[24,128]{1,0:T(8,128)S(1)} %add.20), channel_id=1, source_target_pairs={{0,16},{4,20},{8,24},{12,28},{16,0},{20,4},{24,8},{28,12},{1,17},{... | collective-permute-start | bytes 36872 | tf_op jit(solution)/shard_map/ppermute | solution.py:331
  64.1 1.7 %collective-permute-done.8 = f32[24,128]{1,0:T(8,128)S(1)} collective-permute-done((f32[24,128]{1,0:T(8,128)S(1)}, f32[24,128]{1,0:T(8,128)S(1)}, u32[]{:S(2)}, u32[]{:S(2)}) %collective-permute-start.8) | collective-permute-done | bytes 12320 | tf_op jit(solution)/shard_map/ppermute | solution.py:331
  65.8 1.5 %collective-permute-start.9 = (f32[24,128]{1,0:T(8,128)S(1)}, f32[24,128]{1,0:T(8,128)S(1)}, u32[]{:S(2)}, u32[]{:S(2)}) collective-permute-start(f32[24,128]{1,0:T(8,128)S(1)} %add.21), channel_id=1, source_target_pairs={{0,1},{1,0},{2,3},{3,2},{4,5},{5,4},{6,7},{7,6},{8,9},{9,8},{10,11... | collective-permute-start | bytes 36872 | tf_op jit(solution)/shard_map/ppermute | solution.py:331
  67.2 2.2 %collective-permute-done.9 = f32[24,128]{1,0:T(8,128)S(1)} collective-permute-done((f32[24,128]{1,0:T(8,128)S(1)}, f32[24,128]{1,0:T(8,128)S(1)}, u32[]{:S(2)}, u32[]{:S(2)}) %collective-permute-start.9) | collective-permute-done | bytes 12320 | tf_op jit(solution)/shard_map/ppermute | solution.py:331
  69.5 2.4 %collective-permute-start.10 = (f32[24,128]{1,0:T(8,128)S(1)}, f32[24,128]{1,0:T(8,128)S(1)}, u32[]{:S(2)}, u32[]{:S(2)}) collective-permute-start(f32[24,128]{1,0:T(8,128)S(1)} %add.22), channel_id=1, source_target_pairs={{0,2},{1,3},{2,0},{3,1},{4,6},{5,7},{6,4},{7,5},{8,10},{9,11},{10,... | collective-permute-start | bytes 36872 | tf_op jit(solution)/shard_map/ppermute | solution.py:331
  71.9 2.1 %collective-permute-done.10 = f32[24,128]{1,0:T(8,128)S(1)} collective-permute-done((f32[24,128]{1,0:T(8,128)S(1)}, f32[24,128]{1,0:T(8,128)S(1)}, u32[]{:S(2)}, u32[]{:S(2)}) %collective-permute-start.10) | collective-permute-done | bytes 12320 | tf_op jit(solution)/shard_map/ppermute | solution.py:331
  74.1 6.4 %shard_map.93 = f32[3840,128]{1,0:T(8,128)} custom-call(s32[6]{0:T(128)S(1)} %stack.39.place_ref, s32[24]{0:T(128)S(1)} %copy-done.3, s32[24]{0:T(128)S(1)} %copy-done.4, s32[24]{0:T(128)S(1)} %copy-done.6, f32[24]{0:T(128)S(1)} %copy-done.7, f32[24]{0:T(128)S(1)} %copy-done.8, f32[7]{0:T(128)S(1)} %copy-done.9, f32[24,128]{1,0:T(8,128)S(1)} %add.23.prior_ref, ...), custom_call_target="tpu_custom_call" | custom-call | tf_op jit(solution)/shard_map/pallas_call | solution.py:307
  (35 shorter events, 1.8 us)
Async XLA Ops:
  0.0 1.5 %copy-start = (f32[3,80,16,128]{3,2,1,0:T(8,128)S(1)}, f32[3,80,16,128]{3,2,1,0:T(8,128)}, u32[]{:S(2)}) copy-start(f32[3,80,16,128]{3,2,1,0:T(8,128)} %param.9) | copy-start | bytes 5898244
  1.5 0.7 copy-start.1
  5.4 10.7 %collective-permute-start.2 = (f32[248,128]{1,0:T(8,128)S(1)}, f32[248,128]{1,0:T(8,128)S(1)}, u32[]{:S(2)}, u32[]{:S(2)}) collective-permute-start(f32[248,128]{1,0:T(8,128)S(1)} %get-tuple-element.9), channel_id=1, source_target_pairs={{0,4},{4,8},{8,12},{12,16},{16,20},{20,24},{24,28},{1,5},{5,9},{9,... | collective-permute-start | bytes 380936 | tf_op jit(solution)/shard_map/ppermute | solution.py:320
  7.8 35.1 %copy-start.2 = (f32[16,128]{1,0:T(8,128)S(1)}, f32[16,128]{1,0:T(8,128)}, u32[]{:S(2)}) copy-start(f32[16,128]{1,0:T(8,128)} %drag_ref.3) | copy-start | bytes 24580
  7.8 35.1 %copy-start.3 = (s32[24]{0:T(128)S(1)}, s32[24]{0:T(128)}, u32[]{:S(2)}) copy-start(s32[24]{0:T(128)} %order_ref.3) | copy-start | bytes 292
  7.8 35.1 %copy-start.4 = (s32[24]{0:T(128)S(1)}, s32[24]{0:T(128)}, u32[]{:S(2)}) copy-start(s32[24]{0:T(128)} %owner_ref.3) | copy-start | bytes 292
  7.8 35.1 %copy-start.5 = (s32[24]{0:T(128)S(1)}, s32[24]{0:T(128)}, u32[]{:S(2)}) copy-start(s32[24]{0:T(128)} %cell_ref.1) | copy-start | bytes 292
  7.9 8.2 %collective-permute-start.3 = (f32[248,128]{1,0:T(8,128)S(1)}, f32[248,128]{1,0:T(8,128)S(1)}, u32[]{:S(2)}, u32[]{:S(2)}) collective-permute-start(f32[248,128]{1,0:T(8,128)S(1)} %get-tuple-element.10), channel_id=1, source_target_pairs={{4,0},{8,4},{12,8},{16,12},{20,16},{24,20},{28,24},{5,1},{9,5},{13... | collective-permute-start | bytes 380936 | tf_op jit(solution)/shard_map/ppermute | solution.py:320
  10.4 32.6 %collective-permute-start = (f32[1920,128]{1,0:T(8,128)}, f32[1920,128]{1,0:T(8,128)S(1)}, u32[]{:S(2)}, u32[]{:S(2)}) collective-permute-start(f32[1920,128]{1,0:T(8,128)} %bitcast.6), channel_id=1, source_target_pairs={{0,1},{1,2},{2,3},{4,5},{5,6},{6,7},{8,9},{9,10},{10,11},{12,13},{... | collective-permute-start | bytes 2949128 | tf_op jit(solution)/shard_map/ppermute | solution.py:320
  14.7 28.2 %collective-permute-start.1 = (f32[1920,128]{1,0:T(8,128)S(1)}, f32[1920,128]{1,0:T(8,128)S(1)}, u32[]{:S(2)}, u32[]{:S(2)}) collective-permute-start(f32[1920,128]{1,0:T(8,128)S(1)} %bitcast.11), channel_id=1, source_target_pairs={{1,0},{2,1},{3,2},{5,4},{6,5},{7,6},{9,8},{10,9},{11,10},{13,12},{... | collective-permute-start | bytes 2949128 | tf_op jit(solution)/shard_map/ppermute | solution.py:320
  17.0 21.4 %collective-permute-start.4 = (f32[256,128]{1,0:T(8,128)}, f32[256,128]{1,0:T(8,128)S(1)}, u32[]{:S(2)}, u32[]{:S(2)}) collective-permute-start(f32[256,128]{1,0:T(8,128)} %pad_maximum_fusion), channel_id=1, source_target_pairs={{0,1},{1,2},{2,3},{4,5},{5,6},{6,7},{8,9},{9,10},{10,11},{12,13},{... | collective-permute-start | bytes 393224 | tf_op jit(solution)/shard_map/ppermute | solution.py:320
  22.3 20.6 %collective-permute-start.5 = (f32[256,128]{1,0:T(8,128)}, f32[256,128]{1,0:T(8,128)S(1)}, u32[]{:S(2)}, u32[]{:S(2)}) collective-permute-start(f32[256,128]{1,0:T(8,128)} %pad_maximum_fusion.1), channel_id=1, source_target_pairs={{1,0},{2,1},{3,2},{5,4},{6,5},{7,6},{9,8},{10,9},{11,10},{13,12},{... | collective-permute-start | bytes 393224 | tf_op jit(solution)/shard_map/ppermute | solution.py:320
  42.9 31.2 %copy-start.6 = (s32[24]{0:T(128)S(1)}, s32[24]{0:T(128)}, u32[]{:S(2)}) copy-start(s32[24]{0:T(128)} %reach_ref.1) | copy-start | bytes 292
  42.9 31.2 %copy-start.7 = (f32[24]{0:T(128)S(1)}, f32[24]{0:T(128)}, u32[]{:S(2)}) copy-start(f32[24]{0:T(128)} %value_ref.1) | copy-start | bytes 292
  42.9 31.2 %copy-start.8 = (f32[24]{0:T(128)S(1)}, f32[24]{0:T(128)}, u32[]{:S(2)}) copy-start(f32[24]{0:T(128)} %error_ref.1) | copy-start | bytes 292
  42.9 31.2 %copy-start.9 = (f32[7]{0:T(128)S(1)}, f32[7]{0:T(128)}, u32[]{:S(2)}) copy-start(f32[7]{0:T(128)} %taper_ref.1) | copy-start | bytes 88
  55.2 1.8 %collective-permute-start.6 = (f32[24,128]{1,0:T(8,128)S(1)}, f32[24,128]{1,0:T(8,128)S(1)}, u32[]{:S(2)}, u32[]{:S(2)}) collective-permute-start(f32[24,128]{1,0:T(8,128)S(1)} %get-tuple-element.11), channel_id=1, source_target_pairs={{0,4},{4,0},{8,12},{12,8},{16,20},{20,16},{24,28},{28,24},{1,5},{5... | collective-permute-start | bytes 36872 | tf_op jit(solution)/shard_map/ppermute | solution.py:331
  57.1 4.8 %collective-permute-start.7 = (f32[24,128]{1,0:T(8,128)S(1)}, f32[24,128]{1,0:T(8,128)S(1)}, u32[]{:S(2)}, u32[]{:S(2)}) collective-permute-start(f32[24,128]{1,0:T(8,128)S(1)} %add.19), channel_id=1, source_target_pairs={{0,8},{4,12},{8,0},{12,4},{16,24},{20,28},{24,16},{28,20},{1,9},{5... | collective-permute-start | bytes 36872 | tf_op jit(solution)/shard_map/ppermute | solution.py:331
  61.9 3.8 %collective-permute-start.8 = (f32[24,128]{1,0:T(8,128)S(1)}, f32[24,128]{1,0:T(8,128)S(1)}, u32[]{:S(2)}, u32[]{:S(2)}) collective-permute-start(f32[24,128]{1,0:T(8,128)S(1)} %add.20), channel_id=1, source_target_pairs={{0,16},{4,20},{8,24},{12,28},{16,0},{20,4},{24,8},{28,12},{1,17},{... | collective-permute-start | bytes 36872 | tf_op jit(solution)/shard_map/ppermute | solution.py:331
  65.8 3.7 %collective-permute-start.9 = (f32[24,128]{1,0:T(8,128)S(1)}, f32[24,128]{1,0:T(8,128)S(1)}, u32[]{:S(2)}, u32[]{:S(2)}) collective-permute-start(f32[24,128]{1,0:T(8,128)S(1)} %add.21), channel_id=1, source_target_pairs={{0,1},{1,0},{2,3},{3,2},{4,5},{5,4},{6,7},{7,6},{8,9},{9,8},{10,11... | collective-permute-start | bytes 36872 | tf_op jit(solution)/shard_map/ppermute | solution.py:331
  69.5 4.6 %collective-permute-start.10 = (f32[24,128]{1,0:T(8,128)S(1)}, f32[24,128]{1,0:T(8,128)S(1)}, u32[]{:S(2)}, u32[]{:S(2)}) collective-permute-start(f32[24,128]{1,0:T(8,128)S(1)} %add.22), channel_id=1, source_target_pairs={{0,2},{1,3},{2,0},{3,1},{4,6},{5,7},{6,4},{7,5},{8,10},{9,11},{10,... | collective-permute-start | bytes 36872 | tf_op jit(solution)/shard_map/ppermute | solution.py:331

commit v2 on v1

--- a/solution.py
+++ b/solution.py
@@ -14,7 +14,7 @@
 HIGHEST = lax.Precision.HIGHEST
 F32 = jnp.float32
 BF16 = jnp.bfloat16
-VMEM_LIMIT = 48 * 1024 * 1024
+VMEM_LIMIT = 24 * 1024 * 1024
 
 VSPEC = pl.BlockSpec(memory_space=pltpu.VMEM)
 SSPEC = pl.BlockSpec(memory_space=pltpu.SMEM)
@@ -34,45 +34,131 @@
     return x if shift == 0 else pltpu.roll(x, shift, x.ndim - 1)
 
 
-def pack_kernel(members, rows, x_ref, drag_ref, left_ref, right_ref):
+def arrange_kernel(members, rows, x_ref, out_ref, lower_ref, upper_ref, left_ref, right_ref):
     cols = x_ref.shape[1]
     lane = lanes_of((8, cols))
-    count = 3 * members
 
     def group(g, carry):
-        left = jnp.zeros((8, cols), F32)
-        right = jnp.zeros((8, cols), F32)
-        for r in range(rows):
-            row = x_ref[pl.ds(g * 8 * rows + r, 8, stride=rows), :]
-            here = (lane >= MARGIN * r) & (lane < MARGIN * (r + 1))
-            left = jnp.where(here, roll_lanes(row, MARGIN * r), left)
-            right = jnp.where(here, roll_lanes(row, MARGIN * (r + 1)), right)
-        left_ref[pl.ds(pl.multiple_of(g * 8, 8), 8), :] = left
-        right_ref[pl.ds(pl.multiple_of(g * 8, 8), 8), :] = right
+        here = pl.ds(pl.multiple_of(g * 8, 8), 8)
+        for f in range(3):
+            left = jnp.zeros((8, cols), F32)
+            right = jnp.zeros((8, cols), F32)
+            depth = MARGIN if f == 2 else MARGIN - 1
+            for r in range(rows):
+                row = x_ref[pl.ds((f * members + g * 8) * rows + r, 8, stride=rows), :]
+                out_ref[f * rows + r, here, :] = row
+                if r < depth:
+                    lower_ref[f * (MARGIN - 1) + r, here, :] = row
+                if r >= rows - depth:
+                    upper_ref[f * (MARGIN - 1) + r - rows + depth, here, :] = row
+                there = (lane >= MARGIN * r) & (lane < MARGIN * (r + 1))
+                left = jnp.where(there, roll_lanes(row, MARGIN * r), left)
+                right = jnp.where(there, roll_lanes(row, MARGIN * (r + 1)), right)
+            at = pl.ds(pl.multiple_of(f * members + g * 8, 8), 8)
+            left_ref[at, :] = left
+            right_ref[at, :] = right
         return carry
 
-    lax.fori_loop(0, count // 8, group, 0)
-    left = jnp.zeros((8, cols), F32)
-    right = jnp.zeros((8, cols), F32)
-    for r in range(rows):
-        row = jnp.broadcast_to(drag_ref[r : r + 1, :], (8, cols))
-        here = (lane >= MARGIN * r) & (lane < MARGIN * (r + 1))
-        left = jnp.where(here, roll_lanes(row, MARGIN * r), left)
-        right = jnp.where(here, roll_lanes(row, MARGIN * (r + 1)), right)
-    left_ref[count : count + 8, :] = left
-    right_ref[count : count + 8, :] = right
-
-
-def pack(x, drag, members):
-    rows, cols = drag.shape
-    out = jax.ShapeDtypeStruct((3 * members + 8, cols), F32)
+    lax.fori_loop(0, members // 8, group, 0)
+
+
+def arrange(x, members, rows):
+    cols = x.shape[1]
+    edge = jax.ShapeDtypeStruct((3 * members, cols), F32)
+    band = jax.ShapeDtypeStruct((3 * MARGIN - 2, members, cols), F32)
     return pl.pallas_call(
-        functools.partial(pack_kernel, members, rows),
-        out_shape=(out, out),
-        in_specs=[VSPEC, VSPEC],
+        functools.partial(arrange_kernel, members, rows),
+        out_shape=(jax.ShapeDtypeStruct((3 * rows, members, cols), F32), band, band, edge, edge),
+        in_specs=[VSPEC],
+        out_specs=(VSPEC,) * 5,
+        compiler_params=pltpu.CompilerParams(vmem_limit_bytes=VMEM_LIMIT),
+        cost_estimate=pl.CostEstimate(flops=4_000_000, bytes_accessed=6_000_000, transcendentals=0),
+    )(x)
+
+
+def grid_factor(place_ref, shape, rows, cols):
+    row, col = sublanes_of(shape), lanes_of(shape)
+    wide = 2 * cols
+    low, high = jnp.where(place_ref[3] == 1, MARGIN, 0), jnp.where(place_ref[4] == 1, MARGIN + rows, rows + 2 * MARGIN)
+    first, last = jnp.where(place_ref[1] == 1, wide, wide - MARGIN), jnp.where(place_ref[2] == 1, cols, cols + MARGIN)
+    ok = (row >= low) & (row < high) & ((col < last) | (col >= first))
+    return jnp.where(ok, 1.0, 0.0)
+
+
+def share_kernel(
+    members, rows,
+    place_ref, order_ref, owner_ref, cell_ref, state_ref, drag_ref, even_ref, odd_ref,
+    keep_ref, prior_ref, turned,
+):
+    cols = drag_ref.shape[1]
+    wide = 2 * cols
+    total = rows + 2 * MARGIN
+    size_y = place_ref[5]
+    ix, iy = place_ref[0] // size_y, place_ref[0] % size_y
+    shape = (total, wide)
+    lane = lanes_of((total, cols))
+    odd = (ix % 2) == 1
+    even_part, odd_part = even_ref[...], odd_ref[...]
+    before = jnp.where(odd, even_part, odd_part)
+    after = jnp.where(odd, odd_part, even_part)
+    drag = jnp.concatenate([drag_ref[...], jnp.where(lane < cols // 2, after, before)], axis=1)
+    keep = 1.0 - drag
+    keep_ref[...] = keep
+    slope = 0.2 * grid_factor(place_ref, shape, rows, cols)
+    sub, wlane = sublanes_of(shape), lanes_of(shape)
+    turned[...] = jnp.zeros_like(turned)
+    spot = lanes_of((members, cols))
+
+    def one(i, carry):
+        k = order_ref[i]
+        tile, cell = owner_ref[k], cell_ref[k]
+        field, inner = cell // (rows * cols), cell % (rows * cols)
+        row = (tile % size_y - iy) * rows + inner // cols
+        col = (tile // size_y - ix) * cols + inner % cols
+        near = (row >= -MARGIN) & (row < rows + MARGIN) & (col >= -MARGIN) & (col < cols + MARGIN)
+
+        @pl.when(near)
+        def _():
+            at = jnp.where(col < 0, col + wide, col)
+            start = jnp.where((sub == row + MARGIN) & (wlane == at), 1.0, 0.0)
+            h = jnp.where(field == 0, start, 0.0)
+            u = jnp.where(field == 1, start, 0.0)
+            v = jnp.where(field == 2, start, 0.0)
+            for _step in range(STEPS):
+                h = h + slope * (
+                    (roll_lanes(u, -1) - roll_lanes(u, 1)) + (pltpu.roll(v, total - 1, 0) - pltpu.roll(v, 1, 0))
+                )
+                u, v = (
+                    keep * u + slope * (roll_lanes(h, -1) - roll_lanes(h, 1)) - 0.1 * v,
+                    keep * v + slope * (pltpu.roll(h, total - 1, 0) - pltpu.roll(h, 1, 0)) + 0.1 * u,
+                )
+            sums = jnp.zeros((members, cols), F32)
+            for f, weights in enumerate((h, u, v)):
+                for r in range(rows):
+                    sums = sums + weights[MARGIN + r : MARGIN + r + 1, :cols] * state_ref[f * rows + r]
+            column = jnp.sum(sums, axis=1, keepdims=True)
+            turned[0:members, :] = jnp.where(spot == i, column, turned[0:members, :])
+
+        return carry
+
+    lax.fori_loop(0, order_ref.shape[0], one, 0)
+    prior_ref[...] = jnp.transpose(turned[...])[: prior_ref.shape[0]]
+
+
+def share(place, order, owner, cell, states, drag, even, odd, members, rows):
+    cols = drag.shape[1]
+    return pl.pallas_call(
+        functools.partial(share_kernel, members, rows),
+        out_shape=(
+            jax.ShapeDtypeStruct((drag.shape[0], 2 * cols), F32),
+            jax.ShapeDtypeStruct((order.shape[0], cols), F32),
+        ),
+        in_specs=[SSPEC] * 4 + [VSPEC] * 4,
         out_specs=(VSPEC, VSPEC),
+        scratch_shapes=[pltpu.VMEM((cols, cols), F32)],
         compiler_params=pltpu.CompilerParams(vmem_limit_bytes=VMEM_LIMIT),
-    )(x, drag)
+        cost_estimate=pl.CostEstimate(flops=6_000_000, bytes_accessed=2_000_000, transcendentals=0),
+    )(place, order, owner, cell, states, drag, even, odd)
 
 
 def wide_row(lane, main, left, left_at, right, right_at):
@@ -84,62 +170,38 @@
 
 def forecast_kernel(
     members, rows,
-    place_ref, order_ref, owner_ref, cell_ref,
-    x_ref, above_ref, below_ref, left_ref, right_ref, cabove_ref, cbelow_ref,
-    drag_ref, dabove_ref, dbelow_ref,
-    out_ref, prior_ref,
+    place_ref, state_ref, above_ref, below_ref, left_ref, right_ref, cabove_ref, cbelow_ref, keep_ref,
+    out_ref,
     state, keep, slope,
 ):
-    cols = x_ref.shape[1]
+    cols = state_ref.shape[2]
     wide = 2 * cols
     total = rows + 2 * MARGIN
     lane = lanes_of((8, cols))
     half = cols // 2
-    count = 3 * members
-
-    wlane = lanes_of((8, wide))
-    first_x, last_x = place_ref[1], place_ref[2]
-    first_y, last_y = place_ref[3], place_ref[4]
-    outside = ((first_x == 1) & (wlane >= wide - MARGIN)) | ((last_x == 1) & (wlane >= cols) & (wlane < cols + MARGIN))
-    unused = (wlane >= cols + MARGIN) & (wlane < wide - MARGIN)
-    factor = jnp.where(outside | unused, 0.0, -0.2)
+    factor = -0.2 * grid_factor(place_ref, (total, wide), rows, cols)
     for r in range(total):
-        if r < MARGIN:
-            main = dabove_ref[r : r + 1, :]
-            left, la = cabove_ref[count : count + 8, :], MARGIN * r
-            right, ra = left, half + MARGIN * r
-            ok = jnp.where(first_y == 1, 0.0, 1.0)
-        elif r < MARGIN + rows:
-            main = drag_ref[r - MARGIN : r - MARGIN + 1, :]
-            left, la = left_ref[count : count + 8, :], MARGIN * (r - MARGIN)
-            right, ra = right_ref[count : count + 8, :], MARGIN * (r - MARGIN)
-            ok = 1.0
-        else:
-            main = dbelow_ref[r - MARGIN - rows : r - MARGIN - rows + 1, :]
-            left, la = cbelow_ref[count : count + 8, :], MARGIN * (r - MARGIN - rows)
-            right, ra = left, half + MARGIN * (r - MARGIN - rows)
-            ok = jnp.where(last_y == 1, 0.0, 1.0)
-        main = jnp.broadcast_to(main, (8, cols))
-        keep[r] = 1.0 - wide_row(lane, main, left, la, right, ra)
-        slope[r] = factor * ok
+        keep[r] = jnp.broadcast_to(keep_ref[r : r + 1, :], (8, wide))
+        slope[r] = jnp.broadcast_to(factor[r : r + 1, :], (8, wide))
 
     def group(g, carry):
+        here = pl.ds(pl.multiple_of(g * 8, 8), 8)
         for f in range(3):
-            at = f * members + g * 8
-            at8 = pl.multiple_of(at, 8)
-            ledge, redge = left_ref[pl.ds(at8, 8), :], right_ref[pl.ds(at8, 8), :]
-            cab, cbe = cabove_ref[pl.ds(at8, 8), :], cbelow_ref[pl.ds(at8, 8), :]
-            for r in range(total):
+            at = pl.ds(pl.multiple_of(f * members + g * 8, 8), 8)
+            ledge, redge = left_ref[at, :], right_ref[at, :]
+            cab, cbe = cabove_ref[at, :], cbelow_ref[at, :]
+            depth = MARGIN if f == 2 else MARGIN - 1
+            for r in range(MARGIN - depth, MARGIN + rows + depth):
                 if r < MARGIN:
-                    main = above_ref[pl.ds(at * MARGIN + r, 8, stride=MARGIN), :]
+                    main = above_ref[f * (MARGIN - 1) + r - MARGIN + depth, here, :]
                     value = wide_row(lane, main, cab, MARGIN * r, cab, half + MARGIN * r)
                 elif r < MARGIN + rows:
                     q = r - MARGIN
-                    main = x_ref[pl.ds(at * rows + q, 8, stride=rows), :]
+                    main = state_ref[f * rows + q, here, :]
                     value = wide_row(lane, main, ledge, MARGIN * q, redge, MARGIN * q)
                 else:
                     q = r - MARGIN - rows
-                    main = below_ref[pl.ds(at * MARGIN + q, 8, stride=MARGIN), :]
+                    main = below_ref[f * (MARGIN - 1) + q, here, :]
                     value = wide_row(lane, main, cbe, MARGIN * q, cbe, half + MARGIN * q)
                 state[f, r] = value
         for step in range(STEPS):
@@ -157,43 +219,29 @@
                 state[2, r] = k * v + c * (state[0, r + 1] - state[0, r - 1]) - 0.1 * u
         for f in range(3):
             for r in range(rows):
-                out_ref[f * rows + r, pl.ds(pl.multiple_of(g * 8, 8), 8), :] = state[f, MARGIN + r, :, 0:cols]
+                out_ref[f * rows + r, here, :] = state[f, MARGIN + r, :, 0:cols]
         return carry
 
     lax.fori_loop(0, members // 8, group, 0)
 
-    prior_ref[...] = jnp.zeros_like(prior_ref)
-    for i in range(order_ref.shape[0]):
-        which = order_ref[i]
-
-        @pl.when(owner_ref[which] == place_ref[0])
-        def _():
-            cell = cell_ref[which]
-            column = cell % cols
-            one = jnp.where(lane == column, 1.0, 0.0)
-            prior_ref[i : i + 1, 0:members] = lax.dot_general(
-                one, out_ref[cell // cols], NT, precision=HIGHEST, preferred_element_type=F32
-            )[0:1]
-
-
-def forecast(place, order, owner, cell, x, above, below, left, right, cabove, cbelow, drag, dabove, dbelow, members):
-    rows, cols = drag.shape
+
+def forecast(place, states, above, below, left, right, cabove, cbelow, keep):
+    members, cols = states.shape[1:]
+    rows = states.shape[0] // 3
     total = rows + 2 * MARGIN
     return pl.pallas_call(
         functools.partial(forecast_kernel, members, rows),
-        out_shape=(
-            jax.ShapeDtypeStruct((3 * rows, members, cols), F32),
-            jax.ShapeDtypeStruct((order.shape[0], cols), F32),
-        ),
-        in_specs=[SSPEC] * 4 + [VSPEC] * 10,
-        out_specs=(VSPEC, VSPEC),
+        out_shape=jax.ShapeDtypeStruct(states.shape, F32),
+        in_specs=[SSPEC] + [VSPEC] * 8,
+        out_specs=VSPEC,
         scratch_shapes=[
             pltpu.VMEM((3, total, 8, 2 * cols), F32),
             pltpu.VMEM((total, 8, 2 * cols), F32),
             pltpu.VMEM((total, 8, 2 * cols), F32),
         ],
         compiler_params=pltpu.CompilerParams(vmem_limit_bytes=VMEM_LIMIT),
-    )(place, order, owner, cell, x, above, below, left, right, cabove, cbelow, drag, dabove, dbelow)
+        cost_estimate=pl.CostEstimate(flops=60_000_000, bytes_accessed=30_000_000, transcendentals=0),
+    )(place, states, above, below, left, right, cabove, cbelow, keep)
 
 
 def localize(distance, reach, taper_ref):
@@ -320,6 +368,16 @@
     return lax.ppermute(upper, axis, forward), lax.ppermute(lower, axis, backward)
 
 
+def swap_pairs(x, axis):
+    count = lax.axis_size(axis)
+
+    def swap(start):
+        pairs = [(i, i + 1) for i in range(start, count - 1, 2)]
+        return lax.ppermute(x, axis, pairs + [(b, a) for a, b in pairs])
+
+    return swap(0), swap(1)
+
+
 def add_over(x, axes):
     for axis in axes:
         count = lax.axis_size(axis)
@@ -348,24 +406,22 @@
         ]
     ).astype(jnp.int32)
     flat = status.reshape(3 * members * rows, cols)
-    upper = status[:, :, rows - MARGIN :, :].reshape(-1, cols)
-    lower = status[:, :, :MARGIN, :].reshape(-1, cols)
+    even, odd = swap_pairs(drag, "gy")
+    is_odd = (iy % 2) == 1
+    above = jnp.where(is_odd, even[rows - MARGIN :], odd[rows - MARGIN :])
+    below = jnp.where(is_odd, odd[:MARGIN], even[:MARGIN])
+    drag = jnp.concatenate([above, drag, below], axis=0)
+    even, odd = swap_pairs(drag, "gx")
+
+    states, lower, upper, first, last = arrange(flat, members, rows)
     above, below = to_neighbours("gy", lower, upper)
-    first, last = pack(flat, drag, members)
+    keep, priors = share(place, order, owner, cell, states, drag, even, odd, members, rows)
     left, right = to_neighbours("gx", first, last)
     half = cols // 2
-    count = left.shape[0]
-    small_lower = jnp.concatenate(
-        [jnp.concatenate([left[:, :half], right[:, :half]], axis=1), drag[:MARGIN]], axis=0
-    )
-    small_upper = jnp.concatenate(
-        [jnp.concatenate([left[:, half:], right[:, half:]], axis=1), drag[rows - MARGIN :]], axis=0
-    )
+    small_lower = jnp.concatenate([left[:, :half], right[:, :half]], axis=1)
+    small_upper = jnp.concatenate([left[:, half:], right[:, half:]], axis=1)
     cabove, cbelow = to_neighbours("gy", small_lower, small_upper)
-    states, priors = forecast(
-        place, order, owner, cell, flat, above, below, left, right, cabove, cbelow,
-        drag, cabove[count:], cbelow[count:], members,
-    )
+    states = forecast(place, states, above, below, left, right, cabove, cbelow, keep)
     priors = add_over(priors, ("gx", "gy"))
     result = assimilate(place, order, owner, reach, value, error, taper, priors, states, members, rows)
     return result.reshape(status.shape)

time: 80.8 us -> 76 us (0.941)
  waiting for transfers between devices: 27.7 us -> 9.1 us
  starting transfers between devices: 25.5 us -> 40.3 us
  Pallas kernels: 21.8 us -> 22.7 us
  local copies, waits for them, and re-layouts: 3.63 us -> 2.77 us
    ppermute x3, waiting for transfers between devices: 14.7 us -> 0.01 us  [to_neighbours(): lax.ppermute(upper, axis, forward)]
    ppermute x0 -> x4, starting transfers between devices: none -> 12 us  [swap(): return lax.ppermute(x, axis, pairs + [(b, a) for a, b in pairs])]
    ppermute x3, waiting for transfers between devices: 4.46 us -> 0.01 us  [to_neighbours(): lax.ppermute(lower, axis, backward)]
    ppermute x5, starting transfers between devices: 10.2 us -> 12.2 us  [add_over(): x = x + lax.ppermute(x, axis, [(i, i ^ span) for i in range(count)])]
    pallas_call x1 -> x2, Pallas kernels: 3.18 us -> 4.88 us  [the longest x1 2.48 us: arrange(): pl.pallas_call(functools.partial(arrange_kernel, members, rows), out_shap...]
    slice x6 -> x2, local copies, waits for them, and re-layouts: 1.26 us -> 0.18 us  [body(): small_lower = jnp.concatenate([left[:, :half], right[:, :half]], axis=1)]
    ppermute x3, starting transfers between devices: 11.3 us -> 12.2 us  [to_neighbours(): lax.ppermute(upper, axis, forward)]
  transfers between devices with their start and end apart: 11 -> 15, of which waited for: 7 -> 6; matrix products, arithmetic and copies ran while one was open for 4% -> 1% of each run, Pallas kernels for 0% -> 6%
where the time goes in v2:
time: 76 us
  starting transfers between devices  40.3 us (53%)
  Pallas kernels  22.7 us (30%)
  waiting for transfers between devices  9.1 us (12%)
  local copies, waits for them, and re-layouts  2.77 us (4%)
  other arithmetic  0.87 us (1%)
    ppermute x5, starting transfers between devices, add_over(): x = x + lax.ppermute(x, axis, [(i, i ^ span) for i in range(count)])  12.2 us
    ppermute x3, starting transfers between devices, to_neighbours(): lax.ppermute(upper, axis, forward)  12.2 us
    ppermute x4, starting transfers between devices, swap(): return lax.ppermute(x, axis, pairs + [(b, a) for a, b in pairs])  12 us
    pallas_call x1, Pallas kernels, forecast(): pl.pallas_call(functools.partial(forecast_kernel, members, rows), out_sha...  11.4 us
    ppermute x5, waiting for transfers between devices, add_over(): x = x + lax.ppermute(x, axis, [(i, i ^ span) for i in range(count)])  8.32 us
    pallas_call x1, Pallas kernels, assimilate(): pl.pallas_call(functools.partial(assimilate_kernel, members, rows), out_s...  6.37 us
    ppermute x3, starting transfers between devices, to_neighbours(): lax.ppermute(lower, axis, backward)  3.86 us
    unnamed x20, local copies, waits for them, and re-layouts  2.51 us
  transfers between devices with their start and end apart: 15, of which 6 were waited for; matrix products, arithmetic and copies ran while one was open for 1% of the time, Pallas kernels for 6%

profile of v2, /device:TPU:0, one launch (start us, length us, event | category | flops | bytes accessed | tf_op | source)
XLA Modules:
  0.0 76.0 jit_solution(878188515421764585)
XLA Ops:
  0.0 3.1 %collective-permute-start = (f32[16,128]{1,0:T(8,128)}, f32[16,128]{1,0:T(8,128)S(1)}, u32[]{:S(2)}, u32[]{:S(2)}) collective-permute-start(f32[16,128]{1,0:T(8,128)} %param.10), channel_id=1, source_target_pairs={{0,1},{2,3},{1,0},{3,2},{4,5},{6,7},{5,4},{7,6},{8,9},{10,11},{9,8... | collective-permute-start | bytes 24584 | tf_op jit(solution)/shard_map/ppermute | solution.py:376
  3.8 1.5 %copy-done = f32[3,80,16,128]{3,2,1,0:T(8,128)S(1)} copy-done((f32[3,80,16,128]{3,2,1,0:T(8,128)S(1)}, f32[3,80,16,128]{3,2,1,0:T(8,128)}, u32[]{:S(2)}) %copy-start) | copy-done | bytes 1966104
  5.3 2.5 %shard_map.91 = (f32[48,80,128]{2,1,0:T(8,128)S(1)}, f32[22,80,128]{2,1,0:T(8,128)S(1)}, f32[22,80,128]{2,1,0:T(8,128)}, f32[240,128]{1,0:T(8,128)S(1)}, f32[240,128]{1,0:T(8,128)S(1)}) custom-call(f32[3840,128]{1,0:T(8,128)S(1)} %bitcast.7), custom_call_target="tpu_custom_call" | custom-call | flops 4000000 | bytes 6000000 | tf_op jit(solution)/shard_map/pallas_call | solution.py:69
  7.8 0.9 %copy-done.8 = f32[22,80,128]{2,1,0:T(8,128)} copy-done((f32[22,80,128]{2,1,0:T(8,128)}, f32[22,80,128]{2,1,0:T(8,128)S(1)}, u32[]{:S(2)}) %copy-start.8) | copy-done | bytes 901144
  8.7 1.5 %collective-permute-start.11 = (f32[240,128]{1,0:T(8,128)S(1)}, f32[240,128]{1,0:T(8,128)S(1)}, u32[]{:S(2)}, u32[]{:S(2)}) collective-permute-start(f32[240,128]{1,0:T(8,128)S(1)} %get-tuple-element.16), channel_id=1, source_target_pairs={{0,4},{4,8},{8,12},{12,16},{16,20},{20,24},{24,28},{1,5},{5,9},{9,... | collective-permute-start | bytes 368648 | tf_op jit(solution)/shard_map/ppermute | solution.py:368
  10.2 1.3 %collective-permute-start.12 = (f32[240,128]{1,0:T(8,128)S(1)}, f32[240,128]{1,0:T(8,128)S(1)}, u32[]{:S(2)}, u32[]{:S(2)}) collective-permute-start(f32[240,128]{1,0:T(8,128)S(1)} %get-tuple-element.17), channel_id=1, source_target_pairs={{4,0},{8,4},{12,8},{16,12},{20,16},{24,20},{28,24},{5,1},{9,5},{13... | collective-permute-start | bytes 368648 | tf_op jit(solution)/shard_map/ppermute | solution.py:368
  11.5 6.2 %collective-permute-start.9 = (f32[22,80,128]{2,1,0:T(8,128)}, f32[22,80,128]{2,1,0:T(8,128)S(1)}, u32[]{:S(2)}, u32[]{:S(2)}) collective-permute-start(f32[22,80,128]{2,1,0:T(8,128)} %get-tuple-element.14), channel_id=1, source_target_pairs={{0,1},{1,2},{2,3},{4,5},{5,6},{6,7},{8,9},{9,10},{10,11},{12,13},{... | collective-permute-start | bytes 2703368 | tf_op jit(solution)/shard_map/ppermute | solution.py:368
  17.7 1.3 %collective-permute-start.10 = (f32[22,80,128]{2,1,0:T(8,128)}, f32[22,80,128]{2,1,0:T(8,128)}, u32[]{:S(2)}, u32[]{:S(2)}) collective-permute-start(f32[22,80,128]{2,1,0:T(8,128)} %copy-done.8), channel_id=1, source_target_pairs={{1,0},{2,1},{3,2},{5,4},{6,5},{7,6},{9,8},{10,9},{11,10},{13,12},{... | collective-permute-start | bytes 2703368 | tf_op jit(solution)/shard_map/ppermute | solution.py:368
  19.4 4.6 %collective-permute-start.13 = (f32[240,128]{1,0:T(8,128)S(1)}, f32[240,128]{1,0:T(8,128)S(1)}, u32[]{:S(2)}, u32[]{:S(2)}) collective-permute-start(f32[240,128]{1,0:T(8,128)S(1)} %pad_maximum_fusion), channel_id=1, source_target_pairs={{0,1},{1,2},{2,3},{4,5},{5,6},{6,7},{8,9},{9,10},{10,11},{12,13},{... | collective-permute-start | bytes 368648 | tf_op jit(solution)/shard_map/ppermute | solution.py:368
  24.7 1.3 %collective-permute-start.14 = (f32[240,128]{1,0:T(8,128)}, f32[240,128]{1,0:T(8,128)S(1)}, u32[]{:S(2)}, u32[]{:S(2)}) collective-permute-start(f32[240,128]{1,0:T(8,128)} %pad_maximum_fusion.1), channel_id=1, source_target_pairs={{1,0},{2,1},{3,2},{5,4},{6,5},{7,6},{9,8},{10,9},{11,10},{13,12},{... | collective-permute-start | bytes 368648 | tf_op jit(solution)/shard_map/ppermute | solution.py:368
  26.7 7.6 %collective-permute-start.2 = (f32[32,128]{1,0:T(8,128)S(1)}, f32[32,128]{1,0:T(8,128)S(1)}, u32[]{:S(2)}, u32[]{:S(2)}) collective-permute-start(f32[32,128]{1,0:T(8,128)S(1)} %pad_maximum_fusion.2.drag_ref), channel_id=1, source_target_pairs={{0,4},{8,12},{16,20},{24,28},{4,0},{12,8},{20,16},{28,24},{1,5},{9... | collective-permute-start | bytes 49160 | tf_op jit(solution)/shard_map/ppermute | solution.py:376
  34.4 0.8 collective-permute-done.2.even_ref
  35.1 2.4 %shard_map.92 = (f32[32,256]{1,0:T(8,128)S(1)}, f32[24,128]{1,0:T(8,128)S(1)}) custom-call(s32[6]{0:T(128)S(1)} %stack.39.place_ref, s32[24]{0:T(128)S(1)} %copy-done.1, s32[24]{0:T(128)S(1)} %copy-done.2, s32[24]{0:T(128)S(1)} %copy-done.3, f32[48,80,128]{2,1,0:T(8,128)S(1)} %get-tuple-element.12.state_ref, f32[32,128]{1,0:T(8,128)S(1)} %pad_maximum_fusion.2.drag_ref, ...), custom_call_target="tpu_custom_call" | custom-call | flops 6000000 | bytes 2000000 | tf_op jit(solution)/shard_map/pallas_call | solution.py:150
  37.9 0.8 %collective-permute-done.4 = f32[24,128]{1,0:T(8,128)S(1)} collective-permute-done((f32[24,128]{1,0:T(8,128)S(1)}, f32[24,128]{1,0:T(8,128)S(1)}, u32[]{:S(2)}, u32[]{:S(2)}) %collective-permute-start.4) | collective-permute-done | bytes 12320 | tf_op jit(solution)/shard_map/ppermute | solution.py:389
  38.8 2.9 %collective-permute-start.5 = (f32[24,128]{1,0:T(8,128)S(1)}, f32[24,128]{1,0:T(8,128)S(1)}, u32[]{:S(2)}, u32[]{:S(2)}) collective-permute-start(f32[24,128]{1,0:T(8,128)S(1)} %add.24), channel_id=1, source_target_pairs={{0,8},{4,12},{8,0},{12,4},{16,24},{20,28},{24,16},{28,20},{1,9},{5... | collective-permute-start | bytes 36872 | tf_op jit(solution)/shard_map/ppermute | solution.py:389
  41.7 1.7 %collective-permute-done.5 = f32[24,128]{1,0:T(8,128)S(1)} collective-permute-done((f32[24,128]{1,0:T(8,128)S(1)}, f32[24,128]{1,0:T(8,128)S(1)}, u32[]{:S(2)}, u32[]{:S(2)}) %collective-permute-start.5) | collective-permute-done | bytes 12320 | tf_op jit(solution)/shard_map/ppermute | solution.py:389
  43.3 2.3 %collective-permute-start.6 = (f32[24,128]{1,0:T(8,128)S(1)}, f32[24,128]{1,0:T(8,128)S(1)}, u32[]{:S(2)}, u32[]{:S(2)}) collective-permute-start(f32[24,128]{1,0:T(8,128)S(1)} %add.25), channel_id=1, source_target_pairs={{0,16},{4,20},{8,24},{12,28},{16,0},{20,4},{24,8},{28,12},{1,17},{... | collective-permute-start | bytes 36872 | tf_op jit(solution)/shard_map/ppermute | solution.py:389
  45.7 1.7 %collective-permute-done.6 = f32[24,128]{1,0:T(8,128)S(1)} collective-permute-done((f32[24,128]{1,0:T(8,128)S(1)}, f32[24,128]{1,0:T(8,128)S(1)}, u32[]{:S(2)}, u32[]{:S(2)}) %collective-permute-start.6) | collective-permute-done | bytes 12320 | tf_op jit(solution)/shard_map/ppermute | solution.py:389
  47.3 4.5 %collective-permute-start.7 = (f32[24,128]{1,0:T(8,128)S(1)}, f32[24,128]{1,0:T(8,128)S(1)}, u32[]{:S(2)}, u32[]{:S(2)}) collective-permute-start(f32[24,128]{1,0:T(8,128)S(1)} %add.26), channel_id=1, source_target_pairs={{0,1},{1,0},{2,3},{3,2},{4,5},{5,4},{6,7},{7,6},{8,9},{9,8},{10,11... | collective-permute-start | bytes 36872 | tf_op jit(solution)/shard_map/ppermute | solution.py:389
  51.8 1.7 %collective-permute-done.7 = f32[24,128]{1,0:T(8,128)S(1)} collective-permute-done((f32[24,128]{1,0:T(8,128)S(1)}, f32[24,128]{1,0:T(8,128)S(1)}, u32[]{:S(2)}, u32[]{:S(2)}) %collective-permute-start.7) | collective-permute-done | bytes 12320 | tf_op jit(solution)/shard_map/ppermute | solution.py:389
  53.5 2.1 %collective-permute-start.8 = (f32[24,128]{1,0:T(8,128)S(1)}, f32[24,128]{1,0:T(8,128)S(1)}, u32[]{:S(2)}, u32[]{:S(2)}) collective-permute-start(f32[24,128]{1,0:T(8,128)S(1)} %add.27), channel_id=1, source_target_pairs={{0,2},{1,3},{2,0},{3,1},{4,6},{5,7},{6,4},{7,5},{8,10},{9,11},{10,... | collective-permute-start | bytes 36872 | tf_op jit(solution)/shard_map/ppermute | solution.py:389
  55.6 2.5 %collective-permute-done.8 = f32[24,128]{1,0:T(8,128)S(1)} collective-permute-done((f32[24,128]{1,0:T(8,128)S(1)}, f32[24,128]{1,0:T(8,128)S(1)}, u32[]{:S(2)}, u32[]{:S(2)}) %collective-permute-start.8) | collective-permute-done | bytes 12320 | tf_op jit(solution)/shard_map/ppermute | solution.py:389
  58.1 11.4 %shard_map.93.forecast_ref = f32[48,80,128]{2,1,0:T(8,128)S(1)} custom-call(s32[6]{0:T(128)S(1)} %stack.39.place_ref, f32[48,80,128]{2,1,0:T(8,128)S(1)} %get-tuple-element.12.state_ref, f32[22,80,128]{2,1,0:T(8,128)S(1)} %collective-permute-done.9.above_ref, f32[22,80,128]{2,1,0:T(8,128)} %collective-permute-done.10.below_ref, ...), custom_call_target="tpu_custom_call" | custom-call | flops 60000000 | bytes 30000000 | tf_op jit(solution)/shard_map/pallas_call | solution.py:232
  69.6 6.4 %shard_map.94 = f32[3840,128]{1,0:T(8,128)} custom-call(s32[6]{0:T(128)S(1)} %stack.39.place_ref, s32[24]{0:T(128)S(1)} %copy-done.1, s32[24]{0:T(128)S(1)} %copy-done.2, s32[24]{0:T(128)S(1)} %copy-done.4, f32[24]{0:T(128)S(1)} %copy-done.5, f32[24]{0:T(128)S(1)} %copy-done.6, f32[7]{0:T(128)S(1)} %copy-done.7, f32[24,128]{1,0:T(8,128)S(1)} %add.28.prior_ref, ...), custom_call_target="tpu_custom_call" | custom-call | tf_op jit(solution)/shard_map/pallas_call | solution.py:355
  (42 shorter events, 2.9 us)
Async XLA Ops:
  0.0 35.1 %copy-start.2 = (s32[24]{0:T(128)S(1)}, s32[24]{0:T(128)}, u32[]{:S(2)}) copy-start(s32[24]{0:T(128)} %owner_ref.3) | copy-start | bytes 292
  0.0 35.1 %copy-start.1 = (s32[24]{0:T(128)S(1)}, s32[24]{0:T(128)}, u32[]{:S(2)}) copy-start(s32[24]{0:T(128)} %order_ref.3) | copy-start | bytes 292
  0.0 35.1 %copy-start.3 = (s32[24]{0:T(128)S(1)}, s32[24]{0:T(128)}, u32[]{:S(2)}) copy-start(s32[24]{0:T(128)} %cell_ref.1) | copy-start | bytes 292
  0.0 17.7 %collective-permute-start = (f32[16,128]{1,0:T(8,128)}, f32[16,128]{1,0:T(8,128)S(1)}, u32[]{:S(2)}, u32[]{:S(2)}) collective-permute-start(f32[16,128]{1,0:T(8,128)} %param.10), channel_id=1, source_target_pairs={{0,1},{2,3},{1,0},{3,2},{4,5},{6,7},{5,4},{7,6},{8,9},{10,11},{9,8... | collective-permute-start | bytes 24584 | tf_op jit(solution)/shard_map/ppermute | solution.py:376
  3.1 15.9 %collective-permute-start.1 = (f32[16,128]{1,0:T(8,128)}, f32[16,128]{1,0:T(8,128)S(1)}, u32[]{:S(2)}, u32[]{:S(2)}) collective-permute-start(f32[16,128]{1,0:T(8,128)} %param.10), channel_id=1, source_target_pairs={{1,2},{2,1},{5,6},{6,5},{9,10},{10,9},{13,14},{14,13},{17,18},{18,... | collective-permute-start | bytes 24584 | tf_op jit(solution)/shard_map/ppermute | solution.py:376
  3.8 1.5 %copy-start = (f32[3,80,16,128]{3,2,1,0:T(8,128)S(1)}, f32[3,80,16,128]{3,2,1,0:T(8,128)}, u32[]{:S(2)}) copy-start(f32[3,80,16,128]{3,2,1,0:T(8,128)} %param.9) | copy-start | bytes 5898244
  5.3 20.6 %copy-start.9 = (f32[16,128]{1,0:T(8,128)S(1)}, f32[16,128]{1,0:T(8,128)}, u32[]{:S(2)}) copy-start(f32[16,128]{1,0:T(8,128)} %param.10) | copy-start | bytes 24580
  8.7 10.4 %collective-permute-start.11 = (f32[240,128]{1,0:T(8,128)S(1)}, f32[240,128]{1,0:T(8,128)S(1)}, u32[]{:S(2)}, u32[]{:S(2)}) collective-permute-start(f32[240,128]{1,0:T(8,128)S(1)} %get-tuple-element.16), channel_id=1, source_target_pairs={{0,4},{4,8},{8,12},{12,16},{16,20},{20,24},{24,28},{1,5},{5,9},{9,... | collective-permute-start | bytes 368648 | tf_op jit(solution)/shard_map/ppermute | solution.py:368
  10.2 8.8 %collective-permute-start.12 = (f32[240,128]{1,0:T(8,128)S(1)}, f32[240,128]{1,0:T(8,128)S(1)}, u32[]{:S(2)}, u32[]{:S(2)}) collective-permute-start(f32[240,128]{1,0:T(8,128)S(1)} %get-tuple-element.17), channel_id=1, source_target_pairs={{4,0},{8,4},{12,8},{16,12},{20,16},{24,20},{28,24},{5,1},{9,5},{13... | collective-permute-start | bytes 368648 | tf_op jit(solution)/shard_map/ppermute | solution.py:368
  11.5 46.6 %collective-permute-start.9 = (f32[22,80,128]{2,1,0:T(8,128)}, f32[22,80,128]{2,1,0:T(8,128)S(1)}, u32[]{:S(2)}, u32[]{:S(2)}) collective-permute-start(f32[22,80,128]{2,1,0:T(8,128)} %get-tuple-element.14), channel_id=1, source_target_pairs={{0,1},{1,2},{2,3},{4,5},{5,6},{6,7},{8,9},{9,10},{10,11},{12,13},{... | collective-permute-start | bytes 2703368 | tf_op jit(solution)/shard_map/ppermute | solution.py:368
  17.7 40.4 %collective-permute-start.10 = (f32[22,80,128]{2,1,0:T(8,128)}, f32[22,80,128]{2,1,0:T(8,128)}, u32[]{:S(2)}, u32[]{:S(2)}) collective-permute-start(f32[22,80,128]{2,1,0:T(8,128)} %copy-done.8), channel_id=1, source_target_pairs={{1,0},{2,1},{3,2},{5,4},{6,5},{7,6},{9,8},{10,9},{11,10},{13,12},{... | collective-permute-start | bytes 2703368 | tf_op jit(solution)/shard_map/ppermute | solution.py:368
  19.4 38.7 %collective-permute-start.13 = (f32[240,128]{1,0:T(8,128)S(1)}, f32[240,128]{1,0:T(8,128)S(1)}, u32[]{:S(2)}, u32[]{:S(2)}) collective-permute-start(f32[240,128]{1,0:T(8,128)S(1)} %pad_maximum_fusion), channel_id=1, source_target_pairs={{0,1},{1,2},{2,3},{4,5},{5,6},{6,7},{8,9},{9,10},{10,11},{12,13},{... | collective-permute-start | bytes 368648 | tf_op jit(solution)/shard_map/ppermute | solution.py:368
  24.7 33.4 %collective-permute-start.14 = (f32[240,128]{1,0:T(8,128)}, f32[240,128]{1,0:T(8,128)S(1)}, u32[]{:S(2)}, u32[]{:S(2)}) collective-permute-start(f32[240,128]{1,0:T(8,128)} %pad_maximum_fusion.1), channel_id=1, source_target_pairs={{1,0},{2,1},{3,2},{5,4},{6,5},{7,6},{9,8},{10,9},{11,10},{13,12},{... | collective-permute-start | bytes 368648 | tf_op jit(solution)/shard_map/ppermute | solution.py:368
  26.0 0.7 collective-permute-start.3
  26.7 8.5 %collective-permute-start.2 = (f32[32,128]{1,0:T(8,128)S(1)}, f32[32,128]{1,0:T(8,128)S(1)}, u32[]{:S(2)}, u32[]{:S(2)}) collective-permute-start(f32[32,128]{1,0:T(8,128)S(1)} %pad_maximum_fusion.2.drag_ref), channel_id=1, source_target_pairs={{0,4},{8,12},{16,20},{24,28},{4,0},{12,8},{20,16},{28,24},{1,5},{9... | collective-permute-start | bytes 49160 | tf_op jit(solution)/shard_map/ppermute | solution.py:376
  37.5 1.2 %collective-permute-start.4 = (f32[24,128]{1,0:T(8,128)S(1)}, f32[24,128]{1,0:T(8,128)S(1)}, u32[]{:S(2)}, u32[]{:S(2)}) collective-permute-start(f32[24,128]{1,0:T(8,128)S(1)} %get-tuple-element.13), channel_id=1, source_target_pairs={{0,4},{4,0},{8,12},{12,8},{16,20},{20,16},{24,28},{28,24},{1,5},{5... | collective-permute-start | bytes 36872 | tf_op jit(solution)/shard_map/ppermute | solution.py:389
  38.8 4.6 %collective-permute-start.5 = (f32[24,128]{1,0:T(8,128)S(1)}, f32[24,128]{1,0:T(8,128)S(1)}, u32[]{:S(2)}, u32[]{:S(2)}) collective-permute-start(f32[24,128]{1,0:T(8,128)S(1)} %add.24), channel_id=1, source_target_pairs={{0,8},{4,12},{8,0},{12,4},{16,24},{20,28},{24,16},{28,20},{1,9},{5... | collective-permute-start | bytes 36872 | tf_op jit(solution)/shard_map/ppermute | solution.py:389
  43.3 4.0 %collective-permute-start.6 = (f32[24,128]{1,0:T(8,128)S(1)}, f32[24,128]{1,0:T(8,128)S(1)}, u32[]{:S(2)}, u32[]{:S(2)}) collective-permute-start(f32[24,128]{1,0:T(8,128)S(1)} %add.25), channel_id=1, source_target_pairs={{0,16},{4,20},{8,24},{12,28},{16,0},{20,4},{24,8},{28,12},{1,17},{... | collective-permute-start | bytes 36872 | tf_op jit(solution)/shard_map/ppermute | solution.py:389
  47.3 6.1 %collective-permute-start.7 = (f32[24,128]{1,0:T(8,128)S(1)}, f32[24,128]{1,0:T(8,128)S(1)}, u32[]{:S(2)}, u32[]{:S(2)}) collective-permute-start(f32[24,128]{1,0:T(8,128)S(1)} %add.26), channel_id=1, source_target_pairs={{0,1},{1,0},{2,3},{3,2},{4,5},{5,4},{6,7},{7,6},{8,9},{9,8},{10,11... | collective-permute-start | bytes 36872 | tf_op jit(solution)/shard_map/ppermute | solution.py:389
  53.5 4.6 %collective-permute-start.8 = (f32[24,128]{1,0:T(8,128)S(1)}, f32[24,128]{1,0:T(8,128)S(1)}, u32[]{:S(2)}, u32[]{:S(2)}) collective-permute-start(f32[24,128]{1,0:T(8,128)S(1)} %add.27), channel_id=1, source_target_pairs={{0,2},{1,3},{2,0},{3,1},{4,6},{5,7},{6,4},{7,5},{8,10},{9,11},{10,... | collective-permute-start | bytes 36872 | tf_op jit(solution)/shard_map/ppermute | solution.py:389
  58.1 11.5 %copy-start.4 = (s32[24]{0:T(128)S(1)}, s32[24]{0:T(128)}, u32[]{:S(2)}) copy-start(s32[24]{0:T(128)} %reach_ref.1) | copy-start | bytes 292
  58.1 11.5 %copy-start.5 = (f32[24]{0:T(128)S(1)}, f32[24]{0:T(128)}, u32[]{:S(2)}) copy-start(f32[24]{0:T(128)} %value_ref.1) | copy-start | bytes 292
  58.1 11.5 %copy-start.6 = (f32[24]{0:T(128)S(1)}, f32[24]{0:T(128)}, u32[]{:S(2)}) copy-start(f32[24]{0:T(128)} %error_ref.1) | copy-start | bytes 292
  58.1 11.5 %copy-start.7 = (f32[7]{0:T(128)S(1)}, f32[7]{0:T(128)}, u32[]{:S(2)}) copy-start(f32[7]{0:T(128)} %taper_ref.1) | copy-start | bytes 88
  (1 other events, 0.9 us)

commit v3 on v2

--- a/solution.py
+++ b/solution.py
@@ -14,7 +14,7 @@
 HIGHEST = lax.Precision.HIGHEST
 F32 = jnp.float32
 BF16 = jnp.bfloat16
-VMEM_LIMIT = 24 * 1024 * 1024
+VMEM_LIMIT = 12 * 1024 * 1024
 
 VSPEC = pl.BlockSpec(memory_space=pltpu.VMEM)
 SSPEC = pl.BlockSpec(memory_space=pltpu.SMEM)
@@ -76,6 +76,33 @@
     )(x)
 
 
+def extend_kernel(place_ref, drag_ref, even_ref, odd_ref, first_ref, last_ref, drag_out, lower_ref, upper_ref):
+    rows = drag_ref.shape[0]
+    count = first_ref.shape[0]
+    odd = place_ref[0] % place_ref[5] % 2 == 1
+    above = jnp.where(odd, even_ref[rows - MARGIN :, :], odd_ref[rows - MARGIN :, :])
+    below = jnp.where(odd, odd_ref[:MARGIN, :], even_ref[:MARGIN, :])
+    drag = jnp.concatenate([above, drag_ref[...], below], axis=0)
+    drag_out[...] = drag
+    lower_ref[:count, :] = first_ref[...]
+    upper_ref[:count, :] = last_ref[...]
+    lower_ref[count:, :] = drag
+    upper_ref[count:, :] = drag
+
+
+def extend(place, drag, even, odd, first, last):
+    rows, cols = drag.shape
+    total = rows + 2 * MARGIN
+    message = jax.ShapeDtypeStruct((first.shape[0] + total, cols), F32)
+    return pl.pallas_call(
+        extend_kernel,
+        out_shape=(jax.ShapeDtypeStruct((total, cols), F32), message, message),
+        in_specs=[SSPEC] + [VSPEC] * 5,
+        out_specs=(VSPEC,) * 3,
+        compiler_params=pltpu.CompilerParams(vmem_limit_bytes=VMEM_LIMIT),
+    )(place, drag, even, odd, first, last)
+
+
 def grid_factor(place_ref, shape, rows, cols):
     row, col = sublanes_of(shape), lanes_of(shape)
     wide = 2 * cols
@@ -87,7 +114,7 @@
 
 def share_kernel(
     members, rows,
-    place_ref, order_ref, owner_ref, cell_ref, state_ref, drag_ref, even_ref, odd_ref,
+    place_ref, order_ref, owner_ref, cell_ref, state_ref, drag_ref, before_ref, after_ref,
     keep_ref, prior_ref, turned,
 ):
     cols = drag_ref.shape[1]
@@ -97,11 +124,8 @@
     ix, iy = place_ref[0] // size_y, place_ref[0] % size_y
     shape = (total, wide)
     lane = lanes_of((total, cols))
-    odd = (ix % 2) == 1
-    even_part, odd_part = even_ref[...], odd_ref[...]
-    before = jnp.where(odd, even_part, odd_part)
-    after = jnp.where(odd, odd_part, even_part)
-    drag = jnp.concatenate([drag_ref[...], jnp.where(lane < cols // 2, after, before)], axis=1)
+    margins = jnp.where(lane < cols // 2, after_ref[...], before_ref[...])
+    drag = jnp.concatenate([drag_ref[...], margins], axis=1)
     keep = 1.0 - drag
     keep_ref[...] = keep
     slope = 0.2 * grid_factor(place_ref, shape, rows, cols)
@@ -145,7 +169,7 @@
     prior_ref[...] = jnp.transpose(turned[...])[: prior_ref.shape[0]]
 
 
-def share(place, order, owner, cell, states, drag, even, odd, members, rows):
+def share(place, order, owner, cell, states, drag, before, after, members, rows):
     cols = drag.shape[1]
     return pl.pallas_call(
         functools.partial(share_kernel, members, rows),
@@ -158,7 +182,7 @@
         scratch_shapes=[pltpu.VMEM((cols, cols), F32)],
         compiler_params=pltpu.CompilerParams(vmem_limit_bytes=VMEM_LIMIT),
         cost_estimate=pl.CostEstimate(flops=6_000_000, bytes_accessed=2_000_000, transcendentals=0),
-    )(place, order, owner, cell, states, drag, even, odd)
+    )(place, order, owner, cell, states, drag, before, after)
 
 
 def wide_row(lane, main, left, left_at, right, right_at):
@@ -407,19 +431,18 @@
     ).astype(jnp.int32)
     flat = status.reshape(3 * members * rows, cols)
     even, odd = swap_pairs(drag, "gy")
-    is_odd = (iy % 2) == 1
-    above = jnp.where(is_odd, even[rows - MARGIN :], odd[rows - MARGIN :])
-    below = jnp.where(is_odd, odd[:MARGIN], even[:MARGIN])
-    drag = jnp.concatenate([above, drag, below], axis=0)
-    even, odd = swap_pairs(drag, "gx")
-
     states, lower, upper, first, last = arrange(flat, members, rows)
+    drag, first, last = extend(place, drag, even, odd, first, last)
+    first, last, lower, upper = lax.optimization_barrier((first, last, lower, upper))
+    left, right = to_neighbours("gx", first, last)
     above, below = to_neighbours("gy", lower, upper)
-    keep, priors = share(place, order, owner, cell, states, drag, even, odd, members, rows)
-    left, right = to_neighbours("gx", first, last)
+    count = 3 * members
+    keep, priors = share(place, order, owner, cell, states, drag, left[count:], right[count:], members, rows)
     half = cols // 2
+    left, right = left[:count], right[:count]
     small_lower = jnp.concatenate([left[:, :half], right[:, :half]], axis=1)
     small_upper = jnp.concatenate([left[:, half:], right[:, half:]], axis=1)
+    small_lower, small_upper, priors = lax.optimization_barrier((small_lower, small_upper, priors))
     cabove, cbelow = to_neighbours("gy", small_lower, small_upper)
     states = forecast(place, states, above, below, left, right, cabove, cbelow, keep)
     priors = add_over(priors, ("gx", "gy"))

time: 76 us -> 68.5 us (0.901)
  starting transfers between devices: 40.3 us -> 29.3 us
  waiting for transfers between devices: 9.1 us -> 12.5 us
  Pallas kernels: 22.7 us -> 24 us
  local copies, waits for them, and re-layouts: 2.77 us -> 1.9 us
    ppermute x4 -> x2, starting transfers between devices: 12 us -> 3.75 us  [swap(): return lax.ppermute(x, axis, pairs + [(b, a) for a, b in pairs])]
    ppermute x3, waiting for transfers between devices: 0.01 us -> 3.66 us  [to_neighbours(): lax.ppermute(lower, axis, backward)]
    ppermute x5, starting transfers between devices: 12.2 us -> 9.51 us  [add_over(): x = x + lax.ppermute(x, axis, [(i, i ^ span) for i in range(count)])]
    pallas_call x1, Pallas kernels: 2.4 us -> 4.66 us  [share(): pl.pallas_call(functools.partial(share_kernel, members, rows), out_shape=...]
    unnamed x20 -> x18, local copies, waits for them, and re-layouts: 2.51 us -> 1.59 us
    pallas_call x1, Pallas kernels: 2.48 us -> 1.66 us  [arrange(): pl.pallas_call(functools.partial(arrange_kernel, members, rows), out_shap...]
  transfers between devices with their start and end apart: 15 -> 13, of which waited for: 6 -> 6; matrix products, arithmetic and copies ran while one was open for 1% -> 1% of each run, Pallas kernels for 6% -> 9%
where the time goes in v3:
time: 68.5 us; the launch traced here: 68.2 us
  starting transfers between devices  29.3 us (43%)
  Pallas kernels  24 us (35%)
  waiting for transfers between devices  12.5 us (18%)
  local copies, waits for them, and re-layouts  1.9 us (3%)
    ppermute x3, starting transfers between devices, to_neighbours(): lax.ppermute(upper, axis, forward)  12.2 us
    pallas_call x1, Pallas kernels, forecast(): pl.pallas_call(functools.partial(forecast_kernel, members, rows), out_sha...  10.8 us
    ppermute x5, starting transfers between devices, add_over(): x = x + lax.ppermute(x, axis, [(i, i ^ span) for i in range(count)])  9.51 us
    ppermute x5, waiting for transfers between devices, add_over(): x = x + lax.ppermute(x, axis, [(i, i ^ span) for i in range(count)])  8.82 us
    pallas_call x1, Pallas kernels, assimilate(): pl.pallas_call(functools.partial(assimilate_kernel, members, rows), out_s...  6.37 us
    pallas_call x1, Pallas kernels, share(): pl.pallas_call(functools.partial(share_kernel, members, rows), out_shape=...  4.66 us
    ppermute x3, starting transfers between devices, to_neighbours(): lax.ppermute(lower, axis, backward)  3.88 us
    ppermute x2, starting transfers between devices, swap(): return lax.ppermute(x, axis, pairs + [(b, a) for a, b in pairs])  3.75 us
  transfers between devices with their start and end apart: 13, of which 6 were waited for; matrix products, arithmetic and copies ran while one was open for 1% of the time, Pallas kernels for 9%

profile of v3, /device:TPU:0, one launch (start us, length us, event | category | flops | bytes accessed | tf_op | source)
XLA Modules:
  0.0 68.2 jit_solution(17170345146786958981)
XLA Ops:
  0.0 3.1 %collective-permute-start = (f32[16,128]{1,0:T(8,128)}, f32[16,128]{1,0:T(8,128)S(1)}, u32[]{:S(2)}, u32[]{:S(2)}) collective-permute-start(f32[16,128]{1,0:T(8,128)} %drag_ref.1), channel_id=1, source_target_pairs={{0,1},{2,3},{1,0},{3,2},{4,5},{6,7},{5,4},{7,6},{8,9},{10,11},{9,8... | collective-permute-start | bytes 24584 | tf_op jit(solution)/shard_map/ppermute | solution.py:400
  3.1 0.6 collective-permute-start.1
  3.9 1.5 %copy-done = f32[3,80,16,128]{3,2,1,0:T(8,128)S(1)} copy-done((f32[3,80,16,128]{3,2,1,0:T(8,128)S(1)}, f32[3,80,16,128]{3,2,1,0:T(8,128)}, u32[]{:S(2)}) %copy-start) | copy-done | bytes 1966104
  5.4 1.7 %shard_map.91 = (f32[48,80,128]{2,1,0:T(8,128)S(1)}, f32[22,80,128]{2,1,0:T(8,128)S(1)}, f32[22,80,128]{2,1,0:T(8,128)S(1)}, f32[240,128]{1,0:T(8,128)S(1)}, f32[240,128]{1,0:T(8,128)S(1)}) custom-call(f32[3840,128]{1,0:T(8,128)S(1)} %bitcast.7), custom_call_target="tpu_custom_call" | custom-call | flops 4000000 | bytes 6000000 | tf_op jit(solution)/shard_map/pallas_call | solution.py:69
  7.7 6.4 %collective-permute-start.9 = (f32[22,80,128]{2,1,0:T(8,128)S(1)}, f32[22,80,128]{2,1,0:T(8,128)S(1)}, u32[]{:S(2)}, u32[]{:S(2)}) collective-permute-start(f32[22,80,128]{2,1,0:T(8,128)S(1)} %get-tuple-element.34), channel_id=1, source_target_pairs={{0,1},{1,2},{2,3},{4,5},{5,6},{6,7},{8,9},{9,10},{10,11},{12,13},{... | collective-permute-start | bytes 2703368 | tf_op jit(solution)/shard_map/ppermute | solution.py:392
  14.1 1.3 %collective-permute-start.10 = (f32[22,80,128]{2,1,0:T(8,128)S(1)}, f32[22,80,128]{2,1,0:T(8,128)S(1)}, u32[]{:S(2)}, u32[]{:S(2)}) collective-permute-start(f32[22,80,128]{2,1,0:T(8,128)S(1)} %get-tuple-element.35), channel_id=1, source_target_pairs={{1,0},{2,1},{3,2},{5,4},{6,5},{7,6},{9,8},{10,9},{11,10},{13,12},{... | collective-permute-start | bytes 2703368 | tf_op jit(solution)/shard_map/ppermute | solution.py:392
  15.4 1.3 %collective-permute-start.2 = (f32[272,128]{1,0:T(8,128)S(1)}, f32[272,128]{1,0:T(8,128)S(1)}, u32[]{:S(2)}, u32[]{:S(2)}) collective-permute-start(f32[272,128]{1,0:T(8,128)S(1)} %get-tuple-element.28), channel_id=1, source_target_pairs={{0,4},{4,8},{8,12},{12,16},{16,20},{20,24},{24,28},{1,5},{5,9},{9,... | collective-permute-start | bytes 417800 | tf_op jit(solution)/shard_map/ppermute | solution.py:392
  16.7 1.3 %collective-permute-start.3 = (f32[272,128]{1,0:T(8,128)S(1)}, f32[272,128]{1,0:T(8,128)S(1)}, u32[]{:S(2)}, u32[]{:S(2)}) collective-permute-start(f32[272,128]{1,0:T(8,128)S(1)} %get-tuple-element.29), channel_id=1, source_target_pairs={{4,0},{8,4},{12,8},{16,12},{20,16},{24,20},{28,24},{5,1},{9,5},{13... | collective-permute-start | bytes 417800 | tf_op jit(solution)/shard_map/ppermute | solution.py:392
  18.0 3.7 %collective-permute-done.3 = f32[272,128]{1,0:T(8,128)S(1)} collective-permute-done((f32[272,128]{1,0:T(8,128)S(1)}, f32[272,128]{1,0:T(8,128)S(1)}, u32[]{:S(2)}, u32[]{:S(2)}) %collective-permute-start.3) | collective-permute-done | bytes 139296 | tf_op jit(solution)/shard_map/ppermute | solution.py:392
  21.7 4.7 %shard_map.93 = (f32[32,256]{1,0:T(8,128)S(1)}, f32[24,128]{1,0:T(8,128)S(1)}) custom-call(s32[6]{0:T(128)S(1)} %stack.39.place_ref, s32[24]{0:T(128)S(1)} %copy-done.2, s32[24]{0:T(128)S(1)} %copy-done.3, s32[24]{0:T(128)S(1)} %copy-done.4, f32[48,80,128]{2,1,0:T(8,128)S(1)} %get-tuple-element.30.state_ref, f32[32,128]{1,0:T(8,128)S(1)} %get-tuple-element.31.drag_ref, ...), custom_call_target="tpu_custom_call" | custom-call | flops 6000000 | bytes 2000000 | tf_op jit(solution)/shard_map/pallas_call | solution.py:174
  26.7 4.6 %collective-permute-start.11 = (f32[240,128]{1,0:T(8,128)S(1)}, f32[240,128]{1,0:T(8,128)S(1)}, u32[]{:S(2)}, u32[]{:S(2)}) collective-permute-start(f32[240,128]{1,0:T(8,128)S(1)} %get-tuple-element.36), channel_id=1, source_target_pairs={{0,1},{1,2},{2,3},{4,5},{5,6},{6,7},{8,9},{9,10},{10,11},{12,13},{... | collective-permute-start | bytes 368648 | tf_op jit(solution)/shard_map/ppermute | solution.py:392
  31.2 1.3 %collective-permute-start.12 = (f32[240,128]{1,0:T(8,128)S(1)}, f32[240,128]{1,0:T(8,128)S(1)}, u32[]{:S(2)}, u32[]{:S(2)}) collective-permute-start(f32[240,128]{1,0:T(8,128)S(1)} %get-tuple-element.37), channel_id=1, source_target_pairs={{1,0},{2,1},{3,2},{5,4},{6,5},{7,6},{9,8},{10,9},{11,10},{13,12},{... | collective-permute-start | bytes 368648 | tf_op jit(solution)/shard_map/ppermute | solution.py:392
  32.5 1.4 %collective-permute-start.4 = (f32[24,128]{1,0:T(8,128)S(1)}, f32[24,128]{1,0:T(8,128)S(1)}, u32[]{:S(2)}, u32[]{:S(2)}) collective-permute-start(f32[24,128]{1,0:T(8,128)S(1)} %get-tuple-element.33), channel_id=1, source_target_pairs={{0,4},{4,0},{8,12},{12,8},{16,20},{20,16},{24,28},{28,24},{1,5},{5... | collective-permute-start | bytes 36872 | tf_op jit(solution)/shard_map/ppermute | solution.py:413
  34.0 0.8 %collective-permute-done.4 = f32[24,128]{1,0:T(8,128)S(1)} collective-permute-done((f32[24,128]{1,0:T(8,128)S(1)}, f32[24,128]{1,0:T(8,128)S(1)}, u32[]{:S(2)}, u32[]{:S(2)}) %collective-permute-start.4) | collective-permute-done | bytes 12320 | tf_op jit(solution)/shard_map/ppermute | solution.py:413
  34.8 2.1 %collective-permute-start.5 = (f32[24,128]{1,0:T(8,128)S(1)}, f32[24,128]{1,0:T(8,128)S(1)}, u32[]{:S(2)}, u32[]{:S(2)}) collective-permute-start(f32[24,128]{1,0:T(8,128)S(1)} %add.19), channel_id=1, source_target_pairs={{0,8},{4,12},{8,0},{12,4},{16,24},{20,28},{24,16},{28,20},{1,9},{5... | collective-permute-start | bytes 36872 | tf_op jit(solution)/shard_map/ppermute | solution.py:413
  36.9 1.7 %collective-permute-done.5 = f32[24,128]{1,0:T(8,128)S(1)} collective-permute-done((f32[24,128]{1,0:T(8,128)S(1)}, f32[24,128]{1,0:T(8,128)S(1)}, u32[]{:S(2)}, u32[]{:S(2)}) %collective-permute-start.5) | collective-permute-done | bytes 12320 | tf_op jit(solution)/shard_map/ppermute | solution.py:413
  38.6 1.0 %collective-permute-start.6 = (f32[24,128]{1,0:T(8,128)S(1)}, f32[24,128]{1,0:T(8,128)S(1)}, u32[]{:S(2)}, u32[]{:S(2)}) collective-permute-start(f32[24,128]{1,0:T(8,128)S(1)} %add.20), channel_id=1, source_target_pairs={{0,16},{4,20},{8,24},{12,28},{16,0},{20,4},{24,8},{28,12},{1,17},{... | collective-permute-start | bytes 36872 | tf_op jit(solution)/shard_map/ppermute | solution.py:413
  39.6 2.7 %collective-permute-done.6 = f32[24,128]{1,0:T(8,128)S(1)} collective-permute-done((f32[24,128]{1,0:T(8,128)S(1)}, f32[24,128]{1,0:T(8,128)S(1)}, u32[]{:S(2)}, u32[]{:S(2)}) %collective-permute-start.6) | collective-permute-done | bytes 12320 | tf_op jit(solution)/shard_map/ppermute | solution.py:413
  42.3 2.4 %collective-permute-start.7 = (f32[24,128]{1,0:T(8,128)S(1)}, f32[24,128]{1,0:T(8,128)S(1)}, u32[]{:S(2)}, u32[]{:S(2)}) collective-permute-start(f32[24,128]{1,0:T(8,128)S(1)} %add.21), channel_id=1, source_target_pairs={{0,1},{1,0},{2,3},{3,2},{4,5},{5,4},{6,7},{7,6},{8,9},{9,8},{10,11... | collective-permute-start | bytes 36872 | tf_op jit(solution)/shard_map/ppermute | solution.py:413
  44.7 1.7 %collective-permute-done.7 = f32[24,128]{1,0:T(8,128)S(1)} collective-permute-done((f32[24,128]{1,0:T(8,128)S(1)}, f32[24,128]{1,0:T(8,128)S(1)}, u32[]{:S(2)}, u32[]{:S(2)}) %collective-permute-start.7) | collective-permute-done | bytes 12320 | tf_op jit(solution)/shard_map/ppermute | solution.py:413
  46.3 2.6 %collective-permute-start.8 = (f32[24,128]{1,0:T(8,128)S(1)}, f32[24,128]{1,0:T(8,128)S(1)}, u32[]{:S(2)}, u32[]{:S(2)}) collective-permute-start(f32[24,128]{1,0:T(8,128)S(1)} %add.22), channel_id=1, source_target_pairs={{0,2},{1,3},{2,0},{3,1},{4,6},{5,7},{6,4},{7,5},{8,10},{9,11},{10,... | collective-permute-start | bytes 36872 | tf_op jit(solution)/shard_map/ppermute | solution.py:413
  48.9 2.0 %collective-permute-done.8 = f32[24,128]{1,0:T(8,128)S(1)} collective-permute-done((f32[24,128]{1,0:T(8,128)S(1)}, f32[24,128]{1,0:T(8,128)S(1)}, u32[]{:S(2)}, u32[]{:S(2)}) %collective-permute-start.8) | collective-permute-done | bytes 12320 | tf_op jit(solution)/shard_map/ppermute | solution.py:413
  51.0 10.8 %shard_map.94.forecast_ref = f32[48,80,128]{2,1,0:T(8,128)S(1)} custom-call(s32[6]{0:T(128)S(1)} %stack.39.place_ref, f32[48,80,128]{2,1,0:T(8,128)S(1)} %get-tuple-element.30.state_ref, f32[22,80,128]{2,1,0:T(8,128)S(1)} %collective-permute-done.9.above_ref, f32[22,80,128]{2,1,0:T(8,128)S(1)} %collective-permute-done.10.below_ref, ...), custom_call_target="tpu_custom_call" | custom-call | flops 60000000 | bytes 30000000 | tf_op jit(solution)/shard_map/pallas_call | solution.py:256
  61.8 6.4 %shard_map.95 = f32[3840,128]{1,0:T(8,128)} custom-call(s32[6]{0:T(128)S(1)} %stack.39.place_ref, s32[24]{0:T(128)S(1)} %copy-done.2, s32[24]{0:T(128)S(1)} %copy-done.3, s32[24]{0:T(128)S(1)} %copy-done.5, f32[24]{0:T(128)S(1)} %copy-done.6, f32[24]{0:T(128)S(1)} %copy-done.7, f32[7]{0:T(128)S(1)} %copy-done.8, f32[24,128]{1,0:T(8,128)S(1)} %add.23.prior_ref, ...), custom_call_target="tpu_custom_call" | custom-call | tf_op jit(solution)/shard_map/pallas_call | solution.py:379
  (38 shorter events, 1.1 us)
Async XLA Ops:
  0.0 7.1 %copy-start.1 = (f32[16,128]{1,0:T(8,128)S(1)}, f32[16,128]{1,0:T(8,128)}, u32[]{:S(2)}) copy-start(f32[16,128]{1,0:T(8,128)} %drag_ref.1) | copy-start | bytes 24580
  0.0 21.6 %copy-start.3 = (s32[24]{0:T(128)S(1)}, s32[24]{0:T(128)}, u32[]{:S(2)}) copy-start(s32[24]{0:T(128)} %owner_ref.3) | copy-start | bytes 292
  0.0 21.6 %copy-start.2 = (s32[24]{0:T(128)S(1)}, s32[24]{0:T(128)}, u32[]{:S(2)}) copy-start(s32[24]{0:T(128)} %order_ref.3) | copy-start | bytes 292
  0.0 21.6 %copy-start.4 = (s32[24]{0:T(128)S(1)}, s32[24]{0:T(128)}, u32[]{:S(2)}) copy-start(s32[24]{0:T(128)} %cell_ref.1) | copy-start | bytes 292
  0.0 7.1 %collective-permute-start = (f32[16,128]{1,0:T(8,128)}, f32[16,128]{1,0:T(8,128)S(1)}, u32[]{:S(2)}, u32[]{:S(2)}) collective-permute-start(f32[16,128]{1,0:T(8,128)} %drag_ref.1), channel_id=1, source_target_pairs={{0,1},{2,3},{1,0},{3,2},{4,5},{6,7},{5,4},{7,6},{8,9},{10,11},{9,8... | collective-permute-start | bytes 24584 | tf_op jit(solution)/shard_map/ppermute | solution.py:400
  3.1 4.0 %collective-permute-start.1 = (f32[16,128]{1,0:T(8,128)}, f32[16,128]{1,0:T(8,128)S(1)}, u32[]{:S(2)}, u32[]{:S(2)}) collective-permute-start(f32[16,128]{1,0:T(8,128)} %drag_ref.1), channel_id=1, source_target_pairs={{1,2},{2,1},{5,6},{6,5},{9,10},{10,9},{13,14},{14,13},{17,18},{18,... | collective-permute-start | bytes 24584 | tf_op jit(solution)/shard_map/ppermute | solution.py:400
  3.9 1.5 %copy-start = (f32[3,80,16,128]{3,2,1,0:T(8,128)S(1)}, f32[3,80,16,128]{3,2,1,0:T(8,128)}, u32[]{:S(2)}) copy-start(f32[3,80,16,128]{3,2,1,0:T(8,128)} %param.9) | copy-start | bytes 5898244
  7.7 43.2 %collective-permute-start.9 = (f32[22,80,128]{2,1,0:T(8,128)S(1)}, f32[22,80,128]{2,1,0:T(8,128)S(1)}, u32[]{:S(2)}, u32[]{:S(2)}) collective-permute-start(f32[22,80,128]{2,1,0:T(8,128)S(1)} %get-tuple-element.34), channel_id=1, source_target_pairs={{0,1},{1,2},{2,3},{4,5},{5,6},{6,7},{8,9},{9,10},{10,11},{12,13},{... | collective-permute-start | bytes 2703368 | tf_op jit(solution)/shard_map/ppermute | solution.py:392
  14.1 36.9 %collective-permute-start.10 = (f32[22,80,128]{2,1,0:T(8,128)S(1)}, f32[22,80,128]{2,1,0:T(8,128)S(1)}, u32[]{:S(2)}, u32[]{:S(2)}) collective-permute-start(f32[22,80,128]{2,1,0:T(8,128)S(1)} %get-tuple-element.35), channel_id=1, source_target_pairs={{1,0},{2,1},{3,2},{5,4},{6,5},{7,6},{9,8},{10,9},{11,10},{13,12},{... | collective-permute-start | bytes 2703368 | tf_op jit(solution)/shard_map/ppermute | solution.py:392
  15.4 2.6 %collective-permute-start.2 = (f32[272,128]{1,0:T(8,128)S(1)}, f32[272,128]{1,0:T(8,128)S(1)}, u32[]{:S(2)}, u32[]{:S(2)}) collective-permute-start(f32[272,128]{1,0:T(8,128)S(1)} %get-tuple-element.28), channel_id=1, source_target_pairs={{0,4},{4,8},{8,12},{12,16},{16,20},{20,24},{24,28},{1,5},{5,9},{9,... | collective-permute-start | bytes 417800 | tf_op jit(solution)/shard_map/ppermute | solution.py:392
  16.7 5.0 %collective-permute-start.3 = (f32[272,128]{1,0:T(8,128)S(1)}, f32[272,128]{1,0:T(8,128)S(1)}, u32[]{:S(2)}, u32[]{:S(2)}) collective-permute-start(f32[272,128]{1,0:T(8,128)S(1)} %get-tuple-element.29), channel_id=1, source_target_pairs={{4,0},{8,4},{12,8},{16,12},{20,16},{24,20},{28,24},{5,1},{9,5},{13... | collective-permute-start | bytes 417800 | tf_op jit(solution)/shard_map/ppermute | solution.py:392
  26.7 24.3 %collective-permute-start.11 = (f32[240,128]{1,0:T(8,128)S(1)}, f32[240,128]{1,0:T(8,128)S(1)}, u32[]{:S(2)}, u32[]{:S(2)}) collective-permute-start(f32[240,128]{1,0:T(8,128)S(1)} %get-tuple-element.36), channel_id=1, source_target_pairs={{0,1},{1,2},{2,3},{4,5},{5,6},{6,7},{8,9},{9,10},{10,11},{12,13},{... | collective-permute-start | bytes 368648 | tf_op jit(solution)/shard_map/ppermute | solution.py:392
  31.2 19.7 %collective-permute-start.12 = (f32[240,128]{1,0:T(8,128)S(1)}, f32[240,128]{1,0:T(8,128)S(1)}, u32[]{:S(2)}, u32[]{:S(2)}) collective-permute-start(f32[240,128]{1,0:T(8,128)S(1)} %get-tuple-element.37), channel_id=1, source_target_pairs={{1,0},{2,1},{3,2},{5,4},{6,5},{7,6},{9,8},{10,9},{11,10},{13,12},{... | collective-permute-start | bytes 368648 | tf_op jit(solution)/shard_map/ppermute | solution.py:392
  32.5 2.3 %collective-permute-start.4 = (f32[24,128]{1,0:T(8,128)S(1)}, f32[24,128]{1,0:T(8,128)S(1)}, u32[]{:S(2)}, u32[]{:S(2)}) collective-permute-start(f32[24,128]{1,0:T(8,128)S(1)} %get-tuple-element.33), channel_id=1, source_target_pairs={{0,4},{4,0},{8,12},{12,8},{16,20},{20,16},{24,28},{28,24},{1,5},{5... | collective-permute-start | bytes 36872 | tf_op jit(solution)/shard_map/ppermute | solution.py:413
  34.8 3.8 %collective-permute-start.5 = (f32[24,128]{1,0:T(8,128)S(1)}, f32[24,128]{1,0:T(8,128)S(1)}, u32[]{:S(2)}, u32[]{:S(2)}) collective-permute-start(f32[24,128]{1,0:T(8,128)S(1)} %add.19), channel_id=1, source_target_pairs={{0,8},{4,12},{8,0},{12,4},{16,24},{20,28},{24,16},{28,20},{1,9},{5... | collective-permute-start | bytes 36872 | tf_op jit(solution)/shard_map/ppermute | solution.py:413
  38.6 3.7 %collective-permute-start.6 = (f32[24,128]{1,0:T(8,128)S(1)}, f32[24,128]{1,0:T(8,128)S(1)}, u32[]{:S(2)}, u32[]{:S(2)}) collective-permute-start(f32[24,128]{1,0:T(8,128)S(1)} %add.20), channel_id=1, source_target_pairs={{0,16},{4,20},{8,24},{12,28},{16,0},{20,4},{24,8},{28,12},{1,17},{... | collective-permute-start | bytes 36872 | tf_op jit(solution)/shard_map/ppermute | solution.py:413
  42.3 4.0 %collective-permute-start.7 = (f32[24,128]{1,0:T(8,128)S(1)}, f32[24,128]{1,0:T(8,128)S(1)}, u32[]{:S(2)}, u32[]{:S(2)}) collective-permute-start(f32[24,128]{1,0:T(8,128)S(1)} %add.21), channel_id=1, source_target_pairs={{0,1},{1,0},{2,3},{3,2},{4,5},{5,4},{6,7},{7,6},{8,9},{9,8},{10,11... | collective-permute-start | bytes 36872 | tf_op jit(solution)/shard_map/ppermute | solution.py:413
  46.3 4.6 %collective-permute-start.8 = (f32[24,128]{1,0:T(8,128)S(1)}, f32[24,128]{1,0:T(8,128)S(1)}, u32[]{:S(2)}, u32[]{:S(2)}) collective-permute-start(f32[24,128]{1,0:T(8,128)S(1)} %add.22), channel_id=1, source_target_pairs={{0,2},{1,3},{2,0},{3,1},{4,6},{5,7},{6,4},{7,5},{8,10},{9,11},{10,... | collective-permute-start | bytes 36872 | tf_op jit(solution)/shard_map/ppermute | solution.py:413
  51.0 10.8 %copy-start.5 = (s32[24]{0:T(128)S(1)}, s32[24]{0:T(128)}, u32[]{:S(2)}) copy-start(s32[24]{0:T(128)} %reach_ref.1) | copy-start | bytes 292
  51.0 10.8 %copy-start.6 = (f32[24]{0:T(128)S(1)}, f32[24]{0:T(128)}, u32[]{:S(2)}) copy-start(f32[24]{0:T(128)} %value_ref.1) | copy-start | bytes 292
  51.0 10.8 %copy-start.7 = (f32[24]{0:T(128)S(1)}, f32[24]{0:T(128)}, u32[]{:S(2)}) copy-start(f32[24]{0:T(128)} %error_ref.1) | copy-start | bytes 292
  51.0 10.8 %copy-start.8 = (f32[7]{0:T(128)S(1)}, f32[7]{0:T(128)}, u32[]{:S(2)}) copy-start(f32[7]{0:T(128)} %taper_ref.1) | copy-start | bytes 88

commit v4 on v3

--- a/solution.py
+++ b/solution.py
@@ -76,18 +76,19 @@
     )(x)
 
 
-def extend_kernel(place_ref, drag_ref, even_ref, odd_ref, first_ref, last_ref, drag_out, lower_ref, upper_ref):
+def extend_kernel(place_ref, drag_ref, even_ref, odd_ref, first_ref, last_ref, drag_out, even_out, odd_out):
     rows = drag_ref.shape[0]
     count = first_ref.shape[0]
-    odd = place_ref[0] % place_ref[5] % 2 == 1
-    above = jnp.where(odd, even_ref[rows - MARGIN :, :], odd_ref[rows - MARGIN :, :])
-    below = jnp.where(odd, odd_ref[:MARGIN, :], even_ref[:MARGIN, :])
+    odd_y = place_ref[0] % place_ref[5] % 2 == 1
+    odd_x = place_ref[0] // place_ref[5] % 2 == 1
+    above = jnp.where(odd_y, even_ref[rows - MARGIN :, :], odd_ref[rows - MARGIN :, :])
+    below = jnp.where(odd_y, odd_ref[:MARGIN, :], even_ref[:MARGIN, :])
     drag = jnp.concatenate([above, drag_ref[...], below], axis=0)
     drag_out[...] = drag
-    lower_ref[:count, :] = first_ref[...]
-    upper_ref[:count, :] = last_ref[...]
-    lower_ref[count:, :] = drag
-    upper_ref[count:, :] = drag
+    even_out[:count, :] = jnp.where(odd_x, first_ref[...], last_ref[...])
+    odd_out[:count, :] = jnp.where(odd_x, last_ref[...], first_ref[...])
+    even_out[count:, :] = drag
+    odd_out[count:, :] = drag
 
 
 def extend(place, drag, even, odd, first, last):
@@ -101,6 +102,33 @@
         out_specs=(VSPEC,) * 3,
         compiler_params=pltpu.CompilerParams(vmem_limit_bytes=VMEM_LIMIT),
     )(place, drag, even, odd, first, last)
+
+
+def corner_kernel(place_ref, even_ref, odd_ref, left_ref, right_ref, even_out, odd_out):
+    count, cols = left_ref.shape
+    half = cols // 2
+    odd_y = place_ref[0] % place_ref[5] % 2 == 1
+    odd_x = place_ref[0] // place_ref[5] % 2 == 1
+    even, odd = even_ref[:count, :], odd_ref[:count, :]
+    left, right = jnp.where(odd_x, even, odd), jnp.where(odd_x, odd, even)
+    left_ref[...] = left
+    right_ref[...] = right
+    first_half = lanes_of((count, cols)) < half
+    lower = jnp.where(first_half, left, roll_lanes(right, half))
+    upper = jnp.where(first_half, roll_lanes(left, half), right)
+    even_out[...] = jnp.where(odd_y, lower, upper)
+    odd_out[...] = jnp.where(odd_y, upper, lower)
+
+
+def corner(place, even, odd, count):
+    cols = even.shape[1]
+    return pl.pallas_call(
+        corner_kernel,
+        out_shape=(jax.ShapeDtypeStruct((count, cols), F32),) * 4,
+        in_specs=[SSPEC] + [VSPEC] * 2,
+        out_specs=(VSPEC,) * 4,
+        compiler_params=pltpu.CompilerParams(vmem_limit_bytes=VMEM_LIMIT),
+    )(place, even, odd)
 
 
 def grid_factor(place_ref, shape, rows, cols):
@@ -114,7 +142,7 @@
 
 def share_kernel(
     members, rows,
-    place_ref, order_ref, owner_ref, cell_ref, state_ref, drag_ref, before_ref, after_ref,
+    place_ref, order_ref, owner_ref, cell_ref, state_ref, drag_ref, even_ref, odd_ref,
     keep_ref, prior_ref, turned,
 ):
     cols = drag_ref.shape[1]
@@ -124,7 +152,12 @@
     ix, iy = place_ref[0] // size_y, place_ref[0] % size_y
     shape = (total, wide)
     lane = lanes_of((total, cols))
-    margins = jnp.where(lane < cols // 2, after_ref[...], before_ref[...])
+    odd = ix % 2 == 1
+    here = even_ref.shape[0] - total
+    even_part, odd_part = even_ref[here:, :], odd_ref[here:, :]
+    before = jnp.where(odd, even_part, odd_part)
+    after = jnp.where(odd, odd_part, even_part)
+    margins = jnp.where(lane < cols // 2, after, before)
     drag = jnp.concatenate([drag_ref[...], margins], axis=1)
     keep = 1.0 - drag
     keep_ref[...] = keep
@@ -169,7 +202,7 @@
     prior_ref[...] = jnp.transpose(turned[...])[: prior_ref.shape[0]]
 
 
-def share(place, order, owner, cell, states, drag, before, after, members, rows):
+def share(place, order, owner, cell, states, drag, even, odd, members, rows):
     cols = drag.shape[1]
     return pl.pallas_call(
         functools.partial(share_kernel, members, rows),
@@ -182,7 +215,7 @@
         scratch_shapes=[pltpu.VMEM((cols, cols), F32)],
         compiler_params=pltpu.CompilerParams(vmem_limit_bytes=VMEM_LIMIT),
         cost_estimate=pl.CostEstimate(flops=6_000_000, bytes_accessed=2_000_000, transcendentals=0),
-    )(place, order, owner, cell, states, drag, before, after)
+    )(place, order, owner, cell, states, drag, even, odd)
 
 
 def wide_row(lane, main, left, left_at, right, right_at):
@@ -194,7 +227,7 @@
 
 def forecast_kernel(
     members, rows,
-    place_ref, state_ref, above_ref, below_ref, left_ref, right_ref, cabove_ref, cbelow_ref, keep_ref,
+    place_ref, state_ref, above_ref, below_ref, left_ref, right_ref, ceven_ref, codd_ref, keep_ref,
     out_ref,
     state, keep, slope,
 ):
@@ -204,6 +237,7 @@
     lane = lanes_of((8, cols))
     half = cols // 2
     factor = -0.2 * grid_factor(place_ref, (total, wide), rows, cols)
+    odd_y = place_ref[0] % place_ref[5] % 2 == 1
     for r in range(total):
         keep[r] = jnp.broadcast_to(keep_ref[r : r + 1, :], (8, wide))
         slope[r] = jnp.broadcast_to(factor[r : r + 1, :], (8, wide))
@@ -213,7 +247,8 @@
         for f in range(3):
             at = pl.ds(pl.multiple_of(f * members + g * 8, 8), 8)
             ledge, redge = left_ref[at, :], right_ref[at, :]
-            cab, cbe = cabove_ref[at, :], cbelow_ref[at, :]
+            ceven, codd = ceven_ref[at, :], codd_ref[at, :]
+            cab, cbe = jnp.where(odd_y, ceven, codd), jnp.where(odd_y, codd, ceven)
             depth = MARGIN if f == 2 else MARGIN - 1
             for r in range(MARGIN - depth, MARGIN + rows + depth):
                 if r < MARGIN:
@@ -392,14 +427,9 @@
     return lax.ppermute(upper, axis, forward), lax.ppermute(lower, axis, backward)
 
 
-def swap_pairs(x, axis):
-    count = lax.axis_size(axis)
-
-    def swap(start):
-        pairs = [(i, i + 1) for i in range(start, count - 1, 2)]
-        return lax.ppermute(x, axis, pairs + [(b, a) for a, b in pairs])
-
-    return swap(0), swap(1)
+def swap_pairs(x, axis, start):
+    pairs = [(i, i + 1) for i in range(start, lax.axis_size(axis) - 1, 2)]
+    return lax.ppermute(x, axis, pairs + [(b, a) for a, b in pairs])
 
 
 def add_over(x, axes):
@@ -430,20 +460,19 @@
         ]
     ).astype(jnp.int32)
     flat = status.reshape(3 * members * rows, cols)
-    even, odd = swap_pairs(drag, "gy")
     states, lower, upper, first, last = arrange(flat, members, rows)
-    drag, first, last = extend(place, drag, even, odd, first, last)
-    first, last, lower, upper = lax.optimization_barrier((first, last, lower, upper))
-    left, right = to_neighbours("gx", first, last)
+    drag, lower = lax.optimization_barrier((drag, lower))
+    even, odd = swap_pairs(drag, "gy", 0), swap_pairs(drag, "gy", 1)
+    even, odd, lower, upper = lax.optimization_barrier((even, odd, lower, upper))
     above, below = to_neighbours("gy", lower, upper)
-    count = 3 * members
-    keep, priors = share(place, order, owner, cell, states, drag, left[count:], right[count:], members, rows)
-    half = cols // 2
-    left, right = left[:count], right[:count]
-    small_lower = jnp.concatenate([left[:, :half], right[:, :half]], axis=1)
-    small_upper = jnp.concatenate([left[:, half:], right[:, half:]], axis=1)
-    small_lower, small_upper, priors = lax.optimization_barrier((small_lower, small_upper, priors))
-    cabove, cbelow = to_neighbours("gy", small_lower, small_upper)
+    drag, even, odd = extend(place, drag, even, odd, first, last)
+    even = swap_pairs(even, "gx", 0)
+    odd = swap_pairs(odd, "gx", 1)
+    keep, priors = share(place, order, owner, cell, states, drag, even, odd, members, rows)
+    left, right, even, odd = corner(place, even, odd, 3 * members)
+    even, odd, priors = lax.optimization_barrier((even, odd, priors))
+    cabove = swap_pairs(even, "gy", 0)
+    cbelow = swap_pairs(odd, "gy", 1)
     states = forecast(place, states, above, below, left, right, cabove, cbelow, keep)
     priors = add_over(priors, ("gx", "gy"))
     result = assimilate(place, order, owner, reach, value, error, taper, priors, states, members, rows)

time: 68.5 us -> 69.3 us (1.012)
  starting transfers between devices: 29.3 us -> 31.4 us
  waiting for transfers between devices: 12.5 us -> 11.2 us
    ppermute x3 -> x1, starting transfers between devices: 12.2 us -> 3.97 us  [to_neighbours(): lax.ppermute(upper, axis, forward)]
    ppermute x2 -> x6, starting transfers between devices: 3.75 us -> 10.6 us  [swap_pairs(): return lax.ppermute(x, axis, pairs + [(b, a) for a, b in pairs])]
    ppermute x5, starting transfers between devices: 9.51 us -> 15.5 us  [add_over(): x = x + lax.ppermute(x, axis, [(i, i ^ span) for i in range(count)])]
    ppermute x3 -> x1, waiting for transfers between devices: 3.66 us -> 0.01 us  [to_neighbours(): lax.ppermute(lower, axis, backward)]
    ppermute x3 -> x1, starting transfers between devices: 3.88 us -> 1.29 us  [to_neighbours(): lax.ppermute(lower, axis, backward)]
    ppermute x2 -> x6, waiting for transfers between devices: 0.01 us -> 2.31 us  [swap_pairs(): return lax.ppermute(x, axis, pairs + [(b, a) for a, b in pairs])]
    pallas_call x1, Pallas kernels: 4.66 us -> 2.4 us  [share(): pl.pallas_call(functools.partial(share_kernel, members, rows), out_shape=...]
    pallas_call x1, Pallas kernels: 1.66 us -> 2.79 us  [arrange(): pl.pallas_call(functools.partial(arrange_kernel, members, rows), out_shap...]
  transfers between devices with their start and end apart: 13 -> 13, of which waited for: 6 -> 7; matrix products, arithmetic and copies ran while one was open for 1% -> 0% of each run, Pallas kernels for 9% -> 5%
where the time goes in v4:
time: 69.3 us; the launch traced here: 68.8 us
  starting transfers between devices  31.4 us (45%)
  Pallas kernels  24.3 us (35%)
  waiting for transfers between devices  11.2 us (16%)
  local copies, waits for them, and re-layouts  1.71 us (2%)
    ppermute x5, starting transfers between devices, add_over(): x = x + lax.ppermute(x, axis, [(i, i ^ span) for i in range(count)])  15.5 us
    pallas_call x1, Pallas kernels, forecast(): pl.pallas_call(functools.partial(forecast_kernel, members, rows), out_sha...  11.4 us
    ppermute x6, starting transfers between devices, swap_pairs(): return lax.ppermute(x, axis, pairs + [(b, a) for a, b in pairs])  10.6 us
    ppermute x5, waiting for transfers between devices, add_over(): x = x + lax.ppermute(x, axis, [(i, i ^ span) for i in range(count)])  8.86 us
    pallas_call x1, Pallas kernels, assimilate(): pl.pallas_call(functools.partial(assimilate_kernel, members, rows), out_s...  6.37 us
    ppermute x1, starting transfers between devices, to_neighbours(): lax.ppermute(upper, axis, forward)  3.97 us
    pallas_call x1, Pallas kernels, arrange(): pl.pallas_call(functools.partial(arrange_kernel, members, rows), out_shap...  2.79 us
    pallas_call x1, Pallas kernels, share(): pl.pallas_call(functools.partial(share_kernel, members, rows), out_shape=...  2.4 us
  transfers between devices with their start and end apart: 13, of which 7 were waited for; matrix products, arithmetic and copies ran while one was open for 0% of the time, Pallas kernels for 5%

profile of v4, /device:TPU:0, one launch (start us, length us, event | category | flops | bytes accessed | tf_op | source)
XLA Modules:
  0.0 68.8 jit_solution(8855300056643013275)
XLA Ops:
  0.0 1.6 %copy-done = f32[3,80,16,128]{3,2,1,0:T(8,128)S(1)} copy-done((f32[3,80,16,128]{3,2,1,0:T(8,128)S(1)}, f32[3,80,16,128]{3,2,1,0:T(8,128)}, u32[]{:S(2)}) %copy-start) | copy-done | bytes 1966104
  1.6 2.8 %shard_map.91 = (f32[48,80,128]{2,1,0:T(8,128)S(1)}, f32[22,80,128]{2,1,0:T(8,128)}, f32[22,80,128]{2,1,0:T(8,128)}, f32[240,128]{1,0:T(8,128)S(1)}, f32[240,128]{1,0:T(8,128)S(1)}) custom-call(f32[3840,128]{1,0:T(8,128)S(1)} %bitcast.7), custom_call_target="tpu_custom_call" | custom-call | flops 4000000 | bytes 6000000 | tf_op jit(solution)/shard_map/pallas_call | solution.py:69
  5.0 5.9 %collective-permute-start = (f32[16,128]{1,0:T(8,128)S(1)}, f32[16,128]{1,0:T(8,128)S(1)}, u32[]{:S(2)}, u32[]{:S(2)}) collective-permute-start(f32[16,128]{1,0:T(8,128)S(1)} %copy-done.1), channel_id=1, source_target_pairs={{0,1},{2,3},{1,0},{3,2},{4,5},{6,7},{5,4},{7,6},{8,9},{10,11},{9,8... | collective-permute-start | bytes 24584 | tf_op jit(solution)/shard_map/ppermute | solution.py:432
  11.0 1.6 %collective-permute-done.even_ref = f32[16,128]{1,0:T(8,128)S(1)} collective-permute-done((f32[16,128]{1,0:T(8,128)S(1)}, f32[16,128]{1,0:T(8,128)S(1)}, u32[]{:S(2)}, u32[]{:S(2)}) %collective-permute-start) | collective-permute-done | bytes 8224 | tf_op jit(solution)/shard_map/ppermute | solution.py:432
  12.6 4.0 %collective-permute-start.9 = (f32[22,80,128]{2,1,0:T(8,128)}, f32[22,80,128]{2,1,0:T(8,128)S(1)}, u32[]{:S(2)}, u32[]{:S(2)}) collective-permute-start(f32[22,80,128]{2,1,0:T(8,128)} %get-tuple-element.44), channel_id=1, source_target_pairs={{0,1},{1,2},{2,3},{4,5},{5,6},{6,7},{8,9},{9,10},{10,11},{12,13},{... | collective-permute-start | bytes 2703368 | tf_op jit(solution)/shard_map/ppermute | solution.py:427
  16.6 1.3 %collective-permute-start.10 = (f32[22,80,128]{2,1,0:T(8,128)}, f32[22,80,128]{2,1,0:T(8,128)}, u32[]{:S(2)}, u32[]{:S(2)}) collective-permute-start(f32[22,80,128]{2,1,0:T(8,128)} %get-tuple-element.45), channel_id=1, source_target_pairs={{1,0},{2,1},{3,2},{5,4},{6,5},{7,6},{9,8},{10,9},{11,10},{13,12},{... | collective-permute-start | bytes 2703368 | tf_op jit(solution)/shard_map/ppermute | solution.py:427
  18.6 0.7 collective-permute-start.3
  19.3 0.7 collective-permute-done.2.even_ref
  20.0 0.7 %shard_map.93 = (f32[240,128]{1,0:T(8,128)S(1)}, f32[240,128]{1,0:T(8,128)S(1)}, f32[240,128]{1,0:T(8,128)S(1)}, f32[240,128]{1,0:T(8,128)S(1)}) custom-call(s32[6]{0:T(128)S(1)} %stack.39.place_ref, f32[272,128]{1,0:T(8,128)S(1)} %collective-permute-done.2.even_ref, f32[272,128]{1,0:T(8,128)S(1)} %collective-permute-done.3.odd_ref), custom_call_target="tpu_custom_call" | custom-call | tf_op jit(solution)/shard_map/pallas_call | solution.py:125
  20.7 2.4 %shard_map.94 = (f32[32,256]{1,0:T(8,128)S(1)}, f32[24,128]{1,0:T(8,128)S(1)}) custom-call(s32[6]{0:T(128)S(1)} %stack.39.place_ref, s32[24]{0:T(128)S(1)} %copy-done.2, s32[24]{0:T(128)S(1)} %copy-done.3, s32[24]{0:T(128)S(1)} %copy-done.4, f32[48,80,128]{2,1,0:T(8,128)S(1)} %get-tuple-element.40.state_ref, f32[32,128]{1,0:T(8,128)S(1)} %get-tuple-element.41.drag_ref, ...), custom_call_target="tpu_custom_call" | custom-call | flops 6000000 | bytes 2000000 | tf_op jit(solution)/shard_map/pallas_call | solution.py:207
  23.1 2.7 %collective-permute-start.11 = (f32[240,128]{1,0:T(8,128)S(1)}, f32[240,128]{1,0:T(8,128)S(1)}, u32[]{:S(2)}, u32[]{:S(2)}) collective-permute-start(f32[240,128]{1,0:T(8,128)S(1)} %get-tuple-element.48), channel_id=1, source_target_pairs={{0,1},{2,3},{1,0},{3,2},{4,5},{6,7},{5,4},{7,6},{8,9},{10,11},{9,8... | collective-permute-start | bytes 368648 | tf_op jit(solution)/shard_map/ppermute | solution.py:432
  25.8 0.7 collective-permute-start.12
  26.5 7.6 %collective-permute-start.4 = (f32[24,128]{1,0:T(8,128)S(1)}, f32[24,128]{1,0:T(8,128)S(1)}, u32[]{:S(2)}, u32[]{:S(2)}) collective-permute-start(f32[24,128]{1,0:T(8,128)S(1)} %get-tuple-element.43), channel_id=1, source_target_pairs={{0,4},{4,0},{8,12},{12,8},{16,20},{20,16},{24,28},{28,24},{1,5},{5... | collective-permute-start | bytes 36872 | tf_op jit(solution)/shard_map/ppermute | solution.py:443
  34.1 0.8 %collective-permute-done.4 = f32[24,128]{1,0:T(8,128)S(1)} collective-permute-done((f32[24,128]{1,0:T(8,128)S(1)}, f32[24,128]{1,0:T(8,128)S(1)}, u32[]{:S(2)}, u32[]{:S(2)}) %collective-permute-start.4) | collective-permute-done | bytes 12320 | tf_op jit(solution)/shard_map/ppermute | solution.py:443
  35.0 0.9 %collective-permute-start.5 = (f32[24,128]{1,0:T(8,128)S(1)}, f32[24,128]{1,0:T(8,128)S(1)}, u32[]{:S(2)}, u32[]{:S(2)}) collective-permute-start(f32[24,128]{1,0:T(8,128)S(1)} %add.19), channel_id=1, source_target_pairs={{0,8},{4,12},{8,0},{12,4},{16,24},{20,28},{24,16},{28,20},{1,9},{5... | collective-permute-start | bytes 36872 | tf_op jit(solution)/shard_map/ppermute | solution.py:443
  35.9 2.8 %collective-permute-done.5 = f32[24,128]{1,0:T(8,128)S(1)} collective-permute-done((f32[24,128]{1,0:T(8,128)S(1)}, f32[24,128]{1,0:T(8,128)S(1)}, u32[]{:S(2)}, u32[]{:S(2)}) %collective-permute-start.5) | collective-permute-done | bytes 12320 | tf_op jit(solution)/shard_map/ppermute | solution.py:443
  38.7 2.2 %collective-permute-start.6 = (f32[24,128]{1,0:T(8,128)S(1)}, f32[24,128]{1,0:T(8,128)S(1)}, u32[]{:S(2)}, u32[]{:S(2)}) collective-permute-start(f32[24,128]{1,0:T(8,128)S(1)} %add.20), channel_id=1, source_target_pairs={{0,16},{4,20},{8,24},{12,28},{16,0},{20,4},{24,8},{28,12},{1,17},{... | collective-permute-start | bytes 36872 | tf_op jit(solution)/shard_map/ppermute | solution.py:443
  40.8 1.7 %collective-permute-done.6 = f32[24,128]{1,0:T(8,128)S(1)} collective-permute-done((f32[24,128]{1,0:T(8,128)S(1)}, f32[24,128]{1,0:T(8,128)S(1)}, u32[]{:S(2)}, u32[]{:S(2)}) %collective-permute-start.6) | collective-permute-done | bytes 12320 | tf_op jit(solution)/shard_map/ppermute | solution.py:443
  42.5 2.1 %collective-permute-start.7 = (f32[24,128]{1,0:T(8,128)S(1)}, f32[24,128]{1,0:T(8,128)S(1)}, u32[]{:S(2)}, u32[]{:S(2)}) collective-permute-start(f32[24,128]{1,0:T(8,128)S(1)} %add.21), channel_id=1, source_target_pairs={{0,1},{1,0},{2,3},{3,2},{4,5},{5,4},{6,7},{7,6},{8,9},{9,8},{10,11... | collective-permute-start | bytes 36872 | tf_op jit(solution)/shard_map/ppermute | solution.py:443
  44.6 1.7 %collective-permute-done.7 = f32[24,128]{1,0:T(8,128)S(1)} collective-permute-done((f32[24,128]{1,0:T(8,128)S(1)}, f32[24,128]{1,0:T(8,128)S(1)}, u32[]{:S(2)}, u32[]{:S(2)}) %collective-permute-start.7) | collective-permute-done | bytes 12320 | tf_op jit(solution)/shard_map/ppermute | solution.py:443
  46.3 2.7 %collective-permute-start.8 = (f32[24,128]{1,0:T(8,128)S(1)}, f32[24,128]{1,0:T(8,128)S(1)}, u32[]{:S(2)}, u32[]{:S(2)}) collective-permute-start(f32[24,128]{1,0:T(8,128)S(1)} %add.22), channel_id=1, source_target_pairs={{0,2},{1,3},{2,0},{3,1},{4,6},{5,7},{6,4},{7,5},{8,10},{9,11},{10,... | collective-permute-start | bytes 36872 | tf_op jit(solution)/shard_map/ppermute | solution.py:443
  48.9 1.9 %collective-permute-done.8 = f32[24,128]{1,0:T(8,128)S(1)} collective-permute-done((f32[24,128]{1,0:T(8,128)S(1)}, f32[24,128]{1,0:T(8,128)S(1)}, u32[]{:S(2)}, u32[]{:S(2)}) %collective-permute-start.8) | collective-permute-done | bytes 12320 | tf_op jit(solution)/shard_map/ppermute | solution.py:443
  50.9 11.4 %shard_map.95.forecast_ref = f32[48,80,128]{2,1,0:T(8,128)S(1)} custom-call(s32[6]{0:T(128)S(1)} %stack.39.place_ref, f32[48,80,128]{2,1,0:T(8,128)S(1)} %get-tuple-element.40.state_ref, f32[22,80,128]{2,1,0:T(8,128)S(1)} %collective-permute-done.9.above_ref, f32[22,80,128]{2,1,0:T(8,128)} %collective-permute-done.10.below_ref, ...), custom_call_target="tpu_custom_call" | custom-call | flops 60000000 | bytes 30000000 | tf_op jit(solution)/shard_map/pallas_call | solution.py:291
  62.4 6.4 %shard_map.96 = f32[3840,128]{1,0:T(8,128)} custom-call(s32[6]{0:T(128)S(1)} %stack.39.place_ref, s32[24]{0:T(128)S(1)} %copy-done.2, s32[24]{0:T(128)S(1)} %copy-done.3, s32[24]{0:T(128)S(1)} %copy-done.5, f32[24]{0:T(128)S(1)} %copy-done.6, f32[24]{0:T(128)S(1)} %copy-done.7, f32[7]{0:T(128)S(1)} %copy-done.8, f32[24,128]{1,0:T(8,128)S(1)} %add.23.prior_ref, ...), custom_call_target="tpu_custom_call" | custom-call | tf_op jit(solution)/shard_map/pallas_call | solution.py:414
  (32 shorter events, 1.5 us)
Async XLA Ops:
  0.0 20.7 %copy-start.3 = (s32[24]{0:T(128)S(1)}, s32[24]{0:T(128)}, u32[]{:S(2)}) copy-start(s32[24]{0:T(128)} %owner_ref.3) | copy-start | bytes 292
  0.0 20.7 %copy-start.2 = (s32[24]{0:T(128)S(1)}, s32[24]{0:T(128)}, u32[]{:S(2)}) copy-start(s32[24]{0:T(128)} %order_ref.3) | copy-start | bytes 292
  0.0 20.7 %copy-start.4 = (s32[24]{0:T(128)S(1)}, s32[24]{0:T(128)}, u32[]{:S(2)}) copy-start(s32[24]{0:T(128)} %cell_ref.1) | copy-start | bytes 292
  0.0 1.6 %copy-start = (f32[3,80,16,128]{3,2,1,0:T(8,128)S(1)}, f32[3,80,16,128]{3,2,1,0:T(8,128)}, u32[]{:S(2)}) copy-start(f32[3,80,16,128]{3,2,1,0:T(8,128)} %param.9) | copy-start | bytes 5898244
  1.6 2.8 %copy-start.1 = (f32[16,128]{1,0:T(8,128)S(1)}, f32[16,128]{1,0:T(8,128)}, u32[]{:S(2)}) copy-start(f32[16,128]{1,0:T(8,128)} %drag_ref) | copy-start | bytes 24580
  4.4 6.6 %collective-permute-start.1 = (f32[16,128]{1,0:T(8,128)S(1)}, f32[16,128]{1,0:T(8,128)S(1)}, u32[]{:S(2)}, u32[]{:S(2)}) collective-permute-start(f32[16,128]{1,0:T(8,128)S(1)} %copy-done.1), channel_id=1, source_target_pairs={{1,2},{2,1},{5,6},{6,5},{9,10},{10,9},{13,14},{14,13},{17,18},{18,... | collective-permute-start | bytes 24584 | tf_op jit(solution)/shard_map/ppermute | solution.py:432
  5.0 7.5 %collective-permute-start = (f32[16,128]{1,0:T(8,128)S(1)}, f32[16,128]{1,0:T(8,128)S(1)}, u32[]{:S(2)}, u32[]{:S(2)}) collective-permute-start(f32[16,128]{1,0:T(8,128)S(1)} %copy-done.1), channel_id=1, source_target_pairs={{0,1},{2,3},{1,0},{3,2},{4,5},{6,7},{5,4},{7,6},{8,9},{10,11},{9,8... | collective-permute-start | bytes 24584 | tf_op jit(solution)/shard_map/ppermute | solution.py:432
  12.6 38.3 %collective-permute-start.9 = (f32[22,80,128]{2,1,0:T(8,128)}, f32[22,80,128]{2,1,0:T(8,128)S(1)}, u32[]{:S(2)}, u32[]{:S(2)}) collective-permute-start(f32[22,80,128]{2,1,0:T(8,128)} %get-tuple-element.44), channel_id=1, source_target_pairs={{0,1},{1,2},{2,3},{4,5},{5,6},{6,7},{8,9},{9,10},{10,11},{12,13},{... | collective-permute-start | bytes 2703368 | tf_op jit(solution)/shard_map/ppermute | solution.py:427
  16.6 34.3 %collective-permute-start.10 = (f32[22,80,128]{2,1,0:T(8,128)}, f32[22,80,128]{2,1,0:T(8,128)}, u32[]{:S(2)}, u32[]{:S(2)}) collective-permute-start(f32[22,80,128]{2,1,0:T(8,128)} %get-tuple-element.45), channel_id=1, source_target_pairs={{1,0},{2,1},{3,2},{5,4},{6,5},{7,6},{9,8},{10,9},{11,10},{13,12},{... | collective-permute-start | bytes 2703368 | tf_op jit(solution)/shard_map/ppermute | solution.py:427
  18.6 1.4 %collective-permute-start.2 = (f32[272,128]{1,0:T(8,128)S(1)}, f32[272,128]{1,0:T(8,128)S(1)}, u32[]{:S(2)}, u32[]{:S(2)}) collective-permute-start(f32[272,128]{1,0:T(8,128)S(1)} %get-tuple-element.36), channel_id=1, source_target_pairs={{0,4},{8,12},{16,20},{24,28},{4,0},{12,8},{20,16},{28,24},{1,5},{9... | collective-permute-start | bytes 417800 | tf_op jit(solution)/shard_map/ppermute | solution.py:432
  18.6 1.3 %collective-permute-start.3 = (f32[272,128]{1,0:T(8,128)S(1)}, f32[272,128]{1,0:T(8,128)S(1)}, u32[]{:S(2)}, u32[]{:S(2)}) collective-permute-start(f32[272,128]{1,0:T(8,128)S(1)} %get-tuple-element.37), channel_id=1, source_target_pairs={{4,8},{12,16},{20,24},{8,4},{16,12},{24,20},{5,9},{13,17},{21,25},... | collective-permute-start | bytes 417800 | tf_op jit(solution)/shard_map/ppermute | solution.py:432
  23.1 27.7 %collective-permute-start.11 = (f32[240,128]{1,0:T(8,128)S(1)}, f32[240,128]{1,0:T(8,128)S(1)}, u32[]{:S(2)}, u32[]{:S(2)}) collective-permute-start(f32[240,128]{1,0:T(8,128)S(1)} %get-tuple-element.48), channel_id=1, source_target_pairs={{0,1},{2,3},{1,0},{3,2},{4,5},{6,7},{5,4},{7,6},{8,9},{10,11},{9,8... | collective-permute-start | bytes 368648 | tf_op jit(solution)/shard_map/ppermute | solution.py:432
  25.8 25.0 %collective-permute-start.12 = (f32[240,128]{1,0:T(8,128)S(1)}, f32[240,128]{1,0:T(8,128)S(1)}, u32[]{:S(2)}, u32[]{:S(2)}) collective-permute-start(f32[240,128]{1,0:T(8,128)S(1)} %get-tuple-element.49), channel_id=1, source_target_pairs={{1,2},{2,1},{5,6},{6,5},{9,10},{10,9},{13,14},{14,13},{17,18},{18,... | collective-permute-start | bytes 368648 | tf_op jit(solution)/shard_map/ppermute | solution.py:432
  26.5 8.5 %collective-permute-start.4 = (f32[24,128]{1,0:T(8,128)S(1)}, f32[24,128]{1,0:T(8,128)S(1)}, u32[]{:S(2)}, u32[]{:S(2)}) collective-permute-start(f32[24,128]{1,0:T(8,128)S(1)} %get-tuple-element.43), channel_id=1, source_target_pairs={{0,4},{4,0},{8,12},{12,8},{16,20},{20,16},{24,28},{28,24},{1,5},{5... | collective-permute-start | bytes 36872 | tf_op jit(solution)/shard_map/ppermute | solution.py:443
  35.0 3.7 %collective-permute-start.5 = (f32[24,128]{1,0:T(8,128)S(1)}, f32[24,128]{1,0:T(8,128)S(1)}, u32[]{:S(2)}, u32[]{:S(2)}) collective-permute-start(f32[24,128]{1,0:T(8,128)S(1)} %add.19), channel_id=1, source_target_pairs={{0,8},{4,12},{8,0},{12,4},{16,24},{20,28},{24,16},{28,20},{1,9},{5... | collective-permute-start | bytes 36872 | tf_op jit(solution)/shard_map/ppermute | solution.py:443
  38.7 3.8 %collective-permute-start.6 = (f32[24,128]{1,0:T(8,128)S(1)}, f32[24,128]{1,0:T(8,128)S(1)}, u32[]{:S(2)}, u32[]{:S(2)}) collective-permute-start(f32[24,128]{1,0:T(8,128)S(1)} %add.20), channel_id=1, source_target_pairs={{0,16},{4,20},{8,24},{12,28},{16,0},{20,4},{24,8},{28,12},{1,17},{... | collective-permute-start | bytes 36872 | tf_op jit(solution)/shard_map/ppermute | solution.py:443
  42.5 3.7 %collective-permute-start.7 = (f32[24,128]{1,0:T(8,128)S(1)}, f32[24,128]{1,0:T(8,128)S(1)}, u32[]{:S(2)}, u32[]{:S(2)}) collective-permute-start(f32[24,128]{1,0:T(8,128)S(1)} %add.21), channel_id=1, source_target_pairs={{0,1},{1,0},{2,3},{3,2},{4,5},{5,4},{6,7},{7,6},{8,9},{9,8},{10,11... | collective-permute-start | bytes 36872 | tf_op jit(solution)/shard_map/ppermute | solution.py:443
  46.3 4.6 %collective-permute-start.8 = (f32[24,128]{1,0:T(8,128)S(1)}, f32[24,128]{1,0:T(8,128)S(1)}, u32[]{:S(2)}, u32[]{:S(2)}) collective-permute-start(f32[24,128]{1,0:T(8,128)S(1)} %add.22), channel_id=1, source_target_pairs={{0,2},{1,3},{2,0},{3,1},{4,6},{5,7},{6,4},{7,5},{8,10},{9,11},{10,... | collective-permute-start | bytes 36872 | tf_op jit(solution)/shard_map/ppermute | solution.py:443
  50.9 11.5 %copy-start.5 = (s32[24]{0:T(128)S(1)}, s32[24]{0:T(128)}, u32[]{:S(2)}) copy-start(s32[24]{0:T(128)} %reach_ref.1) | copy-start | bytes 292
  50.9 11.5 %copy-start.6 = (f32[24]{0:T(128)S(1)}, f32[24]{0:T(128)}, u32[]{:S(2)}) copy-start(f32[24]{0:T(128)} %value_ref.1) | copy-start | bytes 292
  50.9 11.5 %copy-start.7 = (f32[24]{0:T(128)S(1)}, f32[24]{0:T(128)}, u32[]{:S(2)}) copy-start(f32[24]{0:T(128)} %error_ref.1) | copy-start | bytes 292
  50.9 11.5 %copy-start.8 = (f32[7]{0:T(128)S(1)}, f32[7]{0:T(128)}, u32[]{:S(2)}) copy-start(f32[7]{0:T(128)} %taper_ref.1) | copy-start | bytes 88

commit v5 on v2

--- a/solution.py
+++ b/solution.py
@@ -14,7 +14,8 @@
 HIGHEST = lax.Precision.HIGHEST
 F32 = jnp.float32
 BF16 = jnp.bfloat16
-VMEM_LIMIT = 24 * 1024 * 1024
+VMEM_LIMIT = 16 * 1024 * 1024
+GROUP = 40
 
 VSPEC = pl.BlockSpec(memory_space=pltpu.VMEM)
 SSPEC = pl.BlockSpec(memory_space=pltpu.SMEM)
@@ -34,9 +35,10 @@
     return x if shift == 0 else pltpu.roll(x, shift, x.ndim - 1)
 
 
-def arrange_kernel(members, rows, x_ref, out_ref, lower_ref, upper_ref, left_ref, right_ref):
+def arrange_kernel(members, rows, place_ref, x_ref, drag_ref, out_ref, lower_ref, upper_ref, even_ref, odd_ref):
     cols = x_ref.shape[1]
     lane = lanes_of((8, cols))
+    odd_x = place_ref[0] // place_ref[5] % 2 == 1
 
     def group(g, carry):
         here = pl.ds(pl.multiple_of(g * 8, 8), 8)
@@ -55,25 +57,66 @@
                 left = jnp.where(there, roll_lanes(row, MARGIN * r), left)
                 right = jnp.where(there, roll_lanes(row, MARGIN * (r + 1)), right)
             at = pl.ds(pl.multiple_of(f * members + g * 8, 8), 8)
-            left_ref[at, :] = left
-            right_ref[at, :] = right
+            even_ref[at, :] = jnp.where(odd_x, left, right)
+            odd_ref[at, :] = jnp.where(odd_x, right, left)
         return carry
 
     lax.fori_loop(0, members // 8, group, 0)
-
-
-def arrange(x, members, rows):
-    cols = x.shape[1]
-    edge = jax.ShapeDtypeStruct((3 * members, cols), F32)
+    even_ref[3 * members :, :] = drag_ref[...]
+    odd_ref[3 * members :, :] = drag_ref[...]
+
+
+def arrange(place, x, drag, members):
+    rows, cols = drag.shape
+    message = jax.ShapeDtypeStruct((3 * members + rows, cols), F32)
     band = jax.ShapeDtypeStruct((3 * MARGIN - 2, members, cols), F32)
     return pl.pallas_call(
         functools.partial(arrange_kernel, members, rows),
-        out_shape=(jax.ShapeDtypeStruct((3 * rows, members, cols), F32), band, band, edge, edge),
-        in_specs=[VSPEC],
+        out_shape=(jax.ShapeDtypeStruct((3 * rows, members, cols), F32), band, band, message, message),
+        in_specs=[SSPEC, VSPEC, VSPEC],
         out_specs=(VSPEC,) * 5,
         compiler_params=pltpu.CompilerParams(vmem_limit_bytes=VMEM_LIMIT),
         cost_estimate=pl.CostEstimate(flops=4_000_000, bytes_accessed=6_000_000, transcendentals=0),
-    )(x)
+    )(place, x, drag)
+
+
+def corner_kernel(place_ref, drag_ref, even_ref, odd_ref, left_ref, right_ref, margin_ref, even_out, odd_out):
+    count, cols = left_ref.shape
+    rows = drag_ref.shape[0]
+    half = cols // 2
+    odd_y = place_ref[0] % place_ref[5] % 2 == 1
+    odd_x = place_ref[0] // place_ref[5] % 2 == 1
+    even, odd = even_ref[...], odd_ref[...]
+    left, right = jnp.where(odd_x, even, odd), jnp.where(odd_x, odd, even)
+    margin = jnp.where(lanes_of((rows, cols)) < half, right[count:], left[count:])
+    margin_ref[...] = margin
+    left, right = left[:count], right[:count]
+    left_ref[...] = left
+    right_ref[...] = right
+    first_half = lanes_of((count, cols)) < half
+    lower = jnp.where(first_half, left, roll_lanes(right, half))
+    upper = jnp.where(first_half, roll_lanes(left, half), right)
+    even_out[:count, :] = jnp.where(odd_y, lower, upper)
+    odd_out[:count, :] = jnp.where(odd_y, upper, lower)
+    drag = drag_ref[...]
+    for at, part in ((count, drag), (count + MARGIN, margin)):
+        lower, upper = part[:MARGIN], part[rows - MARGIN :]
+        even_out[at : at + MARGIN, :] = jnp.where(odd_y, lower, upper)
+        odd_out[at : at + MARGIN, :] = jnp.where(odd_y, upper, lower)
+
+
+def corner(place, drag, even, odd):
+    rows, cols = drag.shape
+    count = even.shape[0] - rows
+    edge = jax.ShapeDtypeStruct((count, cols), F32)
+    message = jax.ShapeDtypeStruct((count + 2 * MARGIN, cols), F32)
+    return pl.pallas_call(
+        corner_kernel,
+        out_shape=(edge, edge, jax.ShapeDtypeStruct((rows, cols), F32), message, message),
+        in_specs=[SSPEC] + [VSPEC] * 3,
+        out_specs=(VSPEC,) * 5,
+        compiler_params=pltpu.CompilerParams(vmem_limit_bytes=VMEM_LIMIT),
+    )(place, drag, even, odd)
 
 
 def grid_factor(place_ref, shape, rows, cols):
@@ -85,82 +128,6 @@
     return jnp.where(ok, 1.0, 0.0)
 
 
-def share_kernel(
-    members, rows,
-    place_ref, order_ref, owner_ref, cell_ref, state_ref, drag_ref, even_ref, odd_ref,
-    keep_ref, prior_ref, turned,
-):
-    cols = drag_ref.shape[1]
-    wide = 2 * cols
-    total = rows + 2 * MARGIN
-    size_y = place_ref[5]
-    ix, iy = place_ref[0] // size_y, place_ref[0] % size_y
-    shape = (total, wide)
-    lane = lanes_of((total, cols))
-    odd = (ix % 2) == 1
-    even_part, odd_part = even_ref[...], odd_ref[...]
-    before = jnp.where(odd, even_part, odd_part)
-    after = jnp.where(odd, odd_part, even_part)
-    drag = jnp.concatenate([drag_ref[...], jnp.where(lane < cols // 2, after, before)], axis=1)
-    keep = 1.0 - drag
-    keep_ref[...] = keep
-    slope = 0.2 * grid_factor(place_ref, shape, rows, cols)
-    sub, wlane = sublanes_of(shape), lanes_of(shape)
-    turned[...] = jnp.zeros_like(turned)
-    spot = lanes_of((members, cols))
-
-    def one(i, carry):
-        k = order_ref[i]
-        tile, cell = owner_ref[k], cell_ref[k]
-        field, inner = cell // (rows * cols), cell % (rows * cols)
-        row = (tile % size_y - iy) * rows + inner // cols
-        col = (tile // size_y - ix) * cols + inner % cols
-        near = (row >= -MARGIN) & (row < rows + MARGIN) & (col >= -MARGIN) & (col < cols + MARGIN)
-
-        @pl.when(near)
-        def _():
-            at = jnp.where(col < 0, col + wide, col)
-            start = jnp.where((sub == row + MARGIN) & (wlane == at), 1.0, 0.0)
-            h = jnp.where(field == 0, start, 0.0)
-            u = jnp.where(field == 1, start, 0.0)
-            v = jnp.where(field == 2, start, 0.0)
-            for _step in range(STEPS):
-                h = h + slope * (
-                    (roll_lanes(u, -1) - roll_lanes(u, 1)) + (pltpu.roll(v, total - 1, 0) - pltpu.roll(v, 1, 0))
-                )
-                u, v = (
-                    keep * u + slope * (roll_lanes(h, -1) - roll_lanes(h, 1)) - 0.1 * v,
-                    keep * v + slope * (pltpu.roll(h, total - 1, 0) - pltpu.roll(h, 1, 0)) + 0.1 * u,
-                )
-            sums = jnp.zeros((members, cols), F32)
-            for f, weights in enumerate((h, u, v)):
-                for r in range(rows):
-                    sums = sums + weights[MARGIN + r : MARGIN + r + 1, :cols] * state_ref[f * rows + r]
-            column = jnp.sum(sums, axis=1, keepdims=True)
-            turned[0:members, :] = jnp.where(spot == i, column, turned[0:members, :])
-
-        return carry
-
-    lax.fori_loop(0, order_ref.shape[0], one, 0)
-    prior_ref[...] = jnp.transpose(turned[...])[: prior_ref.shape[0]]
-
-
-def share(place, order, owner, cell, states, drag, even, odd, members, rows):
-    cols = drag.shape[1]
-    return pl.pallas_call(
-        functools.partial(share_kernel, members, rows),
-        out_shape=(
-            jax.ShapeDtypeStruct((drag.shape[0], 2 * cols), F32),
-            jax.ShapeDtypeStruct((order.shape[0], cols), F32),
-        ),
-        in_specs=[SSPEC] * 4 + [VSPEC] * 4,
-        out_specs=(VSPEC, VSPEC),
-        scratch_shapes=[pltpu.VMEM((cols, cols), F32)],
-        compiler_params=pltpu.CompilerParams(vmem_limit_bytes=VMEM_LIMIT),
-        cost_estimate=pl.CostEstimate(flops=6_000_000, bytes_accessed=2_000_000, transcendentals=0),
-    )(place, order, owner, cell, states, drag, even, odd)
-
-
 def wide_row(lane, main, left, left_at, right, right_at):
     cols = main.shape[1]
     halo = jnp.where(lane >= cols - MARGIN, roll_lanes(left, cols - MARGIN - left_at), 0.0)
@@ -170,26 +137,38 @@
 
 def forecast_kernel(
     members, rows,
-    place_ref, state_ref, above_ref, below_ref, left_ref, right_ref, cabove_ref, cbelow_ref, keep_ref,
-    out_ref,
-    state, keep, slope,
+    place_ref, order_ref, owner_ref, cell_ref,
+    state_ref, above_ref, below_ref, left_ref, right_ref, ceven_ref, codd_ref, drag_ref, margin_ref,
+    out_ref, prior_ref,
+    state, keep, slope, across,
 ):
     cols = state_ref.shape[2]
     wide = 2 * cols
     total = rows + 2 * MARGIN
-    lane = lanes_of((8, cols))
+    lane = lanes_of((GROUP, cols))
     half = cols // 2
     factor = -0.2 * grid_factor(place_ref, (total, wide), rows, cols)
+    odd_y = place_ref[0] % place_ref[5] % 2 == 1
+    source, target = sublanes_of((wide, wide)), lanes_of((wide, wide))
+    shift = jnp.where(source == (target + 1) % wide, 1.0, jnp.where(target == (source + 1) % wide, -1.0, 0.0)).astype(BF16)
+    count = 3 * members
+    parts = []
+    for here, own in ((count, drag_ref), (count + MARGIN, margin_ref)):
+        even, odd = ceven_ref[here : here + MARGIN, :], codd_ref[here : here + MARGIN, :]
+        above, below = jnp.where(odd_y, even, odd), jnp.where(odd_y, odd, even)
+        parts.append(jnp.concatenate([above, own[...], below], axis=0))
+    kept = 1.0 - jnp.concatenate(parts, axis=1)
     for r in range(total):
-        keep[r] = jnp.broadcast_to(keep_ref[r : r + 1, :], (8, wide))
-        slope[r] = jnp.broadcast_to(factor[r : r + 1, :], (8, wide))
+        keep[r] = jnp.broadcast_to(kept[r : r + 1, :], (GROUP, wide))
+        slope[r] = jnp.broadcast_to(factor[r : r + 1, :], (GROUP, wide))
 
     def group(g, carry):
-        here = pl.ds(pl.multiple_of(g * 8, 8), 8)
+        here = pl.ds(pl.multiple_of(g * GROUP, GROUP), GROUP)
         for f in range(3):
-            at = pl.ds(pl.multiple_of(f * members + g * 8, 8), 8)
+            at = pl.ds(pl.multiple_of(f * members + g * GROUP, GROUP), GROUP)
             ledge, redge = left_ref[at, :], right_ref[at, :]
-            cab, cbe = cabove_ref[at, :], cbelow_ref[at, :]
+            ceven, codd = ceven_ref[at, :], codd_ref[at, :]
+            cab, cbe = jnp.where(odd_y, ceven, codd), jnp.where(odd_y, codd, ceven)
             depth = MARGIN if f == 2 else MARGIN - 1
             for r in range(MARGIN - depth, MARGIN + rows + depth):
                 if r < MARGIN:
@@ -204,44 +183,67 @@
                     main = below_ref[f * (MARGIN - 1) + q, here, :]
                     value = wide_row(lane, main, cbe, MARGIN * q, cbe, half + MARGIN * q)
                 state[f, r] = value
+        def column_slope(f, low, high):
+            x = state[f, low:high].reshape((high - low) * GROUP, wide)
+            top = x.astype(BF16)
+            rest = (x - top.astype(F32)).astype(BF16)
+            n = (high - low) * GROUP
+            cut = n // 2 // 16 * 16
+            parts = []
+            for p, q in ((0, cut), (cut, n)):
+                parts.append(jnp.dot(top[p:q], shift, preferred_element_type=F32))
+                parts.append(jnp.dot(rest[p:q], shift, preferred_element_type=F32))
+            d = jnp.concatenate([parts[0] + parts[1], parts[2] + parts[3]], axis=0)
+            across[low:high] = d.reshape(high - low, GROUP, wide)
+
         for step in range(STEPS):
             reach = 2 * (STEPS - step) - 1
-            for r in range(MARGIN - reach, MARGIN + rows + reach):
-                u = state[1, r]
-                div = (roll_lanes(u, -1) - roll_lanes(u, 1)) + (state[2, r + 1] - state[2, r - 1])
+            low, high = MARGIN - reach, MARGIN + rows + reach
+            column_slope(1, low, high)
+            for r in range(low, high):
+                div = across[r] + (state[2, r + 1] - state[2, r - 1])
                 state[0, r] = state[0, r] + slope[r] * div
-            reach -= 1
-            for r in range(MARGIN - reach, MARGIN + rows + reach):
-                h = state[0, r]
+            low, high = low + 1, high - 1
+            column_slope(0, low, high)
+            for r in range(low, high):
                 u, v = state[1, r], state[2, r]
                 k, c = keep[r], slope[r]
-                state[1, r] = k * u + c * (roll_lanes(h, -1) - roll_lanes(h, 1)) + 0.1 * v
+                state[1, r] = k * u + c * across[r] + 0.1 * v
                 state[2, r] = k * v + c * (state[0, r + 1] - state[0, r - 1]) - 0.1 * u
         for f in range(3):
             for r in range(rows):
                 out_ref[f * rows + r, here, :] = state[f, MARGIN + r, :, 0:cols]
         return carry
 
-    lax.fori_loop(0, members // 8, group, 0)
-
-
-def forecast(place, states, above, below, left, right, cabove, cbelow, keep):
+    lax.fori_loop(0, members // GROUP, group, 0)
+
+    prior_ref[...] = jnp.zeros_like(prior_ref)
+    eight = lanes_of((8, cols))
+    for i in range(order_ref.shape[0]):
+        which = order_ref[i]
+
+        @pl.when(owner_ref[which] == place_ref[0])
+        def _():
+            cell = cell_ref[which]
+            one = jnp.where(eight == cell % cols, 1.0, 0.0)
+            prior_ref[i : i + 1, 0:members] = lax.dot_general(
+                one, out_ref[cell // cols], NT, precision=HIGHEST, preferred_element_type=F32
+            )[0:1]
+
+
+def forecast(place, order, owner, cell, states, *arrays):
     members, cols = states.shape[1:]
     rows = states.shape[0] // 3
     total = rows + 2 * MARGIN
     return pl.pallas_call(
         functools.partial(forecast_kernel, members, rows),
-        out_shape=jax.ShapeDtypeStruct(states.shape, F32),
-        in_specs=[SSPEC] + [VSPEC] * 8,
-        out_specs=VSPEC,
-        scratch_shapes=[
-            pltpu.VMEM((3, total, 8, 2 * cols), F32),
-            pltpu.VMEM((total, 8, 2 * cols), F32),
-            pltpu.VMEM((total, 8, 2 * cols), F32),
-        ],
+        out_shape=(jax.ShapeDtypeStruct(states.shape, F32), jax.ShapeDtypeStruct((order.shape[0], cols), F32)),
+        in_specs=[SSPEC] * 4 + [VSPEC] * (1 + len(arrays)),
+        out_specs=(VSPEC, VSPEC),
+        scratch_shapes=[pltpu.VMEM((3, total, GROUP, 2 * cols), F32)] + [pltpu.VMEM((total, GROUP, 2 * cols), F32)] * 3,
         compiler_params=pltpu.CompilerParams(vmem_limit_bytes=VMEM_LIMIT),
         cost_estimate=pl.CostEstimate(flops=60_000_000, bytes_accessed=30_000_000, transcendentals=0),
-    )(place, states, above, below, left, right, cabove, cbelow, keep)
+    )(place, order, owner, cell, states, *arrays)
 
 
 def localize(distance, reach, taper_ref):
@@ -368,14 +370,9 @@
     return lax.ppermute(upper, axis, forward), lax.ppermute(lower, axis, backward)
 
 
-def swap_pairs(x, axis):
-    count = lax.axis_size(axis)
-
-    def swap(start):
-        pairs = [(i, i + 1) for i in range(start, count - 1, 2)]
-        return lax.ppermute(x, axis, pairs + [(b, a) for a, b in pairs])
-
-    return swap(0), swap(1)
+def swap_pairs(x, axis, start):
+    pairs = [(i, i + 1) for i in range(start, lax.axis_size(axis) - 1, 2)]
+    return lax.ppermute(x, axis, pairs + [(b, a) for a, b in pairs])
 
 
 def add_over(x, axes):
@@ -406,22 +403,14 @@
         ]
     ).astype(jnp.int32)
     flat = status.reshape(3 * members * rows, cols)
-    even, odd = swap_pairs(drag, "gy")
-    is_odd = (iy % 2) == 1
-    above = jnp.where(is_odd, even[rows - MARGIN :], odd[rows - MARGIN :])
-    below = jnp.where(is_odd, odd[:MARGIN], even[:MARGIN])
-    drag = jnp.concatenate([above, drag, below], axis=0)
-    even, odd = swap_pairs(drag, "gx")
-
-    states, lower, upper, first, last = arrange(flat, members, rows)
+    states, lower, upper, even, odd = arrange(place, flat, drag, members)
     above, below = to_neighbours("gy", lower, upper)
-    keep, priors = share(place, order, owner, cell, states, drag, even, odd, members, rows)
-    left, right = to_neighbours("gx", first, last)
-    half = cols // 2
-    small_lower = jnp.concatenate([left[:, :half], right[:, :half]], axis=1)
-    small_upper = jnp.concatenate([left[:, half:], right[:, half:]], axis=1)
-    cabove, cbelow = to_neighbours("gy", small_lower, small_upper)
-    states = forecast(place, states, above, below, left, right, cabove, cbelow, keep)
+    even, odd = swap_pairs(even, "gx", 0), swap_pairs(odd, "gx", 1)
+    left, right, margin, even, odd = corner(place, drag, even, odd)
+    even, odd = swap_pairs(even, "gy", 0), swap_pairs(odd, "gy", 1)
+    states, priors = forecast(
+        place, order, owner, cell, states, above, below, left, right, even, odd, drag, margin
+    )
     priors = add_over(priors, ("gx", "gy"))
     result = assimilate(place, order, owner, reach, value, error, taper, priors, states, members, rows)
     return result.reshape(status.shape)

time: 76 us -> 67.5 us (0.89)
  starting transfers between devices: 40.3 us -> 17.6 us
  waiting for transfers between devices: 9.1 us -> 29.7 us
  Pallas kernels: 22.7 us -> 17.3 us
  other arithmetic: 0.87 us -> 0.02 us
    ppermute x4, waiting for transfers between devices: 0.76 us -> 20 us  [swap_pairs(): return lax.ppermute(x, axis, pairs + [(b, a) for a, b in pairs])]
    ppermute x4, starting transfers between devices: 12 us -> 4.1 us  [swap_pairs(): return lax.ppermute(x, axis, pairs + [(b, a) for a, b in pairs])]
    ppermute x3 -> x1, starting transfers between devices: 12.2 us -> 5.01 us  [to_neighbours(): lax.ppermute(upper, axis, forward)]
    ppermute x5, starting transfers between devices: 12.2 us -> 7.2 us  [add_over(): x = x + lax.ppermute(x, axis, [(i, i ^ span) for i in range(count)])]
    pallas_call x1, Pallas kernels: 11.4 us -> 7.99 us  [forecast(): pl.pallas_call(functools.partial(forecast_kernel, members, rows), out_sha...]
    ppermute x3 -> x1, starting transfers between devices: 3.86 us -> 1.29 us  [to_neighbours(): lax.ppermute(lower, axis, backward)]
    pallas_call x1, Pallas kernels: 2.4 us -> 0.7 us  [corner(): pl.pallas_call(corner_kernel, out_shape=(edge, edge, jax.ShapeDtypeStruct...]
    ppermute x5, waiting for transfers between devices: 8.32 us -> 9.7 us  [add_over(): x = x + lax.ppermute(x, axis, [(i, i ^ span) for i in range(count)])]
  transfers between devices with their start and end apart: 15 -> 11, of which waited for: 6 -> 7; matrix products, arithmetic and copies ran while one was open for 1% -> 0% of each run, Pallas kernels for 6% -> 1%
where the time goes in v5:
time: 67.5 us; the launch traced here: 67.2 us
  waiting for transfers between devices  29.7 us (44%)
  starting transfers between devices  17.6 us (26%)
  Pallas kernels  17.3 us (26%)
  local copies, waits for them, and re-layouts  2.37 us (4%)
    ppermute x4, waiting for transfers between devices, swap_pairs(): return lax.ppermute(x, axis, pairs + [(b, a) for a, b in pairs])  20 us
    ppermute x5, waiting for transfers between devices, add_over(): x = x + lax.ppermute(x, axis, [(i, i ^ span) for i in range(count)])  9.7 us
    pallas_call x1, Pallas kernels, forecast(): pl.pallas_call(functools.partial(forecast_kernel, members, rows), out_sha...  7.99 us
    ppermute x5, starting transfers between devices, add_over(): x = x + lax.ppermute(x, axis, [(i, i ^ span) for i in range(count)])  7.2 us
    pallas_call x1, Pallas kernels, assimilate(): pl.pallas_call(functools.partial(assimilate_kernel, members, rows), out_s...  6.36 us
    ppermute x1, starting transfers between devices, to_neighbours(): lax.ppermute(upper, axis, forward)  5.01 us
    ppermute x4, starting transfers between devices, swap_pairs(): return lax.ppermute(x, axis, pairs + [(b, a) for a, b in pairs])  4.1 us
    unnamed x20, local copies, waits for them, and re-layouts  2.28 us
  transfers between devices with their start and end apart: 11, of which 7 were waited for; matrix products, arithmetic and copies ran while one was open for 0% of the time, Pallas kernels for 1%

profile of v5, /device:TPU:0, one launch (start us, length us, event | category | flops | bytes accessed | tf_op | source)
XLA Modules:
  0.0 67.2 jit_solution(153747121107558750)
XLA Ops:
  0.0 0.1 stack.39.place_ref
  0.1 1.5 %copy-done = f32[3,80,16,128]{3,2,1,0:T(8,128)S(1)} copy-done((f32[3,80,16,128]{3,2,1,0:T(8,128)S(1)}, f32[3,80,16,128]{3,2,1,0:T(8,128)}, u32[]{:S(2)}) %copy-start) | copy-done | bytes 1966104
  1.6 0.7 %copy-done.1 = f32[16,128]{1,0:T(8,128)S(1)} copy-done((f32[16,128]{1,0:T(8,128)S(1)}, f32[16,128]{1,0:T(8,128)}, u32[]{:S(2)}) %copy-start.1) | copy-done | bytes 8216
  2.3 2.2 %shard_map.91 = (f32[48,80,128]{2,1,0:T(8,128)S(1)}, f32[22,80,128]{2,1,0:T(8,128)S(1)}, f32[22,80,128]{2,1,0:T(8,128)S(1)}, f32[256,128]{1,0:T(8,128)S(1)}, f32[256,128]{1,0:T(8,128)S(1)}) custom-call(s32[6]{0:T(128)S(1)} %stack.39.place_ref, f32[3840,128]{1,0:T(8,128)S(1)} %bitcast.7, f32[16,128]{1,0:T(8,128)S(1)} %copy-done.1), custom_call_target="tpu_custom_call" | custom-call | flops 4000000 | bytes 6000000 | tf_op jit(solution)/shard_map/pallas_call | solution.py:73
  4.6 5.0 %collective-permute-start = (f32[22,80,128]{2,1,0:T(8,128)S(1)}, f32[22,80,128]{2,1,0:T(8,128)S(1)}, u32[]{:S(2)}, u32[]{:S(2)}) collective-permute-start(f32[22,80,128]{2,1,0:T(8,128)S(1)} %get-tuple-element.18), channel_id=1, source_target_pairs={{0,1},{1,2},{2,3},{4,5},{5,6},{6,7},{8,9},{9,10},{10,11},{12,13},{... | collective-permute-start | bytes 2703368 | tf_op jit(solution)/shard_map/ppermute | solution.py:370
  9.6 1.3 %collective-permute-start.1 = (f32[22,80,128]{2,1,0:T(8,128)S(1)}, f32[22,80,128]{2,1,0:T(8,128)S(1)}, u32[]{:S(2)}, u32[]{:S(2)}) collective-permute-start(f32[22,80,128]{2,1,0:T(8,128)S(1)} %get-tuple-element.19), channel_id=1, source_target_pairs={{1,0},{2,1},{3,2},{5,4},{6,5},{7,6},{9,8},{10,9},{11,10},{13,12},{... | collective-permute-start | bytes 2703368 | tf_op jit(solution)/shard_map/ppermute | solution.py:370
  10.9 0.1 collective-permute-start.2
  11.0 0.7 collective-permute-start.3
  11.6 0.7 collective-permute-done.2.even_ref
  12.3 0.7 %shard_map.92 = (f32[240,128]{1,0:T(8,128)S(1)}, f32[240,128]{1,0:T(8,128)S(1)}, f32[16,128]{1,0:T(8,128)S(1)}, f32[256,128]{1,0:T(8,128)S(1)}, f32[256,128]{1,0:T(8,128)S(1)}) custom-call(s32[6]{0:T(128)S(1)} %stack.39.place_ref, f32[16,128]{1,0:T(8,128)S(1)} %copy-done.1, f32[256,128]{1,0:T(8,128)S(1)} %collective-permute-done.2.even_ref, ...), custom_call_target="tpu_custom_call" | custom-call | tf_op jit(solution)/shard_map/pallas_call | solution.py:113
  13.0 2.7 %collective-permute-start.4 = (f32[256,128]{1,0:T(8,128)S(1)}, f32[256,128]{1,0:T(8,128)S(1)}, u32[]{:S(2)}, u32[]{:S(2)}) collective-permute-start(f32[256,128]{1,0:T(8,128)S(1)} %get-tuple-element.24), channel_id=1, source_target_pairs={{0,1},{2,3},{1,0},{3,2},{4,5},{6,7},{5,4},{7,6},{8,9},{10,11},{9,8... | collective-permute-start | bytes 393224 | tf_op jit(solution)/shard_map/ppermute | solution.py:375
  15.7 0.7 collective-permute-start.5
  16.4 19.4 %collective-permute-done.4.ceven_ref = f32[256,128]{1,0:T(8,128)S(1)} collective-permute-done((f32[256,128]{1,0:T(8,128)S(1)}, f32[256,128]{1,0:T(8,128)S(1)}, u32[]{:S(2)}, u32[]{:S(2)}) %collective-permute-start.4) | collective-permute-done | bytes 131104 | tf_op jit(solution)/shard_map/ppermute | solution.py:375
  35.9 8.0 %shard_map.93 = (f32[48,80,128]{2,1,0:T(8,128)S(1)}, f32[24,128]{1,0:T(8,128)S(1)}) custom-call(s32[6]{0:T(128)S(1)} %stack.39.place_ref, s32[24]{0:T(128)S(1)} %copy-done.3, s32[24]{0:T(128)S(1)} %copy-done.4, s32[24]{0:T(128)S(1)} %copy-done.9, f32[48,80,128]{2,1,0:T(8,128)S(1)} %get-tuple-element.17.state_ref, ...), custom_call_target="tpu_custom_call" | custom-call | flops 60000000 | bytes 30000000 | tf_op jit(solution)/shard_map/pallas_call | solution.py:238
  43.9 1.2 %collective-permute-done.6 = f32[24,128]{1,0:T(8,128)S(1)} collective-permute-done((f32[24,128]{1,0:T(8,128)S(1)}, f32[24,128]{1,0:T(8,128)S(1)}, u32[]{:S(2)}, u32[]{:S(2)}) %collective-permute-start.6) | collective-permute-done | bytes 12320 | tf_op jit(solution)/shard_map/ppermute | solution.py:386
  45.1 1.6 %collective-permute-start.7 = (f32[24,128]{1,0:T(8,128)S(1)}, f32[24,128]{1,0:T(8,128)S(1)}, u32[]{:S(2)}, u32[]{:S(2)}) collective-permute-start(f32[24,128]{1,0:T(8,128)S(1)} %add.19), channel_id=1, source_target_pairs={{0,8},{4,12},{8,0},{12,4},{16,24},{20,28},{24,16},{28,20},{1,9},{5... | collective-permute-start | bytes 36872 | tf_op jit(solution)/shard_map/ppermute | solution.py:386
  46.7 2.1 %collective-permute-done.7 = f32[24,128]{1,0:T(8,128)S(1)} collective-permute-done((f32[24,128]{1,0:T(8,128)S(1)}, f32[24,128]{1,0:T(8,128)S(1)}, u32[]{:S(2)}, u32[]{:S(2)}) %collective-permute-start.7) | collective-permute-done | bytes 12320 | tf_op jit(solution)/shard_map/ppermute | solution.py:386
  48.8 1.5 %collective-permute-start.8 = (f32[24,128]{1,0:T(8,128)S(1)}, f32[24,128]{1,0:T(8,128)S(1)}, u32[]{:S(2)}, u32[]{:S(2)}) collective-permute-start(f32[24,128]{1,0:T(8,128)S(1)} %add.20), channel_id=1, source_target_pairs={{0,16},{4,20},{8,24},{12,28},{16,0},{20,4},{24,8},{28,12},{1,17},{... | collective-permute-start | bytes 36872 | tf_op jit(solution)/shard_map/ppermute | solution.py:386
  50.2 2.2 %collective-permute-done.8 = f32[24,128]{1,0:T(8,128)S(1)} collective-permute-done((f32[24,128]{1,0:T(8,128)S(1)}, f32[24,128]{1,0:T(8,128)S(1)}, u32[]{:S(2)}, u32[]{:S(2)}) %collective-permute-start.8) | collective-permute-done | bytes 12320 | tf_op jit(solution)/shard_map/ppermute | solution.py:386
  52.5 1.5 %collective-permute-start.9 = (f32[24,128]{1,0:T(8,128)S(1)}, f32[24,128]{1,0:T(8,128)S(1)}, u32[]{:S(2)}, u32[]{:S(2)}) collective-permute-start(f32[24,128]{1,0:T(8,128)S(1)} %add.21), channel_id=1, source_target_pairs={{0,1},{1,0},{2,3},{3,2},{4,5},{5,4},{6,7},{7,6},{8,9},{9,8},{10,11... | collective-permute-start | bytes 36872 | tf_op jit(solution)/shard_map/ppermute | solution.py:386
  54.0 2.2 %collective-permute-done.9 = f32[24,128]{1,0:T(8,128)S(1)} collective-permute-done((f32[24,128]{1,0:T(8,128)S(1)}, f32[24,128]{1,0:T(8,128)S(1)}, u32[]{:S(2)}, u32[]{:S(2)}) %collective-permute-start.9) | collective-permute-done | bytes 12320 | tf_op jit(solution)/shard_map/ppermute | solution.py:386
  56.2 2.5 %collective-permute-start.10 = (f32[24,128]{1,0:T(8,128)S(1)}, f32[24,128]{1,0:T(8,128)S(1)}, u32[]{:S(2)}, u32[]{:S(2)}) collective-permute-start(f32[24,128]{1,0:T(8,128)S(1)} %add.22), channel_id=1, source_target_pairs={{0,2},{1,3},{2,0},{3,1},{4,6},{5,7},{6,4},{7,5},{8,10},{9,11},{10,... | collective-permute-start | bytes 36872 | tf_op jit(solution)/shard_map/ppermute | solution.py:386
  58.7 2.1 %collective-permute-done.10 = f32[24,128]{1,0:T(8,128)S(1)} collective-permute-done((f32[24,128]{1,0:T(8,128)S(1)}, f32[24,128]{1,0:T(8,128)S(1)}, u32[]{:S(2)}, u32[]{:S(2)}) %collective-permute-start.10) | collective-permute-done | bytes 12320 | tf_op jit(solution)/shard_map/ppermute | solution.py:386
  60.8 6.4 %shard_map.94 = f32[3840,128]{1,0:T(8,128)} custom-call(s32[6]{0:T(128)S(1)} %stack.39.place_ref, s32[24]{0:T(128)S(1)} %copy-done.3, s32[24]{0:T(128)S(1)} %copy-done.4, s32[24]{0:T(128)S(1)} %copy-done.5, f32[24]{0:T(128)S(1)} %copy-done.6, f32[24]{0:T(128)S(1)} %copy-done.7, f32[7]{0:T(128)S(1)} %copy-done.8, f32[24,128]{1,0:T(8,128)S(1)} %add.23.prior_ref, ...), custom_call_target="tpu_custom_call" | custom-call | tf_op jit(solution)/shard_map/pallas_call | solution.py:357
  (28 shorter events, 0.1 us)
Async XLA Ops:
  0.0 35.8 %copy-start.2 = (f32[16,128]{1,0:T(8,128)S(1)}, f32[16,128]{1,0:T(8,128)}, u32[]{:S(2)}) copy-start(f32[16,128]{1,0:T(8,128)} %drag_ref.5) | copy-start | bytes 24580
  0.0 35.8 %copy-start.4 = (s32[24]{0:T(128)S(1)}, s32[24]{0:T(128)}, u32[]{:S(2)}) copy-start(s32[24]{0:T(128)} %owner_ref.3) | copy-start | bytes 292
  0.0 35.8 %copy-start.3 = (s32[24]{0:T(128)S(1)}, s32[24]{0:T(128)}, u32[]{:S(2)}) copy-start(s32[24]{0:T(128)} %order_ref.3) | copy-start | bytes 292
  0.0 35.8 %copy-start.9 = (s32[24]{0:T(128)S(1)}, s32[24]{0:T(128)}, u32[]{:S(2)}) copy-start(s32[24]{0:T(128)} %cell_ref.1) | copy-start | bytes 292
  0.1 1.5 %copy-start = (f32[3,80,16,128]{3,2,1,0:T(8,128)S(1)}, f32[3,80,16,128]{3,2,1,0:T(8,128)}, u32[]{:S(2)}) copy-start(f32[3,80,16,128]{3,2,1,0:T(8,128)} %param.9) | copy-start | bytes 5898244
  1.6 0.7 %copy-start.1 = (f32[16,128]{1,0:T(8,128)S(1)}, f32[16,128]{1,0:T(8,128)}, u32[]{:S(2)}) copy-start(f32[16,128]{1,0:T(8,128)} %drag_ref.5) | copy-start | bytes 24580
  4.6 31.2 %collective-permute-start = (f32[22,80,128]{2,1,0:T(8,128)S(1)}, f32[22,80,128]{2,1,0:T(8,128)S(1)}, u32[]{:S(2)}, u32[]{:S(2)}) collective-permute-start(f32[22,80,128]{2,1,0:T(8,128)S(1)} %get-tuple-element.18), channel_id=1, source_target_pairs={{0,1},{1,2},{2,3},{4,5},{5,6},{6,7},{8,9},{9,10},{10,11},{12,13},{... | collective-permute-start | bytes 2703368 | tf_op jit(solution)/shard_map/ppermute | solution.py:370
  9.6 26.2 %collective-permute-start.1 = (f32[22,80,128]{2,1,0:T(8,128)S(1)}, f32[22,80,128]{2,1,0:T(8,128)S(1)}, u32[]{:S(2)}, u32[]{:S(2)}) collective-permute-start(f32[22,80,128]{2,1,0:T(8,128)S(1)} %get-tuple-element.19), channel_id=1, source_target_pairs={{1,0},{2,1},{3,2},{5,4},{6,5},{7,6},{9,8},{10,9},{11,10},{13,12},{... | collective-permute-start | bytes 2703368 | tf_op jit(solution)/shard_map/ppermute | solution.py:370
  10.9 1.4 %collective-permute-start.2 = (f32[256,128]{1,0:T(8,128)S(1)}, f32[256,128]{1,0:T(8,128)S(1)}, u32[]{:S(2)}, u32[]{:S(2)}) collective-permute-start(f32[256,128]{1,0:T(8,128)S(1)} %get-tuple-element.20), channel_id=1, source_target_pairs={{0,4},{8,12},{16,20},{24,28},{4,0},{12,8},{20,16},{28,24},{1,5},{9... | collective-permute-start | bytes 393224 | tf_op jit(solution)/shard_map/ppermute | solution.py:375
  11.0 1.3 %collective-permute-start.3 = (f32[256,128]{1,0:T(8,128)S(1)}, f32[256,128]{1,0:T(8,128)S(1)}, u32[]{:S(2)}, u32[]{:S(2)}) collective-permute-start(f32[256,128]{1,0:T(8,128)S(1)} %get-tuple-element.21), channel_id=1, source_target_pairs={{4,8},{12,16},{20,24},{8,4},{16,12},{24,20},{5,9},{13,17},{21,25},... | collective-permute-start | bytes 393224 | tf_op jit(solution)/shard_map/ppermute | solution.py:375
  13.0 22.7 %collective-permute-start.4 = (f32[256,128]{1,0:T(8,128)S(1)}, f32[256,128]{1,0:T(8,128)S(1)}, u32[]{:S(2)}, u32[]{:S(2)}) collective-permute-start(f32[256,128]{1,0:T(8,128)S(1)} %get-tuple-element.24), channel_id=1, source_target_pairs={{0,1},{2,3},{1,0},{3,2},{4,5},{6,7},{5,4},{7,6},{8,9},{10,11},{9,8... | collective-permute-start | bytes 393224 | tf_op jit(solution)/shard_map/ppermute | solution.py:375
  15.7 20.0 %collective-permute-start.5 = (f32[256,128]{1,0:T(8,128)S(1)}, f32[256,128]{1,0:T(8,128)S(1)}, u32[]{:S(2)}, u32[]{:S(2)}) collective-permute-start(f32[256,128]{1,0:T(8,128)S(1)} %get-tuple-element.25), channel_id=1, source_target_pairs={{1,2},{2,1},{5,6},{6,5},{9,10},{10,9},{13,14},{14,13},{17,18},{18,... | collective-permute-start | bytes 393224 | tf_op jit(solution)/shard_map/ppermute | solution.py:375
  35.8 25.0 %copy-start.5 = (s32[24]{0:T(128)S(1)}, s32[24]{0:T(128)}, u32[]{:S(2)}) copy-start(s32[24]{0:T(128)} %reach_ref.1) | copy-start | bytes 292
  35.8 25.0 %copy-start.6 = (f32[24]{0:T(128)S(1)}, f32[24]{0:T(128)}, u32[]{:S(2)}) copy-start(f32[24]{0:T(128)} %value_ref.1) | copy-start | bytes 292
  35.8 25.0 %copy-start.7 = (f32[24]{0:T(128)S(1)}, f32[24]{0:T(128)}, u32[]{:S(2)}) copy-start(f32[24]{0:T(128)} %error_ref.1) | copy-start | bytes 292
  35.8 24.9 %copy-start.8 = (f32[7]{0:T(128)S(1)}, f32[7]{0:T(128)}, u32[]{:S(2)}) copy-start(f32[7]{0:T(128)} %taper_ref.1) | copy-start | bytes 88
  43.8 1.2 %collective-permute-start.6 = (f32[24,128]{1,0:T(8,128)S(1)}, f32[24,128]{1,0:T(8,128)S(1)}, u32[]{:S(2)}, u32[]{:S(2)}) collective-permute-start(f32[24,128]{1,0:T(8,128)S(1)} %get-tuple-element.27), channel_id=1, source_target_pairs={{0,4},{4,0},{8,12},{12,8},{16,20},{20,16},{24,28},{28,24},{1,5},{5... | collective-permute-start | bytes 36872 | tf_op jit(solution)/shard_map/ppermute | solution.py:386
  45.1 3.7 %collective-permute-start.7 = (f32[24,128]{1,0:T(8,128)S(1)}, f32[24,128]{1,0:T(8,128)S(1)}, u32[]{:S(2)}, u32[]{:S(2)}) collective-permute-start(f32[24,128]{1,0:T(8,128)S(1)} %add.19), channel_id=1, source_target_pairs={{0,8},{4,12},{8,0},{12,4},{16,24},{20,28},{24,16},{28,20},{1,9},{5... | collective-permute-start | bytes 36872 | tf_op jit(solution)/shard_map/ppermute | solution.py:386
  48.8 3.7 %collective-permute-start.8 = (f32[24,128]{1,0:T(8,128)S(1)}, f32[24,128]{1,0:T(8,128)S(1)}, u32[]{:S(2)}, u32[]{:S(2)}) collective-permute-start(f32[24,128]{1,0:T(8,128)S(1)} %add.20), channel_id=1, source_target_pairs={{0,16},{4,20},{8,24},{12,28},{16,0},{20,4},{24,8},{28,12},{1,17},{... | collective-permute-start | bytes 36872 | tf_op jit(solution)/shard_map/ppermute | solution.py:386
  52.5 3.7 %collective-permute-start.9 = (f32[24,128]{1,0:T(8,128)S(1)}, f32[24,128]{1,0:T(8,128)S(1)}, u32[]{:S(2)}, u32[]{:S(2)}) collective-permute-start(f32[24,128]{1,0:T(8,128)S(1)} %add.21), channel_id=1, source_target_pairs={{0,1},{1,0},{2,3},{3,2},{4,5},{5,4},{6,7},{7,6},{8,9},{9,8},{10,11... | collective-permute-start | bytes 36872 | tf_op jit(solution)/shard_map/ppermute | solution.py:386
  56.2 4.6 %collective-permute-start.10 = (f32[24,128]{1,0:T(8,128)S(1)}, f32[24,128]{1,0:T(8,128)S(1)}, u32[]{:S(2)}, u32[]{:S(2)}) collective-permute-start(f32[24,128]{1,0:T(8,128)S(1)} %add.22), channel_id=1, source_target_pairs={{0,2},{1,3},{2,0},{3,1},{4,6},{5,7},{6,4},{7,5},{8,10},{9,11},{10,... | collective-permute-start | bytes 36872 | tf_op jit(solution)/shard_map/ppermute | solution.py:386

commit v6 on v5

--- a/solution.py
+++ b/solution.py
@@ -35,24 +35,43 @@
     return x if shift == 0 else pltpu.roll(x, shift, x.ndim - 1)
 
 
-def arrange_kernel(members, rows, place_ref, x_ref, drag_ref, out_ref, lower_ref, upper_ref, even_ref, odd_ref):
+def band_kernel(members, rows, x_ref, lower_ref, upper_ref):
+    def group(g, carry):
+        here = pl.ds(pl.multiple_of(g * 8, 8), 8)
+        for f in range(3):
+            depth = MARGIN if f == 2 else MARGIN - 1
+            for d in range(depth):
+                at = (f * members + g * 8) * rows
+                lower_ref[f * (MARGIN - 1) + d, here, :] = x_ref[pl.ds(at + d, 8, stride=rows), :]
+                upper_ref[f * (MARGIN - 1) + d, here, :] = x_ref[pl.ds(at + rows - depth + d, 8, stride=rows), :]
+        return carry
+
+    lax.fori_loop(0, members // 8, group, 0)
+
+
+def bands(x, members, rows):
+    band = jax.ShapeDtypeStruct((3 * MARGIN - 2, members, x.shape[1]), F32)
+    return pl.pallas_call(
+        functools.partial(band_kernel, members, rows),
+        out_shape=(band, band),
+        in_specs=[VSPEC],
+        out_specs=(VSPEC,) * 2,
+        compiler_params=pltpu.CompilerParams(vmem_limit_bytes=VMEM_LIMIT),
+        cost_estimate=pl.CostEstimate(flops=1_000_000, bytes_accessed=4_000_000, transcendentals=0),
+    )(x)
+
+
+def pack_kernel(members, rows, place_ref, x_ref, drag_ref, even_ref, odd_ref):
     cols = x_ref.shape[1]
     lane = lanes_of((8, cols))
     odd_x = place_ref[0] // place_ref[5] % 2 == 1
 
     def group(g, carry):
-        here = pl.ds(pl.multiple_of(g * 8, 8), 8)
         for f in range(3):
             left = jnp.zeros((8, cols), F32)
             right = jnp.zeros((8, cols), F32)
-            depth = MARGIN if f == 2 else MARGIN - 1
             for r in range(rows):
                 row = x_ref[pl.ds((f * members + g * 8) * rows + r, 8, stride=rows), :]
-                out_ref[f * rows + r, here, :] = row
-                if r < depth:
-                    lower_ref[f * (MARGIN - 1) + r, here, :] = row
-                if r >= rows - depth:
-                    upper_ref[f * (MARGIN - 1) + r - rows + depth, here, :] = row
                 there = (lane >= MARGIN * r) & (lane < MARGIN * (r + 1))
                 left = jnp.where(there, roll_lanes(row, MARGIN * r), left)
                 right = jnp.where(there, roll_lanes(row, MARGIN * (r + 1)), right)
@@ -66,17 +85,16 @@
     odd_ref[3 * members :, :] = drag_ref[...]
 
 
-def arrange(place, x, drag, members):
+def pack(place, x, drag, members):
     rows, cols = drag.shape
     message = jax.ShapeDtypeStruct((3 * members + rows, cols), F32)
-    band = jax.ShapeDtypeStruct((3 * MARGIN - 2, members, cols), F32)
     return pl.pallas_call(
-        functools.partial(arrange_kernel, members, rows),
-        out_shape=(jax.ShapeDtypeStruct((3 * rows, members, cols), F32), band, band, message, message),
+        functools.partial(pack_kernel, members, rows),
+        out_shape=(message, message),
         in_specs=[SSPEC, VSPEC, VSPEC],
-        out_specs=(VSPEC,) * 5,
+        out_specs=(VSPEC,) * 2,
         compiler_params=pltpu.CompilerParams(vmem_limit_bytes=VMEM_LIMIT),
-        cost_estimate=pl.CostEstimate(flops=4_000_000, bytes_accessed=6_000_000, transcendentals=0),
+        cost_estimate=pl.CostEstimate(flops=1_000_000, bytes_accessed=4_000_000, transcendentals=0),
     )(place, x, drag)
 
 
@@ -135,22 +153,96 @@
     return jnp.concatenate([main, halo], axis=1)
 
 
+def shift_matrix(wide):
+    source, target = sublanes_of((wide, wide)), lanes_of((wide, wide))
+    after, before = source == (target + 1) % wide, target == (source + 1) % wide
+    return jnp.where(after, 1.0, jnp.where(before, -1.0, 0.0)).astype(BF16)
+
+
+def column_slope(x, shift):
+    rows, group, wide = x.shape
+    x = x.reshape(rows * group, wide)
+    top = x.astype(BF16)
+    rest = (x - top.astype(F32)).astype(BF16)
+    slope = jnp.dot(top, shift, preferred_element_type=F32) + jnp.dot(rest, shift, preferred_element_type=F32)
+    return slope.reshape(rows, group, wide)
+
+
+def interior_kernel(members, rows, place_ref, x_ref, left_ref, right_ref, drag_ref, margin_ref, state, keep, slope, across):
+    cols = x_ref.shape[1]
+    wide = 2 * cols
+    lane = lanes_of((8, cols))
+    factor = -0.2 * grid_factor(place_ref, (rows + 2 * MARGIN, wide), rows, cols)
+    shift = shift_matrix(wide)
+    kept = 1.0 - jnp.concatenate([drag_ref[...], margin_ref[...]], axis=1)
+    for r in range(rows):
+        keep[r] = jnp.broadcast_to(kept[r : r + 1, :], (GROUP, wide))
+        slope[r] = jnp.broadcast_to(factor[MARGIN + r : MARGIN + r + 1, :], (GROUP, wide))
+
+    def first(g, carry):
+        here = pl.ds(pl.multiple_of(g * 8, 8), 8)
+        for f in range(3):
+            at = pl.ds(pl.multiple_of(f * members + g * 8, 8), 8)
+            left, right = left_ref[at, :], right_ref[at, :]
+            for r in range(rows):
+                main = x_ref[pl.ds((f * members + g * 8) * rows + r, 8, stride=rows), :]
+                state[f, r, here, :] = wide_row(lane, main, left, MARGIN * r, right, MARGIN * r)
+        return carry
+
+    lax.fori_loop(0, members // 8, first, 0)
+
+    def group(g, carry):
+        here = pl.ds(pl.multiple_of(g * GROUP, GROUP), GROUP)
+        for step in range(STEPS):
+            low, high = 1 + 2 * step, rows - 1 - 2 * step
+            if low >= high:
+                break
+            across[low:high] = column_slope(state[1, low:high, here, :], shift)
+            for r in range(low, high):
+                div = across[r] + (state[2, r + 1, here, :] - state[2, r - 1, here, :])
+                state[0, r, here, :] = state[0, r, here, :] + slope[r] * div
+            low, high = low + 1, high - 1
+            if low >= high:
+                break
+            across[low:high] = column_slope(state[0, low:high, here, :], shift)
+            for r in range(low, high):
+                u, v = state[1, r, here, :], state[2, r, here, :]
+                k, c = keep[r], slope[r]
+                state[1, r, here, :] = k * u + c * across[r] + 0.1 * v
+                state[2, r, here, :] = k * v + c * (state[0, r + 1, here, :] - state[0, r - 1, here, :]) - 0.1 * u
+        return carry
+
+    lax.fori_loop(0, members // GROUP, group, 0)
+
+
+def interior(place, x, left, right, drag, margin, members):
+    rows, cols = drag.shape
+    return pl.pallas_call(
+        functools.partial(interior_kernel, members, rows),
+        out_shape=jax.ShapeDtypeStruct((3, rows, members, 2 * cols), F32),
+        in_specs=[SSPEC] + [VSPEC] * 5,
+        out_specs=VSPEC,
+        scratch_shapes=[pltpu.VMEM((rows, GROUP, 2 * cols), F32)] * 3,
+        compiler_params=pltpu.CompilerParams(vmem_limit_bytes=VMEM_LIMIT),
+        cost_estimate=pl.CostEstimate(flops=30_000_000, bytes_accessed=10_000_000, transcendentals=0),
+    )(place, x, left, right, drag, margin)
+
+
 def forecast_kernel(
     members, rows,
     place_ref, order_ref, owner_ref, cell_ref,
-    state_ref, above_ref, below_ref, left_ref, right_ref, ceven_ref, codd_ref, drag_ref, margin_ref,
+    inner_ref, above_ref, below_ref, ceven_ref, codd_ref, drag_ref, margin_ref,
     out_ref, prior_ref,
     state, keep, slope, across,
 ):
-    cols = state_ref.shape[2]
+    cols = above_ref.shape[2]
     wide = 2 * cols
     total = rows + 2 * MARGIN
+    half = cols // 2
     lane = lanes_of((GROUP, cols))
-    half = cols // 2
     factor = -0.2 * grid_factor(place_ref, (total, wide), rows, cols)
     odd_y = place_ref[0] % place_ref[5] % 2 == 1
-    source, target = sublanes_of((wide, wide)), lanes_of((wide, wide))
-    shift = jnp.where(source == (target + 1) % wide, 1.0, jnp.where(target == (source + 1) % wide, -1.0, 0.0)).astype(BF16)
+    shift = shift_matrix(wide)
     count = 3 * members
     parts = []
     for here, own in ((count, drag_ref), (count + MARGIN, margin_ref)):
@@ -165,51 +257,42 @@
     def group(g, carry):
         here = pl.ds(pl.multiple_of(g * GROUP, GROUP), GROUP)
         for f in range(3):
-            at = pl.ds(pl.multiple_of(f * members + g * GROUP, GROUP), GROUP)
-            ledge, redge = left_ref[at, :], right_ref[at, :]
+            at = pl.ds(pl.multiple_of(f * members + g * GROUP, 8), GROUP)
             ceven, codd = ceven_ref[at, :], codd_ref[at, :]
             cab, cbe = jnp.where(odd_y, ceven, codd), jnp.where(odd_y, codd, ceven)
             depth = MARGIN if f == 2 else MARGIN - 1
-            for r in range(MARGIN - depth, MARGIN + rows + depth):
-                if r < MARGIN:
-                    main = above_ref[f * (MARGIN - 1) + r - MARGIN + depth, here, :]
-                    value = wide_row(lane, main, cab, MARGIN * r, cab, half + MARGIN * r)
-                elif r < MARGIN + rows:
-                    q = r - MARGIN
-                    main = state_ref[f * rows + q, here, :]
-                    value = wide_row(lane, main, ledge, MARGIN * q, redge, MARGIN * q)
-                else:
-                    q = r - MARGIN - rows
-                    main = below_ref[f * (MARGIN - 1) + q, here, :]
-                    value = wide_row(lane, main, cbe, MARGIN * q, cbe, half + MARGIN * q)
-                state[f, r] = value
-        def column_slope(f, low, high):
-            x = state[f, low:high].reshape((high - low) * GROUP, wide)
-            top = x.astype(BF16)
-            rest = (x - top.astype(F32)).astype(BF16)
-            n = (high - low) * GROUP
-            cut = n // 2 // 16 * 16
-            parts = []
-            for p, q in ((0, cut), (cut, n)):
-                parts.append(jnp.dot(top[p:q], shift, preferred_element_type=F32))
-                parts.append(jnp.dot(rest[p:q], shift, preferred_element_type=F32))
-            d = jnp.concatenate([parts[0] + parts[1], parts[2] + parts[3]], axis=0)
-            across[low:high] = d.reshape(high - low, GROUP, wide)
-
+            for d in range(depth):
+                r = MARGIN - depth + d
+                main = above_ref[f * (MARGIN - 1) + d, here, :]
+                state[f, r] = wide_row(lane, main, cab, MARGIN * r, cab, half + MARGIN * r)
+                main = below_ref[f * (MARGIN - 1) + d, here, :]
+                state[f, MARGIN + rows + d] = wide_row(lane, main, cbe, MARGIN * d, cbe, half + MARGIN * d)
+            for r in range(rows):
+                state[f, MARGIN + r] = inner_ref[f, r, here, :]
         for step in range(STEPS):
-            reach = 2 * (STEPS - step) - 1
-            low, high = MARGIN - reach, MARGIN + rows + reach
-            column_slope(1, low, high)
-            for r in range(low, high):
-                div = across[r] + (state[2, r + 1] - state[2, r - 1])
-                state[0, r] = state[0, r] + slope[r] * div
-            low, high = low + 1, high - 1
-            column_slope(0, low, high)
-            for r in range(low, high):
-                u, v = state[1, r], state[2, r]
-                k, c = keep[r], slope[r]
-                state[1, r] = k * u + c * across[r] + 0.1 * v
-                state[2, r] = k * v + c * (state[0, r + 1] - state[0, r - 1]) - 0.1 * u
+            first, last = MARGIN - MARGIN + 1 + 2 * step, MARGIN + rows + MARGIN - 1 - 2 * step
+            done, still = MARGIN + 1 + 2 * step, MARGIN + rows - 1 - 2 * step
+            spans = ((first, min(done, still)), (max(done, still), last)) if done < still else ((first, last),)
+            for low, high in spans:
+                across[low:high] = column_slope(state[1, low:high], shift)
+            for low, high in spans:
+                for r in range(low, high):
+                    div = across[r] + (state[2, r + 1] - state[2, r - 1])
+                    state[0, r] = state[0, r] + slope[r] * div
+            first, last, done, still = first + 1, last - 1, done + 1, still - 1
+            spans = ((first, done), (still, last)) if done < still else ((first, MARGIN + rows // 2), (MARGIN + rows // 2, last))
+            for low, high in spans:
+                across[low:high] = column_slope(state[0, low:high], shift)
+            for low, high in spans:
+                for r in range(low, high):
+                    u, v = state[1, r], state[2, r]
+                    k, c = keep[r], slope[r]
+                    u, v = (
+                        k * u + c * across[r] + 0.1 * v,
+                        k * v + c * (state[0, r + 1] - state[0, r - 1]) - 0.1 * u,
+                    )
+                    state[1, r] = u
+                    state[2, r] = v
         for f in range(3):
             for r in range(rows):
                 out_ref[f * rows + r, here, :] = state[f, MARGIN + r, :, 0:cols]
@@ -231,19 +314,22 @@
             )[0:1]
 
 
-def forecast(place, order, owner, cell, states, *arrays):
-    members, cols = states.shape[1:]
-    rows = states.shape[0] // 3
+def forecast(place, order, owner, cell, inner, *arrays):
+    _, rows, members, wide = inner.shape
+    cols = wide // 2
     total = rows + 2 * MARGIN
     return pl.pallas_call(
         functools.partial(forecast_kernel, members, rows),
-        out_shape=(jax.ShapeDtypeStruct(states.shape, F32), jax.ShapeDtypeStruct((order.shape[0], cols), F32)),
+        out_shape=(
+            jax.ShapeDtypeStruct((3 * rows, members, cols), F32),
+            jax.ShapeDtypeStruct((order.shape[0], cols), F32),
+        ),
         in_specs=[SSPEC] * 4 + [VSPEC] * (1 + len(arrays)),
         out_specs=(VSPEC, VSPEC),
-        scratch_shapes=[pltpu.VMEM((3, total, GROUP, 2 * cols), F32)] + [pltpu.VMEM((total, GROUP, 2 * cols), F32)] * 3,
+        scratch_shapes=[pltpu.VMEM((3, total, GROUP, wide), F32)] + [pltpu.VMEM((total, GROUP, wide), F32)] * 3,
         compiler_params=pltpu.CompilerParams(vmem_limit_bytes=VMEM_LIMIT),
         cost_estimate=pl.CostEstimate(flops=60_000_000, bytes_accessed=30_000_000, transcendentals=0),
-    )(place, order, owner, cell, states, *arrays)
+    )(place, order, owner, cell, inner, *arrays)
 
 
 def localize(distance, reach, taper_ref):
@@ -403,14 +489,14 @@
         ]
     ).astype(jnp.int32)
     flat = status.reshape(3 * members * rows, cols)
-    states, lower, upper, even, odd = arrange(place, flat, drag, members)
+    lower, upper = bands(flat, members, rows)
     above, below = to_neighbours("gy", lower, upper)
+    even, odd = pack(place, flat, drag, members)
     even, odd = swap_pairs(even, "gx", 0), swap_pairs(odd, "gx", 1)
     left, right, margin, even, odd = corner(place, drag, even, odd)
     even, odd = swap_pairs(even, "gy", 0), swap_pairs(odd, "gy", 1)
-    states, priors = forecast(
-        place, order, owner, cell, states, above, below, left, right, even, odd, drag, margin
-    )
+    inner = interior(place, flat, left, right, drag, margin, members)
+    states, priors = forecast(place, order, owner, cell, inner, above, below, even, odd, drag, margin)
     priors = add_over(priors, ("gx", "gy"))
     result = assimilate(place, order, owner, reach, value, error, taper, priors, states, members, rows)
     return result.reshape(status.shape)

time: 67.5 us -> 65.6 us (0.972)
  waiting for transfers between devices: 29.7 us -> 21.3 us
  Pallas kernels: 17.3 us -> 24.4 us
  local copies, waits for them, and re-layouts: 2.37 us -> 1.68 us
    ppermute x4, waiting for transfers between devices: 20 us -> 11.6 us  [swap_pairs(): return lax.ppermute(x, axis, pairs + [(b, a) for a, b in pairs])]
    pallas_call x1 -> x3, Pallas kernels: 2.23 us -> 10.2 us  [the longest x1 6.21 us: interior(): pl.pallas_call(functools.partial(interior_kernel, members, rows), out_sha...]
    pallas_call x1, Pallas kernels: 7.99 us -> 7.07 us  [forecast(): pl.pallas_call(functools.partial(forecast_kernel, members, rows), out_sha...]
    unnamed x20, local copies, waits for them, and re-layouts: 2.28 us -> 1.6 us
  transfers between devices with their start and end apart: 11 -> 11, of which waited for: 7 -> 7; matrix products, arithmetic and copies ran while one was open for 0% -> 0% of each run, Pallas kernels for 1% -> 14%
where the time goes in v6:
time: 65.6 us; the launch traced here: 65.2 us
  Pallas kernels  24.4 us (37%)
  waiting for transfers between devices  21.3 us (32%)
  starting transfers between devices  17.6 us (27%)
  local copies, waits for them, and re-layouts  1.68 us (3%)
    ppermute x4, waiting for transfers between devices, swap_pairs(): return lax.ppermute(x, axis, pairs + [(b, a) for a, b in pairs])  11.6 us
    ppermute x5, waiting for transfers between devices, add_over(): x = x + lax.ppermute(x, axis, [(i, i ^ span) for i in range(count)])  9.71 us
    ppermute x5, starting transfers between devices, add_over(): x = x + lax.ppermute(x, axis, [(i, i ^ span) for i in range(count)])  7.2 us
    pallas_call x1, Pallas kernels, forecast(): pl.pallas_call(functools.partial(forecast_kernel, members, rows), out_sha...  7.07 us
    pallas_call x1, Pallas kernels, assimilate(): pl.pallas_call(functools.partial(assimilate_kernel, members, rows), out_s...  6.36 us
    pallas_call x1, Pallas kernels, interior(): pl.pallas_call(functools.partial(interior_kernel, members, rows), out_sha...  6.21 us
    ppermute x1, starting transfers between devices, to_neighbours(): lax.ppermute(upper, axis, forward)  4.97 us
    ppermute x4, starting transfers between devices, swap_pairs(): return lax.ppermute(x, axis, pairs + [(b, a) for a, b in pairs])  4.11 us
  transfers between devices with their start and end apart: 11, of which 7 were waited for; matrix products, arithmetic and copies ran while one was open for 0% of the time, Pallas kernels for 14%

profile of v6, /device:TPU:0, one launch (start us, length us, event | category | flops | bytes accessed | tf_op | source)
XLA Modules:
  0.0 65.2 jit_solution(14850773614104374724)
XLA Ops:
  0.0 1.5 %copy-done = f32[3,80,16,128]{3,2,1,0:T(8,128)S(1)} copy-done((f32[3,80,16,128]{3,2,1,0:T(8,128)S(1)}, f32[3,80,16,128]{3,2,1,0:T(8,128)}, u32[]{:S(2)}) %copy-start) | copy-done | bytes 1966104
  1.6 1.8 %shard_map.94 = (f32[22,80,128]{2,1,0:T(8,128)}, f32[22,80,128]{2,1,0:T(8,128)}) custom-call(f32[3840,128]{1,0:T(8,128)S(1)} %bitcast.7), custom_call_target="tpu_custom_call" | custom-call | flops 1000000 | bytes 4000000 | tf_op jit(solution)/shard_map/pallas_call | solution.py:54
  3.4 5.0 %collective-permute-start.2 = (f32[22,80,128]{2,1,0:T(8,128)}, f32[22,80,128]{2,1,0:T(8,128)S(1)}, u32[]{:S(2)}, u32[]{:S(2)}) collective-permute-start(f32[22,80,128]{2,1,0:T(8,128)} %get-tuple-element.21), channel_id=1, source_target_pairs={{0,1},{1,2},{2,3},{4,5},{5,6},{6,7},{8,9},{9,10},{10,11},{12,13},{... | collective-permute-start | bytes 2703368 | tf_op jit(solution)/shard_map/ppermute | solution.py:456
  8.3 1.3 %collective-permute-start.3 = (f32[22,80,128]{2,1,0:T(8,128)}, f32[22,80,128]{2,1,0:T(8,128)}, u32[]{:S(2)}, u32[]{:S(2)}) collective-permute-start(f32[22,80,128]{2,1,0:T(8,128)} %get-tuple-element.22), channel_id=1, source_target_pairs={{1,0},{2,1},{3,2},{5,4},{6,5},{7,6},{9,8},{10,9},{11,10},{13,12},{... | collective-permute-start | bytes 2703368 | tf_op jit(solution)/shard_map/ppermute | solution.py:456
  9.7 0.1 stack.39.place_ref
  9.7 2.2 %shard_map.91 = (f32[256,128]{1,0:T(8,128)S(1)}, f32[256,128]{1,0:T(8,128)S(1)}) custom-call(s32[6]{0:T(128)S(1)} %stack.39.place_ref, f32[3840,128]{1,0:T(8,128)S(1)} %bitcast.8, f32[16,128]{1,0:T(8,128)S(1)} %copy-done.2), custom_call_target="tpu_custom_call" | custom-call | flops 1000000 | bytes 4000000 | tf_op jit(solution)/shard_map/pallas_call | solution.py:91
  12.1 0.7 %collective-permute-start.1 = (f32[256,128]{1,0:T(8,128)S(1)}, f32[256,128]{1,0:T(8,128)S(1)}, u32[]{:S(2)}, u32[]{:S(2)}) collective-permute-start(f32[256,128]{1,0:T(8,128)S(1)} %get-tuple-element.17), channel_id=1, source_target_pairs={{4,8},{12,16},{20,24},{8,4},{16,12},{24,20},{5,9},{13,17},{21,25},... | collective-permute-start | bytes 393224 | tf_op jit(solution)/shard_map/ppermute | solution.py:461
  12.7 0.7 %collective-permute-done.even_ref = f32[256,128]{1,0:T(8,128)S(1)} collective-permute-done((f32[256,128]{1,0:T(8,128)S(1)}, f32[256,128]{1,0:T(8,128)S(1)}, u32[]{:S(2)}, u32[]{:S(2)}) %collective-permute-start) | collective-permute-done | bytes 131104 | tf_op jit(solution)/shard_map/ppermute | solution.py:461
  13.4 0.7 %shard_map.92 = (f32[240,128]{1,0:T(8,128)S(1)}, f32[240,128]{1,0:T(8,128)S(1)}, f32[16,128]{1,0:T(8,128)S(1)}, f32[256,128]{1,0:T(8,128)S(1)}, f32[256,128]{1,0:T(8,128)S(1)}) custom-call(s32[6]{0:T(128)S(1)} %stack.39.place_ref, f32[16,128]{1,0:T(8,128)S(1)} %copy-done.2, f32[256,128]{1,0:T(8,128)S(1)} %collective-permute-done.even_ref, ...), custom_call_target="tpu_custom_call" | custom-call | tf_op jit(solution)/shard_map/pallas_call | solution.py:131
  14.1 2.7 %collective-permute-start.4 = (f32[256,128]{1,0:T(8,128)S(1)}, f32[256,128]{1,0:T(8,128)S(1)}, u32[]{:S(2)}, u32[]{:S(2)}) collective-permute-start(f32[256,128]{1,0:T(8,128)S(1)} %get-tuple-element.23), channel_id=1, source_target_pairs={{0,1},{2,3},{1,0},{3,2},{4,5},{6,7},{5,4},{7,6},{8,9},{10,11},{9,8... | collective-permute-start | bytes 393224 | tf_op jit(solution)/shard_map/ppermute | solution.py:461
  16.8 0.7 %collective-permute-start.5 = (f32[256,128]{1,0:T(8,128)S(1)}, f32[256,128]{1,0:T(8,128)S(1)}, u32[]{:S(2)}, u32[]{:S(2)}) collective-permute-start(f32[256,128]{1,0:T(8,128)S(1)} %get-tuple-element.24), channel_id=1, source_target_pairs={{1,2},{2,1},{5,6},{6,5},{9,10},{10,9},{13,14},{14,13},{17,18},{18,... | collective-permute-start | bytes 393224 | tf_op jit(solution)/shard_map/ppermute | solution.py:461
  17.5 6.2 %shard_map.93.inner_ref = f32[3,16,80,256]{3,2,1,0:T(8,128)S(1)} custom-call(s32[6]{0:T(128)S(1)} %stack.39.place_ref, f32[3840,128]{1,0:T(8,128)S(1)} %bitcast.9, f32[240,128]{1,0:T(8,128)S(1)} %get-tuple-element.18.left_ref, f32[240,128]{1,0:T(8,128)S(1)} %get-tuple-element.19.right_ref, f32[16,128]{1,0:T(8,128)S(1)} %copy-done.2, ...), custom_call_target="tpu_custom_call" | custom-call | flops 30000000 | bytes 10000000 | tf_op jit(solution)/shard_map/pallas_call | solution.py:220
  23.8 10.9 %collective-permute-done.4.ceven_ref = f32[256,128]{1,0:T(8,128)S(1)} collective-permute-done((f32[256,128]{1,0:T(8,128)S(1)}, f32[256,128]{1,0:T(8,128)S(1)}, u32[]{:S(2)}, u32[]{:S(2)}) %collective-permute-start.4) | collective-permute-done | bytes 131104 | tf_op jit(solution)/shard_map/ppermute | solution.py:461
  34.8 7.1 %shard_map.95 = (f32[48,80,128]{2,1,0:T(8,128)S(1)}, f32[24,128]{1,0:T(8,128)S(1)}) custom-call(s32[6]{0:T(128)S(1)} %stack.39.place_ref, s32[24]{0:T(128)S(1)} %copy-done.3, s32[24]{0:T(128)S(1)} %copy-done.4, s32[24]{0:T(128)S(1)} %copy-done.5, f32[3,16,80,256]{3,2,1,0:T(8,128)S(1)} %shard_map.93.inner_ref, ...), custom_call_target="tpu_custom_call" | custom-call | flops 60000000 | bytes 30000000 | tf_op jit(solution)/shard_map/pallas_call | solution.py:321
  41.9 1.2 %collective-permute-done.6 = f32[24,128]{1,0:T(8,128)S(1)} collective-permute-done((f32[24,128]{1,0:T(8,128)S(1)}, f32[24,128]{1,0:T(8,128)S(1)}, u32[]{:S(2)}, u32[]{:S(2)}) %collective-permute-start.6) | collective-permute-done | bytes 12320 | tf_op jit(solution)/shard_map/ppermute | solution.py:472
  43.1 1.5 %collective-permute-start.7 = (f32[24,128]{1,0:T(8,128)S(1)}, f32[24,128]{1,0:T(8,128)S(1)}, u32[]{:S(2)}, u32[]{:S(2)}) collective-permute-start(f32[24,128]{1,0:T(8,128)S(1)} %add.19), channel_id=1, source_target_pairs={{0,8},{4,12},{8,0},{12,4},{16,24},{20,28},{24,16},{28,20},{1,9},{5... | collective-permute-start | bytes 36872 | tf_op jit(solution)/shard_map/ppermute | solution.py:472
  44.6 2.2 %collective-permute-done.7 = f32[24,128]{1,0:T(8,128)S(1)} collective-permute-done((f32[24,128]{1,0:T(8,128)S(1)}, f32[24,128]{1,0:T(8,128)S(1)}, u32[]{:S(2)}, u32[]{:S(2)}) %collective-permute-start.7) | collective-permute-done | bytes 12320 | tf_op jit(solution)/shard_map/ppermute | solution.py:472
  46.8 1.5 %collective-permute-start.8 = (f32[24,128]{1,0:T(8,128)S(1)}, f32[24,128]{1,0:T(8,128)S(1)}, u32[]{:S(2)}, u32[]{:S(2)}) collective-permute-start(f32[24,128]{1,0:T(8,128)S(1)} %add.20), channel_id=1, source_target_pairs={{0,16},{4,20},{8,24},{12,28},{16,0},{20,4},{24,8},{28,12},{1,17},{... | collective-permute-start | bytes 36872 | tf_op jit(solution)/shard_map/ppermute | solution.py:472
  48.2 2.2 %collective-permute-done.8 = f32[24,128]{1,0:T(8,128)S(1)} collective-permute-done((f32[24,128]{1,0:T(8,128)S(1)}, f32[24,128]{1,0:T(8,128)S(1)}, u32[]{:S(2)}, u32[]{:S(2)}) %collective-permute-start.8) | collective-permute-done | bytes 12320 | tf_op jit(solution)/shard_map/ppermute | solution.py:472
  50.5 1.6 %collective-permute-start.9 = (f32[24,128]{1,0:T(8,128)S(1)}, f32[24,128]{1,0:T(8,128)S(1)}, u32[]{:S(2)}, u32[]{:S(2)}) collective-permute-start(f32[24,128]{1,0:T(8,128)S(1)} %add.21), channel_id=1, source_target_pairs={{0,1},{1,0},{2,3},{3,2},{4,5},{5,4},{6,7},{7,6},{8,9},{9,8},{10,11... | collective-permute-start | bytes 36872 | tf_op jit(solution)/shard_map/ppermute | solution.py:472
  52.1 2.1 %collective-permute-done.9 = f32[24,128]{1,0:T(8,128)S(1)} collective-permute-done((f32[24,128]{1,0:T(8,128)S(1)}, f32[24,128]{1,0:T(8,128)S(1)}, u32[]{:S(2)}, u32[]{:S(2)}) %collective-permute-start.9) | collective-permute-done | bytes 12320 | tf_op jit(solution)/shard_map/ppermute | solution.py:472
  54.2 2.5 %collective-permute-start.10 = (f32[24,128]{1,0:T(8,128)S(1)}, f32[24,128]{1,0:T(8,128)S(1)}, u32[]{:S(2)}, u32[]{:S(2)}) collective-permute-start(f32[24,128]{1,0:T(8,128)S(1)} %add.22), channel_id=1, source_target_pairs={{0,2},{1,3},{2,0},{3,1},{4,6},{5,7},{6,4},{7,5},{8,10},{9,11},{10,... | collective-permute-start | bytes 36872 | tf_op jit(solution)/shard_map/ppermute | solution.py:472
  56.7 2.1 %collective-permute-done.10 = f32[24,128]{1,0:T(8,128)S(1)} collective-permute-done((f32[24,128]{1,0:T(8,128)S(1)}, f32[24,128]{1,0:T(8,128)S(1)}, u32[]{:S(2)}, u32[]{:S(2)}) %collective-permute-start.10) | collective-permute-done | bytes 12320 | tf_op jit(solution)/shard_map/ppermute | solution.py:472
  58.8 6.4 %shard_map.96 = f32[3840,128]{1,0:T(8,128)} custom-call(s32[6]{0:T(128)S(1)} %stack.39.place_ref, s32[24]{0:T(128)S(1)} %copy-done.3, s32[24]{0:T(128)S(1)} %copy-done.4, s32[24]{0:T(128)S(1)} %copy-done.6, f32[24]{0:T(128)S(1)} %copy-done.7, f32[24]{0:T(128)S(1)} %copy-done.8, f32[7]{0:T(128)S(1)} %copy-done.9, f32[24,128]{1,0:T(8,128)S(1)} %add.23.prior_ref, ...), custom_call_target="tpu_custom_call" | custom-call | tf_op jit(solution)/shard_map/pallas_call | solution.py:443
  (30 shorter events, 0.2 us)
Async XLA Ops:
  0.0 1.5 %copy-start = (f32[3,80,16,128]{3,2,1,0:T(8,128)S(1)}, f32[3,80,16,128]{3,2,1,0:T(8,128)}, u32[]{:S(2)}) copy-start(f32[3,80,16,128]{3,2,1,0:T(8,128)} %param.9) | copy-start | bytes 5898244
  1.5 8.2 %copy-start.1 = (f32[3,80,16,128]{3,2,1,0:T(8,128)S(1)}, f32[3,80,16,128]{3,2,1,0:T(8,128)}, u32[]{:S(2)}) copy-start(f32[3,80,16,128]{3,2,1,0:T(8,128)} %param.9) | copy-start | bytes 5898244
  1.5 8.2 %copy-start.2 = (f32[16,128]{1,0:T(8,128)S(1)}, f32[16,128]{1,0:T(8,128)}, u32[]{:S(2)}) copy-start(f32[16,128]{1,0:T(8,128)} %drag_ref.7) | copy-start | bytes 24580
  3.4 31.4 %collective-permute-start.2 = (f32[22,80,128]{2,1,0:T(8,128)}, f32[22,80,128]{2,1,0:T(8,128)S(1)}, u32[]{:S(2)}, u32[]{:S(2)}) collective-permute-start(f32[22,80,128]{2,1,0:T(8,128)} %get-tuple-element.21), channel_id=1, source_target_pairs={{0,1},{1,2},{2,3},{4,5},{5,6},{6,7},{8,9},{9,10},{10,11},{12,13},{... | collective-permute-start | bytes 2703368 | tf_op jit(solution)/shard_map/ppermute | solution.py:456
  8.3 26.4 %collective-permute-start.3 = (f32[22,80,128]{2,1,0:T(8,128)}, f32[22,80,128]{2,1,0:T(8,128)}, u32[]{:S(2)}, u32[]{:S(2)}) collective-permute-start(f32[22,80,128]{2,1,0:T(8,128)} %get-tuple-element.22), channel_id=1, source_target_pairs={{1,0},{2,1},{3,2},{5,4},{6,5},{7,6},{9,8},{10,9},{11,10},{13,12},{... | collective-permute-start | bytes 2703368 | tf_op jit(solution)/shard_map/ppermute | solution.py:456
  12.0 1.4 %collective-permute-start = (f32[256,128]{1,0:T(8,128)S(1)}, f32[256,128]{1,0:T(8,128)S(1)}, u32[]{:S(2)}, u32[]{:S(2)}) collective-permute-start(f32[256,128]{1,0:T(8,128)S(1)} %get-tuple-element.16), channel_id=1, source_target_pairs={{0,4},{8,12},{16,20},{24,28},{4,0},{12,8},{20,16},{28,24},{1,5},{9... | collective-permute-start | bytes 393224 | tf_op jit(solution)/shard_map/ppermute | solution.py:461
  12.1 1.3 %collective-permute-start.1 = (f32[256,128]{1,0:T(8,128)S(1)}, f32[256,128]{1,0:T(8,128)S(1)}, u32[]{:S(2)}, u32[]{:S(2)}) collective-permute-start(f32[256,128]{1,0:T(8,128)S(1)} %get-tuple-element.17), channel_id=1, source_target_pairs={{4,8},{12,16},{20,24},{8,4},{16,12},{24,20},{5,9},{13,17},{21,25},... | collective-permute-start | bytes 393224 | tf_op jit(solution)/shard_map/ppermute | solution.py:461
  14.1 20.6 %collective-permute-start.4 = (f32[256,128]{1,0:T(8,128)S(1)}, f32[256,128]{1,0:T(8,128)S(1)}, u32[]{:S(2)}, u32[]{:S(2)}) collective-permute-start(f32[256,128]{1,0:T(8,128)S(1)} %get-tuple-element.23), channel_id=1, source_target_pairs={{0,1},{2,3},{1,0},{3,2},{4,5},{6,7},{5,4},{7,6},{8,9},{10,11},{9,8... | collective-permute-start | bytes 393224 | tf_op jit(solution)/shard_map/ppermute | solution.py:461
  16.8 17.9 %collective-permute-start.5 = (f32[256,128]{1,0:T(8,128)S(1)}, f32[256,128]{1,0:T(8,128)S(1)}, u32[]{:S(2)}, u32[]{:S(2)}) collective-permute-start(f32[256,128]{1,0:T(8,128)S(1)} %get-tuple-element.24), channel_id=1, source_target_pairs={{1,2},{2,1},{5,6},{6,5},{9,10},{10,9},{13,14},{14,13},{17,18},{18,... | collective-permute-start | bytes 393224 | tf_op jit(solution)/shard_map/ppermute | solution.py:461
  17.5 17.2 %copy-start.3 = (s32[24]{0:T(128)S(1)}, s32[24]{0:T(128)}, u32[]{:S(2)}) copy-start(s32[24]{0:T(128)} %order_ref.3) | copy-start | bytes 292
  17.5 17.2 %copy-start.4 = (s32[24]{0:T(128)S(1)}, s32[24]{0:T(128)}, u32[]{:S(2)}) copy-start(s32[24]{0:T(128)} %owner_ref.3) | copy-start | bytes 292
  17.5 17.2 %copy-start.5 = (s32[24]{0:T(128)S(1)}, s32[24]{0:T(128)}, u32[]{:S(2)}) copy-start(s32[24]{0:T(128)} %cell_ref.1) | copy-start | bytes 292
  23.7 35.0 %copy-start.6 = (s32[24]{0:T(128)S(1)}, s32[24]{0:T(128)}, u32[]{:S(2)}) copy-start(s32[24]{0:T(128)} %reach_ref.1) | copy-start | bytes 292
  23.8 35.0 %copy-start.7 = (f32[24]{0:T(128)S(1)}, f32[24]{0:T(128)}, u32[]{:S(2)}) copy-start(f32[24]{0:T(128)} %value_ref.1) | copy-start | bytes 292
  23.8 35.0 %copy-start.8 = (f32[24]{0:T(128)S(1)}, f32[24]{0:T(128)}, u32[]{:S(2)}) copy-start(f32[24]{0:T(128)} %error_ref.1) | copy-start | bytes 292
  23.8 35.0 %copy-start.9 = (f32[7]{0:T(128)S(1)}, f32[7]{0:T(128)}, u32[]{:S(2)}) copy-start(f32[7]{0:T(128)} %taper_ref.1) | copy-start | bytes 88
  41.8 1.2 %collective-permute-start.6 = (f32[24,128]{1,0:T(8,128)S(1)}, f32[24,128]{1,0:T(8,128)S(1)}, u32[]{:S(2)}, u32[]{:S(2)}) collective-permute-start(f32[24,128]{1,0:T(8,128)S(1)} %get-tuple-element.25), channel_id=1, source_target_pairs={{0,4},{4,0},{8,12},{12,8},{16,20},{20,16},{24,28},{28,24},{1,5},{5... | collective-permute-start | bytes 36872 | tf_op jit(solution)/shard_map/ppermute | solution.py:472
  43.1 3.7 %collective-permute-start.7 = (f32[24,128]{1,0:T(8,128)S(1)}, f32[24,128]{1,0:T(8,128)S(1)}, u32[]{:S(2)}, u32[]{:S(2)}) collective-permute-start(f32[24,128]{1,0:T(8,128)S(1)} %add.19), channel_id=1, source_target_pairs={{0,8},{4,12},{8,0},{12,4},{16,24},{20,28},{24,16},{28,20},{1,9},{5... | collective-permute-start | bytes 36872 | tf_op jit(solution)/shard_map/ppermute | solution.py:472
  46.8 3.7 %collective-permute-start.8 = (f32[24,128]{1,0:T(8,128)S(1)}, f32[24,128]{1,0:T(8,128)S(1)}, u32[]{:S(2)}, u32[]{:S(2)}) collective-permute-start(f32[24,128]{1,0:T(8,128)S(1)} %add.20), channel_id=1, source_target_pairs={{0,16},{4,20},{8,24},{12,28},{16,0},{20,4},{24,8},{28,12},{1,17},{... | collective-permute-start | bytes 36872 | tf_op jit(solution)/shard_map/ppermute | solution.py:472
  50.5 3.7 %collective-permute-start.9 = (f32[24,128]{1,0:T(8,128)S(1)}, f32[24,128]{1,0:T(8,128)S(1)}, u32[]{:S(2)}, u32[]{:S(2)}) collective-permute-start(f32[24,128]{1,0:T(8,128)S(1)} %add.21), channel_id=1, source_target_pairs={{0,1},{1,0},{2,3},{3,2},{4,5},{5,4},{6,7},{7,6},{8,9},{9,8},{10,11... | collective-permute-start | bytes 36872 | tf_op jit(solution)/shard_map/ppermute | solution.py:472
  54.2 4.6 %collective-permute-start.10 = (f32[24,128]{1,0:T(8,128)S(1)}, f32[24,128]{1,0:T(8,128)S(1)}, u32[]{:S(2)}, u32[]{:S(2)}) collective-permute-start(f32[24,128]{1,0:T(8,128)S(1)} %add.22), channel_id=1, source_target_pairs={{0,2},{1,3},{2,0},{3,1},{4,6},{5,7},{6,4},{7,5},{8,10},{9,11},{10,... | collective-permute-start | bytes 36872 | tf_op jit(solution)/shard_map/ppermute | solution.py:472

commit v7 on v6

--- a/solution.py
+++ b/solution.py
@@ -14,7 +14,7 @@
 HIGHEST = lax.Precision.HIGHEST
 F32 = jnp.float32
 BF16 = jnp.bfloat16
-VMEM_LIMIT = 16 * 1024 * 1024
+VMEM_LIMIT = 24 * 1024 * 1024
 GROUP = 40
 
 VSPEC = pl.BlockSpec(memory_space=pltpu.VMEM)
@@ -35,28 +35,42 @@
     return x if shift == 0 else pltpu.roll(x, shift, x.ndim - 1)
 
 
-def band_kernel(members, rows, x_ref, lower_ref, upper_ref):
-    def group(g, carry):
-        here = pl.ds(pl.multiple_of(g * 8, 8), 8)
-        for f in range(3):
-            depth = MARGIN if f == 2 else MARGIN - 1
-            for d in range(depth):
-                at = (f * members + g * 8) * rows
-                lower_ref[f * (MARGIN - 1) + d, here, :] = x_ref[pl.ds(at + d, 8, stride=rows), :]
-                upper_ref[f * (MARGIN - 1) + d, here, :] = x_ref[pl.ds(at + rows - depth + d, 8, stride=rows), :]
-        return carry
-
-    lax.fori_loop(0, members // 8, group, 0)
+def band_kernel(members, rows, x_hbm, lower_hbm, upper_hbm, x_ref, lower_ref, upper_ref, sems):
+    def arrive(f):
+        field = pl.ds(f * members * rows, members * rows)
+        return pltpu.make_async_copy(x_hbm.at[field], x_ref.at[field], sems.at[0, f])
+
+    def leave(f, side):
+        source, target = ((lower_ref, lower_hbm), (upper_ref, upper_hbm))[side]
+        here = pl.ds(f * (MARGIN - 1), MARGIN if f == 2 else MARGIN - 1)
+        return pltpu.make_async_copy(source.at[here], target.at[here], sems.at[1 + side, f])
+
+    for f in range(3):
+        arrive(f).start()
+    for f in range(3):
+        arrive(f).wait()
+        depth = MARGIN if f == 2 else MARGIN - 1
+        for d in range(depth):
+            at = f * members * rows + d
+            lower_ref[f * (MARGIN - 1) + d] = x_ref[pl.ds(at, members, stride=rows), :]
+            upper_ref[f * (MARGIN - 1) + d] = x_ref[pl.ds(at + rows - depth, members, stride=rows), :]
+        leave(f, 0).start()
+        leave(f, 1).start()
+    for f in range(3):
+        leave(f, 0).wait()
+        leave(f, 1).wait()
 
 
 def bands(x, members, rows):
-    band = jax.ShapeDtypeStruct((3 * MARGIN - 2, members, x.shape[1]), F32)
+    cols = x.shape[1]
+    shape = (3 * MARGIN - 2, members, cols)
     return pl.pallas_call(
         functools.partial(band_kernel, members, rows),
-        out_shape=(band, band),
-        in_specs=[VSPEC],
-        out_specs=(VSPEC,) * 2,
-        compiler_params=pltpu.CompilerParams(vmem_limit_bytes=VMEM_LIMIT),
+        out_shape=(jax.ShapeDtypeStruct(shape, F32),) * 2,
+        in_specs=[pl.BlockSpec(memory_space=pltpu.HBM)],
+        out_specs=(pl.BlockSpec(memory_space=pl.ANY),) * 2,
+        scratch_shapes=[pltpu.VMEM(x.shape, F32)] + [pltpu.VMEM(shape, F32)] * 2 + [pltpu.SemaphoreType.DMA((3, 3))],
+        compiler_params=pltpu.CompilerParams(vmem_limit_bytes=60 * 1024 * 1024),
         cost_estimate=pl.CostEstimate(flops=1_000_000, bytes_accessed=4_000_000, transcendentals=0),
     )(x)
 
@@ -159,6 +173,10 @@
     return jnp.where(after, 1.0, jnp.where(before, -1.0, 0.0)).astype(BF16)
 
 
+def tall(x):
+    return jnp.concatenate([x] * (GROUP // 8), axis=0)
+
+
 def column_slope(x, shift):
     rows, group, wide = x.shape
     x = x.reshape(rows * group, wide)
@@ -168,7 +186,7 @@
     return slope.reshape(rows, group, wide)
 
 
-def interior_kernel(members, rows, place_ref, x_ref, left_ref, right_ref, drag_ref, margin_ref, state, keep, slope, across):
+def interior_kernel(members, rows, place_ref, x_ref, left_ref, right_ref, drag_ref, margin_ref, state, keep, slope):
     cols = x_ref.shape[1]
     wide = 2 * cols
     lane = lanes_of((8, cols))
@@ -176,8 +194,8 @@
     shift = shift_matrix(wide)
     kept = 1.0 - jnp.concatenate([drag_ref[...], margin_ref[...]], axis=1)
     for r in range(rows):
-        keep[r] = jnp.broadcast_to(kept[r : r + 1, :], (GROUP, wide))
-        slope[r] = jnp.broadcast_to(factor[MARGIN + r : MARGIN + r + 1, :], (GROUP, wide))
+        keep[r] = jnp.broadcast_to(kept[r : r + 1, :], (8, wide))
+        slope[r] = jnp.broadcast_to(factor[MARGIN + r : MARGIN + r + 1, :], (8, wide))
 
     def first(g, carry):
         here = pl.ds(pl.multiple_of(g * 8, 8), 8)
@@ -191,28 +209,26 @@
 
     lax.fori_loop(0, members // 8, first, 0)
 
-    def group(g, carry):
-        here = pl.ds(pl.multiple_of(g * GROUP, GROUP), GROUP)
-        for step in range(STEPS):
-            low, high = 1 + 2 * step, rows - 1 - 2 * step
-            if low >= high:
-                break
-            across[low:high] = column_slope(state[1, low:high, here, :], shift)
+    groups = [pl.ds(m, GROUP) for m in range(0, members, GROUP)]
+    for step in range(STEPS):
+        low, high = 1 + 2 * step, rows - 1 - 2 * step
+        if low >= high:
+            break
+        for here in groups:
+            d = column_slope(state[1, low:high, here, :], shift)
             for r in range(low, high):
-                div = across[r] + (state[2, r + 1, here, :] - state[2, r - 1, here, :])
-                state[0, r, here, :] = state[0, r, here, :] + slope[r] * div
-            low, high = low + 1, high - 1
-            if low >= high:
-                break
-            across[low:high] = column_slope(state[0, low:high, here, :], shift)
+                div = d[r - low] + (state[2, r + 1, here, :] - state[2, r - 1, here, :])
+                state[0, r, here, :] = state[0, r, here, :] + tall(slope[r]) * div
+        low, high = low + 1, high - 1
+        if low >= high:
+            break
+        for here in groups:
+            d = column_slope(state[0, low:high, here, :], shift)
             for r in range(low, high):
                 u, v = state[1, r, here, :], state[2, r, here, :]
-                k, c = keep[r], slope[r]
-                state[1, r, here, :] = k * u + c * across[r] + 0.1 * v
+                k, c = tall(keep[r]), tall(slope[r])
+                state[1, r, here, :] = k * u + c * d[r - low] + 0.1 * v
                 state[2, r, here, :] = k * v + c * (state[0, r + 1, here, :] - state[0, r - 1, here, :]) - 0.1 * u
-        return carry
-
-    lax.fori_loop(0, members // GROUP, group, 0)
 
 
 def interior(place, x, left, right, drag, margin, members):
@@ -222,7 +238,7 @@
         out_shape=jax.ShapeDtypeStruct((3, rows, members, 2 * cols), F32),
         in_specs=[SSPEC] + [VSPEC] * 5,
         out_specs=VSPEC,
-        scratch_shapes=[pltpu.VMEM((rows, GROUP, 2 * cols), F32)] * 3,
+        scratch_shapes=[pltpu.VMEM((rows, 8, 2 * cols), F32)] * 2,
         compiler_params=pltpu.CompilerParams(vmem_limit_bytes=VMEM_LIMIT),
         cost_estimate=pl.CostEstimate(flops=30_000_000, bytes_accessed=10_000_000, transcendentals=0),
     )(place, x, left, right, drag, margin)
@@ -233,7 +249,7 @@
     place_ref, order_ref, owner_ref, cell_ref,
     inner_ref, above_ref, below_ref, ceven_ref, codd_ref, drag_ref, margin_ref,
     out_ref, prior_ref,
-    state, keep, slope, across,
+    state, keep, slope,
 ):
     cols = above_ref.shape[2]
     wide = 2 * cols
@@ -251,54 +267,54 @@
         parts.append(jnp.concatenate([above, own[...], below], axis=0))
     kept = 1.0 - jnp.concatenate(parts, axis=1)
     for r in range(total):
-        keep[r] = jnp.broadcast_to(kept[r : r + 1, :], (GROUP, wide))
-        slope[r] = jnp.broadcast_to(factor[r : r + 1, :], (GROUP, wide))
-
-    def group(g, carry):
-        here = pl.ds(pl.multiple_of(g * GROUP, GROUP), GROUP)
+        keep[r] = jnp.broadcast_to(kept[r : r + 1, :], (8, wide))
+        slope[r] = jnp.broadcast_to(factor[r : r + 1, :], (8, wide))
+
+    groups = range(members // GROUP)
+    for g in groups:
+        here = pl.ds(g * GROUP, GROUP)
         for f in range(3):
-            at = pl.ds(pl.multiple_of(f * members + g * GROUP, 8), GROUP)
+            at = pl.ds(f * members + g * GROUP, GROUP)
             ceven, codd = ceven_ref[at, :], codd_ref[at, :]
             cab, cbe = jnp.where(odd_y, ceven, codd), jnp.where(odd_y, codd, ceven)
             depth = MARGIN if f == 2 else MARGIN - 1
             for d in range(depth):
                 r = MARGIN - depth + d
                 main = above_ref[f * (MARGIN - 1) + d, here, :]
-                state[f, r] = wide_row(lane, main, cab, MARGIN * r, cab, half + MARGIN * r)
+                state[g, f, r] = wide_row(lane, main, cab, MARGIN * r, cab, half + MARGIN * r)
                 main = below_ref[f * (MARGIN - 1) + d, here, :]
-                state[f, MARGIN + rows + d] = wide_row(lane, main, cbe, MARGIN * d, cbe, half + MARGIN * d)
+                state[g, f, MARGIN + rows + d] = wide_row(lane, main, cbe, MARGIN * d, cbe, half + MARGIN * d)
             for r in range(rows):
-                state[f, MARGIN + r] = inner_ref[f, r, here, :]
-        for step in range(STEPS):
-            first, last = MARGIN - MARGIN + 1 + 2 * step, MARGIN + rows + MARGIN - 1 - 2 * step
-            done, still = MARGIN + 1 + 2 * step, MARGIN + rows - 1 - 2 * step
-            spans = ((first, min(done, still)), (max(done, still), last)) if done < still else ((first, last),)
-            for low, high in spans:
-                across[low:high] = column_slope(state[1, low:high], shift)
-            for low, high in spans:
-                for r in range(low, high):
-                    div = across[r] + (state[2, r + 1] - state[2, r - 1])
-                    state[0, r] = state[0, r] + slope[r] * div
-            first, last, done, still = first + 1, last - 1, done + 1, still - 1
-            spans = ((first, done), (still, last)) if done < still else ((first, MARGIN + rows // 2), (MARGIN + rows // 2, last))
-            for low, high in spans:
-                across[low:high] = column_slope(state[0, low:high], shift)
-            for low, high in spans:
-                for r in range(low, high):
-                    u, v = state[1, r], state[2, r]
-                    k, c = keep[r], slope[r]
-                    u, v = (
-                        k * u + c * across[r] + 0.1 * v,
-                        k * v + c * (state[0, r + 1] - state[0, r - 1]) - 0.1 * u,
-                    )
-                    state[1, r] = u
-                    state[2, r] = v
+                state[g, f, MARGIN + r] = inner_ref[f, r, here, :]
+
+    def heights(g, spans):
+        for low, high in spans:
+            d = column_slope(state[g, 1, low:high], shift)
+            for r in range(low, high):
+                div = d[r - low] + (state[g, 2, r + 1] - state[g, 2, r - 1])
+                state[g, 0, r] = state[g, 0, r] + tall(slope[r]) * div
+
+    def flows(g, spans):
+        for low, high in spans:
+            d = column_slope(state[g, 0, low:high], shift)
+            for r in range(low, high):
+                u, v = state[g, 1, r], state[g, 2, r]
+                k, c = tall(keep[r]), tall(slope[r])
+                state[g, 1, r] = k * u + c * d[r - low] + 0.1 * v
+                state[g, 2, r] = k * v + c * (state[g, 0, r + 1] - state[g, 0, r - 1]) - 0.1 * u
+
+    for step in range(STEPS):
+        first, last = MARGIN - MARGIN + 1 + 2 * step, MARGIN + rows + MARGIN - 1 - 2 * step
+        done, still = MARGIN + 1 + 2 * step, MARGIN + rows - 1 - 2 * step
+        for g in groups:
+            heights(g, ((first, done), (still, last)))
+        for g in groups:
+            flows(g, ((first + 1, done + 1), (still - 1, last - 1)))
+    for g in groups:
+        here = pl.ds(g * GROUP, GROUP)
         for f in range(3):
             for r in range(rows):
-                out_ref[f * rows + r, here, :] = state[f, MARGIN + r, :, 0:cols]
-        return carry
-
-    lax.fori_loop(0, members // GROUP, group, 0)
+                out_ref[f * rows + r, here, :] = state[g, f, MARGIN + r, :, 0:cols]
 
     prior_ref[...] = jnp.zeros_like(prior_ref)
     eight = lanes_of((8, cols))
@@ -326,7 +342,7 @@
         ),
         in_specs=[SSPEC] * 4 + [VSPEC] * (1 + len(arrays)),
         out_specs=(VSPEC, VSPEC),
-        scratch_shapes=[pltpu.VMEM((3, total, GROUP, wide), F32)] + [pltpu.VMEM((total, GROUP, wide), F32)] * 3,
+        scratch_shapes=[pltpu.VMEM((members // GROUP, 3, total, GROUP, wide), F32)] + [pltpu.VMEM((total, 8, wide), F32)] * 2,
         compiler_params=pltpu.CompilerParams(vmem_limit_bytes=VMEM_LIMIT),
         cost_estimate=pl.CostEstimate(flops=60_000_000, bytes_accessed=30_000_000, transcendentals=0),
     )(place, order, owner, cell, inner, *arrays)
@@ -345,7 +361,8 @@
     members, rows,
     place_ref, order_ref, owner_ref, reach_ref, value_ref, error_ref, taper_ref,
     prior_ref, forecast_ref,
-    out_ref,
+    result_ref,
+    out_ref, sems,
 ):
     n_obs = order_ref.shape[0]
     cols = prior_ref.shape[1]
@@ -436,6 +453,12 @@
         for b in range(block):
             f, r = divmod(at + b, rows)
             out_ref[pl.ds(f * members * rows + r, members, stride=rows), :] = y[:, b * cols : (b + 1) * cols]
+        if (at + block) % rows == 0:
+            field = pl.ds(at // rows * members * rows, members * rows)
+            pltpu.make_async_copy(out_ref.at[field], result_ref.at[field], sems.at[at // rows]).start()
+    for f in range(3):
+        field = pl.ds(f * members * rows, members * rows)
+        pltpu.make_async_copy(out_ref.at[field], result_ref.at[field], sems.at[f]).wait()
 
 
 def assimilate(place, order, owner, reach, value, error, taper, priors, states, members, rows):
@@ -444,7 +467,8 @@
         functools.partial(assimilate_kernel, members, rows),
         out_shape=jax.ShapeDtypeStruct((3 * members * rows, cols), F32),
         in_specs=[SSPEC] * 7 + [VSPEC] * 2,
-        out_specs=VSPEC,
+        out_specs=pl.BlockSpec(memory_space=pl.ANY),
+        scratch_shapes=[pltpu.VMEM((3 * members * rows, cols), F32), pltpu.SemaphoreType.DMA((3,))],
         compiler_params=pltpu.CompilerParams(vmem_limit_bytes=VMEM_LIMIT),
     )(place, order, owner, reach, value, error, taper, priors, states)
 

time: 65.6 us -> 64.2 us (0.979)
  local copies, waits for them, and re-layouts: 1.68 us -> 0.14 us
  waiting for transfers between devices: 21.3 us -> 22.4 us
  Pallas kernels: 24.4 us -> 23.6 us
    unnamed x20 -> x18, local copies, waits for them, and re-layouts: 1.6 us -> 0.05 us
    pallas_call x1, Pallas kernels: 6.21 us -> 5.24 us  [interior(): pl.pallas_call(functools.partial(interior_kernel, members, rows), out_sha...]
    ppermute x4, waiting for transfers between devices: 11.6 us -> 12.6 us  [swap_pairs(): return lax.ppermute(x, axis, pairs + [(b, a) for a, b in pairs])]
    pallas_call x1, Pallas kernels: 1.81 us -> 2.65 us  [bands(): pl.pallas_call(functools.partial(band_kernel, members, rows), out_shape=(...]
  transfers between devices with their start and end apart: 11 -> 11, of which waited for: 7 -> 7; matrix products, arithmetic and copies ran while one was open for 0% -> 0% of each run, Pallas kernels for 14% -> 13%
where the time goes in v7:
time: 64.2 us; the launch traced here: 64 us
  Pallas kernels  23.6 us (37%)
  waiting for transfers between devices  22.4 us (35%)
  starting transfers between devices  17.5 us (27%)
    ppermute x4, waiting for transfers between devices, swap_pairs(): return lax.ppermute(x, axis, pairs + [(b, a) for a, b in pairs])  12.6 us
    ppermute x5, waiting for transfers between devices, add_over(): x = x + lax.ppermute(x, axis, [(i, i ^ span) for i in range(count)])  9.82 us
    ppermute x5, starting transfers between devices, add_over(): x = x + lax.ppermute(x, axis, [(i, i ^ span) for i in range(count)])  7.09 us
    pallas_call x1, Pallas kernels, forecast(): pl.pallas_call(functools.partial(forecast_kernel, members, rows), out_sha...  6.68 us
    pallas_call x1, Pallas kernels, assimilate(): pl.pallas_call(functools.partial(assimilate_kernel, members, rows), out_s...  6.08 us
    pallas_call x1, Pallas kernels, interior(): pl.pallas_call(functools.partial(interior_kernel, members, rows), out_sha...  5.24 us
    ppermute x1, starting transfers between devices, to_neighbours(): lax.ppermute(upper, axis, forward)  4.98 us
    ppermute x4, starting transfers between devices, swap_pairs(): return lax.ppermute(x, axis, pairs + [(b, a) for a, b in pairs])  4.11 us
  transfers between devices with their start and end apart: 11, of which 7 were waited for; matrix products, arithmetic and copies ran while one was open for 0% of the time, Pallas kernels for 13%

profile of v7, /device:TPU:0, one launch (start us, length us, event | category | flops | bytes accessed | tf_op | source)
XLA Modules:
  0.0 64.0 jit_solution(7167945270977290978)
XLA Ops:
  0.0 2.7 %shard_map.94 = (f32[22,80,128]{2,1,0:T(8,128)}, f32[22,80,128]{2,1,0:T(8,128)}) custom-call(f32[3840,128]{1,0:T(8,128)} %bitcast.7), custom_call_target="tpu_custom_call" | custom-call | flops 1000000 | bytes 4000000 | tf_op jit(solution)/shard_map/pallas_call | solution.py:67
  2.7 5.0 %collective-permute-start.2 = (f32[22,80,128]{2,1,0:T(8,128)}, f32[22,80,128]{2,1,0:T(8,128)S(1)}, u32[]{:S(2)}, u32[]{:S(2)}) collective-permute-start(f32[22,80,128]{2,1,0:T(8,128)} %get-tuple-element.21), channel_id=1, source_target_pairs={{0,1},{1,2},{2,3},{4,5},{5,6},{6,7},{8,9},{9,10},{10,11},{12,13},{... | collective-permute-start | bytes 2703368 | tf_op jit(solution)/shard_map/ppermute | solution.py:480
  7.7 1.3 %collective-permute-start.3 = (f32[22,80,128]{2,1,0:T(8,128)}, f32[22,80,128]{2,1,0:T(8,128)}, u32[]{:S(2)}, u32[]{:S(2)}) collective-permute-start(f32[22,80,128]{2,1,0:T(8,128)} %get-tuple-element.22), channel_id=1, source_target_pairs={{1,0},{2,1},{3,2},{5,4},{6,5},{7,6},{9,8},{10,9},{11,10},{13,12},{... | collective-permute-start | bytes 2703368 | tf_op jit(solution)/shard_map/ppermute | solution.py:480
  9.0 0.1 stack.39.place_ref
  9.1 2.2 %shard_map.91 = (f32[256,128]{1,0:T(8,128)S(1)}, f32[256,128]{1,0:T(8,128)S(1)}) custom-call(s32[6]{0:T(128)S(1)} %stack.39.place_ref, f32[3840,128]{1,0:T(8,128)S(1)} %bitcast.8, f32[16,128]{1,0:T(8,128)S(1)} %copy-done.1), custom_call_target="tpu_custom_call" | custom-call | flops 1000000 | bytes 4000000 | tf_op jit(solution)/shard_map/pallas_call | solution.py:105
  11.3 0.1 collective-permute-start
  11.4 0.7 %collective-permute-start.1 = (f32[256,128]{1,0:T(8,128)S(1)}, f32[256,128]{1,0:T(8,128)S(1)}, u32[]{:S(2)}, u32[]{:S(2)}) collective-permute-start(f32[256,128]{1,0:T(8,128)S(1)} %get-tuple-element.17), channel_id=1, source_target_pairs={{4,8},{12,16},{20,24},{8,4},{16,12},{24,20},{5,9},{13,17},{21,25},... | collective-permute-start | bytes 393224 | tf_op jit(solution)/shard_map/ppermute | solution.py:485
  12.1 0.7 %collective-permute-done.even_ref = f32[256,128]{1,0:T(8,128)S(1)} collective-permute-done((f32[256,128]{1,0:T(8,128)S(1)}, f32[256,128]{1,0:T(8,128)S(1)}, u32[]{:S(2)}, u32[]{:S(2)}) %collective-permute-start) | collective-permute-done | bytes 131104 | tf_op jit(solution)/shard_map/ppermute | solution.py:485
  12.7 0.7 %shard_map.92 = (f32[240,128]{1,0:T(8,128)S(1)}, f32[240,128]{1,0:T(8,128)S(1)}, f32[16,128]{1,0:T(8,128)S(1)}, f32[256,128]{1,0:T(8,128)S(1)}, f32[256,128]{1,0:T(8,128)S(1)}) custom-call(s32[6]{0:T(128)S(1)} %stack.39.place_ref, f32[16,128]{1,0:T(8,128)S(1)} %copy-done.1, f32[256,128]{1,0:T(8,128)S(1)} %collective-permute-done.even_ref, ...), custom_call_target="tpu_custom_call" | custom-call | tf_op jit(solution)/shard_map/pallas_call | solution.py:145
  13.4 2.7 %collective-permute-start.4 = (f32[256,128]{1,0:T(8,128)S(1)}, f32[256,128]{1,0:T(8,128)S(1)}, u32[]{:S(2)}, u32[]{:S(2)}) collective-permute-start(f32[256,128]{1,0:T(8,128)S(1)} %get-tuple-element.23), channel_id=1, source_target_pairs={{0,1},{2,3},{1,0},{3,2},{4,5},{6,7},{5,4},{7,6},{8,9},{10,11},{9,8... | collective-permute-start | bytes 393224 | tf_op jit(solution)/shard_map/ppermute | solution.py:485
  16.1 0.7 %collective-permute-start.5 = (f32[256,128]{1,0:T(8,128)S(1)}, f32[256,128]{1,0:T(8,128)S(1)}, u32[]{:S(2)}, u32[]{:S(2)}) collective-permute-start(f32[256,128]{1,0:T(8,128)S(1)} %get-tuple-element.24), channel_id=1, source_target_pairs={{1,2},{2,1},{5,6},{6,5},{9,10},{10,9},{13,14},{14,13},{17,18},{18,... | collective-permute-start | bytes 393224 | tf_op jit(solution)/shard_map/ppermute | solution.py:485
  16.8 5.2 %shard_map.93.inner_ref = f32[3,16,80,256]{3,2,1,0:T(8,128)S(1)} custom-call(s32[6]{0:T(128)S(1)} %stack.39.place_ref, f32[3840,128]{1,0:T(8,128)S(1)} %bitcast.9, f32[240,128]{1,0:T(8,128)S(1)} %get-tuple-element.18.left_ref, f32[240,128]{1,0:T(8,128)S(1)} %get-tuple-element.19.right_ref, f32[16,128]{1,0:T(8,128)S(1)} %copy-done.1, ...), custom_call_target="tpu_custom_call" | custom-call | flops 30000000 | bytes 10000000 | tf_op jit(solution)/shard_map/pallas_call | solution.py:236
  22.1 11.9 %collective-permute-done.4.ceven_ref = f32[256,128]{1,0:T(8,128)S(1)} collective-permute-done((f32[256,128]{1,0:T(8,128)S(1)}, f32[256,128]{1,0:T(8,128)S(1)}, u32[]{:S(2)}, u32[]{:S(2)}) %collective-permute-start.4) | collective-permute-done | bytes 131104 | tf_op jit(solution)/shard_map/ppermute | solution.py:485
  34.1 6.7 %shard_map.95 = (f32[48,80,128]{2,1,0:T(8,128)S(1)}, f32[24,128]{1,0:T(8,128)S(1)}) custom-call(s32[6]{0:T(128)S(1)} %stack.39.place_ref, s32[24]{0:T(128)S(1)} %copy-done.2, s32[24]{0:T(128)S(1)} %copy-done.3, s32[24]{0:T(128)S(1)} %copy-done.4, f32[3,16,80,256]{3,2,1,0:T(8,128)S(1)} %shard_map.93.inner_ref, ...), custom_call_target="tpu_custom_call" | custom-call | flops 60000000 | bytes 30000000 | tf_op jit(solution)/shard_map/pallas_call | solution.py:337
  40.8 1.2 %collective-permute-done.6 = f32[24,128]{1,0:T(8,128)S(1)} collective-permute-done((f32[24,128]{1,0:T(8,128)S(1)}, f32[24,128]{1,0:T(8,128)S(1)}, u32[]{:S(2)}, u32[]{:S(2)}) %collective-permute-start.6) | collective-permute-done | bytes 12320 | tf_op jit(solution)/shard_map/ppermute | solution.py:496
  42.0 1.4 %collective-permute-start.7 = (f32[24,128]{1,0:T(8,128)S(1)}, f32[24,128]{1,0:T(8,128)S(1)}, u32[]{:S(2)}, u32[]{:S(2)}) collective-permute-start(f32[24,128]{1,0:T(8,128)S(1)} %add.19), channel_id=1, source_target_pairs={{0,8},{4,12},{8,0},{12,4},{16,24},{20,28},{24,16},{28,20},{1,9},{5... | collective-permute-start | bytes 36872 | tf_op jit(solution)/shard_map/ppermute | solution.py:496
  43.5 2.3 %collective-permute-done.7 = f32[24,128]{1,0:T(8,128)S(1)} collective-permute-done((f32[24,128]{1,0:T(8,128)S(1)}, f32[24,128]{1,0:T(8,128)S(1)}, u32[]{:S(2)}, u32[]{:S(2)}) %collective-permute-start.7) | collective-permute-done | bytes 12320 | tf_op jit(solution)/shard_map/ppermute | solution.py:496
  45.7 1.5 %collective-permute-start.8 = (f32[24,128]{1,0:T(8,128)S(1)}, f32[24,128]{1,0:T(8,128)S(1)}, u32[]{:S(2)}, u32[]{:S(2)}) collective-permute-start(f32[24,128]{1,0:T(8,128)S(1)} %add.20), channel_id=1, source_target_pairs={{0,16},{4,20},{8,24},{12,28},{16,0},{20,4},{24,8},{28,12},{1,17},{... | collective-permute-start | bytes 36872 | tf_op jit(solution)/shard_map/ppermute | solution.py:496
  47.2 2.2 %collective-permute-done.8 = f32[24,128]{1,0:T(8,128)S(1)} collective-permute-done((f32[24,128]{1,0:T(8,128)S(1)}, f32[24,128]{1,0:T(8,128)S(1)}, u32[]{:S(2)}, u32[]{:S(2)}) %collective-permute-start.8) | collective-permute-done | bytes 12320 | tf_op jit(solution)/shard_map/ppermute | solution.py:496
  49.4 1.5 %collective-permute-start.9 = (f32[24,128]{1,0:T(8,128)S(1)}, f32[24,128]{1,0:T(8,128)S(1)}, u32[]{:S(2)}, u32[]{:S(2)}) collective-permute-start(f32[24,128]{1,0:T(8,128)S(1)} %add.21), channel_id=1, source_target_pairs={{0,1},{1,0},{2,3},{3,2},{4,5},{5,4},{6,7},{7,6},{8,9},{9,8},{10,11... | collective-permute-start | bytes 36872 | tf_op jit(solution)/shard_map/ppermute | solution.py:496
  50.9 2.2 %collective-permute-done.9 = f32[24,128]{1,0:T(8,128)S(1)} collective-permute-done((f32[24,128]{1,0:T(8,128)S(1)}, f32[24,128]{1,0:T(8,128)S(1)}, u32[]{:S(2)}, u32[]{:S(2)}) %collective-permute-start.9) | collective-permute-done | bytes 12320 | tf_op jit(solution)/shard_map/ppermute | solution.py:496
  53.1 2.6 %collective-permute-start.10 = (f32[24,128]{1,0:T(8,128)S(1)}, f32[24,128]{1,0:T(8,128)S(1)}, u32[]{:S(2)}, u32[]{:S(2)}) collective-permute-start(f32[24,128]{1,0:T(8,128)S(1)} %add.22), channel_id=1, source_target_pairs={{0,2},{1,3},{2,0},{3,1},{4,6},{5,7},{6,4},{7,5},{8,10},{9,11},{10,... | collective-permute-start | bytes 36872 | tf_op jit(solution)/shard_map/ppermute | solution.py:496
  55.7 2.0 %collective-permute-done.10 = f32[24,128]{1,0:T(8,128)S(1)} collective-permute-done((f32[24,128]{1,0:T(8,128)S(1)}, f32[24,128]{1,0:T(8,128)S(1)}, u32[]{:S(2)}, u32[]{:S(2)}) %collective-permute-start.10) | collective-permute-done | bytes 12320 | tf_op jit(solution)/shard_map/ppermute | solution.py:496
  57.7 6.1 %shard_map.96 = f32[3840,128]{1,0:T(8,128)} custom-call(s32[6]{0:T(128)S(1)} %stack.39.place_ref, s32[24]{0:T(128)S(1)} %copy-done.2, s32[24]{0:T(128)S(1)} %copy-done.3, s32[24]{0:T(128)S(1)} %copy-done.5, f32[24]{0:T(128)S(1)} %copy-done.6, f32[24]{0:T(128)S(1)} %copy-done.7, f32[7]{0:T(128)S(1)} %copy-done.8, f32[24,128]{1,0:T(8,128)S(1)} %add.23.prior_ref, ...), custom_call_target="tpu_custom_call" | custom-call | tf_op jit(solution)/shard_map/pallas_call | solution.py:466
  (28 shorter events, 0.2 us)
Async XLA Ops:
  0.0 9.1 %copy-start = (f32[3,80,16,128]{3,2,1,0:T(8,128)S(1)}, f32[3,80,16,128]{3,2,1,0:T(8,128)}, u32[]{:S(2)}) copy-start(f32[3,80,16,128]{3,2,1,0:T(8,128)} %param.9) | copy-start | bytes 5898244
  0.0 9.1 %copy-start.1 = (f32[16,128]{1,0:T(8,128)S(1)}, f32[16,128]{1,0:T(8,128)}, u32[]{:S(2)}) copy-start(f32[16,128]{1,0:T(8,128)} %drag_ref.7) | copy-start | bytes 24580
  2.7 31.4 %collective-permute-start.2 = (f32[22,80,128]{2,1,0:T(8,128)}, f32[22,80,128]{2,1,0:T(8,128)S(1)}, u32[]{:S(2)}, u32[]{:S(2)}) collective-permute-start(f32[22,80,128]{2,1,0:T(8,128)} %get-tuple-element.21), channel_id=1, source_target_pairs={{0,1},{1,2},{2,3},{4,5},{5,6},{6,7},{8,9},{9,10},{10,11},{12,13},{... | collective-permute-start | bytes 2703368 | tf_op jit(solution)/shard_map/ppermute | solution.py:480
  7.7 26.4 %collective-permute-start.3 = (f32[22,80,128]{2,1,0:T(8,128)}, f32[22,80,128]{2,1,0:T(8,128)}, u32[]{:S(2)}, u32[]{:S(2)}) collective-permute-start(f32[22,80,128]{2,1,0:T(8,128)} %get-tuple-element.22), channel_id=1, source_target_pairs={{1,0},{2,1},{3,2},{5,4},{6,5},{7,6},{9,8},{10,9},{11,10},{13,12},{... | collective-permute-start | bytes 2703368 | tf_op jit(solution)/shard_map/ppermute | solution.py:480
  11.3 1.4 %collective-permute-start = (f32[256,128]{1,0:T(8,128)S(1)}, f32[256,128]{1,0:T(8,128)S(1)}, u32[]{:S(2)}, u32[]{:S(2)}) collective-permute-start(f32[256,128]{1,0:T(8,128)S(1)} %get-tuple-element.16), channel_id=1, source_target_pairs={{0,4},{8,12},{16,20},{24,28},{4,0},{12,8},{20,16},{28,24},{1,5},{9... | collective-permute-start | bytes 393224 | tf_op jit(solution)/shard_map/ppermute | solution.py:485
  11.4 1.3 %collective-permute-start.1 = (f32[256,128]{1,0:T(8,128)S(1)}, f32[256,128]{1,0:T(8,128)S(1)}, u32[]{:S(2)}, u32[]{:S(2)}) collective-permute-start(f32[256,128]{1,0:T(8,128)S(1)} %get-tuple-element.17), channel_id=1, source_target_pairs={{4,8},{12,16},{20,24},{8,4},{16,12},{24,20},{5,9},{13,17},{21,25},... | collective-permute-start | bytes 393224 | tf_op jit(solution)/shard_map/ppermute | solution.py:485
  13.4 20.6 %collective-permute-start.4 = (f32[256,128]{1,0:T(8,128)S(1)}, f32[256,128]{1,0:T(8,128)S(1)}, u32[]{:S(2)}, u32[]{:S(2)}) collective-permute-start(f32[256,128]{1,0:T(8,128)S(1)} %get-tuple-element.23), channel_id=1, source_target_pairs={{0,1},{2,3},{1,0},{3,2},{4,5},{6,7},{5,4},{7,6},{8,9},{10,11},{9,8... | collective-permute-start | bytes 393224 | tf_op jit(solution)/shard_map/ppermute | solution.py:485
  16.1 17.9 %collective-permute-start.5 = (f32[256,128]{1,0:T(8,128)S(1)}, f32[256,128]{1,0:T(8,128)S(1)}, u32[]{:S(2)}, u32[]{:S(2)}) collective-permute-start(f32[256,128]{1,0:T(8,128)S(1)} %get-tuple-element.24), channel_id=1, source_target_pairs={{1,2},{2,1},{5,6},{6,5},{9,10},{10,9},{13,14},{14,13},{17,18},{18,... | collective-permute-start | bytes 393224 | tf_op jit(solution)/shard_map/ppermute | solution.py:485
  16.8 17.2 %copy-start.2 = (s32[24]{0:T(128)S(1)}, s32[24]{0:T(128)}, u32[]{:S(2)}) copy-start(s32[24]{0:T(128)} %order_ref.3) | copy-start | bytes 292
  16.8 17.2 %copy-start.3 = (s32[24]{0:T(128)S(1)}, s32[24]{0:T(128)}, u32[]{:S(2)}) copy-start(s32[24]{0:T(128)} %owner_ref.3) | copy-start | bytes 292
  16.8 17.2 %copy-start.4 = (s32[24]{0:T(128)S(1)}, s32[24]{0:T(128)}, u32[]{:S(2)}) copy-start(s32[24]{0:T(128)} %cell_ref.1) | copy-start | bytes 292
  22.1 35.6 %copy-start.5 = (s32[24]{0:T(128)S(1)}, s32[24]{0:T(128)}, u32[]{:S(2)}) copy-start(s32[24]{0:T(128)} %reach_ref.1) | copy-start | bytes 292
  22.1 35.6 %copy-start.6 = (f32[24]{0:T(128)S(1)}, f32[24]{0:T(128)}, u32[]{:S(2)}) copy-start(f32[24]{0:T(128)} %value_ref.1) | copy-start | bytes 292
  22.1 35.6 %copy-start.7 = (f32[24]{0:T(128)S(1)}, f32[24]{0:T(128)}, u32[]{:S(2)}) copy-start(f32[24]{0:T(128)} %error_ref.1) | copy-start | bytes 292
  22.1 35.6 %copy-start.8 = (f32[7]{0:T(128)S(1)}, f32[7]{0:T(128)}, u32[]{:S(2)}) copy-start(f32[7]{0:T(128)} %taper_ref.1) | copy-start | bytes 88
  40.8 1.2 %collective-permute-start.6 = (f32[24,128]{1,0:T(8,128)S(1)}, f32[24,128]{1,0:T(8,128)S(1)}, u32[]{:S(2)}, u32[]{:S(2)}) collective-permute-start(f32[24,128]{1,0:T(8,128)S(1)} %get-tuple-element.25), channel_id=1, source_target_pairs={{0,4},{4,0},{8,12},{12,8},{16,20},{20,16},{24,28},{28,24},{1,5},{5... | collective-permute-start | bytes 36872 | tf_op jit(solution)/shard_map/ppermute | solution.py:496
  42.0 3.7 %collective-permute-start.7 = (f32[24,128]{1,0:T(8,128)S(1)}, f32[24,128]{1,0:T(8,128)S(1)}, u32[]{:S(2)}, u32[]{:S(2)}) collective-permute-start(f32[24,128]{1,0:T(8,128)S(1)} %add.19), channel_id=1, source_target_pairs={{0,8},{4,12},{8,0},{12,4},{16,24},{20,28},{24,16},{28,20},{1,9},{5... | collective-permute-start | bytes 36872 | tf_op jit(solution)/shard_map/ppermute | solution.py:496
  45.7 3.7 %collective-permute-start.8 = (f32[24,128]{1,0:T(8,128)S(1)}, f32[24,128]{1,0:T(8,128)S(1)}, u32[]{:S(2)}, u32[]{:S(2)}) collective-permute-start(f32[24,128]{1,0:T(8,128)S(1)} %add.20), channel_id=1, source_target_pairs={{0,16},{4,20},{8,24},{12,28},{16,0},{20,4},{24,8},{28,12},{1,17},{... | collective-permute-start | bytes 36872 | tf_op jit(solution)/shard_map/ppermute | solution.py:496
  49.4 3.7 %collective-permute-start.9 = (f32[24,128]{1,0:T(8,128)S(1)}, f32[24,128]{1,0:T(8,128)S(1)}, u32[]{:S(2)}, u32[]{:S(2)}) collective-permute-start(f32[24,128]{1,0:T(8,128)S(1)} %add.21), channel_id=1, source_target_pairs={{0,1},{1,0},{2,3},{3,2},{4,5},{5,4},{6,7},{7,6},{8,9},{9,8},{10,11... | collective-permute-start | bytes 36872 | tf_op jit(solution)/shard_map/ppermute | solution.py:496
  53.1 4.6 %collective-permute-start.10 = (f32[24,128]{1,0:T(8,128)S(1)}, f32[24,128]{1,0:T(8,128)S(1)}, u32[]{:S(2)}, u32[]{:S(2)}) collective-permute-start(f32[24,128]{1,0:T(8,128)S(1)} %add.22), channel_id=1, source_target_pairs={{0,2},{1,3},{2,0},{3,1},{4,6},{5,7},{6,4},{7,5},{8,10},{9,11},{10,... | collective-permute-start | bytes 36872 | tf_op jit(solution)/shard_map/ppermute | solution.py:496

commit v8 on v7

--- a/solution.py
+++ b/solution.py
@@ -86,9 +86,9 @@
             right = jnp.zeros((8, cols), F32)
             for r in range(rows):
                 row = x_ref[pl.ds((f * members + g * 8) * rows + r, 8, stride=rows), :]
-                there = (lane >= MARGIN * r) & (lane < MARGIN * (r + 1))
-                left = jnp.where(there, roll_lanes(row, MARGIN * r), left)
-                right = jnp.where(there, roll_lanes(row, MARGIN * (r + 1)), right)
+                slot = lane // MARGIN
+                left = jnp.where(slot == rows - 1 - r, roll_lanes(row, MARGIN * (rows - 1 - r)), left)
+                right = jnp.where(slot == r, roll_lanes(row, MARGIN * (r + 1)), right)
             at = pl.ds(pl.multiple_of(f * members + g * 8, 8), 8)
             even_ref[at, :] = jnp.where(odd_x, left, right)
             odd_ref[at, :] = jnp.where(odd_x, right, left)
@@ -125,9 +125,15 @@
     left, right = left[:count], right[:count]
     left_ref[...] = left
     right_ref[...] = right
+    lane = lanes_of((count, cols))
+    slot, column = lane % half // MARGIN, lane % MARGIN
+    mine = column > jnp.where(lane < half, slot, MARGIN - 1 - slot)
+    both = jnp.where(mine, left, roll_lanes(right, half))
+    count = count // 2
+    head, tail = both[:count], both[count:]
     first_half = lanes_of((count, cols)) < half
-    lower = jnp.where(first_half, left, roll_lanes(right, half))
-    upper = jnp.where(first_half, roll_lanes(left, half), right)
+    lower = jnp.where(first_half, head, roll_lanes(tail, half))
+    upper = jnp.where(first_half, roll_lanes(head, half), tail)
     even_out[:count, :] = jnp.where(odd_y, lower, upper)
     odd_out[:count, :] = jnp.where(odd_y, upper, lower)
     drag = drag_ref[...]
@@ -141,7 +147,7 @@
     rows, cols = drag.shape
     count = even.shape[0] - rows
     edge = jax.ShapeDtypeStruct((count, cols), F32)
-    message = jax.ShapeDtypeStruct((count + 2 * MARGIN, cols), F32)
+    message = jax.ShapeDtypeStruct((count // 2 + 2 * MARGIN, cols), F32)
     return pl.pallas_call(
         corner_kernel,
         out_shape=(edge, edge, jax.ShapeDtypeStruct((rows, cols), F32), message, message),
@@ -204,7 +210,7 @@
             left, right = left_ref[at, :], right_ref[at, :]
             for r in range(rows):
                 main = x_ref[pl.ds((f * members + g * 8) * rows + r, 8, stride=rows), :]
-                state[f, r, here, :] = wide_row(lane, main, left, MARGIN * r, right, MARGIN * r)
+                state[f, r, here, :] = wide_row(lane, main, left, MARGIN * r, right, MARGIN * (rows - 1 - r))
         return carry
 
     lax.fori_loop(0, members // 8, first, 0)
@@ -259,7 +265,7 @@
     factor = -0.2 * grid_factor(place_ref, (total, wide), rows, cols)
     odd_y = place_ref[0] % place_ref[5] % 2 == 1
     shift = shift_matrix(wide)
-    count = 3 * members
+    count = 3 * members // 2
     parts = []
     for here, own in ((count, drag_ref), (count + MARGIN, margin_ref)):
         even, odd = ceven_ref[here : here + MARGIN, :], codd_ref[here : here + MARGIN, :]
@@ -274,16 +280,20 @@
     for g in groups:
         here = pl.ds(g * GROUP, GROUP)
         for f in range(3):
-            at = pl.ds(f * members + g * GROUP, GROUP)
+            at = f * members + g * GROUP
+            base = half if at >= count else 0
+            at = pl.ds(at % count, GROUP)
             ceven, codd = ceven_ref[at, :], codd_ref[at, :]
             cab, cbe = jnp.where(odd_y, ceven, codd), jnp.where(odd_y, codd, ceven)
             depth = MARGIN if f == 2 else MARGIN - 1
             for d in range(depth):
                 r = MARGIN - depth + d
                 main = above_ref[f * (MARGIN - 1) + d, here, :]
-                state[g, f, r] = wide_row(lane, main, cab, MARGIN * r, cab, half + MARGIN * r)
+                state[g, f, r] = wide_row(lane, main, cab, base + MARGIN * r, cab, base + MARGIN * (MARGIN - 1 - r))
                 main = below_ref[f * (MARGIN - 1) + d, here, :]
-                state[g, f, MARGIN + rows + d] = wide_row(lane, main, cbe, MARGIN * d, cbe, half + MARGIN * d)
+                state[g, f, MARGIN + rows + d] = wide_row(
+                    lane, main, cbe, base + MARGIN * d, cbe, base + MARGIN * (MARGIN - 1 - d)
+                )
             for r in range(rows):
                 state[g, f, MARGIN + r] = inner_ref[f, r, here, :]
 
@@ -294,14 +304,23 @@
                 div = d[r - low] + (state[g, 2, r + 1] - state[g, 2, r - 1])
                 state[g, 0, r] = state[g, 0, r] + tall(slope[r]) * div
 
-    def flows(g, spans):
+    def flows(g, spans, final):
+        here = pl.ds(g * GROUP, GROUP)
         for low, high in spans:
             d = column_slope(state[g, 0, low:high], shift)
             for r in range(low, high):
                 u, v = state[g, 1, r], state[g, 2, r]
                 k, c = tall(keep[r]), tall(slope[r])
-                state[g, 1, r] = k * u + c * d[r - low] + 0.1 * v
-                state[g, 2, r] = k * v + c * (state[g, 0, r + 1] - state[g, 0, r - 1]) - 0.1 * u
+                u, v = (
+                    k * u + c * d[r - low] + 0.1 * v,
+                    k * v + c * (state[g, 0, r + 1] - state[g, 0, r - 1]) - 0.1 * u,
+                )
+                if final:
+                    for f, value in enumerate((state[g, 0, r], u, v)):
+                        out_ref[f * rows + r - MARGIN, here, :] = value[:, 0:cols]
+                else:
+                    state[g, 1, r] = u
+                    state[g, 2, r] = v
 
     for step in range(STEPS):
         first, last = MARGIN - MARGIN + 1 + 2 * step, MARGIN + rows + MARGIN - 1 - 2 * step
@@ -309,13 +328,7 @@
         for g in groups:
             heights(g, ((first, done), (still, last)))
         for g in groups:
-            flows(g, ((first + 1, done + 1), (still - 1, last - 1)))
-    for g in groups:
-        here = pl.ds(g * GROUP, GROUP)
-        for f in range(3):
-            for r in range(rows):
-                out_ref[f * rows + r, here, :] = state[g, f, MARGIN + r, :, 0:cols]
-
+            flows(g, ((first + 1, done + 1), (still - 1, last - 1)), step == STEPS - 1)
     prior_ref[...] = jnp.zeros_like(prior_ref)
     eight = lanes_of((8, cols))
     for i in range(order_ref.shape[0]):
@@ -412,10 +425,10 @@
         column = table[:, i : i + 1]
         power = row[:, i : i + 1]
         variance = power / (members - 1) + EPS
-        inverse = 1.0 / (variance + error)
+        root = lax.rsqrt(1.0 + variance * (1.0 / error))
         scaled = 1.0 / ((members - 1) * variance)
-        shift = variance * (value_ref[k] - mean[:, i : i + 1]) * inverse
-        shrink = jnp.sqrt(error * inverse) - 1.0
+        shift = variance * (value_ref[k] - mean[:, i : i + 1]) * (root * root * (1.0 / error))
+        shrink = root - 1.0
         weight = scaled * own[:, i : i + 1]
         alpha_row = onto_t[i : i + 1, :] * row * scaled
         later = lane1 > i

time: 64.2 us -> 62.8 us (0.978)
  waiting for transfers between devices: 22.4 us -> 21 us
    ppermute x4, waiting for transfers between devices: 12.6 us -> 11 us  [swap_pairs(): return lax.ppermute(x, axis, pairs + [(b, a) for a, b in pairs])]
where the time goes in v8:
time: 62.8 us; the launch traced here: 62.5 us
  Pallas kernels  23.7 us (38%)
  waiting for transfers between devices  21 us (33%)
  starting transfers between devices  17.3 us (28%)
    ppermute x4, waiting for transfers between devices, swap_pairs(): return lax.ppermute(x, axis, pairs + [(b, a) for a, b in pairs])  11 us
    ppermute x5, waiting for transfers between devices, add_over(): x = x + lax.ppermute(x, axis, [(i, i ^ span) for i in range(count)])  10 us
    ppermute x5, starting transfers between devices, add_over(): x = x + lax.ppermute(x, axis, [(i, i ^ span) for i in range(count)])  6.9 us
    pallas_call x1, Pallas kernels, forecast(): pl.pallas_call(functools.partial(forecast_kernel, members, rows), out_sha...  6.63 us
    pallas_call x1, Pallas kernels, assimilate(): pl.pallas_call(functools.partial(assimilate_kernel, members, rows), out_s...  6.01 us
    pallas_call x1, Pallas kernels, interior(): pl.pallas_call(functools.partial(interior_kernel, members, rows), out_sha...  5.45 us
    ppermute x1, starting transfers between devices, to_neighbours(): lax.ppermute(upper, axis, forward)  4.98 us
    ppermute x4, starting transfers between devices, swap_pairs(): return lax.ppermute(x, axis, pairs + [(b, a) for a, b in pairs])  4.1 us
  transfers between devices with their start and end apart: 11, of which 7 were waited for; matrix products, arithmetic and copies ran while one was open for 0% of the time, Pallas kernels for 13%

profile of v8, /device:TPU:0, one launch (start us, length us, event | category | flops | bytes accessed | tf_op | source)
XLA Modules:
  0.0 62.5 jit_solution(16891286069053444513)
XLA Ops:
  0.0 2.7 %shard_map.94 = (f32[22,80,128]{2,1,0:T(8,128)}, f32[22,80,128]{2,1,0:T(8,128)}) custom-call(f32[3840,128]{1,0:T(8,128)} %bitcast.7), custom_call_target="tpu_custom_call" | custom-call | flops 1000000 | bytes 4000000 | tf_op jit(solution)/shard_map/pallas_call | solution.py:67
  2.7 5.0 %collective-permute-start.2 = (f32[22,80,128]{2,1,0:T(8,128)}, f32[22,80,128]{2,1,0:T(8,128)S(1)}, u32[]{:S(2)}, u32[]{:S(2)}) collective-permute-start(f32[22,80,128]{2,1,0:T(8,128)} %get-tuple-element.21), channel_id=1, source_target_pairs={{0,1},{1,2},{2,3},{4,5},{5,6},{6,7},{8,9},{9,10},{10,11},{12,13},{... | collective-permute-start | bytes 2703368 | tf_op jit(solution)/shard_map/ppermute | solution.py:493
  7.7 1.3 %collective-permute-start.3 = (f32[22,80,128]{2,1,0:T(8,128)}, f32[22,80,128]{2,1,0:T(8,128)}, u32[]{:S(2)}, u32[]{:S(2)}) collective-permute-start(f32[22,80,128]{2,1,0:T(8,128)} %get-tuple-element.22), channel_id=1, source_target_pairs={{1,0},{2,1},{3,2},{5,4},{6,5},{7,6},{9,8},{10,9},{11,10},{13,12},{... | collective-permute-start | bytes 2703368 | tf_op jit(solution)/shard_map/ppermute | solution.py:493
  9.0 0.1 stack.39.place_ref
  9.1 2.2 %shard_map.91 = (f32[256,128]{1,0:T(8,128)S(1)}, f32[256,128]{1,0:T(8,128)S(1)}) custom-call(s32[6]{0:T(128)S(1)} %stack.39.place_ref, f32[3840,128]{1,0:T(8,128)S(1)} %bitcast.8, f32[16,128]{1,0:T(8,128)S(1)} %copy-done.1), custom_call_target="tpu_custom_call" | custom-call | flops 1000000 | bytes 4000000 | tf_op jit(solution)/shard_map/pallas_call | solution.py:105
  11.3 0.1 collective-permute-start
  11.4 0.7 %collective-permute-start.1 = (f32[256,128]{1,0:T(8,128)S(1)}, f32[256,128]{1,0:T(8,128)S(1)}, u32[]{:S(2)}, u32[]{:S(2)}) collective-permute-start(f32[256,128]{1,0:T(8,128)S(1)} %get-tuple-element.17), channel_id=1, source_target_pairs={{4,8},{12,16},{20,24},{8,4},{16,12},{24,20},{5,9},{13,17},{21,25},... | collective-permute-start | bytes 393224 | tf_op jit(solution)/shard_map/ppermute | solution.py:498
  12.0 0.7 %collective-permute-done.even_ref = f32[256,128]{1,0:T(8,128)S(1)} collective-permute-done((f32[256,128]{1,0:T(8,128)S(1)}, f32[256,128]{1,0:T(8,128)S(1)}, u32[]{:S(2)}, u32[]{:S(2)}) %collective-permute-start) | collective-permute-done | bytes 131104 | tf_op jit(solution)/shard_map/ppermute | solution.py:498
  12.7 0.8 %shard_map.92 = (f32[240,128]{1,0:T(8,128)S(1)}, f32[240,128]{1,0:T(8,128)S(1)}, f32[16,128]{1,0:T(8,128)S(1)}, f32[136,128]{1,0:T(8,128)S(1)}, f32[136,128]{1,0:T(8,128)S(1)}) custom-call(s32[6]{0:T(128)S(1)} %stack.39.place_ref, f32[16,128]{1,0:T(8,128)S(1)} %copy-done.1, f32[256,128]{1,0:T(8,128)S(1)} %collective-permute-done.even_ref, ...), custom_call_target="tpu_custom_call" | custom-call | tf_op jit(solution)/shard_map/pallas_call | solution.py:151
  13.5 2.7 %collective-permute-start.4 = (f32[136,128]{1,0:T(8,128)S(1)}, f32[136,128]{1,0:T(8,128)S(1)}, u32[]{:S(2)}, u32[]{:S(2)}) collective-permute-start(f32[136,128]{1,0:T(8,128)S(1)} %get-tuple-element.23), channel_id=1, source_target_pairs={{0,1},{2,3},{1,0},{3,2},{4,5},{6,7},{5,4},{7,6},{8,9},{10,11},{9,8... | collective-permute-start | bytes 208904 | tf_op jit(solution)/shard_map/ppermute | solution.py:498
  16.2 0.7 %collective-permute-start.5 = (f32[136,128]{1,0:T(8,128)S(1)}, f32[136,128]{1,0:T(8,128)S(1)}, u32[]{:S(2)}, u32[]{:S(2)}) collective-permute-start(f32[136,128]{1,0:T(8,128)S(1)} %get-tuple-element.24), channel_id=1, source_target_pairs={{1,2},{2,1},{5,6},{6,5},{9,10},{10,9},{13,14},{14,13},{17,18},{18,... | collective-permute-start | bytes 208904 | tf_op jit(solution)/shard_map/ppermute | solution.py:498
  16.9 5.5 %shard_map.93.inner_ref = f32[3,16,80,256]{3,2,1,0:T(8,128)S(1)} custom-call(s32[6]{0:T(128)S(1)} %stack.39.place_ref, f32[3840,128]{1,0:T(8,128)S(1)} %bitcast.9, f32[240,128]{1,0:T(8,128)S(1)} %get-tuple-element.18.left_ref, f32[240,128]{1,0:T(8,128)S(1)} %get-tuple-element.19.right_ref, f32[16,128]{1,0:T(8,128)S(1)} %copy-done.1, ...), custom_call_target="tpu_custom_call" | custom-call | flops 30000000 | bytes 10000000 | tf_op jit(solution)/shard_map/pallas_call | solution.py:242
  22.4 10.3 %collective-permute-done.4.ceven_ref = f32[136,128]{1,0:T(8,128)S(1)} collective-permute-done((f32[136,128]{1,0:T(8,128)S(1)}, f32[136,128]{1,0:T(8,128)S(1)}, u32[]{:S(2)}, u32[]{:S(2)}) %collective-permute-start.4) | collective-permute-done | bytes 69664 | tf_op jit(solution)/shard_map/ppermute | solution.py:498
  32.8 6.6 %shard_map.95 = (f32[48,80,128]{2,1,0:T(8,128)S(1)}, f32[24,128]{1,0:T(8,128)S(1)}) custom-call(s32[6]{0:T(128)S(1)} %stack.39.place_ref, s32[24]{0:T(128)S(1)} %copy-done.2, s32[24]{0:T(128)S(1)} %copy-done.3, s32[24]{0:T(128)S(1)} %copy-done.8, f32[3,16,80,256]{3,2,1,0:T(8,128)S(1)} %shard_map.93.inner_ref, ...), custom_call_target="tpu_custom_call" | custom-call | flops 60000000 | bytes 30000000 | tf_op jit(solution)/shard_map/pallas_call | solution.py:350
  39.5 1.2 %collective-permute-done.6 = f32[24,128]{1,0:T(8,128)S(1)} collective-permute-done((f32[24,128]{1,0:T(8,128)S(1)}, f32[24,128]{1,0:T(8,128)S(1)}, u32[]{:S(2)}, u32[]{:S(2)}) %collective-permute-start.6) | collective-permute-done | bytes 12320 | tf_op jit(solution)/shard_map/ppermute | solution.py:509
  40.6 1.4 %collective-permute-start.7 = (f32[24,128]{1,0:T(8,128)S(1)}, f32[24,128]{1,0:T(8,128)S(1)}, u32[]{:S(2)}, u32[]{:S(2)}) collective-permute-start(f32[24,128]{1,0:T(8,128)S(1)} %add.19), channel_id=1, source_target_pairs={{0,8},{4,12},{8,0},{12,4},{16,24},{20,28},{24,16},{28,20},{1,9},{5... | collective-permute-start | bytes 36872 | tf_op jit(solution)/shard_map/ppermute | solution.py:509
  42.0 2.3 %collective-permute-done.7 = f32[24,128]{1,0:T(8,128)S(1)} collective-permute-done((f32[24,128]{1,0:T(8,128)S(1)}, f32[24,128]{1,0:T(8,128)S(1)}, u32[]{:S(2)}, u32[]{:S(2)}) %collective-permute-start.7) | collective-permute-done | bytes 12320 | tf_op jit(solution)/shard_map/ppermute | solution.py:509
  44.3 1.5 %collective-permute-start.8 = (f32[24,128]{1,0:T(8,128)S(1)}, f32[24,128]{1,0:T(8,128)S(1)}, u32[]{:S(2)}, u32[]{:S(2)}) collective-permute-start(f32[24,128]{1,0:T(8,128)S(1)} %add.20), channel_id=1, source_target_pairs={{0,16},{4,20},{8,24},{12,28},{16,0},{20,4},{24,8},{28,12},{1,17},{... | collective-permute-start | bytes 36872 | tf_op jit(solution)/shard_map/ppermute | solution.py:509
  45.8 2.2 %collective-permute-done.8 = f32[24,128]{1,0:T(8,128)S(1)} collective-permute-done((f32[24,128]{1,0:T(8,128)S(1)}, f32[24,128]{1,0:T(8,128)S(1)}, u32[]{:S(2)}, u32[]{:S(2)}) %collective-permute-start.8) | collective-permute-done | bytes 12320 | tf_op jit(solution)/shard_map/ppermute | solution.py:509
  48.0 1.5 %collective-permute-start.9 = (f32[24,128]{1,0:T(8,128)S(1)}, f32[24,128]{1,0:T(8,128)S(1)}, u32[]{:S(2)}, u32[]{:S(2)}) collective-permute-start(f32[24,128]{1,0:T(8,128)S(1)} %add.21), channel_id=1, source_target_pairs={{0,1},{1,0},{2,3},{3,2},{4,5},{5,4},{6,7},{7,6},{8,9},{9,8},{10,11... | collective-permute-start | bytes 36872 | tf_op jit(solution)/shard_map/ppermute | solution.py:509
  49.5 2.2 %collective-permute-done.9 = f32[24,128]{1,0:T(8,128)S(1)} collective-permute-done((f32[24,128]{1,0:T(8,128)S(1)}, f32[24,128]{1,0:T(8,128)S(1)}, u32[]{:S(2)}, u32[]{:S(2)}) %collective-permute-start.9) | collective-permute-done | bytes 12320 | tf_op jit(solution)/shard_map/ppermute | solution.py:509
  51.7 2.5 %collective-permute-start.10 = (f32[24,128]{1,0:T(8,128)S(1)}, f32[24,128]{1,0:T(8,128)S(1)}, u32[]{:S(2)}, u32[]{:S(2)}) collective-permute-start(f32[24,128]{1,0:T(8,128)S(1)} %add.22), channel_id=1, source_target_pairs={{0,2},{1,3},{2,0},{3,1},{4,6},{5,7},{6,4},{7,5},{8,10},{9,11},{10,... | collective-permute-start | bytes 36872 | tf_op jit(solution)/shard_map/ppermute | solution.py:509
  54.2 2.1 %collective-permute-done.10 = f32[24,128]{1,0:T(8,128)S(1)} collective-permute-done((f32[24,128]{1,0:T(8,128)S(1)}, f32[24,128]{1,0:T(8,128)S(1)}, u32[]{:S(2)}, u32[]{:S(2)}) %collective-permute-start.10) | collective-permute-done | bytes 12320 | tf_op jit(solution)/shard_map/ppermute | solution.py:509
  56.4 6.0 %shard_map.96 = f32[3840,128]{1,0:T(8,128)} custom-call(s32[6]{0:T(128)S(1)} %stack.39.place_ref, s32[24]{0:T(128)S(1)} %copy-done.2, s32[24]{0:T(128)S(1)} %copy-done.3, s32[24]{0:T(128)S(1)} %copy-done.4, f32[24]{0:T(128)S(1)} %copy-done.5, f32[24]{0:T(128)S(1)} %copy-done.6, f32[7]{0:T(128)S(1)} %copy-done.7, f32[24,128]{1,0:T(8,128)S(1)} %add.23.prior_ref, ...), custom_call_target="tpu_custom_call" | custom-call | tf_op jit(solution)/shard_map/pallas_call | solution.py:479
  (28 shorter events, 0.2 us)
Async XLA Ops:
  0.0 9.1 %copy-start = (f32[3,80,16,128]{3,2,1,0:T(8,128)S(1)}, f32[3,80,16,128]{3,2,1,0:T(8,128)}, u32[]{:S(2)}) copy-start(f32[3,80,16,128]{3,2,1,0:T(8,128)} %param.9) | copy-start | bytes 5898244
  0.0 9.1 %copy-start.1 = (f32[16,128]{1,0:T(8,128)S(1)}, f32[16,128]{1,0:T(8,128)}, u32[]{:S(2)}) copy-start(f32[16,128]{1,0:T(8,128)} %drag_ref.7) | copy-start | bytes 24580
  2.7 30.1 %collective-permute-start.2 = (f32[22,80,128]{2,1,0:T(8,128)}, f32[22,80,128]{2,1,0:T(8,128)S(1)}, u32[]{:S(2)}, u32[]{:S(2)}) collective-permute-start(f32[22,80,128]{2,1,0:T(8,128)} %get-tuple-element.21), channel_id=1, source_target_pairs={{0,1},{1,2},{2,3},{4,5},{5,6},{6,7},{8,9},{9,10},{10,11},{12,13},{... | collective-permute-start | bytes 2703368 | tf_op jit(solution)/shard_map/ppermute | solution.py:493
  7.7 25.1 %collective-permute-start.3 = (f32[22,80,128]{2,1,0:T(8,128)}, f32[22,80,128]{2,1,0:T(8,128)}, u32[]{:S(2)}, u32[]{:S(2)}) collective-permute-start(f32[22,80,128]{2,1,0:T(8,128)} %get-tuple-element.22), channel_id=1, source_target_pairs={{1,0},{2,1},{3,2},{5,4},{6,5},{7,6},{9,8},{10,9},{11,10},{13,12},{... | collective-permute-start | bytes 2703368 | tf_op jit(solution)/shard_map/ppermute | solution.py:493
  11.3 1.4 %collective-permute-start = (f32[256,128]{1,0:T(8,128)S(1)}, f32[256,128]{1,0:T(8,128)S(1)}, u32[]{:S(2)}, u32[]{:S(2)}) collective-permute-start(f32[256,128]{1,0:T(8,128)S(1)} %get-tuple-element.16), channel_id=1, source_target_pairs={{0,4},{8,12},{16,20},{24,28},{4,0},{12,8},{20,16},{28,24},{1,5},{9... | collective-permute-start | bytes 393224 | tf_op jit(solution)/shard_map/ppermute | solution.py:498
  11.4 1.3 %collective-permute-start.1 = (f32[256,128]{1,0:T(8,128)S(1)}, f32[256,128]{1,0:T(8,128)S(1)}, u32[]{:S(2)}, u32[]{:S(2)}) collective-permute-start(f32[256,128]{1,0:T(8,128)S(1)} %get-tuple-element.17), channel_id=1, source_target_pairs={{4,8},{12,16},{20,24},{8,4},{16,12},{24,20},{5,9},{13,17},{21,25},... | collective-permute-start | bytes 393224 | tf_op jit(solution)/shard_map/ppermute | solution.py:498
  13.5 19.3 %collective-permute-start.4 = (f32[136,128]{1,0:T(8,128)S(1)}, f32[136,128]{1,0:T(8,128)S(1)}, u32[]{:S(2)}, u32[]{:S(2)}) collective-permute-start(f32[136,128]{1,0:T(8,128)S(1)} %get-tuple-element.23), channel_id=1, source_target_pairs={{0,1},{2,3},{1,0},{3,2},{4,5},{6,7},{5,4},{7,6},{8,9},{10,11},{9,8... | collective-permute-start | bytes 208904 | tf_op jit(solution)/shard_map/ppermute | solution.py:498
  16.2 16.6 %collective-permute-start.5 = (f32[136,128]{1,0:T(8,128)S(1)}, f32[136,128]{1,0:T(8,128)S(1)}, u32[]{:S(2)}, u32[]{:S(2)}) collective-permute-start(f32[136,128]{1,0:T(8,128)S(1)} %get-tuple-element.24), channel_id=1, source_target_pairs={{1,2},{2,1},{5,6},{6,5},{9,10},{10,9},{13,14},{14,13},{17,18},{18,... | collective-permute-start | bytes 208904 | tf_op jit(solution)/shard_map/ppermute | solution.py:498
  16.8 15.9 %copy-start.2 = (s32[24]{0:T(128)S(1)}, s32[24]{0:T(128)}, u32[]{:S(2)}) copy-start(s32[24]{0:T(128)} %order_ref.3) | copy-start | bytes 292
  16.8 15.9 %copy-start.3 = (s32[24]{0:T(128)S(1)}, s32[24]{0:T(128)}, u32[]{:S(2)}) copy-start(s32[24]{0:T(128)} %owner_ref.3) | copy-start | bytes 292
  16.8 15.9 %copy-start.8 = (s32[24]{0:T(128)S(1)}, s32[24]{0:T(128)}, u32[]{:S(2)}) copy-start(s32[24]{0:T(128)} %cell_ref.1) | copy-start | bytes 292
  22.3 34.0 %copy-start.4 = (s32[24]{0:T(128)S(1)}, s32[24]{0:T(128)}, u32[]{:S(2)}) copy-start(s32[24]{0:T(128)} %reach_ref.1) | copy-start | bytes 292
  22.3 34.0 %copy-start.5 = (f32[24]{0:T(128)S(1)}, f32[24]{0:T(128)}, u32[]{:S(2)}) copy-start(f32[24]{0:T(128)} %value_ref.1) | copy-start | bytes 292
  22.3 34.0 %copy-start.6 = (f32[24]{0:T(128)S(1)}, f32[24]{0:T(128)}, u32[]{:S(2)}) copy-start(f32[24]{0:T(128)} %error_ref.1) | copy-start | bytes 292
  22.4 34.0 %copy-start.7 = (f32[7]{0:T(128)S(1)}, f32[7]{0:T(128)}, u32[]{:S(2)}) copy-start(f32[7]{0:T(128)} %taper_ref.1) | copy-start | bytes 88
  39.4 1.2 %collective-permute-start.6 = (f32[24,128]{1,0:T(8,128)S(1)}, f32[24,128]{1,0:T(8,128)S(1)}, u32[]{:S(2)}, u32[]{:S(2)}) collective-permute-start(f32[24,128]{1,0:T(8,128)S(1)} %get-tuple-element.25), channel_id=1, source_target_pairs={{0,4},{4,0},{8,12},{12,8},{16,20},{20,16},{24,28},{28,24},{1,5},{5... | collective-permute-start | bytes 36872 | tf_op jit(solution)/shard_map/ppermute | solution.py:509
  40.6 3.7 %collective-permute-start.7 = (f32[24,128]{1,0:T(8,128)S(1)}, f32[24,128]{1,0:T(8,128)S(1)}, u32[]{:S(2)}, u32[]{:S(2)}) collective-permute-start(f32[24,128]{1,0:T(8,128)S(1)} %add.19), channel_id=1, source_target_pairs={{0,8},{4,12},{8,0},{12,4},{16,24},{20,28},{24,16},{28,20},{1,9},{5... | collective-permute-start | bytes 36872 | tf_op jit(solution)/shard_map/ppermute | solution.py:509
  44.3 3.7 %collective-permute-start.8 = (f32[24,128]{1,0:T(8,128)S(1)}, f32[24,128]{1,0:T(8,128)S(1)}, u32[]{:S(2)}, u32[]{:S(2)}) collective-permute-start(f32[24,128]{1,0:T(8,128)S(1)} %add.20), channel_id=1, source_target_pairs={{0,16},{4,20},{8,24},{12,28},{16,0},{20,4},{24,8},{28,12},{1,17},{... | collective-permute-start | bytes 36872 | tf_op jit(solution)/shard_map/ppermute | solution.py:509
  48.0 3.7 %collective-permute-start.9 = (f32[24,128]{1,0:T(8,128)S(1)}, f32[24,128]{1,0:T(8,128)S(1)}, u32[]{:S(2)}, u32[]{:S(2)}) collective-permute-start(f32[24,128]{1,0:T(8,128)S(1)} %add.21), channel_id=1, source_target_pairs={{0,1},{1,0},{2,3},{3,2},{4,5},{5,4},{6,7},{7,6},{8,9},{9,8},{10,11... | collective-permute-start | bytes 36872 | tf_op jit(solution)/shard_map/ppermute | solution.py:509
  51.7 4.6 %collective-permute-start.10 = (f32[24,128]{1,0:T(8,128)S(1)}, f32[24,128]{1,0:T(8,128)S(1)}, u32[]{:S(2)}, u32[]{:S(2)}) collective-permute-start(f32[24,128]{1,0:T(8,128)S(1)} %add.22), channel_id=1, source_target_pairs={{0,2},{1,3},{2,0},{3,1},{4,6},{5,7},{6,4},{7,5},{8,10},{9,11},{10,... | collective-permute-start | bytes 36872 | tf_op jit(solution)/shard_map/ppermute | solution.py:509

commit v9 on v8

--- a/solution.py
+++ b/solution.py
@@ -409,34 +409,39 @@
     mean_col = jnp.sum(jnp.where(inside, priors, 0.0), axis=1, keepdims=True) / members
     anomalies = jnp.where(inside, priors - mean_col, 0.0)
     padded = jnp.concatenate([anomalies, jnp.zeros((cols - n_obs, cols), F32)], axis=0)
-    unit = jnp.where(lanes_of((members, cols)) == sublanes_of((members, cols)), 1.0, 0.0)
-    table = lax.dot_general(
-        jnp.concatenate([anomalies, unit], axis=0), padded, NT, precision=HIGHEST, preferred_element_type=F32
-    )
+    table = lax.dot_general(anomalies, padded, NT, precision=HIGHEST, preferred_element_type=F32)
+    table = jnp.concatenate([table, jnp.transpose(padded)[:members]], axis=0)
     mean = jnp.zeros((1, cols), F32)
     for i in range(n_obs):
         mean = jnp.where(lane1 == i, mean_col[i : i + 1, :], mean)
 
     scales = jnp.zeros((1, cols), F32)
     increments = []
+    power = jnp.broadcast_to(table[0:1, 0:1], (1, cols))
     for i, k in enumerate(which):
         error = error_ref[k]
         row = table[i : i + 1, :]
-        column = table[:, i : i + 1]
-        power = row[:, i : i + 1]
+        column = jnp.broadcast_to(table[:, i : i + 1], table.shape)
         variance = power / (members - 1) + EPS
         root = lax.rsqrt(1.0 + variance * (1.0 / error))
         scaled = 1.0 / ((members - 1) * variance)
-        shift = variance * (value_ref[k] - mean[:, i : i + 1]) * (root * root * (1.0 / error))
+        shift = variance * (value_ref[k] - jnp.broadcast_to(mean[:, i : i + 1], row.shape)) * (root * root * (1.0 / error))
         shrink = root - 1.0
-        weight = scaled * own[:, i : i + 1]
+        weight = scaled * jnp.broadcast_to(own[:, i : i + 1], row.shape)
         alpha_row = onto_t[i : i + 1, :] * row * scaled
         later = lane1 > i
         h = jnp.where(later, shrink * alpha_row, 0.0)
         q = jnp.where(later, shrink * (row + h * power), 0.0)
         alpha = jnp.concatenate(
-            [onto[:, i : i + 1] * column[:n_obs] * scaled, column[n_obs:] * weight], axis=0
+            [jnp.broadcast_to(onto[:, i : i + 1], onto.shape) * column[:n_obs] * scaled, column[n_obs:] * weight], axis=0
         )
+        if i + 1 < n_obs:
+            beside, ahead, reach_on = (
+                jnp.broadcast_to(x[:, i + 1 : i + 2], row.shape)
+                for x in (row, table[i + 1 : i + 2, :], onto_t[i : i + 1, :])
+            )
+            step = reach_on * beside * scaled
+            power = ahead + beside * (shrink * step) + step * (shrink * (beside + shrink * step * power))
         table = table + column * h + alpha * q
         mean = mean + alpha_row * shift
         now = anomalies[i : i + 1, :]

time: 62.8 us -> 61.8 us (0.984)
  Pallas kernels: 23.7 us -> 22.7 us
    pallas_call x1, Pallas kernels: 6.01 us -> 5.07 us  [assimilate(): pl.pallas_call(functools.partial(assimilate_kernel, members, rows), out_s...]
  transfers between devices with their start and end apart: 11 -> 11, of which waited for: 7 -> 7; matrix products, arithmetic and copies ran while one was open for 0% -> 0% of each run, Pallas kernels for 13% -> 14%
where the time goes in v9:
time: 61.8 us; the launch traced here: 61.6 us
  Pallas kernels  22.7 us (37%)
  waiting for transfers between devices  20.7 us (33%)
  starting transfers between devices  17.6 us (28%)
    ppermute x4, waiting for transfers between devices, swap_pairs(): return lax.ppermute(x, axis, pairs + [(b, a) for a, b in pairs])  11 us
    ppermute x5, waiting for transfers between devices, add_over(): x = x + lax.ppermute(x, axis, [(i, i ^ span) for i in range(count)])  9.65 us
    ppermute x5, starting transfers between devices, add_over(): x = x + lax.ppermute(x, axis, [(i, i ^ span) for i in range(count)])  7.26 us
    pallas_call x1, Pallas kernels, forecast(): pl.pallas_call(functools.partial(forecast_kernel, members, rows), out_sha...  6.59 us
    pallas_call x1, Pallas kernels, interior(): pl.pallas_call(functools.partial(interior_kernel, members, rows), out_sha...  5.45 us
    pallas_call x1, Pallas kernels, assimilate(): pl.pallas_call(functools.partial(assimilate_kernel, members, rows), out_s...  5.07 us
    ppermute x1, starting transfers between devices, to_neighbours(): lax.ppermute(upper, axis, forward)  4.98 us
    ppermute x4, starting transfers between devices, swap_pairs(): return lax.ppermute(x, axis, pairs + [(b, a) for a, b in pairs])  4.1 us
  transfers between devices with their start and end apart: 11, of which 7 were waited for; matrix products, arithmetic and copies ran while one was open for 0% of the time, Pallas kernels for 14%

profile of v9, /device:TPU:0, one launch (start us, length us, event | category | flops | bytes accessed | tf_op | source)
XLA Modules:
  0.0 61.6 jit_solution(610998289854473322)
XLA Ops:
  0.0 2.7 %shard_map.94 = (f32[22,80,128]{2,1,0:T(8,128)}, f32[22,80,128]{2,1,0:T(8,128)}) custom-call(f32[3840,128]{1,0:T(8,128)} %bitcast.7), custom_call_target="tpu_custom_call" | custom-call | flops 1000000 | bytes 4000000 | tf_op jit(solution)/shard_map/pallas_call | solution.py:67
  2.7 5.0 %collective-permute-start.2 = (f32[22,80,128]{2,1,0:T(8,128)}, f32[22,80,128]{2,1,0:T(8,128)S(1)}, u32[]{:S(2)}, u32[]{:S(2)}) collective-permute-start(f32[22,80,128]{2,1,0:T(8,128)} %get-tuple-element.21), channel_id=1, source_target_pairs={{0,1},{1,2},{2,3},{4,5},{5,6},{6,7},{8,9},{9,10},{10,11},{12,13},{... | collective-permute-start | bytes 2703368 | tf_op jit(solution)/shard_map/ppermute | solution.py:498
  7.7 1.3 %collective-permute-start.3 = (f32[22,80,128]{2,1,0:T(8,128)}, f32[22,80,128]{2,1,0:T(8,128)}, u32[]{:S(2)}, u32[]{:S(2)}) collective-permute-start(f32[22,80,128]{2,1,0:T(8,128)} %get-tuple-element.22), channel_id=1, source_target_pairs={{1,0},{2,1},{3,2},{5,4},{6,5},{7,6},{9,8},{10,9},{11,10},{13,12},{... | collective-permute-start | bytes 2703368 | tf_op jit(solution)/shard_map/ppermute | solution.py:498
  9.0 0.1 stack.39.place_ref
  9.1 2.2 %shard_map.91 = (f32[256,128]{1,0:T(8,128)S(1)}, f32[256,128]{1,0:T(8,128)S(1)}) custom-call(s32[6]{0:T(128)S(1)} %stack.39.place_ref, f32[3840,128]{1,0:T(8,128)S(1)} %bitcast.8, f32[16,128]{1,0:T(8,128)S(1)} %copy-done.1), custom_call_target="tpu_custom_call" | custom-call | flops 1000000 | bytes 4000000 | tf_op jit(solution)/shard_map/pallas_call | solution.py:105
  11.3 0.1 collective-permute-start
  11.4 0.7 %collective-permute-start.1 = (f32[256,128]{1,0:T(8,128)S(1)}, f32[256,128]{1,0:T(8,128)S(1)}, u32[]{:S(2)}, u32[]{:S(2)}) collective-permute-start(f32[256,128]{1,0:T(8,128)S(1)} %get-tuple-element.17), channel_id=1, source_target_pairs={{4,8},{12,16},{20,24},{8,4},{16,12},{24,20},{5,9},{13,17},{21,25},... | collective-permute-start | bytes 393224 | tf_op jit(solution)/shard_map/ppermute | solution.py:503
  12.0 0.7 %collective-permute-done.even_ref = f32[256,128]{1,0:T(8,128)S(1)} collective-permute-done((f32[256,128]{1,0:T(8,128)S(1)}, f32[256,128]{1,0:T(8,128)S(1)}, u32[]{:S(2)}, u32[]{:S(2)}) %collective-permute-start) | collective-permute-done | bytes 131104 | tf_op jit(solution)/shard_map/ppermute | solution.py:503
  12.7 0.8 %shard_map.92 = (f32[240,128]{1,0:T(8,128)S(1)}, f32[240,128]{1,0:T(8,128)S(1)}, f32[16,128]{1,0:T(8,128)S(1)}, f32[136,128]{1,0:T(8,128)S(1)}, f32[136,128]{1,0:T(8,128)S(1)}) custom-call(s32[6]{0:T(128)S(1)} %stack.39.place_ref, f32[16,128]{1,0:T(8,128)S(1)} %copy-done.1, f32[256,128]{1,0:T(8,128)S(1)} %collective-permute-done.even_ref, ...), custom_call_target="tpu_custom_call" | custom-call | tf_op jit(solution)/shard_map/pallas_call | solution.py:151
  13.5 2.7 %collective-permute-start.4 = (f32[136,128]{1,0:T(8,128)S(1)}, f32[136,128]{1,0:T(8,128)S(1)}, u32[]{:S(2)}, u32[]{:S(2)}) collective-permute-start(f32[136,128]{1,0:T(8,128)S(1)} %get-tuple-element.23), channel_id=1, source_target_pairs={{0,1},{2,3},{1,0},{3,2},{4,5},{6,7},{5,4},{7,6},{8,9},{10,11},{9,8... | collective-permute-start | bytes 208904 | tf_op jit(solution)/shard_map/ppermute | solution.py:503
  16.2 0.7 %collective-permute-start.5 = (f32[136,128]{1,0:T(8,128)S(1)}, f32[136,128]{1,0:T(8,128)S(1)}, u32[]{:S(2)}, u32[]{:S(2)}) collective-permute-start(f32[136,128]{1,0:T(8,128)S(1)} %get-tuple-element.24), channel_id=1, source_target_pairs={{1,2},{2,1},{5,6},{6,5},{9,10},{10,9},{13,14},{14,13},{17,18},{18,... | collective-permute-start | bytes 208904 | tf_op jit(solution)/shard_map/ppermute | solution.py:503
  16.9 5.5 %shard_map.93.inner_ref = f32[3,16,80,256]{3,2,1,0:T(8,128)S(1)} custom-call(s32[6]{0:T(128)S(1)} %stack.39.place_ref, f32[3840,128]{1,0:T(8,128)S(1)} %bitcast.9, f32[240,128]{1,0:T(8,128)S(1)} %get-tuple-element.18.left_ref, f32[240,128]{1,0:T(8,128)S(1)} %get-tuple-element.19.right_ref, f32[16,128]{1,0:T(8,128)S(1)} %copy-done.1, ...), custom_call_target="tpu_custom_call" | custom-call | flops 30000000 | bytes 10000000 | tf_op jit(solution)/shard_map/pallas_call | solution.py:242
  22.4 10.3 %collective-permute-done.4.ceven_ref = f32[136,128]{1,0:T(8,128)S(1)} collective-permute-done((f32[136,128]{1,0:T(8,128)S(1)}, f32[136,128]{1,0:T(8,128)S(1)}, u32[]{:S(2)}, u32[]{:S(2)}) %collective-permute-start.4) | collective-permute-done | bytes 69664 | tf_op jit(solution)/shard_map/ppermute | solution.py:503
  32.8 6.6 %shard_map.95 = (f32[48,80,128]{2,1,0:T(8,128)S(1)}, f32[24,128]{1,0:T(8,128)S(1)}) custom-call(s32[6]{0:T(128)S(1)} %stack.39.place_ref, s32[24]{0:T(128)S(1)} %copy-done.2, s32[24]{0:T(128)S(1)} %copy-done.3, s32[24]{0:T(128)S(1)} %copy-done.8, f32[3,16,80,256]{3,2,1,0:T(8,128)S(1)} %shard_map.93.inner_ref, ...), custom_call_target="tpu_custom_call" | custom-call | flops 60000000 | bytes 30000000 | tf_op jit(solution)/shard_map/pallas_call | solution.py:350
  39.4 1.2 %collective-permute-done.6 = f32[24,128]{1,0:T(8,128)S(1)} collective-permute-done((f32[24,128]{1,0:T(8,128)S(1)}, f32[24,128]{1,0:T(8,128)S(1)}, u32[]{:S(2)}, u32[]{:S(2)}) %collective-permute-start.6) | collective-permute-done | bytes 12320 | tf_op jit(solution)/shard_map/ppermute | solution.py:514
  40.6 1.5 %collective-permute-start.7 = (f32[24,128]{1,0:T(8,128)S(1)}, f32[24,128]{1,0:T(8,128)S(1)}, u32[]{:S(2)}, u32[]{:S(2)}) collective-permute-start(f32[24,128]{1,0:T(8,128)S(1)} %add.19), channel_id=1, source_target_pairs={{0,8},{4,12},{8,0},{12,4},{16,24},{20,28},{24,16},{28,20},{1,9},{5... | collective-permute-start | bytes 36872 | tf_op jit(solution)/shard_map/ppermute | solution.py:514
  42.1 2.2 %collective-permute-done.7 = f32[24,128]{1,0:T(8,128)S(1)} collective-permute-done((f32[24,128]{1,0:T(8,128)S(1)}, f32[24,128]{1,0:T(8,128)S(1)}, u32[]{:S(2)}, u32[]{:S(2)}) %collective-permute-start.7) | collective-permute-done | bytes 12320 | tf_op jit(solution)/shard_map/ppermute | solution.py:514
  44.3 1.5 %collective-permute-start.8 = (f32[24,128]{1,0:T(8,128)S(1)}, f32[24,128]{1,0:T(8,128)S(1)}, u32[]{:S(2)}, u32[]{:S(2)}) collective-permute-start(f32[24,128]{1,0:T(8,128)S(1)} %add.20), channel_id=1, source_target_pairs={{0,16},{4,20},{8,24},{12,28},{16,0},{20,4},{24,8},{28,12},{1,17},{... | collective-permute-start | bytes 36872 | tf_op jit(solution)/shard_map/ppermute | solution.py:514
  45.8 2.2 %collective-permute-done.8 = f32[24,128]{1,0:T(8,128)S(1)} collective-permute-done((f32[24,128]{1,0:T(8,128)S(1)}, f32[24,128]{1,0:T(8,128)S(1)}, u32[]{:S(2)}, u32[]{:S(2)}) %collective-permute-start.8) | collective-permute-done | bytes 12320 | tf_op jit(solution)/shard_map/ppermute | solution.py:514
  48.0 1.6 %collective-permute-start.9 = (f32[24,128]{1,0:T(8,128)S(1)}, f32[24,128]{1,0:T(8,128)S(1)}, u32[]{:S(2)}, u32[]{:S(2)}) collective-permute-start(f32[24,128]{1,0:T(8,128)S(1)} %add.21), channel_id=1, source_target_pairs={{0,1},{1,0},{2,3},{3,2},{4,5},{5,4},{6,7},{7,6},{8,9},{9,8},{10,11... | collective-permute-start | bytes 36872 | tf_op jit(solution)/shard_map/ppermute | solution.py:514
  49.7 2.0 %collective-permute-done.9 = f32[24,128]{1,0:T(8,128)S(1)} collective-permute-done((f32[24,128]{1,0:T(8,128)S(1)}, f32[24,128]{1,0:T(8,128)S(1)}, u32[]{:S(2)}, u32[]{:S(2)}) %collective-permute-start.9) | collective-permute-done | bytes 12320 | tf_op jit(solution)/shard_map/ppermute | solution.py:514
  51.7 2.5 %collective-permute-start.10 = (f32[24,128]{1,0:T(8,128)S(1)}, f32[24,128]{1,0:T(8,128)S(1)}, u32[]{:S(2)}, u32[]{:S(2)}) collective-permute-start(f32[24,128]{1,0:T(8,128)S(1)} %add.22), channel_id=1, source_target_pairs={{0,2},{1,3},{2,0},{3,1},{4,6},{5,7},{6,4},{7,5},{8,10},{9,11},{10,... | collective-permute-start | bytes 36872 | tf_op jit(solution)/shard_map/ppermute | solution.py:514
  54.2 2.1 %collective-permute-done.10 = f32[24,128]{1,0:T(8,128)S(1)} collective-permute-done((f32[24,128]{1,0:T(8,128)S(1)}, f32[24,128]{1,0:T(8,128)S(1)}, u32[]{:S(2)}, u32[]{:S(2)}) %collective-permute-start.10) | collective-permute-done | bytes 12320 | tf_op jit(solution)/shard_map/ppermute | solution.py:514
  56.3 5.1 %shard_map.96 = f32[3840,128]{1,0:T(8,128)} custom-call(s32[6]{0:T(128)S(1)} %stack.39.place_ref, s32[24]{0:T(128)S(1)} %copy-done.2, s32[24]{0:T(128)S(1)} %copy-done.3, s32[24]{0:T(128)S(1)} %copy-done.4, f32[24]{0:T(128)S(1)} %copy-done.5, f32[24]{0:T(128)S(1)} %copy-done.6, f32[7]{0:T(128)S(1)} %copy-done.7, f32[24,128]{1,0:T(8,128)S(1)} %add.23.prior_ref, ...), custom_call_target="tpu_custom_call" | custom-call | tf_op jit(solution)/shard_map/pallas_call | solution.py:484
  (28 shorter events, 0.2 us)
Async XLA Ops:
  0.0 9.1 %copy-start = (f32[3,80,16,128]{3,2,1,0:T(8,128)S(1)}, f32[3,80,16,128]{3,2,1,0:T(8,128)}, u32[]{:S(2)}) copy-start(f32[3,80,16,128]{3,2,1,0:T(8,128)} %param.9) | copy-start | bytes 5898244
  0.0 9.1 %copy-start.1 = (f32[16,128]{1,0:T(8,128)S(1)}, f32[16,128]{1,0:T(8,128)}, u32[]{:S(2)}) copy-start(f32[16,128]{1,0:T(8,128)} %drag_ref.7) | copy-start | bytes 24580
  2.7 30.1 %collective-permute-start.2 = (f32[22,80,128]{2,1,0:T(8,128)}, f32[22,80,128]{2,1,0:T(8,128)S(1)}, u32[]{:S(2)}, u32[]{:S(2)}) collective-permute-start(f32[22,80,128]{2,1,0:T(8,128)} %get-tuple-element.21), channel_id=1, source_target_pairs={{0,1},{1,2},{2,3},{4,5},{5,6},{6,7},{8,9},{9,10},{10,11},{12,13},{... | collective-permute-start | bytes 2703368 | tf_op jit(solution)/shard_map/ppermute | solution.py:498
  7.7 25.1 %collective-permute-start.3 = (f32[22,80,128]{2,1,0:T(8,128)}, f32[22,80,128]{2,1,0:T(8,128)}, u32[]{:S(2)}, u32[]{:S(2)}) collective-permute-start(f32[22,80,128]{2,1,0:T(8,128)} %get-tuple-element.22), channel_id=1, source_target_pairs={{1,0},{2,1},{3,2},{5,4},{6,5},{7,6},{9,8},{10,9},{11,10},{13,12},{... | collective-permute-start | bytes 2703368 | tf_op jit(solution)/shard_map/ppermute | solution.py:498
  11.3 1.4 %collective-permute-start = (f32[256,128]{1,0:T(8,128)S(1)}, f32[256,128]{1,0:T(8,128)S(1)}, u32[]{:S(2)}, u32[]{:S(2)}) collective-permute-start(f32[256,128]{1,0:T(8,128)S(1)} %get-tuple-element.16), channel_id=1, source_target_pairs={{0,4},{8,12},{16,20},{24,28},{4,0},{12,8},{20,16},{28,24},{1,5},{9... | collective-permute-start | bytes 393224 | tf_op jit(solution)/shard_map/ppermute | solution.py:503
  11.4 1.3 %collective-permute-start.1 = (f32[256,128]{1,0:T(8,128)S(1)}, f32[256,128]{1,0:T(8,128)S(1)}, u32[]{:S(2)}, u32[]{:S(2)}) collective-permute-start(f32[256,128]{1,0:T(8,128)S(1)} %get-tuple-element.17), channel_id=1, source_target_pairs={{4,8},{12,16},{20,24},{8,4},{16,12},{24,20},{5,9},{13,17},{21,25},... | collective-permute-start | bytes 393224 | tf_op jit(solution)/shard_map/ppermute | solution.py:503
  13.5 19.3 %collective-permute-start.4 = (f32[136,128]{1,0:T(8,128)S(1)}, f32[136,128]{1,0:T(8,128)S(1)}, u32[]{:S(2)}, u32[]{:S(2)}) collective-permute-start(f32[136,128]{1,0:T(8,128)S(1)} %get-tuple-element.23), channel_id=1, source_target_pairs={{0,1},{2,3},{1,0},{3,2},{4,5},{6,7},{5,4},{7,6},{8,9},{10,11},{9,8... | collective-permute-start | bytes 208904 | tf_op jit(solution)/shard_map/ppermute | solution.py:503
  16.2 16.6 %collective-permute-start.5 = (f32[136,128]{1,0:T(8,128)S(1)}, f32[136,128]{1,0:T(8,128)S(1)}, u32[]{:S(2)}, u32[]{:S(2)}) collective-permute-start(f32[136,128]{1,0:T(8,128)S(1)} %get-tuple-element.24), channel_id=1, source_target_pairs={{1,2},{2,1},{5,6},{6,5},{9,10},{10,9},{13,14},{14,13},{17,18},{18,... | collective-permute-start | bytes 208904 | tf_op jit(solution)/shard_map/ppermute | solution.py:503
  16.8 15.9 %copy-start.2 = (s32[24]{0:T(128)S(1)}, s32[24]{0:T(128)}, u32[]{:S(2)}) copy-start(s32[24]{0:T(128)} %order_ref.3) | copy-start | bytes 292
  16.8 15.9 %copy-start.3 = (s32[24]{0:T(128)S(1)}, s32[24]{0:T(128)}, u32[]{:S(2)}) copy-start(s32[24]{0:T(128)} %owner_ref.3) | copy-start | bytes 292
  16.8 15.9 %copy-start.8 = (s32[24]{0:T(128)S(1)}, s32[24]{0:T(128)}, u32[]{:S(2)}) copy-start(s32[24]{0:T(128)} %cell_ref.1) | copy-start | bytes 292
  22.3 34.0 %copy-start.4 = (s32[24]{0:T(128)S(1)}, s32[24]{0:T(128)}, u32[]{:S(2)}) copy-start(s32[24]{0:T(128)} %reach_ref.1) | copy-start | bytes 292
  22.3 34.0 %copy-start.5 = (f32[24]{0:T(128)S(1)}, f32[24]{0:T(128)}, u32[]{:S(2)}) copy-start(f32[24]{0:T(128)} %value_ref.1) | copy-start | bytes 292
  22.3 34.0 %copy-start.6 = (f32[24]{0:T(128)S(1)}, f32[24]{0:T(128)}, u32[]{:S(2)}) copy-start(f32[24]{0:T(128)} %error_ref.1) | copy-start | bytes 292
  22.4 34.0 %copy-start.7 = (f32[7]{0:T(128)S(1)}, f32[7]{0:T(128)}, u32[]{:S(2)}) copy-start(f32[7]{0:T(128)} %taper_ref.1) | copy-start | bytes 88
  39.4 1.2 %collective-permute-start.6 = (f32[24,128]{1,0:T(8,128)S(1)}, f32[24,128]{1,0:T(8,128)S(1)}, u32[]{:S(2)}, u32[]{:S(2)}) collective-permute-start(f32[24,128]{1,0:T(8,128)S(1)} %get-tuple-element.25), channel_id=1, source_target_pairs={{0,4},{4,0},{8,12},{12,8},{16,20},{20,16},{24,28},{28,24},{1,5},{5... | collective-permute-start | bytes 36872 | tf_op jit(solution)/shard_map/ppermute | solution.py:514
  40.6 3.7 %collective-permute-start.7 = (f32[24,128]{1,0:T(8,128)S(1)}, f32[24,128]{1,0:T(8,128)S(1)}, u32[]{:S(2)}, u32[]{:S(2)}) collective-permute-start(f32[24,128]{1,0:T(8,128)S(1)} %add.19), channel_id=1, source_target_pairs={{0,8},{4,12},{8,0},{12,4},{16,24},{20,28},{24,16},{28,20},{1,9},{5... | collective-permute-start | bytes 36872 | tf_op jit(solution)/shard_map/ppermute | solution.py:514
  44.3 3.7 %collective-permute-start.8 = (f32[24,128]{1,0:T(8,128)S(1)}, f32[24,128]{1,0:T(8,128)S(1)}, u32[]{:S(2)}, u32[]{:S(2)}) collective-permute-start(f32[24,128]{1,0:T(8,128)S(1)} %add.20), channel_id=1, source_target_pairs={{0,16},{4,20},{8,24},{12,28},{16,0},{20,4},{24,8},{28,12},{1,17},{... | collective-permute-start | bytes 36872 | tf_op jit(solution)/shard_map/ppermute | solution.py:514
  48.0 3.7 %collective-permute-start.9 = (f32[24,128]{1,0:T(8,128)S(1)}, f32[24,128]{1,0:T(8,128)S(1)}, u32[]{:S(2)}, u32[]{:S(2)}) collective-permute-start(f32[24,128]{1,0:T(8,128)S(1)} %add.21), channel_id=1, source_target_pairs={{0,1},{1,0},{2,3},{3,2},{4,5},{5,4},{6,7},{7,6},{8,9},{9,8},{10,11... | collective-permute-start | bytes 36872 | tf_op jit(solution)/shard_map/ppermute | solution.py:514
  51.7 4.6 %collective-permute-start.10 = (f32[24,128]{1,0:T(8,128)S(1)}, f32[24,128]{1,0:T(8,128)S(1)}, u32[]{:S(2)}, u32[]{:S(2)}) collective-permute-start(f32[24,128]{1,0:T(8,128)S(1)} %add.22), channel_id=1, source_target_pairs={{0,2},{1,3},{2,0},{3,1},{4,6},{5,7},{6,4},{7,5},{8,10},{9,11},{10,... | collective-permute-start | bytes 36872 | tf_op jit(solution)/shard_map/ppermute | solution.py:514

commit v10 on v9

--- a/solution.py
+++ b/solution.py
@@ -78,17 +78,17 @@
 def pack_kernel(members, rows, place_ref, x_ref, drag_ref, even_ref, odd_ref):
     cols = x_ref.shape[1]
     lane = lanes_of((8, cols))
+    slot = lane // MARGIN
     odd_x = place_ref[0] // place_ref[5] % 2 == 1
 
     def group(g, carry):
         for f in range(3):
-            left = jnp.zeros((8, cols), F32)
-            right = jnp.zeros((8, cols), F32)
-            for r in range(rows):
-                row = x_ref[pl.ds((f * members + g * 8) * rows + r, 8, stride=rows), :]
-                slot = lane // MARGIN
-                left = jnp.where(slot == rows - 1 - r, roll_lanes(row, MARGIN * (rows - 1 - r)), left)
-                right = jnp.where(slot == r, roll_lanes(row, MARGIN * (r + 1)), right)
+            row = [x_ref[pl.ds((f * members + g * 8) * rows + r, 8, stride=rows), :] for r in range(rows)]
+            left, right = row[rows - 1], roll_lanes(row[rows - 1], MARGIN * rows)
+            for r in range(rows - 1):
+                both = roll_lanes(jnp.where(lane < cols // 2, row[rows - 2 - r], row[r]), MARGIN * (r + 1))
+                left = jnp.where(slot == r + 1, both, left)
+                right = jnp.where(slot == r, both, right)
             at = pl.ds(pl.multiple_of(f * members + g * 8, 8), 8)
             even_ref[at, :] = jnp.where(odd_x, left, right)
             odd_ref[at, :] = jnp.where(odd_x, right, left)
@@ -539,7 +539,7 @@
     even, odd = swap_pairs(even, "gy", 0), swap_pairs(odd, "gy", 1)
     inner = interior(place, flat, left, right, drag, margin, members)
     states, priors = forecast(place, order, owner, cell, inner, above, below, even, odd, drag, margin)
-    priors = add_over(priors, ("gx", "gy"))
+    priors = add_over(priors, ("gy", "gx"))
     result = assimilate(place, order, owner, reach, value, error, taper, priors, states, members, rows)
     return result.reshape(status.shape)
 

time: 61.8 us -> 62 us (level)
  waiting for transfers between devices: 20.7 us -> 22.8 us
  starting transfers between devices: 17.6 us -> 15.7 us
    ppermute x5, waiting for transfers between devices: 9.65 us -> 11.6 us  [add_over(): x = x + lax.ppermute(x, axis, [(i, i ^ span) for i in range(count)])]
    ppermute x5, starting transfers between devices: 7.26 us -> 5.29 us  [add_over(): x = x + lax.ppermute(x, axis, [(i, i ^ span) for i in range(count)])]
  transfers between devices with their start and end apart: 11 -> 11, of which waited for: 7 -> 7; matrix products, arithmetic and copies ran while one was open for 0% -> 0% of each run, Pallas kernels for 14% -> 13%
where the time goes in v10:
time: 62 us
  Pallas kernels  23 us (37%)
  waiting for transfers between devices  22.8 us (37%)
  starting transfers between devices  15.7 us (25%)
    ppermute x5, waiting for transfers between devices, add_over(): x = x + lax.ppermute(x, axis, [(i, i ^ span) for i in range(count)])  11.6 us
    ppermute x4, waiting for transfers between devices, swap_pairs(): return lax.ppermute(x, axis, pairs + [(b, a) for a, b in pairs])  11.2 us
    pallas_call x1, Pallas kernels, forecast(): pl.pallas_call(functools.partial(forecast_kernel, members, rows), out_sha...  7.02 us
    pallas_call x1, Pallas kernels, interior(): pl.pallas_call(functools.partial(interior_kernel, members, rows), out_sha...  5.45 us
    ppermute x5, starting transfers between devices, add_over(): x = x + lax.ppermute(x, axis, [(i, i ^ span) for i in range(count)])  5.29 us
    pallas_call x1, Pallas kernels, assimilate(): pl.pallas_call(functools.partial(assimilate_kernel, members, rows), out_s...  5.07 us
    ppermute x1, starting transfers between devices, to_neighbours(): lax.ppermute(upper, axis, forward)  4.98 us
    ppermute x4, starting transfers between devices, swap_pairs(): return lax.ppermute(x, axis, pairs + [(b, a) for a, b in pairs])  4.1 us
  transfers between devices with their start and end apart: 11, of which 7 were waited for; matrix products, arithmetic and copies ran while one was open for 0% of the time, Pallas kernels for 13%

profile of v10, /device:TPU:0, one launch (start us, length us, event | category | flops | bytes accessed | tf_op | source)
XLA Modules:
  0.0 62.0 jit_solution(10589504917644604928)
XLA Ops:
  0.0 2.7 %shard_map.94 = (f32[22,80,128]{2,1,0:T(8,128)}, f32[22,80,128]{2,1,0:T(8,128)}) custom-call(f32[3840,128]{1,0:T(8,128)} %bitcast.7), custom_call_target="tpu_custom_call" | custom-call | flops 1000000 | bytes 4000000 | tf_op jit(solution)/shard_map/pallas_call | solution.py:67
  2.7 5.0 %collective-permute-start.2 = (f32[22,80,128]{2,1,0:T(8,128)}, f32[22,80,128]{2,1,0:T(8,128)S(1)}, u32[]{:S(2)}, u32[]{:S(2)}) collective-permute-start(f32[22,80,128]{2,1,0:T(8,128)} %get-tuple-element.21), channel_id=1, source_target_pairs={{0,1},{1,2},{2,3},{4,5},{5,6},{6,7},{8,9},{9,10},{10,11},{12,13},{... | collective-permute-start | bytes 2703368 | tf_op jit(solution)/shard_map/ppermute | solution.py:498
  7.7 1.3 %collective-permute-start.3 = (f32[22,80,128]{2,1,0:T(8,128)}, f32[22,80,128]{2,1,0:T(8,128)}, u32[]{:S(2)}, u32[]{:S(2)}) collective-permute-start(f32[22,80,128]{2,1,0:T(8,128)} %get-tuple-element.22), channel_id=1, source_target_pairs={{1,0},{2,1},{3,2},{5,4},{6,5},{7,6},{9,8},{10,9},{11,10},{13,12},{... | collective-permute-start | bytes 2703368 | tf_op jit(solution)/shard_map/ppermute | solution.py:498
  9.0 0.1 stack.39.place_ref
  9.1 2.0 %shard_map.91 = (f32[256,128]{1,0:T(8,128)S(1)}, f32[256,128]{1,0:T(8,128)S(1)}) custom-call(s32[6]{0:T(128)S(1)} %stack.39.place_ref, f32[3840,128]{1,0:T(8,128)S(1)} %bitcast.8, f32[16,128]{1,0:T(8,128)S(1)} %copy-done.1), custom_call_target="tpu_custom_call" | custom-call | flops 1000000 | bytes 4000000 | tf_op jit(solution)/shard_map/pallas_call | solution.py:105
  11.1 0.1 collective-permute-start
  11.2 0.7 %collective-permute-start.1 = (f32[256,128]{1,0:T(8,128)S(1)}, f32[256,128]{1,0:T(8,128)S(1)}, u32[]{:S(2)}, u32[]{:S(2)}) collective-permute-start(f32[256,128]{1,0:T(8,128)S(1)} %get-tuple-element.17), channel_id=1, source_target_pairs={{4,8},{12,16},{20,24},{8,4},{16,12},{24,20},{5,9},{13,17},{21,25},... | collective-permute-start | bytes 393224 | tf_op jit(solution)/shard_map/ppermute | solution.py:503
  11.8 0.7 %collective-permute-done.even_ref = f32[256,128]{1,0:T(8,128)S(1)} collective-permute-done((f32[256,128]{1,0:T(8,128)S(1)}, f32[256,128]{1,0:T(8,128)S(1)}, u32[]{:S(2)}, u32[]{:S(2)}) %collective-permute-start) | collective-permute-done | bytes 131104 | tf_op jit(solution)/shard_map/ppermute | solution.py:503
  12.5 0.8 %shard_map.92 = (f32[240,128]{1,0:T(8,128)S(1)}, f32[240,128]{1,0:T(8,128)S(1)}, f32[16,128]{1,0:T(8,128)S(1)}, f32[136,128]{1,0:T(8,128)S(1)}, f32[136,128]{1,0:T(8,128)S(1)}) custom-call(s32[6]{0:T(128)S(1)} %stack.39.place_ref, f32[16,128]{1,0:T(8,128)S(1)} %copy-done.1, f32[256,128]{1,0:T(8,128)S(1)} %collective-permute-done.even_ref, ...), custom_call_target="tpu_custom_call" | custom-call | tf_op jit(solution)/shard_map/pallas_call | solution.py:151
  13.3 2.7 %collective-permute-start.4 = (f32[136,128]{1,0:T(8,128)S(1)}, f32[136,128]{1,0:T(8,128)S(1)}, u32[]{:S(2)}, u32[]{:S(2)}) collective-permute-start(f32[136,128]{1,0:T(8,128)S(1)} %get-tuple-element.23), channel_id=1, source_target_pairs={{0,1},{2,3},{1,0},{3,2},{4,5},{6,7},{5,4},{7,6},{8,9},{10,11},{9,8... | collective-permute-start | bytes 208904 | tf_op jit(solution)/shard_map/ppermute | solution.py:503
  16.0 0.7 %collective-permute-start.5 = (f32[136,128]{1,0:T(8,128)S(1)}, f32[136,128]{1,0:T(8,128)S(1)}, u32[]{:S(2)}, u32[]{:S(2)}) collective-permute-start(f32[136,128]{1,0:T(8,128)S(1)} %get-tuple-element.24), channel_id=1, source_target_pairs={{1,2},{2,1},{5,6},{6,5},{9,10},{10,9},{13,14},{14,13},{17,18},{18,... | collective-permute-start | bytes 208904 | tf_op jit(solution)/shard_map/ppermute | solution.py:503
  16.7 5.5 %shard_map.93.inner_ref = f32[3,16,80,256]{3,2,1,0:T(8,128)S(1)} custom-call(s32[6]{0:T(128)S(1)} %stack.39.place_ref, f32[3840,128]{1,0:T(8,128)S(1)} %bitcast.9, f32[240,128]{1,0:T(8,128)S(1)} %get-tuple-element.18.left_ref, f32[240,128]{1,0:T(8,128)S(1)} %get-tuple-element.19.right_ref, f32[16,128]{1,0:T(8,128)S(1)} %copy-done.1, ...), custom_call_target="tpu_custom_call" | custom-call | flops 30000000 | bytes 10000000 | tf_op jit(solution)/shard_map/pallas_call | solution.py:242
  22.2 10.5 %collective-permute-done.4.ceven_ref = f32[136,128]{1,0:T(8,128)S(1)} collective-permute-done((f32[136,128]{1,0:T(8,128)S(1)}, f32[136,128]{1,0:T(8,128)S(1)}, u32[]{:S(2)}, u32[]{:S(2)}) %collective-permute-start.4) | collective-permute-done | bytes 69664 | tf_op jit(solution)/shard_map/ppermute | solution.py:503
  32.8 7.0 %shard_map.95 = (f32[48,80,128]{2,1,0:T(8,128)S(1)}, f32[24,128]{1,0:T(8,128)S(1)}) custom-call(s32[6]{0:T(128)S(1)} %stack.39.place_ref, s32[24]{0:T(128)S(1)} %copy-done.2, s32[24]{0:T(128)S(1)} %copy-done.3, s32[24]{0:T(128)S(1)} %copy-done.8, f32[3,16,80,256]{3,2,1,0:T(8,128)S(1)} %shard_map.93.inner_ref, ...), custom_call_target="tpu_custom_call" | custom-call | flops 60000000 | bytes 30000000 | tf_op jit(solution)/shard_map/pallas_call | solution.py:350
  39.8 1.1 %collective-permute-start.6 = (f32[24,128]{1,0:T(8,128)S(1)}, f32[24,128]{1,0:T(8,128)S(1)}, u32[]{:S(2)}, u32[]{:S(2)}) collective-permute-start(f32[24,128]{1,0:T(8,128)S(1)} %get-tuple-element.25), channel_id=1, source_target_pairs={{0,1},{1,0},{2,3},{3,2},{4,5},{5,4},{6,7},{7,6},{8,9},{9,8},{10,11... | collective-permute-start | bytes 36872 | tf_op jit(solution)/shard_map/ppermute | solution.py:514
  40.9 2.6 %collective-permute-done.6 = f32[24,128]{1,0:T(8,128)S(1)} collective-permute-done((f32[24,128]{1,0:T(8,128)S(1)}, f32[24,128]{1,0:T(8,128)S(1)}, u32[]{:S(2)}, u32[]{:S(2)}) %collective-permute-start.6) | collective-permute-done | bytes 12320 | tf_op jit(solution)/shard_map/ppermute | solution.py:514
  43.6 2.1 %collective-permute-start.7 = (f32[24,128]{1,0:T(8,128)S(1)}, f32[24,128]{1,0:T(8,128)S(1)}, u32[]{:S(2)}, u32[]{:S(2)}) collective-permute-start(f32[24,128]{1,0:T(8,128)S(1)} %add.19), channel_id=1, source_target_pairs={{0,2},{1,3},{2,0},{3,1},{4,6},{5,7},{6,4},{7,5},{8,10},{9,11},{10,... | collective-permute-start | bytes 36872 | tf_op jit(solution)/shard_map/ppermute | solution.py:514
  45.7 2.5 %collective-permute-done.7 = f32[24,128]{1,0:T(8,128)S(1)} collective-permute-done((f32[24,128]{1,0:T(8,128)S(1)}, f32[24,128]{1,0:T(8,128)S(1)}, u32[]{:S(2)}, u32[]{:S(2)}) %collective-permute-start.7) | collective-permute-done | bytes 12320 | tf_op jit(solution)/shard_map/ppermute | solution.py:514
  48.2 1.2 %collective-permute-done.8 = f32[24,128]{1,0:T(8,128)S(1)} collective-permute-done((f32[24,128]{1,0:T(8,128)S(1)}, f32[24,128]{1,0:T(8,128)S(1)}, u32[]{:S(2)}, u32[]{:S(2)}) %collective-permute-start.8) | collective-permute-done | bytes 12320 | tf_op jit(solution)/shard_map/ppermute | solution.py:514
  49.3 1.0 %collective-permute-start.9 = (f32[24,128]{1,0:T(8,128)S(1)}, f32[24,128]{1,0:T(8,128)S(1)}, u32[]{:S(2)}, u32[]{:S(2)}) collective-permute-start(f32[24,128]{1,0:T(8,128)S(1)} %add.21), channel_id=1, source_target_pairs={{0,8},{4,12},{8,0},{12,4},{16,24},{20,28},{24,16},{28,20},{1,9},{5... | collective-permute-start | bytes 36872 | tf_op jit(solution)/shard_map/ppermute | solution.py:514
  50.3 2.7 %collective-permute-done.9 = f32[24,128]{1,0:T(8,128)S(1)} collective-permute-done((f32[24,128]{1,0:T(8,128)S(1)}, f32[24,128]{1,0:T(8,128)S(1)}, u32[]{:S(2)}, u32[]{:S(2)}) %collective-permute-start.9) | collective-permute-done | bytes 12320 | tf_op jit(solution)/shard_map/ppermute | solution.py:514
  53.0 1.0 %collective-permute-start.10 = (f32[24,128]{1,0:T(8,128)S(1)}, f32[24,128]{1,0:T(8,128)S(1)}, u32[]{:S(2)}, u32[]{:S(2)}) collective-permute-start(f32[24,128]{1,0:T(8,128)S(1)} %add.22), channel_id=1, source_target_pairs={{0,16},{4,20},{8,24},{12,28},{16,0},{20,4},{24,8},{28,12},{1,17},{... | collective-permute-start | bytes 36872 | tf_op jit(solution)/shard_map/ppermute | solution.py:514
  54.1 2.7 %collective-permute-done.10 = f32[24,128]{1,0:T(8,128)S(1)} collective-permute-done((f32[24,128]{1,0:T(8,128)S(1)}, f32[24,128]{1,0:T(8,128)S(1)}, u32[]{:S(2)}, u32[]{:S(2)}) %collective-permute-start.10) | collective-permute-done | bytes 12320 | tf_op jit(solution)/shard_map/ppermute | solution.py:514
  56.8 5.1 %shard_map.96 = f32[3840,128]{1,0:T(8,128)} custom-call(s32[6]{0:T(128)S(1)} %stack.39.place_ref, s32[24]{0:T(128)S(1)} %copy-done.2, s32[24]{0:T(128)S(1)} %copy-done.3, s32[24]{0:T(128)S(1)} %copy-done.4, f32[24]{0:T(128)S(1)} %copy-done.5, f32[24]{0:T(128)S(1)} %copy-done.6, f32[7]{0:T(128)S(1)} %copy-done.7, f32[24,128]{1,0:T(8,128)S(1)} %add.23.prior_ref, ...), custom_call_target="tpu_custom_call" | custom-call | tf_op jit(solution)/shard_map/pallas_call | solution.py:484
  (28 shorter events, 0.1 us)
Async XLA Ops:
  0.0 9.1 %copy-start = (f32[3,80,16,128]{3,2,1,0:T(8,128)S(1)}, f32[3,80,16,128]{3,2,1,0:T(8,128)}, u32[]{:S(2)}) copy-start(f32[3,80,16,128]{3,2,1,0:T(8,128)} %param.9) | copy-start | bytes 5898244
  0.0 9.1 %copy-start.1 = (f32[16,128]{1,0:T(8,128)S(1)}, f32[16,128]{1,0:T(8,128)}, u32[]{:S(2)}) copy-start(f32[16,128]{1,0:T(8,128)} %drag_ref.7) | copy-start | bytes 24580
  2.7 30.1 %collective-permute-start.2 = (f32[22,80,128]{2,1,0:T(8,128)}, f32[22,80,128]{2,1,0:T(8,128)S(1)}, u32[]{:S(2)}, u32[]{:S(2)}) collective-permute-start(f32[22,80,128]{2,1,0:T(8,128)} %get-tuple-element.21), channel_id=1, source_target_pairs={{0,1},{1,2},{2,3},{4,5},{5,6},{6,7},{8,9},{9,10},{10,11},{12,13},{... | collective-permute-start | bytes 2703368 | tf_op jit(solution)/shard_map/ppermute | solution.py:498
  7.7 25.1 %collective-permute-start.3 = (f32[22,80,128]{2,1,0:T(8,128)}, f32[22,80,128]{2,1,0:T(8,128)}, u32[]{:S(2)}, u32[]{:S(2)}) collective-permute-start(f32[22,80,128]{2,1,0:T(8,128)} %get-tuple-element.22), channel_id=1, source_target_pairs={{1,0},{2,1},{3,2},{5,4},{6,5},{7,6},{9,8},{10,9},{11,10},{13,12},{... | collective-permute-start | bytes 2703368 | tf_op jit(solution)/shard_map/ppermute | solution.py:498
  11.1 1.4 %collective-permute-start = (f32[256,128]{1,0:T(8,128)S(1)}, f32[256,128]{1,0:T(8,128)S(1)}, u32[]{:S(2)}, u32[]{:S(2)}) collective-permute-start(f32[256,128]{1,0:T(8,128)S(1)} %get-tuple-element.16), channel_id=1, source_target_pairs={{0,4},{8,12},{16,20},{24,28},{4,0},{12,8},{20,16},{28,24},{1,5},{9... | collective-permute-start | bytes 393224 | tf_op jit(solution)/shard_map/ppermute | solution.py:503
  11.2 1.3 %collective-permute-start.1 = (f32[256,128]{1,0:T(8,128)S(1)}, f32[256,128]{1,0:T(8,128)S(1)}, u32[]{:S(2)}, u32[]{:S(2)}) collective-permute-start(f32[256,128]{1,0:T(8,128)S(1)} %get-tuple-element.17), channel_id=1, source_target_pairs={{4,8},{12,16},{20,24},{8,4},{16,12},{24,20},{5,9},{13,17},{21,25},... | collective-permute-start | bytes 393224 | tf_op jit(solution)/shard_map/ppermute | solution.py:503
  13.3 19.5 %collective-permute-start.4 = (f32[136,128]{1,0:T(8,128)S(1)}, f32[136,128]{1,0:T(8,128)S(1)}, u32[]{:S(2)}, u32[]{:S(2)}) collective-permute-start(f32[136,128]{1,0:T(8,128)S(1)} %get-tuple-element.23), channel_id=1, source_target_pairs={{0,1},{2,3},{1,0},{3,2},{4,5},{6,7},{5,4},{7,6},{8,9},{10,11},{9,8... | collective-permute-start | bytes 208904 | tf_op jit(solution)/shard_map/ppermute | solution.py:503
  16.0 16.8 %collective-permute-start.5 = (f32[136,128]{1,0:T(8,128)S(1)}, f32[136,128]{1,0:T(8,128)S(1)}, u32[]{:S(2)}, u32[]{:S(2)}) collective-permute-start(f32[136,128]{1,0:T(8,128)S(1)} %get-tuple-element.24), channel_id=1, source_target_pairs={{1,2},{2,1},{5,6},{6,5},{9,10},{10,9},{13,14},{14,13},{17,18},{18,... | collective-permute-start | bytes 208904 | tf_op jit(solution)/shard_map/ppermute | solution.py:503
  16.6 16.1 %copy-start.2 = (s32[24]{0:T(128)S(1)}, s32[24]{0:T(128)}, u32[]{:S(2)}) copy-start(s32[24]{0:T(128)} %order_ref.3) | copy-start | bytes 292
  16.6 16.1 %copy-start.3 = (s32[24]{0:T(128)S(1)}, s32[24]{0:T(128)}, u32[]{:S(2)}) copy-start(s32[24]{0:T(128)} %owner_ref.3) | copy-start | bytes 292
  16.7 16.1 %copy-start.8 = (s32[24]{0:T(128)S(1)}, s32[24]{0:T(128)}, u32[]{:S(2)}) copy-start(s32[24]{0:T(128)} %cell_ref.1) | copy-start | bytes 292
  22.1 34.6 %copy-start.4 = (s32[24]{0:T(128)S(1)}, s32[24]{0:T(128)}, u32[]{:S(2)}) copy-start(s32[24]{0:T(128)} %reach_ref.1) | copy-start | bytes 292
  22.1 34.6 %copy-start.5 = (f32[24]{0:T(128)S(1)}, f32[24]{0:T(128)}, u32[]{:S(2)}) copy-start(f32[24]{0:T(128)} %value_ref.1) | copy-start | bytes 292
  22.1 34.6 %copy-start.6 = (f32[24]{0:T(128)S(1)}, f32[24]{0:T(128)}, u32[]{:S(2)}) copy-start(f32[24]{0:T(128)} %error_ref.1) | copy-start | bytes 292
  22.2 34.6 %copy-start.7 = (f32[7]{0:T(128)S(1)}, f32[7]{0:T(128)}, u32[]{:S(2)}) copy-start(f32[7]{0:T(128)} %taper_ref.1) | copy-start | bytes 88
  39.8 3.8 %collective-permute-start.6 = (f32[24,128]{1,0:T(8,128)S(1)}, f32[24,128]{1,0:T(8,128)S(1)}, u32[]{:S(2)}, u32[]{:S(2)}) collective-permute-start(f32[24,128]{1,0:T(8,128)S(1)} %get-tuple-element.25), channel_id=1, source_target_pairs={{0,1},{1,0},{2,3},{3,2},{4,5},{5,4},{6,7},{7,6},{8,9},{9,8},{10,11... | collective-permute-start | bytes 36872 | tf_op jit(solution)/shard_map/ppermute | solution.py:514
  43.6 4.6 %collective-permute-start.7 = (f32[24,128]{1,0:T(8,128)S(1)}, f32[24,128]{1,0:T(8,128)S(1)}, u32[]{:S(2)}, u32[]{:S(2)}) collective-permute-start(f32[24,128]{1,0:T(8,128)S(1)} %add.19), channel_id=1, source_target_pairs={{0,2},{1,3},{2,0},{3,1},{4,6},{5,7},{6,4},{7,5},{8,10},{9,11},{10,... | collective-permute-start | bytes 36872 | tf_op jit(solution)/shard_map/ppermute | solution.py:514
  48.2 1.2 %collective-permute-start.8 = (f32[24,128]{1,0:T(8,128)S(1)}, f32[24,128]{1,0:T(8,128)S(1)}, u32[]{:S(2)}, u32[]{:S(2)}) collective-permute-start(f32[24,128]{1,0:T(8,128)S(1)} %add.20), channel_id=1, source_target_pairs={{0,4},{4,0},{8,12},{12,8},{16,20},{20,16},{24,28},{28,24},{1,5},{5... | collective-permute-start | bytes 36872 | tf_op jit(solution)/shard_map/ppermute | solution.py:514
  49.3 3.7 %collective-permute-start.9 = (f32[24,128]{1,0:T(8,128)S(1)}, f32[24,128]{1,0:T(8,128)S(1)}, u32[]{:S(2)}, u32[]{:S(2)}) collective-permute-start(f32[24,128]{1,0:T(8,128)S(1)} %add.21), channel_id=1, source_target_pairs={{0,8},{4,12},{8,0},{12,4},{16,24},{20,28},{24,16},{28,20},{1,9},{5... | collective-permute-start | bytes 36872 | tf_op jit(solution)/shard_map/ppermute | solution.py:514
  53.0 3.7 %collective-permute-start.10 = (f32[24,128]{1,0:T(8,128)S(1)}, f32[24,128]{1,0:T(8,128)S(1)}, u32[]{:S(2)}, u32[]{:S(2)}) collective-permute-start(f32[24,128]{1,0:T(8,128)S(1)} %add.22), channel_id=1, source_target_pairs={{0,16},{4,20},{8,24},{12,28},{16,0},{20,4},{24,8},{28,12},{1,17},{... | collective-permute-start | bytes 36872 | tf_op jit(solution)/shard_map/ppermute | solution.py:514

commit v11 on v10

--- a/solution.py
+++ b/solution.py
@@ -536,10 +536,11 @@
     even, odd = pack(place, flat, drag, members)
     even, odd = swap_pairs(even, "gx", 0), swap_pairs(odd, "gx", 1)
     left, right, margin, even, odd = corner(place, drag, even, odd)
+    inner = interior(place, flat, left, right, drag, margin, members)
+    even, odd, inner = lax.optimization_barrier((even, odd, inner))
     even, odd = swap_pairs(even, "gy", 0), swap_pairs(odd, "gy", 1)
-    inner = interior(place, flat, left, right, drag, margin, members)
     states, priors = forecast(place, order, owner, cell, inner, above, below, even, odd, drag, margin)
-    priors = add_over(priors, ("gy", "gx"))
+    priors = add_over(priors, ("gx", "gy"))
     result = assimilate(place, order, owner, reach, value, error, taper, priors, states, members, rows)
     return result.reshape(status.shape)
 

time: 62 us -> 63.7 us (1.027)
  starting transfers between devices: 15.7 us -> 20.5 us
  waiting for transfers between devices: 22.8 us -> 20 us
    ppermute x5, starting transfers between devices: 5.29 us -> 10.1 us  [add_over(): x = x + lax.ppermute(x, axis, [(i, i ^ span) for i in range(count)])]
    ppermute x5, waiting for transfers between devices: 11.6 us -> 8.74 us  [add_over(): x = x + lax.ppermute(x, axis, [(i, i ^ span) for i in range(count)])]
where the time goes in v11:
time: 63.7 us; the launch traced here: 63.5 us
  Pallas kernels  22.5 us (35%)
  starting transfers between devices  20.5 us (32%)
  waiting for transfers between devices  20 us (31%)
    ppermute x4, waiting for transfers between devices, swap_pairs(): return lax.ppermute(x, axis, pairs + [(b, a) for a, b in pairs])  11.2 us
    ppermute x5, starting transfers between devices, add_over(): x = x + lax.ppermute(x, axis, [(i, i ^ span) for i in range(count)])  10.1 us
    ppermute x5, waiting for transfers between devices, add_over(): x = x + lax.ppermute(x, axis, [(i, i ^ span) for i in range(count)])  8.74 us
    pallas_call x1, Pallas kernels, forecast(): pl.pallas_call(functools.partial(forecast_kernel, members, rows), out_sha...  6.6 us
    pallas_call x1, Pallas kernels, interior(): pl.pallas_call(functools.partial(interior_kernel, members, rows), out_sha...  5.44 us
    pallas_call x1, Pallas kernels, assimilate(): pl.pallas_call(functools.partial(assimilate_kernel, members, rows), out_s...  5.07 us
    ppermute x1, starting transfers between devices, to_neighbours(): lax.ppermute(upper, axis, forward)  4.98 us
    ppermute x4, starting transfers between devices, swap_pairs(): return lax.ppermute(x, axis, pairs + [(b, a) for a, b in pairs])  4.11 us
  transfers between devices with their start and end apart: 11, of which 7 were waited for; matrix products, arithmetic and copies ran while one was open for 0% of the time, Pallas kernels for 13%

profile of v11, /device:TPU:0, one launch (start us, length us, event | category | flops | bytes accessed | tf_op | source)
XLA Modules:
  0.0 63.5 jit_solution(4305200018749470219)
XLA Ops:
  0.0 2.7 %shard_map.94 = (f32[22,80,128]{2,1,0:T(8,128)}, f32[22,80,128]{2,1,0:T(8,128)}) custom-call(f32[3840,128]{1,0:T(8,128)} %bitcast.7), custom_call_target="tpu_custom_call" | custom-call | flops 1000000 | bytes 4000000 | tf_op jit(solution)/shard_map/pallas_call | solution.py:67
  2.7 5.0 %collective-permute-start.2 = (f32[22,80,128]{2,1,0:T(8,128)}, f32[22,80,128]{2,1,0:T(8,128)S(1)}, u32[]{:S(2)}, u32[]{:S(2)}) collective-permute-start(f32[22,80,128]{2,1,0:T(8,128)} %get-tuple-element.27), channel_id=1, source_target_pairs={{0,1},{1,2},{2,3},{4,5},{5,6},{6,7},{8,9},{9,10},{10,11},{12,13},{... | collective-permute-start | bytes 2703368 | tf_op jit(solution)/shard_map/ppermute | solution.py:498
  7.7 1.3 %collective-permute-start.3 = (f32[22,80,128]{2,1,0:T(8,128)}, f32[22,80,128]{2,1,0:T(8,128)}, u32[]{:S(2)}, u32[]{:S(2)}) collective-permute-start(f32[22,80,128]{2,1,0:T(8,128)} %get-tuple-element.28), channel_id=1, source_target_pairs={{1,0},{2,1},{3,2},{5,4},{6,5},{7,6},{9,8},{10,9},{11,10},{13,12},{... | collective-permute-start | bytes 2703368 | tf_op jit(solution)/shard_map/ppermute | solution.py:498
  9.0 0.1 stack.39.place_ref
  9.1 2.0 %shard_map.91 = (f32[256,128]{1,0:T(8,128)S(1)}, f32[256,128]{1,0:T(8,128)S(1)}) custom-call(s32[6]{0:T(128)S(1)} %stack.39.place_ref, f32[3840,128]{1,0:T(8,128)S(1)} %bitcast.8, f32[16,128]{1,0:T(8,128)S(1)} %copy-done.1), custom_call_target="tpu_custom_call" | custom-call | flops 1000000 | bytes 4000000 | tf_op jit(solution)/shard_map/pallas_call | solution.py:105
  11.2 0.7 %collective-permute-start.1 = (f32[256,128]{1,0:T(8,128)S(1)}, f32[256,128]{1,0:T(8,128)S(1)}, u32[]{:S(2)}, u32[]{:S(2)}) collective-permute-start(f32[256,128]{1,0:T(8,128)S(1)} %get-tuple-element.20), channel_id=1, source_target_pairs={{4,8},{12,16},{20,24},{8,4},{16,12},{24,20},{5,9},{13,17},{21,25},... | collective-permute-start | bytes 393224 | tf_op jit(solution)/shard_map/ppermute | solution.py:503
  11.8 0.7 %collective-permute-done.even_ref = f32[256,128]{1,0:T(8,128)S(1)} collective-permute-done((f32[256,128]{1,0:T(8,128)S(1)}, f32[256,128]{1,0:T(8,128)S(1)}, u32[]{:S(2)}, u32[]{:S(2)}) %collective-permute-start) | collective-permute-done | bytes 131104 | tf_op jit(solution)/shard_map/ppermute | solution.py:503
  12.5 0.8 %shard_map.92 = (f32[240,128]{1,0:T(8,128)S(1)}, f32[240,128]{1,0:T(8,128)S(1)}, f32[16,128]{1,0:T(8,128)S(1)}, f32[136,128]{1,0:T(8,128)S(1)}, f32[136,128]{1,0:T(8,128)S(1)}) custom-call(s32[6]{0:T(128)S(1)} %stack.39.place_ref, f32[16,128]{1,0:T(8,128)S(1)} %copy-done.1, f32[256,128]{1,0:T(8,128)S(1)} %collective-permute-done.even_ref, ...), custom_call_target="tpu_custom_call" | custom-call | tf_op jit(solution)/shard_map/pallas_call | solution.py:151
  13.3 5.4 %shard_map.93.inner_ref = f32[3,16,80,256]{3,2,1,0:T(8,128)S(1)} custom-call(s32[6]{0:T(128)S(1)} %stack.39.place_ref, f32[3840,128]{1,0:T(8,128)S(1)} %bitcast.9, f32[240,128]{1,0:T(8,128)S(1)} %get-tuple-element.23.left_ref, f32[240,128]{1,0:T(8,128)S(1)} %get-tuple-element.24.right_ref, f32[16,128]{1,0:T(8,128)S(1)} %copy-done.1, ...), custom_call_target="tpu_custom_call" | custom-call | flops 30000000 | bytes 10000000 | tf_op jit(solution)/shard_map/pallas_call | solution.py:242
  18.8 2.7 %collective-permute-start.4 = (f32[136,128]{1,0:T(8,128)S(1)}, f32[136,128]{1,0:T(8,128)S(1)}, u32[]{:S(2)}, u32[]{:S(2)}) collective-permute-start(f32[136,128]{1,0:T(8,128)S(1)} %get-tuple-element.29), channel_id=1, source_target_pairs={{0,1},{2,3},{1,0},{3,2},{4,5},{6,7},{5,4},{7,6},{8,9},{10,11},{9,8... | collective-permute-start | bytes 208904 | tf_op jit(solution)/shard_map/ppermute | solution.py:503
  21.5 0.7 %collective-permute-start.5 = (f32[136,128]{1,0:T(8,128)S(1)}, f32[136,128]{1,0:T(8,128)S(1)}, u32[]{:S(2)}, u32[]{:S(2)}) collective-permute-start(f32[136,128]{1,0:T(8,128)S(1)} %get-tuple-element.30), channel_id=1, source_target_pairs={{1,2},{2,1},{5,6},{6,5},{9,10},{10,9},{13,14},{14,13},{17,18},{18,... | collective-permute-start | bytes 208904 | tf_op jit(solution)/shard_map/ppermute | solution.py:503
  22.2 10.6 %collective-permute-done.4.ceven_ref = f32[136,128]{1,0:T(8,128)S(1)} collective-permute-done((f32[136,128]{1,0:T(8,128)S(1)}, f32[136,128]{1,0:T(8,128)S(1)}, u32[]{:S(2)}, u32[]{:S(2)}) %collective-permute-start.4) | collective-permute-done | bytes 69664 | tf_op jit(solution)/shard_map/ppermute | solution.py:503
  32.8 6.6 %shard_map.95 = (f32[48,80,128]{2,1,0:T(8,128)S(1)}, f32[24,128]{1,0:T(8,128)S(1)}) custom-call(s32[6]{0:T(128)S(1)} %stack.39.place_ref, s32[24]{0:T(128)S(1)} %copy-done.2, s32[24]{0:T(128)S(1)} %copy-done.3, s32[24]{0:T(128)S(1)} %copy-done.8, f32[3,16,80,256]{3,2,1,0:T(8,128)S(1)} %shard_map.93.inner_ref, ...), custom_call_target="tpu_custom_call" | custom-call | flops 60000000 | bytes 30000000 | tf_op jit(solution)/shard_map/pallas_call | solution.py:350
  39.4 0.1 collective-permute-start.6
  39.4 1.2 %collective-permute-done.6 = f32[24,128]{1,0:T(8,128)S(1)} collective-permute-done((f32[24,128]{1,0:T(8,128)S(1)}, f32[24,128]{1,0:T(8,128)S(1)}, u32[]{:S(2)}, u32[]{:S(2)}) %collective-permute-start.6) | collective-permute-done | bytes 12320 | tf_op jit(solution)/shard_map/ppermute | solution.py:514
  40.6 1.6 %collective-permute-start.7 = (f32[24,128]{1,0:T(8,128)S(1)}, f32[24,128]{1,0:T(8,128)S(1)}, u32[]{:S(2)}, u32[]{:S(2)}) collective-permute-start(f32[24,128]{1,0:T(8,128)S(1)} %add.19), channel_id=1, source_target_pairs={{0,8},{4,12},{8,0},{12,4},{16,24},{20,28},{24,16},{28,20},{1,9},{5... | collective-permute-start | bytes 36872 | tf_op jit(solution)/shard_map/ppermute | solution.py:514
  42.3 2.1 %collective-permute-done.7 = f32[24,128]{1,0:T(8,128)S(1)} collective-permute-done((f32[24,128]{1,0:T(8,128)S(1)}, f32[24,128]{1,0:T(8,128)S(1)}, u32[]{:S(2)}, u32[]{:S(2)}) %collective-permute-start.7) | collective-permute-done | bytes 12320 | tf_op jit(solution)/shard_map/ppermute | solution.py:514
  44.3 1.5 %collective-permute-start.8 = (f32[24,128]{1,0:T(8,128)S(1)}, f32[24,128]{1,0:T(8,128)S(1)}, u32[]{:S(2)}, u32[]{:S(2)}) collective-permute-start(f32[24,128]{1,0:T(8,128)S(1)} %add.20), channel_id=1, source_target_pairs={{0,16},{4,20},{8,24},{12,28},{16,0},{20,4},{24,8},{28,12},{1,17},{... | collective-permute-start | bytes 36872 | tf_op jit(solution)/shard_map/ppermute | solution.py:514
  45.8 2.2 %collective-permute-done.8 = f32[24,128]{1,0:T(8,128)S(1)} collective-permute-done((f32[24,128]{1,0:T(8,128)S(1)}, f32[24,128]{1,0:T(8,128)S(1)}, u32[]{:S(2)}, u32[]{:S(2)}) %collective-permute-start.8) | collective-permute-done | bytes 12320 | tf_op jit(solution)/shard_map/ppermute | solution.py:514
  48.0 3.4 %collective-permute-start.9 = (f32[24,128]{1,0:T(8,128)S(1)}, f32[24,128]{1,0:T(8,128)S(1)}, u32[]{:S(2)}, u32[]{:S(2)}) collective-permute-start(f32[24,128]{1,0:T(8,128)S(1)} %add.21), channel_id=1, source_target_pairs={{0,1},{1,0},{2,3},{3,2},{4,5},{5,4},{6,7},{7,6},{8,9},{9,8},{10,11... | collective-permute-start | bytes 36872 | tf_op jit(solution)/shard_map/ppermute | solution.py:514
  51.5 1.7 %collective-permute-done.9 = f32[24,128]{1,0:T(8,128)S(1)} collective-permute-done((f32[24,128]{1,0:T(8,128)S(1)}, f32[24,128]{1,0:T(8,128)S(1)}, u32[]{:S(2)}, u32[]{:S(2)}) %collective-permute-start.9) | collective-permute-done | bytes 12320 | tf_op jit(solution)/shard_map/ppermute | solution.py:514
  53.1 3.4 %collective-permute-start.10 = (f32[24,128]{1,0:T(8,128)S(1)}, f32[24,128]{1,0:T(8,128)S(1)}, u32[]{:S(2)}, u32[]{:S(2)}) collective-permute-start(f32[24,128]{1,0:T(8,128)S(1)} %add.22), channel_id=1, source_target_pairs={{0,2},{1,3},{2,0},{3,1},{4,6},{5,7},{6,4},{7,5},{8,10},{9,11},{10,... | collective-permute-start | bytes 36872 | tf_op jit(solution)/shard_map/ppermute | solution.py:514
  56.6 1.7 %collective-permute-done.10 = f32[24,128]{1,0:T(8,128)S(1)} collective-permute-done((f32[24,128]{1,0:T(8,128)S(1)}, f32[24,128]{1,0:T(8,128)S(1)}, u32[]{:S(2)}, u32[]{:S(2)}) %collective-permute-start.10) | collective-permute-done | bytes 12320 | tf_op jit(solution)/shard_map/ppermute | solution.py:514
  58.3 5.1 %shard_map.96 = f32[3840,128]{1,0:T(8,128)} custom-call(s32[6]{0:T(128)S(1)} %stack.39.place_ref, s32[24]{0:T(128)S(1)} %copy-done.2, s32[24]{0:T(128)S(1)} %copy-done.3, s32[24]{0:T(128)S(1)} %copy-done.4, f32[24]{0:T(128)S(1)} %copy-done.5, f32[24]{0:T(128)S(1)} %copy-done.6, f32[7]{0:T(128)S(1)} %copy-done.7, f32[24,128]{1,0:T(8,128)S(1)} %add.23.prior_ref, ...), custom_call_target="tpu_custom_call" | custom-call | tf_op jit(solution)/shard_map/pallas_call | solution.py:484
  (28 shorter events, 0.2 us)
Async XLA Ops:
  0.0 9.1 %copy-start = (f32[3,80,16,128]{3,2,1,0:T(8,128)S(1)}, f32[3,80,16,128]{3,2,1,0:T(8,128)}, u32[]{:S(2)}) copy-start(f32[3,80,16,128]{3,2,1,0:T(8,128)} %param.9) | copy-start | bytes 5898244
  0.0 9.1 %copy-start.1 = (f32[16,128]{1,0:T(8,128)S(1)}, f32[16,128]{1,0:T(8,128)}, u32[]{:S(2)}) copy-start(f32[16,128]{1,0:T(8,128)} %drag_ref.7) | copy-start | bytes 24580
  2.7 30.1 %collective-permute-start.2 = (f32[22,80,128]{2,1,0:T(8,128)}, f32[22,80,128]{2,1,0:T(8,128)S(1)}, u32[]{:S(2)}, u32[]{:S(2)}) collective-permute-start(f32[22,80,128]{2,1,0:T(8,128)} %get-tuple-element.27), channel_id=1, source_target_pairs={{0,1},{1,2},{2,3},{4,5},{5,6},{6,7},{8,9},{9,10},{10,11},{12,13},{... | collective-permute-start | bytes 2703368 | tf_op jit(solution)/shard_map/ppermute | solution.py:498
  7.7 25.1 %collective-permute-start.3 = (f32[22,80,128]{2,1,0:T(8,128)}, f32[22,80,128]{2,1,0:T(8,128)}, u32[]{:S(2)}, u32[]{:S(2)}) collective-permute-start(f32[22,80,128]{2,1,0:T(8,128)} %get-tuple-element.28), channel_id=1, source_target_pairs={{1,0},{2,1},{3,2},{5,4},{6,5},{7,6},{9,8},{10,9},{11,10},{13,12},{... | collective-permute-start | bytes 2703368 | tf_op jit(solution)/shard_map/ppermute | solution.py:498
  11.1 1.4 %collective-permute-start = (f32[256,128]{1,0:T(8,128)S(1)}, f32[256,128]{1,0:T(8,128)S(1)}, u32[]{:S(2)}, u32[]{:S(2)}) collective-permute-start(f32[256,128]{1,0:T(8,128)S(1)} %get-tuple-element.19), channel_id=1, source_target_pairs={{0,4},{8,12},{16,20},{24,28},{4,0},{12,8},{20,16},{28,24},{1,5},{9... | collective-permute-start | bytes 393224 | tf_op jit(solution)/shard_map/ppermute | solution.py:503
  11.2 1.3 %collective-permute-start.1 = (f32[256,128]{1,0:T(8,128)S(1)}, f32[256,128]{1,0:T(8,128)S(1)}, u32[]{:S(2)}, u32[]{:S(2)}) collective-permute-start(f32[256,128]{1,0:T(8,128)S(1)} %get-tuple-element.20), channel_id=1, source_target_pairs={{4,8},{12,16},{20,24},{8,4},{16,12},{24,20},{5,9},{13,17},{21,25},... | collective-permute-start | bytes 393224 | tf_op jit(solution)/shard_map/ppermute | solution.py:503
  13.3 19.5 %copy-start.2 = (s32[24]{0:T(128)S(1)}, s32[24]{0:T(128)}, u32[]{:S(2)}) copy-start(s32[24]{0:T(128)} %order_ref.3) | copy-start | bytes 292
  13.3 19.5 %copy-start.3 = (s32[24]{0:T(128)S(1)}, s32[24]{0:T(128)}, u32[]{:S(2)}) copy-start(s32[24]{0:T(128)} %owner_ref.3) | copy-start | bytes 292
  13.3 19.5 %copy-start.8 = (s32[24]{0:T(128)S(1)}, s32[24]{0:T(128)}, u32[]{:S(2)}) copy-start(s32[24]{0:T(128)} %cell_ref.1) | copy-start | bytes 292
  18.7 39.5 %copy-start.4 = (s32[24]{0:T(128)S(1)}, s32[24]{0:T(128)}, u32[]{:S(2)}) copy-start(s32[24]{0:T(128)} %reach_ref.1) | copy-start | bytes 292
  18.8 39.5 %copy-start.5 = (f32[24]{0:T(128)S(1)}, f32[24]{0:T(128)}, u32[]{:S(2)}) copy-start(f32[24]{0:T(128)} %value_ref.1) | copy-start | bytes 292
  18.8 39.5 %copy-start.6 = (f32[24]{0:T(128)S(1)}, f32[24]{0:T(128)}, u32[]{:S(2)}) copy-start(f32[24]{0:T(128)} %error_ref.1) | copy-start | bytes 292
  18.8 39.5 %copy-start.7 = (f32[7]{0:T(128)S(1)}, f32[7]{0:T(128)}, u32[]{:S(2)}) copy-start(f32[7]{0:T(128)} %taper_ref.1) | copy-start | bytes 88
  18.8 13.9 %collective-permute-start.4 = (f32[136,128]{1,0:T(8,128)S(1)}, f32[136,128]{1,0:T(8,128)S(1)}, u32[]{:S(2)}, u32[]{:S(2)}) collective-permute-start(f32[136,128]{1,0:T(8,128)S(1)} %get-tuple-element.29), channel_id=1, source_target_pairs={{0,1},{2,3},{1,0},{3,2},{4,5},{6,7},{5,4},{7,6},{8,9},{10,11},{9,8... | collective-permute-start | bytes 208904 | tf_op jit(solution)/shard_map/ppermute | solution.py:503
  21.5 11.2 %collective-permute-start.5 = (f32[136,128]{1,0:T(8,128)S(1)}, f32[136,128]{1,0:T(8,128)S(1)}, u32[]{:S(2)}, u32[]{:S(2)}) collective-permute-start(f32[136,128]{1,0:T(8,128)S(1)} %get-tuple-element.30), channel_id=1, source_target_pairs={{1,2},{2,1},{5,6},{6,5},{9,10},{10,9},{13,14},{14,13},{17,18},{18,... | collective-permute-start | bytes 208904 | tf_op jit(solution)/shard_map/ppermute | solution.py:503
  39.4 1.2 %collective-permute-start.6 = (f32[24,128]{1,0:T(8,128)S(1)}, f32[24,128]{1,0:T(8,128)S(1)}, u32[]{:S(2)}, u32[]{:S(2)}) collective-permute-start(f32[24,128]{1,0:T(8,128)S(1)} %get-tuple-element.31), channel_id=1, source_target_pairs={{0,4},{4,0},{8,12},{12,8},{16,20},{20,16},{24,28},{28,24},{1,5},{5... | collective-permute-start | bytes 36872 | tf_op jit(solution)/shard_map/ppermute | solution.py:514
  40.6 3.7 %collective-permute-start.7 = (f32[24,128]{1,0:T(8,128)S(1)}, f32[24,128]{1,0:T(8,128)S(1)}, u32[]{:S(2)}, u32[]{:S(2)}) collective-permute-start(f32[24,128]{1,0:T(8,128)S(1)} %add.19), channel_id=1, source_target_pairs={{0,8},{4,12},{8,0},{12,4},{16,24},{20,28},{24,16},{28,20},{1,9},{5... | collective-permute-start | bytes 36872 | tf_op jit(solution)/shard_map/ppermute | solution.py:514
  44.3 3.7 %collective-permute-start.8 = (f32[24,128]{1,0:T(8,128)S(1)}, f32[24,128]{1,0:T(8,128)S(1)}, u32[]{:S(2)}, u32[]{:S(2)}) collective-permute-start(f32[24,128]{1,0:T(8,128)S(1)} %add.20), channel_id=1, source_target_pairs={{0,16},{4,20},{8,24},{12,28},{16,0},{20,4},{24,8},{28,12},{1,17},{... | collective-permute-start | bytes 36872 | tf_op jit(solution)/shard_map/ppermute | solution.py:514
  48.0 5.1 %collective-permute-start.9 = (f32[24,128]{1,0:T(8,128)S(1)}, f32[24,128]{1,0:T(8,128)S(1)}, u32[]{:S(2)}, u32[]{:S(2)}) collective-permute-start(f32[24,128]{1,0:T(8,128)S(1)} %add.21), channel_id=1, source_target_pairs={{0,1},{1,0},{2,3},{3,2},{4,5},{5,4},{6,7},{7,6},{8,9},{9,8},{10,11... | collective-permute-start | bytes 36872 | tf_op jit(solution)/shard_map/ppermute | solution.py:514
  53.1 5.1 %collective-permute-start.10 = (f32[24,128]{1,0:T(8,128)S(1)}, f32[24,128]{1,0:T(8,128)S(1)}, u32[]{:S(2)}, u32[]{:S(2)}) collective-permute-start(f32[24,128]{1,0:T(8,128)S(1)} %add.22), channel_id=1, source_target_pairs={{0,2},{1,3},{2,0},{3,1},{4,6},{5,7},{6,4},{7,5},{8,10},{9,11},{10,... | collective-permute-start | bytes 36872 | tf_op jit(solution)/shard_map/ppermute | solution.py:514

commit v12 on v10

--- a/solution.py
+++ b/solution.py
@@ -16,6 +16,7 @@
 BF16 = jnp.bfloat16
 VMEM_LIMIT = 24 * 1024 * 1024
 GROUP = 40
+AHEAD = 3
 
 VSPEC = pl.BlockSpec(memory_space=pltpu.VMEM)
 SSPEC = pl.BlockSpec(memory_space=pltpu.SMEM)
@@ -216,7 +217,7 @@
     lax.fori_loop(0, members // 8, first, 0)
 
     groups = [pl.ds(m, GROUP) for m in range(0, members, GROUP)]
-    for step in range(STEPS):
+    for step in range(AHEAD):
         low, high = 1 + 2 * step, rows - 1 - 2 * step
         if low >= high:
             break
@@ -325,10 +326,12 @@
     for step in range(STEPS):
         first, last = MARGIN - MARGIN + 1 + 2 * step, MARGIN + rows + MARGIN - 1 - 2 * step
         done, still = MARGIN + 1 + 2 * step, MARGIN + rows - 1 - 2 * step
+        if step >= AHEAD:
+            done = still = MARGIN + rows // 2
         for g in groups:
             heights(g, ((first, done), (still, last)))
         for g in groups:
-            flows(g, ((first + 1, done + 1), (still - 1, last - 1)), step == STEPS - 1)
+            flows(g, ((first + 1, done + (step < AHEAD)), (still - (step < AHEAD), last - 1)), step == STEPS - 1)
     prior_ref[...] = jnp.zeros_like(prior_ref)
     eight = lanes_of((8, cols))
     for i in range(order_ref.shape[0]):
@@ -539,7 +542,7 @@
     even, odd = swap_pairs(even, "gy", 0), swap_pairs(odd, "gy", 1)
     inner = interior(place, flat, left, right, drag, margin, members)
     states, priors = forecast(place, order, owner, cell, inner, above, below, even, odd, drag, margin)
-    priors = add_over(priors, ("gy", "gx"))
+    priors = add_over(priors, ("gx", "gy"))
     result = assimilate(place, order, owner, reach, value, error, taper, priors, states, members, rows)
     return result.reshape(status.shape)
 

time: 62 us -> 61.8 us (level)
  starting transfers between devices: 15.7 us -> 17.4 us
  waiting for transfers between devices: 22.8 us -> 21.3 us
    ppermute x5, waiting for transfers between devices: 11.6 us -> 9.88 us  [add_over(): x = x + lax.ppermute(x, axis, [(i, i ^ span) for i in range(count)])]
    ppermute x5, starting transfers between devices: 5.29 us -> 7.03 us  [add_over(): x = x + lax.ppermute(x, axis, [(i, i ^ span) for i in range(count)])]
where the time goes in v12:
time: 61.8 us; the launch traced here: 61.6 us
  Pallas kernels  22.4 us (36%)
  waiting for transfers between devices  21.3 us (34%)
  starting transfers between devices  17.4 us (28%)
    ppermute x4, waiting for transfers between devices, swap_pairs(): return lax.ppermute(x, axis, pairs + [(b, a) for a, b in pairs])  11.4 us
    ppermute x5, waiting for transfers between devices, add_over(): x = x + lax.ppermute(x, axis, [(i, i ^ span) for i in range(count)])  9.88 us
    ppermute x5, starting transfers between devices, add_over(): x = x + lax.ppermute(x, axis, [(i, i ^ span) for i in range(count)])  7.03 us
    pallas_call x1, Pallas kernels, forecast(): pl.pallas_call(functools.partial(forecast_kernel, members, rows), out_sha...  6.66 us
    pallas_call x1, Pallas kernels, interior(): pl.pallas_call(functools.partial(interior_kernel, members, rows), out_sha...  5.29 us
    pallas_call x1, Pallas kernels, assimilate(): pl.pallas_call(functools.partial(assimilate_kernel, members, rows), out_s...  5.07 us
    ppermute x1, starting transfers between devices, to_neighbours(): lax.ppermute(upper, axis, forward)  4.98 us
    ppermute x4, starting transfers between devices, swap_pairs(): return lax.ppermute(x, axis, pairs + [(b, a) for a, b in pairs])  4.1 us
  transfers between devices with their start and end apart: 11, of which 7 were waited for; matrix products, arithmetic and copies ran while one was open for 0% of the time, Pallas kernels for 13%

profile of v12, /device:TPU:0, one launch (start us, length us, event | category | flops | bytes accessed | tf_op | source)
XLA Modules:
  0.0 61.6 jit_solution(4668748572795439885)
XLA Ops:
  0.0 2.7 %shard_map.94 = (f32[22,80,128]{2,1,0:T(8,128)}, f32[22,80,128]{2,1,0:T(8,128)}) custom-call(f32[3840,128]{1,0:T(8,128)} %bitcast.7), custom_call_target="tpu_custom_call" | custom-call | flops 1000000 | bytes 4000000 | tf_op jit(solution)/shard_map/pallas_call | solution.py:68
  2.7 5.0 %collective-permute-start.2 = (f32[22,80,128]{2,1,0:T(8,128)}, f32[22,80,128]{2,1,0:T(8,128)S(1)}, u32[]{:S(2)}, u32[]{:S(2)}) collective-permute-start(f32[22,80,128]{2,1,0:T(8,128)} %get-tuple-element.21), channel_id=1, source_target_pairs={{0,1},{1,2},{2,3},{4,5},{5,6},{6,7},{8,9},{9,10},{10,11},{12,13},{... | collective-permute-start | bytes 2703368 | tf_op jit(solution)/shard_map/ppermute | solution.py:501
  7.7 1.3 %collective-permute-start.3 = (f32[22,80,128]{2,1,0:T(8,128)}, f32[22,80,128]{2,1,0:T(8,128)}, u32[]{:S(2)}, u32[]{:S(2)}) collective-permute-start(f32[22,80,128]{2,1,0:T(8,128)} %get-tuple-element.22), channel_id=1, source_target_pairs={{1,0},{2,1},{3,2},{5,4},{6,5},{7,6},{9,8},{10,9},{11,10},{13,12},{... | collective-permute-start | bytes 2703368 | tf_op jit(solution)/shard_map/ppermute | solution.py:501
  9.0 0.1 stack.39.place_ref
  9.1 2.0 %shard_map.91 = (f32[256,128]{1,0:T(8,128)S(1)}, f32[256,128]{1,0:T(8,128)S(1)}) custom-call(s32[6]{0:T(128)S(1)} %stack.39.place_ref, f32[3840,128]{1,0:T(8,128)S(1)} %bitcast.8, f32[16,128]{1,0:T(8,128)S(1)} %copy-done.1), custom_call_target="tpu_custom_call" | custom-call | flops 1000000 | bytes 4000000 | tf_op jit(solution)/shard_map/pallas_call | solution.py:106
  11.1 0.1 collective-permute-start
  11.2 0.7 %collective-permute-start.1 = (f32[256,128]{1,0:T(8,128)S(1)}, f32[256,128]{1,0:T(8,128)S(1)}, u32[]{:S(2)}, u32[]{:S(2)}) collective-permute-start(f32[256,128]{1,0:T(8,128)S(1)} %get-tuple-element.17), channel_id=1, source_target_pairs={{4,8},{12,16},{20,24},{8,4},{16,12},{24,20},{5,9},{13,17},{21,25},... | collective-permute-start | bytes 393224 | tf_op jit(solution)/shard_map/ppermute | solution.py:506
  11.8 0.7 %collective-permute-done.even_ref = f32[256,128]{1,0:T(8,128)S(1)} collective-permute-done((f32[256,128]{1,0:T(8,128)S(1)}, f32[256,128]{1,0:T(8,128)S(1)}, u32[]{:S(2)}, u32[]{:S(2)}) %collective-permute-start) | collective-permute-done | bytes 131104 | tf_op jit(solution)/shard_map/ppermute | solution.py:506
  12.5 0.8 %shard_map.92 = (f32[240,128]{1,0:T(8,128)S(1)}, f32[240,128]{1,0:T(8,128)S(1)}, f32[16,128]{1,0:T(8,128)S(1)}, f32[136,128]{1,0:T(8,128)S(1)}, f32[136,128]{1,0:T(8,128)S(1)}) custom-call(s32[6]{0:T(128)S(1)} %stack.39.place_ref, f32[16,128]{1,0:T(8,128)S(1)} %copy-done.1, f32[256,128]{1,0:T(8,128)S(1)} %collective-permute-done.even_ref, ...), custom_call_target="tpu_custom_call" | custom-call | tf_op jit(solution)/shard_map/pallas_call | solution.py:152
  13.3 2.7 %collective-permute-start.4 = (f32[136,128]{1,0:T(8,128)S(1)}, f32[136,128]{1,0:T(8,128)S(1)}, u32[]{:S(2)}, u32[]{:S(2)}) collective-permute-start(f32[136,128]{1,0:T(8,128)S(1)} %get-tuple-element.23), channel_id=1, source_target_pairs={{0,1},{2,3},{1,0},{3,2},{4,5},{6,7},{5,4},{7,6},{8,9},{10,11},{9,8... | collective-permute-start | bytes 208904 | tf_op jit(solution)/shard_map/ppermute | solution.py:506
  16.0 0.7 %collective-permute-start.5 = (f32[136,128]{1,0:T(8,128)S(1)}, f32[136,128]{1,0:T(8,128)S(1)}, u32[]{:S(2)}, u32[]{:S(2)}) collective-permute-start(f32[136,128]{1,0:T(8,128)S(1)} %get-tuple-element.24), channel_id=1, source_target_pairs={{1,2},{2,1},{5,6},{6,5},{9,10},{10,9},{13,14},{14,13},{17,18},{18,... | collective-permute-start | bytes 208904 | tf_op jit(solution)/shard_map/ppermute | solution.py:506
  16.7 5.3 %shard_map.93.inner_ref = f32[3,16,80,256]{3,2,1,0:T(8,128)S(1)} custom-call(s32[6]{0:T(128)S(1)} %stack.39.place_ref, f32[3840,128]{1,0:T(8,128)S(1)} %bitcast.9, f32[240,128]{1,0:T(8,128)S(1)} %get-tuple-element.18.left_ref, f32[240,128]{1,0:T(8,128)S(1)} %get-tuple-element.19.right_ref, f32[16,128]{1,0:T(8,128)S(1)} %copy-done.1, ...), custom_call_target="tpu_custom_call" | custom-call | flops 30000000 | bytes 10000000 | tf_op jit(solution)/shard_map/pallas_call | solution.py:243
  22.0 10.7 %collective-permute-done.4.ceven_ref = f32[136,128]{1,0:T(8,128)S(1)} collective-permute-done((f32[136,128]{1,0:T(8,128)S(1)}, f32[136,128]{1,0:T(8,128)S(1)}, u32[]{:S(2)}, u32[]{:S(2)}) %collective-permute-start.4) | collective-permute-done | bytes 69664 | tf_op jit(solution)/shard_map/ppermute | solution.py:506
  32.8 6.7 %shard_map.95 = (f32[48,80,128]{2,1,0:T(8,128)S(1)}, f32[24,128]{1,0:T(8,128)S(1)}) custom-call(s32[6]{0:T(128)S(1)} %stack.39.place_ref, s32[24]{0:T(128)S(1)} %copy-done.2, s32[24]{0:T(128)S(1)} %copy-done.3, s32[24]{0:T(128)S(1)} %copy-done.8, f32[3,16,80,256]{3,2,1,0:T(8,128)S(1)} %shard_map.93.inner_ref, ...), custom_call_target="tpu_custom_call" | custom-call | flops 60000000 | bytes 30000000 | tf_op jit(solution)/shard_map/pallas_call | solution.py:353
  39.5 1.2 %collective-permute-done.6 = f32[24,128]{1,0:T(8,128)S(1)} collective-permute-done((f32[24,128]{1,0:T(8,128)S(1)}, f32[24,128]{1,0:T(8,128)S(1)}, u32[]{:S(2)}, u32[]{:S(2)}) %collective-permute-start.6) | collective-permute-done | bytes 12320 | tf_op jit(solution)/shard_map/ppermute | solution.py:517
  40.7 1.5 %collective-permute-start.7 = (f32[24,128]{1,0:T(8,128)S(1)}, f32[24,128]{1,0:T(8,128)S(1)}, u32[]{:S(2)}, u32[]{:S(2)}) collective-permute-start(f32[24,128]{1,0:T(8,128)S(1)} %add.19), channel_id=1, source_target_pairs={{0,8},{4,12},{8,0},{12,4},{16,24},{20,28},{24,16},{28,20},{1,9},{5... | collective-permute-start | bytes 36872 | tf_op jit(solution)/shard_map/ppermute | solution.py:517
  42.2 2.2 %collective-permute-done.7 = f32[24,128]{1,0:T(8,128)S(1)} collective-permute-done((f32[24,128]{1,0:T(8,128)S(1)}, f32[24,128]{1,0:T(8,128)S(1)}, u32[]{:S(2)}, u32[]{:S(2)}) %collective-permute-start.7) | collective-permute-done | bytes 12320 | tf_op jit(solution)/shard_map/ppermute | solution.py:517
  44.4 1.5 %collective-permute-start.8 = (f32[24,128]{1,0:T(8,128)S(1)}, f32[24,128]{1,0:T(8,128)S(1)}, u32[]{:S(2)}, u32[]{:S(2)}) collective-permute-start(f32[24,128]{1,0:T(8,128)S(1)} %add.20), channel_id=1, source_target_pairs={{0,16},{4,20},{8,24},{12,28},{16,0},{20,4},{24,8},{28,12},{1,17},{... | collective-permute-start | bytes 36872 | tf_op jit(solution)/shard_map/ppermute | solution.py:517
  45.8 2.2 %collective-permute-done.8 = f32[24,128]{1,0:T(8,128)S(1)} collective-permute-done((f32[24,128]{1,0:T(8,128)S(1)}, f32[24,128]{1,0:T(8,128)S(1)}, u32[]{:S(2)}, u32[]{:S(2)}) %collective-permute-start.8) | collective-permute-done | bytes 12320 | tf_op jit(solution)/shard_map/ppermute | solution.py:517
  48.1 1.5 %collective-permute-start.9 = (f32[24,128]{1,0:T(8,128)S(1)}, f32[24,128]{1,0:T(8,128)S(1)}, u32[]{:S(2)}, u32[]{:S(2)}) collective-permute-start(f32[24,128]{1,0:T(8,128)S(1)} %add.21), channel_id=1, source_target_pairs={{0,1},{1,0},{2,3},{3,2},{4,5},{5,4},{6,7},{7,6},{8,9},{9,8},{10,11... | collective-permute-start | bytes 36872 | tf_op jit(solution)/shard_map/ppermute | solution.py:517
  49.5 2.2 %collective-permute-done.9 = f32[24,128]{1,0:T(8,128)S(1)} collective-permute-done((f32[24,128]{1,0:T(8,128)S(1)}, f32[24,128]{1,0:T(8,128)S(1)}, u32[]{:S(2)}, u32[]{:S(2)}) %collective-permute-start.9) | collective-permute-done | bytes 12320 | tf_op jit(solution)/shard_map/ppermute | solution.py:517
  51.8 2.5 %collective-permute-start.10 = (f32[24,128]{1,0:T(8,128)S(1)}, f32[24,128]{1,0:T(8,128)S(1)}, u32[]{:S(2)}, u32[]{:S(2)}) collective-permute-start(f32[24,128]{1,0:T(8,128)S(1)} %add.22), channel_id=1, source_target_pairs={{0,2},{1,3},{2,0},{3,1},{4,6},{5,7},{6,4},{7,5},{8,10},{9,11},{10,... | collective-permute-start | bytes 36872 | tf_op jit(solution)/shard_map/ppermute | solution.py:517
  54.3 2.1 %collective-permute-done.10 = f32[24,128]{1,0:T(8,128)S(1)} collective-permute-done((f32[24,128]{1,0:T(8,128)S(1)}, f32[24,128]{1,0:T(8,128)S(1)}, u32[]{:S(2)}, u32[]{:S(2)}) %collective-permute-start.10) | collective-permute-done | bytes 12320 | tf_op jit(solution)/shard_map/ppermute | solution.py:517
  56.4 5.1 %shard_map.96 = f32[3840,128]{1,0:T(8,128)} custom-call(s32[6]{0:T(128)S(1)} %stack.39.place_ref, s32[24]{0:T(128)S(1)} %copy-done.2, s32[24]{0:T(128)S(1)} %copy-done.3, s32[24]{0:T(128)S(1)} %copy-done.4, f32[24]{0:T(128)S(1)} %copy-done.5, f32[24]{0:T(128)S(1)} %copy-done.6, f32[7]{0:T(128)S(1)} %copy-done.7, f32[24,128]{1,0:T(8,128)S(1)} %add.23.prior_ref, ...), custom_call_target="tpu_custom_call" | custom-call | tf_op jit(solution)/shard_map/pallas_call | solution.py:487
  (28 shorter events, 0.2 us)
Async XLA Ops:
  0.0 9.1 %copy-start = (f32[3,80,16,128]{3,2,1,0:T(8,128)S(1)}, f32[3,80,16,128]{3,2,1,0:T(8,128)}, u32[]{:S(2)}) copy-start(f32[3,80,16,128]{3,2,1,0:T(8,128)} %param.9) | copy-start | bytes 5898244
  0.0 9.1 %copy-start.1 = (f32[16,128]{1,0:T(8,128)S(1)}, f32[16,128]{1,0:T(8,128)}, u32[]{:S(2)}) copy-start(f32[16,128]{1,0:T(8,128)} %drag_ref.7) | copy-start | bytes 24580
  2.7 30.1 %collective-permute-start.2 = (f32[22,80,128]{2,1,0:T(8,128)}, f32[22,80,128]{2,1,0:T(8,128)S(1)}, u32[]{:S(2)}, u32[]{:S(2)}) collective-permute-start(f32[22,80,128]{2,1,0:T(8,128)} %get-tuple-element.21), channel_id=1, source_target_pairs={{0,1},{1,2},{2,3},{4,5},{5,6},{6,7},{8,9},{9,10},{10,11},{12,13},{... | collective-permute-start | bytes 2703368 | tf_op jit(solution)/shard_map/ppermute | solution.py:501
  7.7 25.1 %collective-permute-start.3 = (f32[22,80,128]{2,1,0:T(8,128)}, f32[22,80,128]{2,1,0:T(8,128)}, u32[]{:S(2)}, u32[]{:S(2)}) collective-permute-start(f32[22,80,128]{2,1,0:T(8,128)} %get-tuple-element.22), channel_id=1, source_target_pairs={{1,0},{2,1},{3,2},{5,4},{6,5},{7,6},{9,8},{10,9},{11,10},{13,12},{... | collective-permute-start | bytes 2703368 | tf_op jit(solution)/shard_map/ppermute | solution.py:501
  11.1 1.4 %collective-permute-start = (f32[256,128]{1,0:T(8,128)S(1)}, f32[256,128]{1,0:T(8,128)S(1)}, u32[]{:S(2)}, u32[]{:S(2)}) collective-permute-start(f32[256,128]{1,0:T(8,128)S(1)} %get-tuple-element.16), channel_id=1, source_target_pairs={{0,4},{8,12},{16,20},{24,28},{4,0},{12,8},{20,16},{28,24},{1,5},{9... | collective-permute-start | bytes 393224 | tf_op jit(solution)/shard_map/ppermute | solution.py:506
  11.2 1.3 %collective-permute-start.1 = (f32[256,128]{1,0:T(8,128)S(1)}, f32[256,128]{1,0:T(8,128)S(1)}, u32[]{:S(2)}, u32[]{:S(2)}) collective-permute-start(f32[256,128]{1,0:T(8,128)S(1)} %get-tuple-element.17), channel_id=1, source_target_pairs={{4,8},{12,16},{20,24},{8,4},{16,12},{24,20},{5,9},{13,17},{21,25},... | collective-permute-start | bytes 393224 | tf_op jit(solution)/shard_map/ppermute | solution.py:506
  13.3 19.5 %collective-permute-start.4 = (f32[136,128]{1,0:T(8,128)S(1)}, f32[136,128]{1,0:T(8,128)S(1)}, u32[]{:S(2)}, u32[]{:S(2)}) collective-permute-start(f32[136,128]{1,0:T(8,128)S(1)} %get-tuple-element.23), channel_id=1, source_target_pairs={{0,1},{2,3},{1,0},{3,2},{4,5},{6,7},{5,4},{7,6},{8,9},{10,11},{9,8... | collective-permute-start | bytes 208904 | tf_op jit(solution)/shard_map/ppermute | solution.py:506
  16.0 16.8 %collective-permute-start.5 = (f32[136,128]{1,0:T(8,128)S(1)}, f32[136,128]{1,0:T(8,128)S(1)}, u32[]{:S(2)}, u32[]{:S(2)}) collective-permute-start(f32[136,128]{1,0:T(8,128)S(1)} %get-tuple-element.24), channel_id=1, source_target_pairs={{1,2},{2,1},{5,6},{6,5},{9,10},{10,9},{13,14},{14,13},{17,18},{18,... | collective-permute-start | bytes 208904 | tf_op jit(solution)/shard_map/ppermute | solution.py:506
  16.6 16.1 %copy-start.2 = (s32[24]{0:T(128)S(1)}, s32[24]{0:T(128)}, u32[]{:S(2)}) copy-start(s32[24]{0:T(128)} %order_ref.3) | copy-start | bytes 292
  16.6 16.1 %copy-start.3 = (s32[24]{0:T(128)S(1)}, s32[24]{0:T(128)}, u32[]{:S(2)}) copy-start(s32[24]{0:T(128)} %owner_ref.3) | copy-start | bytes 292
  16.7 16.1 %copy-start.8 = (s32[24]{0:T(128)S(1)}, s32[24]{0:T(128)}, u32[]{:S(2)}) copy-start(s32[24]{0:T(128)} %cell_ref.1) | copy-start | bytes 292
  22.0 34.4 %copy-start.4 = (s32[24]{0:T(128)S(1)}, s32[24]{0:T(128)}, u32[]{:S(2)}) copy-start(s32[24]{0:T(128)} %reach_ref.1) | copy-start | bytes 292
  22.0 34.4 %copy-start.5 = (f32[24]{0:T(128)S(1)}, f32[24]{0:T(128)}, u32[]{:S(2)}) copy-start(f32[24]{0:T(128)} %value_ref.1) | copy-start | bytes 292
  22.0 34.4 %copy-start.6 = (f32[24]{0:T(128)S(1)}, f32[24]{0:T(128)}, u32[]{:S(2)}) copy-start(f32[24]{0:T(128)} %error_ref.1) | copy-start | bytes 292
  22.0 34.4 %copy-start.7 = (f32[7]{0:T(128)S(1)}, f32[7]{0:T(128)}, u32[]{:S(2)}) copy-start(f32[7]{0:T(128)} %taper_ref.1) | copy-start | bytes 88
  39.4 1.2 %collective-permute-start.6 = (f32[24,128]{1,0:T(8,128)S(1)}, f32[24,128]{1,0:T(8,128)S(1)}, u32[]{:S(2)}, u32[]{:S(2)}) collective-permute-start(f32[24,128]{1,0:T(8,128)S(1)} %get-tuple-element.25), channel_id=1, source_target_pairs={{0,4},{4,0},{8,12},{12,8},{16,20},{20,16},{24,28},{28,24},{1,5},{5... | collective-permute-start | bytes 36872 | tf_op jit(solution)/shard_map/ppermute | solution.py:517
  40.7 3.7 %collective-permute-start.7 = (f32[24,128]{1,0:T(8,128)S(1)}, f32[24,128]{1,0:T(8,128)S(1)}, u32[]{:S(2)}, u32[]{:S(2)}) collective-permute-start(f32[24,128]{1,0:T(8,128)S(1)} %add.19), channel_id=1, source_target_pairs={{0,8},{4,12},{8,0},{12,4},{16,24},{20,28},{24,16},{28,20},{1,9},{5... | collective-permute-start | bytes 36872 | tf_op jit(solution)/shard_map/ppermute | solution.py:517
  44.4 3.7 %collective-permute-start.8 = (f32[24,128]{1,0:T(8,128)S(1)}, f32[24,128]{1,0:T(8,128)S(1)}, u32[]{:S(2)}, u32[]{:S(2)}) collective-permute-start(f32[24,128]{1,0:T(8,128)S(1)} %add.20), channel_id=1, source_target_pairs={{0,16},{4,20},{8,24},{12,28},{16,0},{20,4},{24,8},{28,12},{1,17},{... | collective-permute-start | bytes 36872 | tf_op jit(solution)/shard_map/ppermute | solution.py:517
  48.1 3.7 %collective-permute-start.9 = (f32[24,128]{1,0:T(8,128)S(1)}, f32[24,128]{1,0:T(8,128)S(1)}, u32[]{:S(2)}, u32[]{:S(2)}) collective-permute-start(f32[24,128]{1,0:T(8,128)S(1)} %add.21), channel_id=1, source_target_pairs={{0,1},{1,0},{2,3},{3,2},{4,5},{5,4},{6,7},{7,6},{8,9},{9,8},{10,11... | collective-permute-start | bytes 36872 | tf_op jit(solution)/shard_map/ppermute | solution.py:517
  51.8 4.6 %collective-permute-start.10 = (f32[24,128]{1,0:T(8,128)S(1)}, f32[24,128]{1,0:T(8,128)S(1)}, u32[]{:S(2)}, u32[]{:S(2)}) collective-permute-start(f32[24,128]{1,0:T(8,128)S(1)} %add.22), channel_id=1, source_target_pairs={{0,2},{1,3},{2,0},{3,1},{4,6},{5,7},{6,4},{7,5},{8,10},{9,11},{10,... | collective-permute-start | bytes 36872 | tf_op jit(solution)/shard_map/ppermute | solution.py:517

commit v13 on v10

--- a/solution.py
+++ b/solution.py
@@ -509,10 +509,10 @@
         if count & (count - 1):
             x = lax.psum(x, axis)
             continue
-        span = 1
-        while span < count:
+        span = count // 2
+        while span:
             x = x + lax.ppermute(x, axis, [(i, i ^ span) for i in range(count)])
-            span *= 2
+            span //= 2
     return x
 
 
@@ -539,7 +539,7 @@
     even, odd = swap_pairs(even, "gy", 0), swap_pairs(odd, "gy", 1)
     inner = interior(place, flat, left, right, drag, margin, members)
     states, priors = forecast(place, order, owner, cell, inner, above, below, even, odd, drag, margin)
-    priors = add_over(priors, ("gy", "gx"))
+    priors = add_over(priors, ("gx", "gy"))
     result = assimilate(place, order, owner, reach, value, error, taper, priors, states, members, rows)
     return result.reshape(status.shape)
 

time: 62 us -> 61.9 us (level)
  starting transfers between devices: 15.7 us -> 17 us
  waiting for transfers between devices: 22.8 us -> 21.5 us
    ppermute x5, starting transfers between devices: 5.29 us -> 6.62 us  [add_over(): x = x + lax.ppermute(x, axis, [(i, i ^ span) for i in range(count)])]
    ppermute x5, waiting for transfers between devices: 11.6 us -> 10.3 us  [add_over(): x = x + lax.ppermute(x, axis, [(i, i ^ span) for i in range(count)])]
where the time goes in v13:
time: 61.9 us; the launch traced here: 61.7 us
  Pallas kernels  22.7 us (37%)
  waiting for transfers between devices  21.5 us (35%)
  starting transfers between devices  17 us (27%)
    ppermute x4, waiting for transfers between devices, swap_pairs(): return lax.ppermute(x, axis, pairs + [(b, a) for a, b in pairs])  11.2 us
    ppermute x5, waiting for transfers between devices, add_over(): x = x + lax.ppermute(x, axis, [(i, i ^ span) for i in range(count)])  10.3 us
    pallas_call x1, Pallas kernels, forecast(): pl.pallas_call(functools.partial(forecast_kernel, members, rows), out_sha...  6.75 us
    ppermute x5, starting transfers between devices, add_over(): x = x + lax.ppermute(x, axis, [(i, i ^ span) for i in range(count)])  6.62 us
    pallas_call x1, Pallas kernels, interior(): pl.pallas_call(functools.partial(interior_kernel, members, rows), out_sha...  5.45 us
    pallas_call x1, Pallas kernels, assimilate(): pl.pallas_call(functools.partial(assimilate_kernel, members, rows), out_s...  5.07 us
    ppermute x1, starting transfers between devices, to_neighbours(): lax.ppermute(upper, axis, forward)  4.98 us
    ppermute x4, starting transfers between devices, swap_pairs(): return lax.ppermute(x, axis, pairs + [(b, a) for a, b in pairs])  4.1 us
  transfers between devices with their start and end apart: 11, of which 7 were waited for; matrix products, arithmetic and copies ran while one was open for 0% of the time, Pallas kernels for 13%

profile of v13, /device:TPU:0, one launch (start us, length us, event | category | flops | bytes accessed | tf_op | source)
XLA Modules:
  0.0 61.7 jit_solution(9268060971680519009)
XLA Ops:
  0.0 2.7 %shard_map.94 = (f32[22,80,128]{2,1,0:T(8,128)}, f32[22,80,128]{2,1,0:T(8,128)}) custom-call(f32[3840,128]{1,0:T(8,128)} %bitcast.7), custom_call_target="tpu_custom_call" | custom-call | flops 1000000 | bytes 4000000 | tf_op jit(solution)/shard_map/pallas_call | solution.py:67
  2.7 5.0 %collective-permute-start.2 = (f32[22,80,128]{2,1,0:T(8,128)}, f32[22,80,128]{2,1,0:T(8,128)S(1)}, u32[]{:S(2)}, u32[]{:S(2)}) collective-permute-start(f32[22,80,128]{2,1,0:T(8,128)} %get-tuple-element.21), channel_id=1, source_target_pairs={{0,1},{1,2},{2,3},{4,5},{5,6},{6,7},{8,9},{9,10},{10,11},{12,13},{... | collective-permute-start | bytes 2703368 | tf_op jit(solution)/shard_map/ppermute | solution.py:498
  7.7 1.3 %collective-permute-start.3 = (f32[22,80,128]{2,1,0:T(8,128)}, f32[22,80,128]{2,1,0:T(8,128)}, u32[]{:S(2)}, u32[]{:S(2)}) collective-permute-start(f32[22,80,128]{2,1,0:T(8,128)} %get-tuple-element.22), channel_id=1, source_target_pairs={{1,0},{2,1},{3,2},{5,4},{6,5},{7,6},{9,8},{10,9},{11,10},{13,12},{... | collective-permute-start | bytes 2703368 | tf_op jit(solution)/shard_map/ppermute | solution.py:498
  9.0 0.1 stack.39.place_ref
  9.1 2.0 %shard_map.91 = (f32[256,128]{1,0:T(8,128)S(1)}, f32[256,128]{1,0:T(8,128)S(1)}) custom-call(s32[6]{0:T(128)S(1)} %stack.39.place_ref, f32[3840,128]{1,0:T(8,128)S(1)} %bitcast.8, f32[16,128]{1,0:T(8,128)S(1)} %copy-done.1), custom_call_target="tpu_custom_call" | custom-call | flops 1000000 | bytes 4000000 | tf_op jit(solution)/shard_map/pallas_call | solution.py:105
  11.1 0.1 collective-permute-start
  11.2 0.7 %collective-permute-start.1 = (f32[256,128]{1,0:T(8,128)S(1)}, f32[256,128]{1,0:T(8,128)S(1)}, u32[]{:S(2)}, u32[]{:S(2)}) collective-permute-start(f32[256,128]{1,0:T(8,128)S(1)} %get-tuple-element.17), channel_id=1, source_target_pairs={{4,8},{12,16},{20,24},{8,4},{16,12},{24,20},{5,9},{13,17},{21,25},... | collective-permute-start | bytes 393224 | tf_op jit(solution)/shard_map/ppermute | solution.py:503
  11.8 0.7 %collective-permute-done.even_ref = f32[256,128]{1,0:T(8,128)S(1)} collective-permute-done((f32[256,128]{1,0:T(8,128)S(1)}, f32[256,128]{1,0:T(8,128)S(1)}, u32[]{:S(2)}, u32[]{:S(2)}) %collective-permute-start) | collective-permute-done | bytes 131104 | tf_op jit(solution)/shard_map/ppermute | solution.py:503
  12.5 0.8 %shard_map.92 = (f32[240,128]{1,0:T(8,128)S(1)}, f32[240,128]{1,0:T(8,128)S(1)}, f32[16,128]{1,0:T(8,128)S(1)}, f32[136,128]{1,0:T(8,128)S(1)}, f32[136,128]{1,0:T(8,128)S(1)}) custom-call(s32[6]{0:T(128)S(1)} %stack.39.place_ref, f32[16,128]{1,0:T(8,128)S(1)} %copy-done.1, f32[256,128]{1,0:T(8,128)S(1)} %collective-permute-done.even_ref, ...), custom_call_target="tpu_custom_call" | custom-call | tf_op jit(solution)/shard_map/pallas_call | solution.py:151
  13.3 2.7 %collective-permute-start.4 = (f32[136,128]{1,0:T(8,128)S(1)}, f32[136,128]{1,0:T(8,128)S(1)}, u32[]{:S(2)}, u32[]{:S(2)}) collective-permute-start(f32[136,128]{1,0:T(8,128)S(1)} %get-tuple-element.23), channel_id=1, source_target_pairs={{0,1},{2,3},{1,0},{3,2},{4,5},{6,7},{5,4},{7,6},{8,9},{10,11},{9,8... | collective-permute-start | bytes 208904 | tf_op jit(solution)/shard_map/ppermute | solution.py:503
  16.0 0.7 %collective-permute-start.5 = (f32[136,128]{1,0:T(8,128)S(1)}, f32[136,128]{1,0:T(8,128)S(1)}, u32[]{:S(2)}, u32[]{:S(2)}) collective-permute-start(f32[136,128]{1,0:T(8,128)S(1)} %get-tuple-element.24), channel_id=1, source_target_pairs={{1,2},{2,1},{5,6},{6,5},{9,10},{10,9},{13,14},{14,13},{17,18},{18,... | collective-permute-start | bytes 208904 | tf_op jit(solution)/shard_map/ppermute | solution.py:503
  16.7 5.5 %shard_map.93.inner_ref = f32[3,16,80,256]{3,2,1,0:T(8,128)S(1)} custom-call(s32[6]{0:T(128)S(1)} %stack.39.place_ref, f32[3840,128]{1,0:T(8,128)S(1)} %bitcast.9, f32[240,128]{1,0:T(8,128)S(1)} %get-tuple-element.18.left_ref, f32[240,128]{1,0:T(8,128)S(1)} %get-tuple-element.19.right_ref, f32[16,128]{1,0:T(8,128)S(1)} %copy-done.1, ...), custom_call_target="tpu_custom_call" | custom-call | flops 30000000 | bytes 10000000 | tf_op jit(solution)/shard_map/pallas_call | solution.py:242
  22.2 10.5 %collective-permute-done.4.ceven_ref = f32[136,128]{1,0:T(8,128)S(1)} collective-permute-done((f32[136,128]{1,0:T(8,128)S(1)}, f32[136,128]{1,0:T(8,128)S(1)}, u32[]{:S(2)}, u32[]{:S(2)}) %collective-permute-start.4) | collective-permute-done | bytes 69664 | tf_op jit(solution)/shard_map/ppermute | solution.py:503
  32.8 6.7 %shard_map.95 = (f32[48,80,128]{2,1,0:T(8,128)S(1)}, f32[24,128]{1,0:T(8,128)S(1)}) custom-call(s32[6]{0:T(128)S(1)} %stack.39.place_ref, s32[24]{0:T(128)S(1)} %copy-done.2, s32[24]{0:T(128)S(1)} %copy-done.3, s32[24]{0:T(128)S(1)} %copy-done.8, f32[3,16,80,256]{3,2,1,0:T(8,128)S(1)} %shard_map.93.inner_ref, ...), custom_call_target="tpu_custom_call" | custom-call | flops 60000000 | bytes 30000000 | tf_op jit(solution)/shard_map/pallas_call | solution.py:350
  39.5 1.6 %collective-permute-start.6 = (f32[24,128]{1,0:T(8,128)S(1)}, f32[24,128]{1,0:T(8,128)S(1)}, u32[]{:S(2)}, u32[]{:S(2)}) collective-permute-start(f32[24,128]{1,0:T(8,128)S(1)} %get-tuple-element.25), channel_id=1, source_target_pairs={{0,16},{4,20},{8,24},{12,28},{16,0},{20,4},{24,8},{28,12},{1,17},{... | collective-permute-start | bytes 36872 | tf_op jit(solution)/shard_map/ppermute | solution.py:514
  41.1 2.2 %collective-permute-done.6 = f32[24,128]{1,0:T(8,128)S(1)} collective-permute-done((f32[24,128]{1,0:T(8,128)S(1)}, f32[24,128]{1,0:T(8,128)S(1)}, u32[]{:S(2)}, u32[]{:S(2)}) %collective-permute-start.6) | collective-permute-done | bytes 12320 | tf_op jit(solution)/shard_map/ppermute | solution.py:514
  43.3 1.3 %collective-permute-start.7 = (f32[24,128]{1,0:T(8,128)S(1)}, f32[24,128]{1,0:T(8,128)S(1)}, u32[]{:S(2)}, u32[]{:S(2)}) collective-permute-start(f32[24,128]{1,0:T(8,128)S(1)} %add.19), channel_id=1, source_target_pairs={{0,8},{4,12},{8,0},{12,4},{16,24},{20,28},{24,16},{28,20},{1,9},{5... | collective-permute-start | bytes 36872 | tf_op jit(solution)/shard_map/ppermute | solution.py:514
  44.6 2.4 %collective-permute-done.7 = f32[24,128]{1,0:T(8,128)S(1)} collective-permute-done((f32[24,128]{1,0:T(8,128)S(1)}, f32[24,128]{1,0:T(8,128)S(1)}, u32[]{:S(2)}, u32[]{:S(2)}) %collective-permute-start.7) | collective-permute-done | bytes 12320 | tf_op jit(solution)/shard_map/ppermute | solution.py:514
  47.0 1.2 %collective-permute-done.8 = f32[24,128]{1,0:T(8,128)S(1)} collective-permute-done((f32[24,128]{1,0:T(8,128)S(1)}, f32[24,128]{1,0:T(8,128)S(1)}, u32[]{:S(2)}, u32[]{:S(2)}) %collective-permute-start.8) | collective-permute-done | bytes 12320 | tf_op jit(solution)/shard_map/ppermute | solution.py:514
  48.2 2.3 %collective-permute-start.9 = (f32[24,128]{1,0:T(8,128)S(1)}, f32[24,128]{1,0:T(8,128)S(1)}, u32[]{:S(2)}, u32[]{:S(2)}) collective-permute-start(f32[24,128]{1,0:T(8,128)S(1)} %add.21), channel_id=1, source_target_pairs={{0,2},{1,3},{2,0},{3,1},{4,6},{5,7},{6,4},{7,5},{8,10},{9,11},{10,... | collective-permute-start | bytes 36872 | tf_op jit(solution)/shard_map/ppermute | solution.py:514
  50.5 2.3 %collective-permute-done.9 = f32[24,128]{1,0:T(8,128)S(1)} collective-permute-done((f32[24,128]{1,0:T(8,128)S(1)}, f32[24,128]{1,0:T(8,128)S(1)}, u32[]{:S(2)}, u32[]{:S(2)}) %collective-permute-start.9) | collective-permute-done | bytes 12320 | tf_op jit(solution)/shard_map/ppermute | solution.py:514
  52.8 1.4 %collective-permute-start.10 = (f32[24,128]{1,0:T(8,128)S(1)}, f32[24,128]{1,0:T(8,128)S(1)}, u32[]{:S(2)}, u32[]{:S(2)}) collective-permute-start(f32[24,128]{1,0:T(8,128)S(1)} %add.22), channel_id=1, source_target_pairs={{0,1},{1,0},{2,3},{3,2},{4,5},{5,4},{6,7},{7,6},{8,9},{9,8},{10,11... | collective-permute-start | bytes 36872 | tf_op jit(solution)/shard_map/ppermute | solution.py:514
  54.2 2.3 %collective-permute-done.10 = f32[24,128]{1,0:T(8,128)S(1)} collective-permute-done((f32[24,128]{1,0:T(8,128)S(1)}, f32[24,128]{1,0:T(8,128)S(1)}, u32[]{:S(2)}, u32[]{:S(2)}) %collective-permute-start.10) | collective-permute-done | bytes 12320 | tf_op jit(solution)/shard_map/ppermute | solution.py:514
  56.5 5.1 %shard_map.96 = f32[3840,128]{1,0:T(8,128)} custom-call(s32[6]{0:T(128)S(1)} %stack.39.place_ref, s32[24]{0:T(128)S(1)} %copy-done.2, s32[24]{0:T(128)S(1)} %copy-done.3, s32[24]{0:T(128)S(1)} %copy-done.4, f32[24]{0:T(128)S(1)} %copy-done.5, f32[24]{0:T(128)S(1)} %copy-done.6, f32[7]{0:T(128)S(1)} %copy-done.7, f32[24,128]{1,0:T(8,128)S(1)} %add.23.prior_ref, ...), custom_call_target="tpu_custom_call" | custom-call | tf_op jit(solution)/shard_map/pallas_call | solution.py:484
  (28 shorter events, 0.1 us)
Async XLA Ops:
  0.0 9.1 %copy-start = (f32[3,80,16,128]{3,2,1,0:T(8,128)S(1)}, f32[3,80,16,128]{3,2,1,0:T(8,128)}, u32[]{:S(2)}) copy-start(f32[3,80,16,128]{3,2,1,0:T(8,128)} %param.9) | copy-start | bytes 5898244
  0.0 9.1 %copy-start.1 = (f32[16,128]{1,0:T(8,128)S(1)}, f32[16,128]{1,0:T(8,128)}, u32[]{:S(2)}) copy-start(f32[16,128]{1,0:T(8,128)} %drag_ref.7) | copy-start | bytes 24580
  2.7 30.1 %collective-permute-start.2 = (f32[22,80,128]{2,1,0:T(8,128)}, f32[22,80,128]{2,1,0:T(8,128)S(1)}, u32[]{:S(2)}, u32[]{:S(2)}) collective-permute-start(f32[22,80,128]{2,1,0:T(8,128)} %get-tuple-element.21), channel_id=1, source_target_pairs={{0,1},{1,2},{2,3},{4,5},{5,6},{6,7},{8,9},{9,10},{10,11},{12,13},{... | collective-permute-start | bytes 2703368 | tf_op jit(solution)/shard_map/ppermute | solution.py:498
  7.7 25.1 %collective-permute-start.3 = (f32[22,80,128]{2,1,0:T(8,128)}, f32[22,80,128]{2,1,0:T(8,128)}, u32[]{:S(2)}, u32[]{:S(2)}) collective-permute-start(f32[22,80,128]{2,1,0:T(8,128)} %get-tuple-element.22), channel_id=1, source_target_pairs={{1,0},{2,1},{3,2},{5,4},{6,5},{7,6},{9,8},{10,9},{11,10},{13,12},{... | collective-permute-start | bytes 2703368 | tf_op jit(solution)/shard_map/ppermute | solution.py:498
  11.1 1.4 %collective-permute-start = (f32[256,128]{1,0:T(8,128)S(1)}, f32[256,128]{1,0:T(8,128)S(1)}, u32[]{:S(2)}, u32[]{:S(2)}) collective-permute-start(f32[256,128]{1,0:T(8,128)S(1)} %get-tuple-element.16), channel_id=1, source_target_pairs={{0,4},{8,12},{16,20},{24,28},{4,0},{12,8},{20,16},{28,24},{1,5},{9... | collective-permute-start | bytes 393224 | tf_op jit(solution)/shard_map/ppermute | solution.py:503
  11.2 1.3 %collective-permute-start.1 = (f32[256,128]{1,0:T(8,128)S(1)}, f32[256,128]{1,0:T(8,128)S(1)}, u32[]{:S(2)}, u32[]{:S(2)}) collective-permute-start(f32[256,128]{1,0:T(8,128)S(1)} %get-tuple-element.17), channel_id=1, source_target_pairs={{4,8},{12,16},{20,24},{8,4},{16,12},{24,20},{5,9},{13,17},{21,25},... | collective-permute-start | bytes 393224 | tf_op jit(solution)/shard_map/ppermute | solution.py:503
  13.3 19.5 %collective-permute-start.4 = (f32[136,128]{1,0:T(8,128)S(1)}, f32[136,128]{1,0:T(8,128)S(1)}, u32[]{:S(2)}, u32[]{:S(2)}) collective-permute-start(f32[136,128]{1,0:T(8,128)S(1)} %get-tuple-element.23), channel_id=1, source_target_pairs={{0,1},{2,3},{1,0},{3,2},{4,5},{6,7},{5,4},{7,6},{8,9},{10,11},{9,8... | collective-permute-start | bytes 208904 | tf_op jit(solution)/shard_map/ppermute | solution.py:503
  16.0 16.8 %collective-permute-start.5 = (f32[136,128]{1,0:T(8,128)S(1)}, f32[136,128]{1,0:T(8,128)S(1)}, u32[]{:S(2)}, u32[]{:S(2)}) collective-permute-start(f32[136,128]{1,0:T(8,128)S(1)} %get-tuple-element.24), channel_id=1, source_target_pairs={{1,2},{2,1},{5,6},{6,5},{9,10},{10,9},{13,14},{14,13},{17,18},{18,... | collective-permute-start | bytes 208904 | tf_op jit(solution)/shard_map/ppermute | solution.py:503
  16.6 16.1 %copy-start.2 = (s32[24]{0:T(128)S(1)}, s32[24]{0:T(128)}, u32[]{:S(2)}) copy-start(s32[24]{0:T(128)} %order_ref.3) | copy-start | bytes 292
  16.6 16.1 %copy-start.3 = (s32[24]{0:T(128)S(1)}, s32[24]{0:T(128)}, u32[]{:S(2)}) copy-start(s32[24]{0:T(128)} %owner_ref.3) | copy-start | bytes 292
  16.7 16.1 %copy-start.8 = (s32[24]{0:T(128)S(1)}, s32[24]{0:T(128)}, u32[]{:S(2)}) copy-start(s32[24]{0:T(128)} %cell_ref.1) | copy-start | bytes 292
  22.1 34.3 %copy-start.4 = (s32[24]{0:T(128)S(1)}, s32[24]{0:T(128)}, u32[]{:S(2)}) copy-start(s32[24]{0:T(128)} %reach_ref.1) | copy-start | bytes 292
  22.1 34.3 %copy-start.5 = (f32[24]{0:T(128)S(1)}, f32[24]{0:T(128)}, u32[]{:S(2)}) copy-start(f32[24]{0:T(128)} %value_ref.1) | copy-start | bytes 292
  22.1 34.3 %copy-start.6 = (f32[24]{0:T(128)S(1)}, f32[24]{0:T(128)}, u32[]{:S(2)}) copy-start(f32[24]{0:T(128)} %error_ref.1) | copy-start | bytes 292
  22.2 34.3 %copy-start.7 = (f32[7]{0:T(128)S(1)}, f32[7]{0:T(128)}, u32[]{:S(2)}) copy-start(f32[7]{0:T(128)} %taper_ref.1) | copy-start | bytes 88
  39.5 3.8 %collective-permute-start.6 = (f32[24,128]{1,0:T(8,128)S(1)}, f32[24,128]{1,0:T(8,128)S(1)}, u32[]{:S(2)}, u32[]{:S(2)}) collective-permute-start(f32[24,128]{1,0:T(8,128)S(1)} %get-tuple-element.25), channel_id=1, source_target_pairs={{0,16},{4,20},{8,24},{12,28},{16,0},{20,4},{24,8},{28,12},{1,17},{... | collective-permute-start | bytes 36872 | tf_op jit(solution)/shard_map/ppermute | solution.py:514
  43.3 3.7 %collective-permute-start.7 = (f32[24,128]{1,0:T(8,128)S(1)}, f32[24,128]{1,0:T(8,128)S(1)}, u32[]{:S(2)}, u32[]{:S(2)}) collective-permute-start(f32[24,128]{1,0:T(8,128)S(1)} %add.19), channel_id=1, source_target_pairs={{0,8},{4,12},{8,0},{12,4},{16,24},{20,28},{24,16},{28,20},{1,9},{5... | collective-permute-start | bytes 36872 | tf_op jit(solution)/shard_map/ppermute | solution.py:514
  47.0 1.2 %collective-permute-start.8 = (f32[24,128]{1,0:T(8,128)S(1)}, f32[24,128]{1,0:T(8,128)S(1)}, u32[]{:S(2)}, u32[]{:S(2)}) collective-permute-start(f32[24,128]{1,0:T(8,128)S(1)} %add.20), channel_id=1, source_target_pairs={{0,4},{4,0},{8,12},{12,8},{16,20},{20,16},{24,28},{28,24},{1,5},{5... | collective-permute-start | bytes 36872 | tf_op jit(solution)/shard_map/ppermute | solution.py:514
  48.2 4.6 %collective-permute-start.9 = (f32[24,128]{1,0:T(8,128)S(1)}, f32[24,128]{1,0:T(8,128)S(1)}, u32[]{:S(2)}, u32[]{:S(2)}) collective-permute-start(f32[24,128]{1,0:T(8,128)S(1)} %add.21), channel_id=1, source_target_pairs={{0,2},{1,3},{2,0},{3,1},{4,6},{5,7},{6,4},{7,5},{8,10},{9,11},{10,... | collective-permute-start | bytes 36872 | tf_op jit(solution)/shard_map/ppermute | solution.py:514
  52.8 3.7 %collective-permute-start.10 = (f32[24,128]{1,0:T(8,128)S(1)}, f32[24,128]{1,0:T(8,128)S(1)}, u32[]{:S(2)}, u32[]{:S(2)}) collective-permute-start(f32[24,128]{1,0:T(8,128)S(1)} %add.22), channel_id=1, source_target_pairs={{0,1},{1,0},{2,3},{3,2},{4,5},{5,4},{6,7},{7,6},{8,9},{9,8},{10,11... | collective-permute-start | bytes 36872 | tf_op jit(solution)/shard_map/ppermute | solution.py:514

commit v14 on v10

--- a/solution.py
+++ b/solution.py
@@ -461,7 +461,7 @@
     low = jnp.concatenate([low, zero], axis=1)
     factor = (high + roll_lanes(high, members) + roll_lanes(low, 2 * members)).astype(BF16)
 
-    block = 4
+    block = 8
     for at in range(0, 3 * rows, block):
         x = jnp.concatenate([forecast_ref[at + b] for b in range(block)], axis=1)
         xh = x.astype(BF16)
@@ -539,7 +539,7 @@
     even, odd = swap_pairs(even, "gy", 0), swap_pairs(odd, "gy", 1)
     inner = interior(place, flat, left, right, drag, margin, members)
     states, priors = forecast(place, order, owner, cell, inner, above, below, even, odd, drag, margin)
-    priors = add_over(priors, ("gy", "gx"))
+    priors = add_over(priors, ("gx", "gy"))
     result = assimilate(place, order, owner, reach, value, error, taper, priors, states, members, rows)
     return result.reshape(status.shape)
 

time: 62 us -> 61.8 us (level)
  starting transfers between devices: 15.7 us -> 17.3 us
  waiting for transfers between devices: 22.8 us -> 21.2 us
    ppermute x5, waiting for transfers between devices: 11.6 us -> 9.99 us  [add_over(): x = x + lax.ppermute(x, axis, [(i, i ^ span) for i in range(count)])]
    ppermute x5, starting transfers between devices: 5.29 us -> 6.92 us  [add_over(): x = x + lax.ppermute(x, axis, [(i, i ^ span) for i in range(count)])]
where the time goes in v14:
time: 61.8 us; the launch traced here: 61.6 us
  Pallas kernels  22.6 us (37%)
  waiting for transfers between devices  21.2 us (34%)
  starting transfers between devices  17.3 us (28%)
    ppermute x4, waiting for transfers between devices, swap_pairs(): return lax.ppermute(x, axis, pairs + [(b, a) for a, b in pairs])  11.2 us
    ppermute x5, waiting for transfers between devices, add_over(): x = x + lax.ppermute(x, axis, [(i, i ^ span) for i in range(count)])  9.99 us
    ppermute x5, starting transfers between devices, add_over(): x = x + lax.ppermute(x, axis, [(i, i ^ span) for i in range(count)])  6.92 us
    pallas_call x1, Pallas kernels, forecast(): pl.pallas_call(functools.partial(forecast_kernel, members, rows), out_sha...  6.63 us
    pallas_call x1, Pallas kernels, interior(): pl.pallas_call(functools.partial(interior_kernel, members, rows), out_sha...  5.45 us
    pallas_call x1, Pallas kernels, assimilate(): pl.pallas_call(functools.partial(assimilate_kernel, members, rows), out_s...  5.07 us
    ppermute x1, starting transfers between devices, to_neighbours(): lax.ppermute(upper, axis, forward)  4.98 us
    ppermute x4, starting transfers between devices, swap_pairs(): return lax.ppermute(x, axis, pairs + [(b, a) for a, b in pairs])  4.1 us
  transfers between devices with their start and end apart: 11, of which 7 were waited for; matrix products, arithmetic and copies ran while one was open for 0% of the time, Pallas kernels for 13%

profile of v14, /device:TPU:0, one launch (start us, length us, event | category | flops | bytes accessed | tf_op | source)
XLA Modules:
  0.0 61.6 jit_solution(13323263920191671673)
XLA Ops:
  0.0 2.7 %shard_map.94 = (f32[22,80,128]{2,1,0:T(8,128)}, f32[22,80,128]{2,1,0:T(8,128)}) custom-call(f32[3840,128]{1,0:T(8,128)} %bitcast.7), custom_call_target="tpu_custom_call" | custom-call | flops 1000000 | bytes 4000000 | tf_op jit(solution)/shard_map/pallas_call | solution.py:67
  2.7 5.0 %collective-permute-start.2 = (f32[22,80,128]{2,1,0:T(8,128)}, f32[22,80,128]{2,1,0:T(8,128)S(1)}, u32[]{:S(2)}, u32[]{:S(2)}) collective-permute-start(f32[22,80,128]{2,1,0:T(8,128)} %get-tuple-element.21), channel_id=1, source_target_pairs={{0,1},{1,2},{2,3},{4,5},{5,6},{6,7},{8,9},{9,10},{10,11},{12,13},{... | collective-permute-start | bytes 2703368 | tf_op jit(solution)/shard_map/ppermute | solution.py:498
  7.7 1.3 %collective-permute-start.3 = (f32[22,80,128]{2,1,0:T(8,128)}, f32[22,80,128]{2,1,0:T(8,128)}, u32[]{:S(2)}, u32[]{:S(2)}) collective-permute-start(f32[22,80,128]{2,1,0:T(8,128)} %get-tuple-element.22), channel_id=1, source_target_pairs={{1,0},{2,1},{3,2},{5,4},{6,5},{7,6},{9,8},{10,9},{11,10},{13,12},{... | collective-permute-start | bytes 2703368 | tf_op jit(solution)/shard_map/ppermute | solution.py:498
  9.0 0.1 stack.39.place_ref
  9.1 2.0 %shard_map.91 = (f32[256,128]{1,0:T(8,128)S(1)}, f32[256,128]{1,0:T(8,128)S(1)}) custom-call(s32[6]{0:T(128)S(1)} %stack.39.place_ref, f32[3840,128]{1,0:T(8,128)S(1)} %bitcast.8, f32[16,128]{1,0:T(8,128)S(1)} %copy-done.1), custom_call_target="tpu_custom_call" | custom-call | flops 1000000 | bytes 4000000 | tf_op jit(solution)/shard_map/pallas_call | solution.py:105
  11.1 0.1 collective-permute-start
  11.2 0.7 %collective-permute-start.1 = (f32[256,128]{1,0:T(8,128)S(1)}, f32[256,128]{1,0:T(8,128)S(1)}, u32[]{:S(2)}, u32[]{:S(2)}) collective-permute-start(f32[256,128]{1,0:T(8,128)S(1)} %get-tuple-element.17), channel_id=1, source_target_pairs={{4,8},{12,16},{20,24},{8,4},{16,12},{24,20},{5,9},{13,17},{21,25},... | collective-permute-start | bytes 393224 | tf_op jit(solution)/shard_map/ppermute | solution.py:503
  11.8 0.7 %collective-permute-done.even_ref = f32[256,128]{1,0:T(8,128)S(1)} collective-permute-done((f32[256,128]{1,0:T(8,128)S(1)}, f32[256,128]{1,0:T(8,128)S(1)}, u32[]{:S(2)}, u32[]{:S(2)}) %collective-permute-start) | collective-permute-done | bytes 131104 | tf_op jit(solution)/shard_map/ppermute | solution.py:503
  12.5 0.8 %shard_map.92 = (f32[240,128]{1,0:T(8,128)S(1)}, f32[240,128]{1,0:T(8,128)S(1)}, f32[16,128]{1,0:T(8,128)S(1)}, f32[136,128]{1,0:T(8,128)S(1)}, f32[136,128]{1,0:T(8,128)S(1)}) custom-call(s32[6]{0:T(128)S(1)} %stack.39.place_ref, f32[16,128]{1,0:T(8,128)S(1)} %copy-done.1, f32[256,128]{1,0:T(8,128)S(1)} %collective-permute-done.even_ref, ...), custom_call_target="tpu_custom_call" | custom-call | tf_op jit(solution)/shard_map/pallas_call | solution.py:151
  13.3 2.7 %collective-permute-start.4 = (f32[136,128]{1,0:T(8,128)S(1)}, f32[136,128]{1,0:T(8,128)S(1)}, u32[]{:S(2)}, u32[]{:S(2)}) collective-permute-start(f32[136,128]{1,0:T(8,128)S(1)} %get-tuple-element.23), channel_id=1, source_target_pairs={{0,1},{2,3},{1,0},{3,2},{4,5},{6,7},{5,4},{7,6},{8,9},{10,11},{9,8... | collective-permute-start | bytes 208904 | tf_op jit(solution)/shard_map/ppermute | solution.py:503
  16.0 0.7 %collective-permute-start.5 = (f32[136,128]{1,0:T(8,128)S(1)}, f32[136,128]{1,0:T(8,128)S(1)}, u32[]{:S(2)}, u32[]{:S(2)}) collective-permute-start(f32[136,128]{1,0:T(8,128)S(1)} %get-tuple-element.24), channel_id=1, source_target_pairs={{1,2},{2,1},{5,6},{6,5},{9,10},{10,9},{13,14},{14,13},{17,18},{18,... | collective-permute-start | bytes 208904 | tf_op jit(solution)/shard_map/ppermute | solution.py:503
  16.7 5.5 %shard_map.93.inner_ref = f32[3,16,80,256]{3,2,1,0:T(8,128)S(1)} custom-call(s32[6]{0:T(128)S(1)} %stack.39.place_ref, f32[3840,128]{1,0:T(8,128)S(1)} %bitcast.9, f32[240,128]{1,0:T(8,128)S(1)} %get-tuple-element.18.left_ref, f32[240,128]{1,0:T(8,128)S(1)} %get-tuple-element.19.right_ref, f32[16,128]{1,0:T(8,128)S(1)} %copy-done.1, ...), custom_call_target="tpu_custom_call" | custom-call | flops 30000000 | bytes 10000000 | tf_op jit(solution)/shard_map/pallas_call | solution.py:242
  22.2 10.5 %collective-permute-done.4.ceven_ref = f32[136,128]{1,0:T(8,128)S(1)} collective-permute-done((f32[136,128]{1,0:T(8,128)S(1)}, f32[136,128]{1,0:T(8,128)S(1)}, u32[]{:S(2)}, u32[]{:S(2)}) %collective-permute-start.4) | collective-permute-done | bytes 69664 | tf_op jit(solution)/shard_map/ppermute | solution.py:503
  32.8 6.6 %shard_map.95 = (f32[48,80,128]{2,1,0:T(8,128)S(1)}, f32[24,128]{1,0:T(8,128)S(1)}) custom-call(s32[6]{0:T(128)S(1)} %stack.39.place_ref, s32[24]{0:T(128)S(1)} %copy-done.2, s32[24]{0:T(128)S(1)} %copy-done.3, s32[24]{0:T(128)S(1)} %copy-done.8, f32[3,16,80,256]{3,2,1,0:T(8,128)S(1)} %shard_map.93.inner_ref, ...), custom_call_target="tpu_custom_call" | custom-call | flops 60000000 | bytes 30000000 | tf_op jit(solution)/shard_map/pallas_call | solution.py:350
  39.5 1.2 %collective-permute-done.6 = f32[24,128]{1,0:T(8,128)S(1)} collective-permute-done((f32[24,128]{1,0:T(8,128)S(1)}, f32[24,128]{1,0:T(8,128)S(1)}, u32[]{:S(2)}, u32[]{:S(2)}) %collective-permute-start.6) | collective-permute-done | bytes 12320 | tf_op jit(solution)/shard_map/ppermute | solution.py:514
  40.6 1.6 %collective-permute-start.7 = (f32[24,128]{1,0:T(8,128)S(1)}, f32[24,128]{1,0:T(8,128)S(1)}, u32[]{:S(2)}, u32[]{:S(2)}) collective-permute-start(f32[24,128]{1,0:T(8,128)S(1)} %add.19), channel_id=1, source_target_pairs={{0,8},{4,12},{8,0},{12,4},{16,24},{20,28},{24,16},{28,20},{1,9},{5... | collective-permute-start | bytes 36872 | tf_op jit(solution)/shard_map/ppermute | solution.py:514
  42.2 2.1 %collective-permute-done.7 = f32[24,128]{1,0:T(8,128)S(1)} collective-permute-done((f32[24,128]{1,0:T(8,128)S(1)}, f32[24,128]{1,0:T(8,128)S(1)}, u32[]{:S(2)}, u32[]{:S(2)}) %collective-permute-start.7) | collective-permute-done | bytes 12320 | tf_op jit(solution)/shard_map/ppermute | solution.py:514
  44.3 1.4 %collective-permute-start.8 = (f32[24,128]{1,0:T(8,128)S(1)}, f32[24,128]{1,0:T(8,128)S(1)}, u32[]{:S(2)}, u32[]{:S(2)}) collective-permute-start(f32[24,128]{1,0:T(8,128)S(1)} %add.20), channel_id=1, source_target_pairs={{0,16},{4,20},{8,24},{12,28},{16,0},{20,4},{24,8},{28,12},{1,17},{... | collective-permute-start | bytes 36872 | tf_op jit(solution)/shard_map/ppermute | solution.py:514
  45.8 2.3 %collective-permute-done.8 = f32[24,128]{1,0:T(8,128)S(1)} collective-permute-done((f32[24,128]{1,0:T(8,128)S(1)}, f32[24,128]{1,0:T(8,128)S(1)}, u32[]{:S(2)}, u32[]{:S(2)}) %collective-permute-start.8) | collective-permute-done | bytes 12320 | tf_op jit(solution)/shard_map/ppermute | solution.py:514
  48.0 1.4 %collective-permute-start.9 = (f32[24,128]{1,0:T(8,128)S(1)}, f32[24,128]{1,0:T(8,128)S(1)}, u32[]{:S(2)}, u32[]{:S(2)}) collective-permute-start(f32[24,128]{1,0:T(8,128)S(1)} %add.21), channel_id=1, source_target_pairs={{0,1},{1,0},{2,3},{3,2},{4,5},{5,4},{6,7},{7,6},{8,9},{9,8},{10,11... | collective-permute-start | bytes 36872 | tf_op jit(solution)/shard_map/ppermute | solution.py:514
  49.5 2.3 %collective-permute-done.9 = f32[24,128]{1,0:T(8,128)S(1)} collective-permute-done((f32[24,128]{1,0:T(8,128)S(1)}, f32[24,128]{1,0:T(8,128)S(1)}, u32[]{:S(2)}, u32[]{:S(2)}) %collective-permute-start.9) | collective-permute-done | bytes 12320 | tf_op jit(solution)/shard_map/ppermute | solution.py:514
  51.7 2.4 %collective-permute-start.10 = (f32[24,128]{1,0:T(8,128)S(1)}, f32[24,128]{1,0:T(8,128)S(1)}, u32[]{:S(2)}, u32[]{:S(2)}) collective-permute-start(f32[24,128]{1,0:T(8,128)S(1)} %add.22), channel_id=1, source_target_pairs={{0,2},{1,3},{2,0},{3,1},{4,6},{5,7},{6,4},{7,5},{8,10},{9,11},{10,... | collective-permute-start | bytes 36872 | tf_op jit(solution)/shard_map/ppermute | solution.py:514
  54.2 2.2 %collective-permute-done.10 = f32[24,128]{1,0:T(8,128)S(1)} collective-permute-done((f32[24,128]{1,0:T(8,128)S(1)}, f32[24,128]{1,0:T(8,128)S(1)}, u32[]{:S(2)}, u32[]{:S(2)}) %collective-permute-start.10) | collective-permute-done | bytes 12320 | tf_op jit(solution)/shard_map/ppermute | solution.py:514
  56.4 5.1 %shard_map.96 = f32[3840,128]{1,0:T(8,128)} custom-call(s32[6]{0:T(128)S(1)} %stack.39.place_ref, s32[24]{0:T(128)S(1)} %copy-done.2, s32[24]{0:T(128)S(1)} %copy-done.3, s32[24]{0:T(128)S(1)} %copy-done.4, f32[24]{0:T(128)S(1)} %copy-done.5, f32[24]{0:T(128)S(1)} %copy-done.6, f32[7]{0:T(128)S(1)} %copy-done.7, f32[24,128]{1,0:T(8,128)S(1)} %add.23.prior_ref, ...), custom_call_target="tpu_custom_call" | custom-call | tf_op jit(solution)/shard_map/pallas_call | solution.py:484
  (28 shorter events, 0.2 us)
Async XLA Ops:
  0.0 9.1 %copy-start = (f32[3,80,16,128]{3,2,1,0:T(8,128)S(1)}, f32[3,80,16,128]{3,2,1,0:T(8,128)}, u32[]{:S(2)}) copy-start(f32[3,80,16,128]{3,2,1,0:T(8,128)} %param.9) | copy-start | bytes 5898244
  0.0 9.1 %copy-start.1 = (f32[16,128]{1,0:T(8,128)S(1)}, f32[16,128]{1,0:T(8,128)}, u32[]{:S(2)}) copy-start(f32[16,128]{1,0:T(8,128)} %drag_ref.7) | copy-start | bytes 24580
  2.7 30.1 %collective-permute-start.2 = (f32[22,80,128]{2,1,0:T(8,128)}, f32[22,80,128]{2,1,0:T(8,128)S(1)}, u32[]{:S(2)}, u32[]{:S(2)}) collective-permute-start(f32[22,80,128]{2,1,0:T(8,128)} %get-tuple-element.21), channel_id=1, source_target_pairs={{0,1},{1,2},{2,3},{4,5},{5,6},{6,7},{8,9},{9,10},{10,11},{12,13},{... | collective-permute-start | bytes 2703368 | tf_op jit(solution)/shard_map/ppermute | solution.py:498
  7.7 25.1 %collective-permute-start.3 = (f32[22,80,128]{2,1,0:T(8,128)}, f32[22,80,128]{2,1,0:T(8,128)}, u32[]{:S(2)}, u32[]{:S(2)}) collective-permute-start(f32[22,80,128]{2,1,0:T(8,128)} %get-tuple-element.22), channel_id=1, source_target_pairs={{1,0},{2,1},{3,2},{5,4},{6,5},{7,6},{9,8},{10,9},{11,10},{13,12},{... | collective-permute-start | bytes 2703368 | tf_op jit(solution)/shard_map/ppermute | solution.py:498
  11.1 1.4 %collective-permute-start = (f32[256,128]{1,0:T(8,128)S(1)}, f32[256,128]{1,0:T(8,128)S(1)}, u32[]{:S(2)}, u32[]{:S(2)}) collective-permute-start(f32[256,128]{1,0:T(8,128)S(1)} %get-tuple-element.16), channel_id=1, source_target_pairs={{0,4},{8,12},{16,20},{24,28},{4,0},{12,8},{20,16},{28,24},{1,5},{9... | collective-permute-start | bytes 393224 | tf_op jit(solution)/shard_map/ppermute | solution.py:503
  11.2 1.3 %collective-permute-start.1 = (f32[256,128]{1,0:T(8,128)S(1)}, f32[256,128]{1,0:T(8,128)S(1)}, u32[]{:S(2)}, u32[]{:S(2)}) collective-permute-start(f32[256,128]{1,0:T(8,128)S(1)} %get-tuple-element.17), channel_id=1, source_target_pairs={{4,8},{12,16},{20,24},{8,4},{16,12},{24,20},{5,9},{13,17},{21,25},... | collective-permute-start | bytes 393224 | tf_op jit(solution)/shard_map/ppermute | solution.py:503
  13.3 19.5 %collective-permute-start.4 = (f32[136,128]{1,0:T(8,128)S(1)}, f32[136,128]{1,0:T(8,128)S(1)}, u32[]{:S(2)}, u32[]{:S(2)}) collective-permute-start(f32[136,128]{1,0:T(8,128)S(1)} %get-tuple-element.23), channel_id=1, source_target_pairs={{0,1},{2,3},{1,0},{3,2},{4,5},{6,7},{5,4},{7,6},{8,9},{10,11},{9,8... | collective-permute-start | bytes 208904 | tf_op jit(solution)/shard_map/ppermute | solution.py:503
  16.0 16.8 %collective-permute-start.5 = (f32[136,128]{1,0:T(8,128)S(1)}, f32[136,128]{1,0:T(8,128)S(1)}, u32[]{:S(2)}, u32[]{:S(2)}) collective-permute-start(f32[136,128]{1,0:T(8,128)S(1)} %get-tuple-element.24), channel_id=1, source_target_pairs={{1,2},{2,1},{5,6},{6,5},{9,10},{10,9},{13,14},{14,13},{17,18},{18,... | collective-permute-start | bytes 208904 | tf_op jit(solution)/shard_map/ppermute | solution.py:503
  16.6 16.1 %copy-start.2 = (s32[24]{0:T(128)S(1)}, s32[24]{0:T(128)}, u32[]{:S(2)}) copy-start(s32[24]{0:T(128)} %order_ref.3) | copy-start | bytes 292
  16.6 16.1 %copy-start.3 = (s32[24]{0:T(128)S(1)}, s32[24]{0:T(128)}, u32[]{:S(2)}) copy-start(s32[24]{0:T(128)} %owner_ref.3) | copy-start | bytes 292
  16.7 16.1 %copy-start.8 = (s32[24]{0:T(128)S(1)}, s32[24]{0:T(128)}, u32[]{:S(2)}) copy-start(s32[24]{0:T(128)} %cell_ref.1) | copy-start | bytes 292
  22.1 34.2 %copy-start.4 = (s32[24]{0:T(128)S(1)}, s32[24]{0:T(128)}, u32[]{:S(2)}) copy-start(s32[24]{0:T(128)} %reach_ref.1) | copy-start | bytes 292
  22.1 34.2 %copy-start.5 = (f32[24]{0:T(128)S(1)}, f32[24]{0:T(128)}, u32[]{:S(2)}) copy-start(f32[24]{0:T(128)} %value_ref.1) | copy-start | bytes 292
  22.1 34.2 %copy-start.6 = (f32[24]{0:T(128)S(1)}, f32[24]{0:T(128)}, u32[]{:S(2)}) copy-start(f32[24]{0:T(128)} %error_ref.1) | copy-start | bytes 292
  22.2 34.2 %copy-start.7 = (f32[7]{0:T(128)S(1)}, f32[7]{0:T(128)}, u32[]{:S(2)}) copy-start(f32[7]{0:T(128)} %taper_ref.1) | copy-start | bytes 88
  39.4 1.2 %collective-permute-start.6 = (f32[24,128]{1,0:T(8,128)S(1)}, f32[24,128]{1,0:T(8,128)S(1)}, u32[]{:S(2)}, u32[]{:S(2)}) collective-permute-start(f32[24,128]{1,0:T(8,128)S(1)} %get-tuple-element.25), channel_id=1, source_target_pairs={{0,4},{4,0},{8,12},{12,8},{16,20},{20,16},{24,28},{28,24},{1,5},{5... | collective-permute-start | bytes 36872 | tf_op jit(solution)/shard_map/ppermute | solution.py:514
  40.6 3.7 %collective-permute-start.7 = (f32[24,128]{1,0:T(8,128)S(1)}, f32[24,128]{1,0:T(8,128)S(1)}, u32[]{:S(2)}, u32[]{:S(2)}) collective-permute-start(f32[24,128]{1,0:T(8,128)S(1)} %add.19), channel_id=1, source_target_pairs={{0,8},{4,12},{8,0},{12,4},{16,24},{20,28},{24,16},{28,20},{1,9},{5... | collective-permute-start | bytes 36872 | tf_op jit(solution)/shard_map/ppermute | solution.py:514
  44.3 3.7 %collective-permute-start.8 = (f32[24,128]{1,0:T(8,128)S(1)}, f32[24,128]{1,0:T(8,128)S(1)}, u32[]{:S(2)}, u32[]{:S(2)}) collective-permute-start(f32[24,128]{1,0:T(8,128)S(1)} %add.20), channel_id=1, source_target_pairs={{0,16},{4,20},{8,24},{12,28},{16,0},{20,4},{24,8},{28,12},{1,17},{... | collective-permute-start | bytes 36872 | tf_op jit(solution)/shard_map/ppermute | solution.py:514
  48.0 3.7 %collective-permute-start.9 = (f32[24,128]{1,0:T(8,128)S(1)}, f32[24,128]{1,0:T(8,128)S(1)}, u32[]{:S(2)}, u32[]{:S(2)}) collective-permute-start(f32[24,128]{1,0:T(8,128)S(1)} %add.21), channel_id=1, source_target_pairs={{0,1},{1,0},{2,3},{3,2},{4,5},{5,4},{6,7},{7,6},{8,9},{9,8},{10,11... | collective-permute-start | bytes 36872 | tf_op jit(solution)/shard_map/ppermute | solution.py:514
  51.7 4.6 %collective-permute-start.10 = (f32[24,128]{1,0:T(8,128)S(1)}, f32[24,128]{1,0:T(8,128)S(1)}, u32[]{:S(2)}, u32[]{:S(2)}) collective-permute-start(f32[24,128]{1,0:T(8,128)S(1)} %add.22), channel_id=1, source_target_pairs={{0,2},{1,3},{2,0},{3,1},{4,6},{5,7},{6,4},{7,5},{8,10},{9,11},{10,... | collective-permute-start | bytes 36872 | tf_op jit(solution)/shard_map/ppermute | solution.py:514
